TPU v7x, 32 devices: a whole 2x2x4 slice. The times are simulated.
32 devices in a mesh: expert: 8 (over z, y), tensor: 4 (over x, core).
Axes of the slice: x: 2, y: 2, z: 4, core: 2. Of those that a mesh axis runs over, the one named last changes fastest.
Arguments:
- attn_heads: bfloat16 [1024, 4096], P('expert', 'tensor'), may hold values from -6 to 6
- out_proj: bfloat16 [4096, 4096], P('tensor', 'expert'), may hold values from -0.09375 to 0.09375
- residual: bfloat16 [1024, 4096], P('expert'), may hold values from -6 to 6
- norm_gain: float32 [4096], replicated, may hold values from 0.1 to 1.9
- route_ids: int32 [1024, 8], P('expert'), may hold values from 0 to 63, all different within a row; in each aligned block of 128 rows (0 to 127, 128 to 255, ...) at most 18 rows name the same one
- route_weights: float32 [1024, 8], P('expert'), may hold values from 0.05 to 1
- w_gate: bfloat16 [64, 4096, 1536], P('expert', None, 'tensor'), may hold values from -0.09375 to 0.09375
- w_up: bfloat16 [64, 4096, 1536], P('expert', None, 'tensor'), may hold values from -0.09375 to 0.09375
- w_down: bfloat16 [64, 1536, 4096], P('expert', 'tensor'), may hold values from -0.15625 to 0.15625
Outputs:
- layer_out: bfloat16 [1024, 4096], P('expert', 'tensor')
Inputs may be any that keep to these rules, and one draw needn't show every extreme that they name: `route_ids`: each row names 8 different experts. In aligned blocks of 128 rows no expert is named more than 18 times, a bound that some block reaches.
All inputs are finite; a program needn't handle non-finite values.
Results may differ from a plain program's by a relative error of at most 0.015.
Values may be sent and summed in bfloat16 or wider, within the bound.
No kernel may reach another device: no remote copies, remote signals or barrier semaphores. Data moves between devices by JAX's collectives and lax.ppermute only.
A program may use at most 192 MiB of HBM per device.

v0:
```python
import jax
import jax.numpy as jnp
from jax import lax
from jax.sharding import PartitionSpec as P

EXPERTS = 64
CAP = 18


def slot_places(ids, experts, capacity):
    row_count, top_count = ids.shape
    onehot = (ids[:, :, None] == jnp.arange(experts, dtype=jnp.int32)[None, None, :]).astype(
        jnp.int32
    )
    flattened = onehot.reshape(row_count * top_count, experts)
    before = jnp.cumsum(flattened, axis=0) - flattened
    slot_rank = jnp.sum(before * flattened, axis=1).reshape(row_count, top_count)
    return ids * capacity + slot_rank


def per_device(
    attn_heads, out_proj, residual, norm_gain, route_ids, route_weights, w_gate, w_up, w_down
):
    model_width = residual.shape[1]
    groups = lax.axis_size("expert")
    members = lax.axis_size("tensor")
    member = lax.axis_index("tensor")
    per_group = w_gate.shape[0]
    slot_count = EXPERTS * CAP
    block_cols = model_width // members
    heads_out = jnp.dot(
        attn_heads,
        lax.all_gather(out_proj, "expert", axis=1, tiled=True),
        preferred_element_type=jnp.float32,
    )
    attn_out = lax.psum(heads_out.astype(jnp.bfloat16), "tensor").astype(jnp.float32)
    hidden = residual.astype(jnp.float32) + attn_out
    normed = (
        hidden * lax.rsqrt(jnp.mean(hidden * hidden, axis=-1, keepdims=True) + 1e-06) * norm_gain
    ).astype(jnp.bfloat16)
    slot_index = slot_places(route_ids, EXPERTS, CAP)
    slot_range = jnp.arange(slot_count, dtype=jnp.int32)
    slot_hits = jnp.sum(
        (slot_index[:, :, None] == slot_range[None, None, :]).astype(jnp.bfloat16), axis=1
    )
    buffer = jnp.einsum("rj,rd->jd", slot_hits, normed, preferred_element_type=jnp.float32).astype(
        jnp.bfloat16
    )
    buffer = buffer.reshape(groups, per_group, CAP, model_width)
    arrived = lax.all_to_all(buffer, "expert", split_axis=0, concat_axis=0, tiled=True)
    gate_acc = jnp.einsum("gxcd,xdf->gxcf", arrived, w_gate, preferred_element_type=jnp.float32)
    upper = jnp.einsum("gxcd,xdf->gxcf", arrived, w_up, preferred_element_type=jnp.float32)
    activation = (jax.nn.silu(gate_acc) * upper).astype(jnp.bfloat16)
    product_term = jnp.einsum(
        "gxcf,xfd->gxcd", activation, w_down, preferred_element_type=jnp.float32
    )
    product_term = lax.optimization_barrier(product_term.astype(jnp.bfloat16)).astype(jnp.float32)
    product_term = product_term.reshape(
        groups, per_group, CAP, 1 * lax.axis_size("tensor"), block_cols
    )
    shares = lax.psum_scatter(
        jnp.transpose(product_term, (3, 0, 1, 2, 4)).astype(jnp.bfloat16),
        "tensor",
        scatter_dimension=0,
        tiled=True,
    ).astype(jnp.float32)
    expert_out = shares[0].astype(jnp.bfloat16)
    returned = lax.all_to_all(expert_out, "expert", split_axis=0, concat_axis=0, tiled=True)
    weights = route_weights / jnp.sum(route_weights, axis=-1, keepdims=True)
    picked = returned.reshape(slot_count, block_cols)[slot_index]
    mixture = jnp.sum(weights[:, :, None] * picked.astype(jnp.float32), axis=1)
    own_hidden = lax.dynamic_slice_in_dim(hidden, member * block_cols, block_cols, 1)
    return (own_hidden + mixture).astype(jnp.bfloat16)


def solution(mesh):
    placed = (
        P("expert", "tensor"),
        P("tensor", "expert"),
        P("expert", None),
        P(),
        P("expert", None),
        P("expert", None),
        P("expert", None, "tensor"),
        P("expert", None, "tensor"),
        P("expert", "tensor", None),
    )
    return jax.shard_map(
        per_device, mesh=mesh, in_specs=placed, out_specs=P("expert", "tensor"), check_vma=False
    )
```

profile of v0, /device:TPU:0, one launch (start us, length us, event | category | flops | bytes accessed | tf_op | source)
XLA Modules:
  0.0 689.8 jit_solution(7179085933123367455)
XLA Ops:
  6.5 0.0 copy-start
  6.5 0.0 all-gather.2.cloned.1.call-start
  6.5 0.7 all-gather.2.cloned.1.call-update
  7.3 0.0 all-reduce.2.cloned.1.call-start
  7.3 0.8 copy.51
  8.1 0.1 eq.43
  8.2 0.1 eq.39
  8.3 18.0 %reduce-window.6 = s32[64,8,128]{2,1,0:T(8,128)S(1)} reduce-window(s32[64,8,128]{2,1,0:T(8,128)S(1)} %fusion.31, s32[]{:T(128)} %constant.11.clone.1), window={size=1x1x128 pad=0_0x0_0x127_0}, to_apply=%region_2.0 | reduce-window | flops 8323072 | bytes 524292 | tf_op jit(solution)/shard_map/reduce-window
  26.3 0.1 slice.10
  26.4 0.1 copy.53
  26.6 0.1 copy.54
  26.7 0.1 broadcast_add_fusion
  26.9 0.0 copy-start.5
  26.9 0.0 copy-start.2
  26.9 110.8 %all-gather.2.cloned.1.call-done = bf16[1024,4096]{1,0:T(8,128)(2,1)} async-done(((bf16[1024,512]{1,0:T(8,128)(2,1)}), bf16[1024,4096]{1,0:T(8,128)(2,1)}) %all-gather.2.cloned.1.call-update) | async-done | bytes 8388624 | tf_op jit(solution)/shard_map/all_gather | solution.py:33
  137.7 0.0 copy-done
  137.7 5.7 convolution_convert_fusion.1
  143.4 0.0 copy-start.6
  143.4 0.0 all-reduce.2.cloned.1.call-update
  143.4 0.0 reduce-scatter.2.cloned.1.call-start
  143.5 0.1 fusion.30
  143.6 0.1 reshape.43
  143.7 0.0 copy-done.5
  143.7 0.1 copy.56
  143.8 1.5 fusion.12
  145.3 32.5 %all-reduce.2.cloned.1.call-done = bf16[128,4096]{1,0:T(8,128)(2,1)} async-done(((bf16[128,4096]{1,0:T(8,128)(2,1)}), bf16[128,4096]{1,0:T(8,128)(2,1)}) %all-reduce.2.cloned.1.call-update) | async-done | bytes 1048592 | tf_op jit(solution)/shard_map/psum | solution.py:36
  177.8 0.0 copy-done.2
  177.8 0.0 copy-start.3
  177.8 3.0 convert_add_fusion
  180.9 0.0 copy-done.6
  180.9 0.0 copy-done.3
  180.9 5.1 convolution_convert_fusion
  186.0 13.9 %reshape.44 = bf16[8,8,18,4096]{3,2,1,0:T(8,128)(2,1)} reshape(bf16[1152,4096]{1,0:T(8,128)(2,1)} %convolution_convert_fusion) | data formatting | bytes 18874368 | tf_op jit(solution)/shard_map/reshape | solution.py:49
  199.9 14.2 %copy.57 = bf16[8,8,18,4096]{3,1,2,0:T(8,128)(2,1)} copy(bf16[8,8,18,4096]{3,2,1,0:T(8,128)(2,1)} %reshape.44) | data formatting | bytes 18874368 | tf_op jit(solution)/shard_map/reshape | solution.py:49
  214.1 211.7 %all_to_all.10 = bf16[8,8,18,4096]{3,1,2,0:T(8,128)(2,1)} all-to-all(bf16[8,8,18,4096]{3,1,2,0:T(8,128)(2,1)} %copy.57), channel_id=1, replica_groups=mesh['expert'=8,'tensor'=4] {'expert'}, dimensions={0} | all-to-all | bytes 18874368 | tf_op jit(solution)/shard_map/all_to_all | solution.py:50
  425.9 25.5 %fusion.2 = f32[8,8,18,384]{3,2,1,0:T(8,128)} fusion(bf16[8,4096,384]{2,1,0:T(8,128)(2,1)} %param.16, bf16[8,8,18,4096]{3,1,2,0:T(8,128)(2,1)} %all_to_all.10), kind=kOutput, calls=%fused_computation.3 | convolution fusion | flops 3623878656 | bytes 36372480 | tf_op jit(solution)/shard_map/gxcd,xdf->gxcf/dot_general | solution.py:52
  451.3 29.4 %fusion.13.clone.4 = bf16[8,8,18,384]{3,2,0,1:T(8,128)(2,1)S(1)} fusion(f32[8,8,18,384]{3,2,1,0:T(8,128)} %fusion.2, bf16[8,4096,384]{2,1,0:T(8,128)(2,1)} %param.15, bf16[8,8,18,4096]{3,1,2,0:T(8,128)(2,1)} %all_to_all.10), kind=kOutput, calls=%fused_computation.18.clone.clone.clone.1 | convolution fusion | flops 3626532864 | bytes 37257216 | tf_op jit(solution)/shard_map/gxcd,xdf->gxcf/dot_general | solution.py:51
  480.7 20.9 %convert_bitcast_fusion = bf16[8,8,18,4096]{3,2,0,1:T(8,128)(2,1)} fusion(bf16[8,384,4096]{2,1,0:T(8,128)(2,1)} %param.17, bf16[8,8,18,384]{3,2,0,1:T(8,128)(2,1)S(1)} %fusion.13.clone.4), kind=kOutput, calls=%fused_computation.10 | convolution fusion | flops 3628597248 | bytes 35487744 | tf_op jit(solution)/shard_map/gxcf,xfd->gxcd/dot_general | solution.py:54
  501.6 15.5 %reshape.60 = bf16[8,8,18,4,1024]{4,3,2,0,1:T(4,128)(2,1)} reshape(bf16[8,8,18,4096]{3,2,0,1:T(8,128)(2,1)} %convert_bitcast_fusion) | data formatting | bytes 18874368 | tf_op jit(solution)/shard_map/convert_element_type | solution.py:62
  517.1 12.6 %copy.61 = bf16[4,8,8,18,1024]{4,2,3,1,0:T(8,128)(2,1)} copy(bf16[4,8,8,18,1024]{4,0,3,1,2:T(4,128)(2,1)} %bitcast.85) | data formatting | bytes 18874368 | tf_op jit(solution)/shard_map/convert_element_type | solution.py:62
  529.7 0.0 reduce-scatter.2.cloned.1.call-update
  529.7 0.0 copy-start.4
  529.8 77.1 %reduce-scatter.2.cloned.1.call-done = bf16[1,8,8,18,1024]{4,2,3,1,0:T(8,128)(2,1)} async-done(((bf16[4,8,8,18,1024]{4,2,3,1,0:T(8,128)(2,1)}), bf16[1,8,8,18,1024]{4,2,3,1,0:T(8,128)(2,1)}) %reduce-scatter.2.cloned.1.call-update) | async-done | bytes 2359312 | tf_op jit(solution)/shard_map/reduce_scatter | solution.py:61
  606.9 5.8 all-to-all-start.1
  612.7 0.1 copy.63
  612.8 0.1 reshape.48
  612.9 0.0 copy-done.4
  613.0 0.1 copy.50
  613.1 53.4 %all-to-all-done.1 = bf16[8,8,18,1024]{3,1,2,0:T(8,128)(2,1)S(1)} async-done(((bf16[8,8,18,1024]{3,1,2,0:T(8,128)(2,1)}), bf16[8,8,18,1024]{3,1,2,0:T(8,128)(2,1)S(1)}, u32[]{:S(2)}, u32[]{:S(2)}) %all-to-all-start.1) | async-done | bytes 2359328 | tf_op jit(solution)/shard_map/all_to_all | solution.py:68
  666.5 3.2 copy.62
  669.7 2.9 reshape.45
  672.6 0.0 copy-start.1
  672.7 5.4 gather_fusion
  678.0 2.9 fusion.11
  680.9 1.8 add_convert_fusion
  682.8 0.0 copy-done.1
  (9 shorter events, 0.1 us)
Async XLA Ops:
  6.5 131.1 %copy-start = (bf16[128,1024]{1,0:T(8,128)(2,1)S(1)}, bf16[128,1024]{1,0:T(8,128)(2,1)}, u32[]{:S(2)}) copy-start(bf16[128,1024]{1,0:T(8,128)(2,1)} %param.9) | copy-start | bytes 786436
  6.5 131.1 %all-gather.2.cloned.1.call-start = ((), (), s32[]{:S(2)}) async-start(), calls=%async_computation.3 | async-start | bytes 9437184 | tf_op jit(solution)/shard_map/all_gather | solution.py:33
  7.3 170.6 %all-reduce.2.cloned.1.call-start = ((), (), s32[]{:S(2)}) async-start(), calls=%async_computation.4 | async-start | bytes 2097152 | tf_op jit(solution)/shard_map/psum | solution.py:36
  26.9 116.8 %copy-start.5 = (s32[128,8]{0,1:T(8,128)S(1)}, s32[128,8]{0,1:T(8,128)}, u32[]{:S(2)}) copy-start(s32[128,8]{0,1:T(8,128)} %param.13) | copy-start | bytes 12292
  26.9 151.0 %copy-start.2 = (bf16[128,4096]{1,0:T(8,128)(2,1)S(1)}, bf16[128,4096]{1,0:T(8,128)(2,1)}, u32[]{:S(2)}) copy-start(bf16[128,4096]{1,0:T(8,128)(2,1)} %param.11) | copy-start | bytes 3145732
  143.4 37.5 %copy-start.6 = (f32[4096]{0:T(1024)S(1)}, f32[4096]{0:T(1024)}, u32[]{:S(2)}) copy-start(f32[4096]{0:T(1024)} %param.12) | copy-start | bytes 49156
  143.4 463.4 %reduce-scatter.2.cloned.1.call-start = ((), (), s32[]{:S(2)}) async-start(), calls=%async_computation.5 | async-start | bytes 11796480 | tf_op jit(solution)/shard_map/reduce_scatter | solution.py:61
  177.8 3.0 copy-start.3
  529.7 83.2 %copy-start.4 = (f32[128,8]{0,1:T(8,128)S(1)}, f32[128,8]{0,1:T(8,128)}, u32[]{:S(2)}) copy-start(f32[128,8]{0,1:T(8,128)} %param.14) | copy-start | bytes 12292
  606.9 59.6 %all-to-all-start.1 = ((bf16[8,8,18,1024]{3,1,2,0:T(8,128)(2,1)}), bf16[8,8,18,1024]{3,1,2,0:T(8,128)(2,1)S(1)}, u32[]{:S(2)}, u32[]{:S(2)}) async-start(bf16[8,8,18,1024]{3,1,2,0:T(8,128)(2,1)} %bitcast.86), calls=%async_computation.2 | async-start | bytes 4718592 | tf_op jit(solution)/shard_map/all_to_all | solution.py:68
  672.6 10.1 %copy-start.1 = (bf16[128,1024]{1,0:T(8,128)(2,1)S(1)}, bf16[128,1024]{1,0:T(8,128)(2,1)}, u32[]{:S(2)}) copy-start(bf16[128,1024]{1,0:T(8,128)(2,1)} %param.9) | copy-start | bytes 786436
Sparse Core Ops, SparseCore 0:
  9.4 128.2 all-gather.1
  143.5 34.2 all-reduce.1
  529.9 76.9 reduce-scatter.1
where the time goes:
time: 699 us; the launch traced here: 690 us
  waiting for transfers between devices  275 us (39%)
  blocking collectives  212 us (30%)
  matrix products  86.6 us (12%)
  local copies, waits for them, and re-layouts  69.6 us (10%)
  other arithmetic  27.5 us (4%)
  between operations  13.8 us (2%)
    all_to_all x1, blocking collectives, per_device(): lax.all_to_all(buffer, 'expert', split_axis=0, concat_axis=0, tiled=True)  212 us
    all_gather x1, waiting for transfers between devices, per_device(): lax.all_gather(out_proj, 'expert', axis=1, tiled=True)  111 us
    reduce_scatter x1, waiting for transfers between devices, per_device(): lax.psum_scatter(jnp.transpose(product_term, (3, 0, 1, 2, 4)).astype(jnp....  77.1 us
    all_to_all x1, waiting for transfers between devices, per_device(): lax.all_to_all(expert_out, 'expert', split_axis=0, concat_axis=0, tiled=T...  53.4 us
    psum x1, waiting for transfers between devices, per_device(): lax.psum(heads_out.astype(jnp.bfloat16), 'tensor').astype(jnp.float32)  32.5 us
    dot_general x1, matrix products, per_device(): jnp.einsum('gxcd,xdf->gxcf', arrived, w_gate, preferred_element_type=jnp....  29.4 us
    reshape x2, local copies, waits for them, and re-layouts, per_device(): buffer = buffer.reshape(groups, per_group, CAP, model_width)  28.1 us
    convert_element_type x2, local copies, waits for them, and re-layouts, per_device(): jnp.transpose(product_term, (3, 0, 1, 2, 4)).astype(jnp.bfloat16)  28.1 us
  transfers between devices with their start and end apart: 4, of which 4 were waited for; matrix products, arithmetic and copies ran while one was open for 3% of the time, Pallas kernels for 0%

commit v1 on v0

v1 whole, which is shorter than its diff:
```python
import functools

import jax
import jax.numpy as jnp
from jax import lax
from jax.experimental import pallas as pl
from jax.experimental.pallas import tpu as pltpu
from jax.sharding import PartitionSpec as P

EXPERTS = 64
CAP = 18
BF16 = jnp.bfloat16
F32 = jnp.float32
PAIR = 2
LANES = 128
VMEM_BYTES = 56 * 1024 * 1024


def slot_places(ids, experts, capacity):
    row_count, top_count = ids.shape
    onehot = (ids[:, :, None] == jnp.arange(experts, dtype=jnp.int32)[None, None, :]).astype(
        jnp.int32
    )
    flattened = onehot.reshape(row_count * top_count, experts)
    before = jnp.cumsum(flattened, axis=0) - flattened
    slot_rank = jnp.sum(before * flattened, axis=1).reshape(row_count, top_count)
    return ids * capacity + slot_rank


def per_device_slots(
    attn_heads, out_proj, residual, norm_gain, route_ids, route_weights, w_gate, w_up, w_down
):
    model_width = residual.shape[1]
    groups = lax.axis_size("expert")
    members = lax.axis_size("tensor")
    member = lax.axis_index("tensor")
    per_group = w_gate.shape[0]
    slot_count = EXPERTS * CAP
    block_cols = model_width // members
    heads_out = jnp.dot(
        attn_heads,
        lax.all_gather(out_proj, "expert", axis=1, tiled=True),
        preferred_element_type=F32,
    )
    attn_out = lax.psum(heads_out.astype(BF16), "tensor").astype(F32)
    hidden = residual.astype(F32) + attn_out
    normed = (
        hidden * lax.rsqrt(jnp.mean(hidden * hidden, axis=-1, keepdims=True) + 1e-06) * norm_gain
    ).astype(BF16)
    slot_index = slot_places(route_ids, EXPERTS, CAP)
    slot_range = jnp.arange(slot_count, dtype=jnp.int32)
    slot_hits = jnp.sum(
        (slot_index[:, :, None] == slot_range[None, None, :]).astype(BF16), axis=1
    )
    buffer = jnp.einsum("rj,rd->jd", slot_hits, normed, preferred_element_type=F32).astype(BF16)
    buffer = buffer.reshape(groups, per_group, CAP, model_width)
    arrived = lax.all_to_all(buffer, "expert", split_axis=0, concat_axis=0, tiled=True)
    gate_acc = jnp.einsum("gxcd,xdf->gxcf", arrived, w_gate, preferred_element_type=F32)
    upper = jnp.einsum("gxcd,xdf->gxcf", arrived, w_up, preferred_element_type=F32)
    activation = (jax.nn.silu(gate_acc) * upper).astype(BF16)
    product_term = jnp.einsum("gxcf,xfd->gxcd", activation, w_down, preferred_element_type=F32)
    product_term = product_term.astype(BF16).reshape(groups, per_group, CAP, members, block_cols)
    expert_out = lax.psum_scatter(
        jnp.transpose(product_term, (3, 0, 1, 2, 4)), "tensor", scatter_dimension=0, tiled=True
    )[0]
    returned = lax.all_to_all(expert_out, "expert", split_axis=0, concat_axis=0, tiled=True)
    weights = route_weights / jnp.sum(route_weights, axis=-1, keepdims=True)
    picked = returned.reshape(slot_count, block_cols)[slot_index]
    mixture = jnp.sum(weights[:, :, None] * picked.astype(F32), axis=1)
    own_hidden = lax.dynamic_slice_in_dim(hidden, member * block_cols, block_cols, 1)
    return (own_hidden + mixture).astype(BF16)


def hits_of(slot_row, rows):
    places = lax.broadcasted_iota(jnp.int32, (rows, slot_row.shape[1]), 0)
    return places == slot_row


def gate_up_kernel(
    experts, rows, width, slot_ref, weight_ref, x_ref, invgain_ref, wg_ref, wu_ref, act_ref,
    xs_ref, acc_ref, sq_ref, scale_ref
):
    chunk, expert = pl.program_id(0), pl.program_id(1)
    blocks, tokens, lanes = x_ref.shape
    span = PAIR * 128
    parts = tokens // span

    @pl.when(expert == 0)
    def _():
        @pl.when(chunk == 0)
        def _():
            sq_ref[...] = jnp.zeros_like(sq_ref)

        for part in range(parts):
            window = slice(part * span, (part + 1) * span)
            hits = jnp.concatenate(
                [hits_of(slot_ref[e : e + 1, window], rows) for e in range(experts)], axis=0
            )
            pieces = [x_ref[b, window, :] for b in range(blocks)]
            total = sq_ref[window, :]
            for b in range(blocks):
                value = pieces[b].astype(F32) * invgain_ref[b : b + 1, :]
                total = total + value * value
            sq_ref[window, :] = total
            picked = jnp.dot(
                hits.astype(F32).astype(BF16),
                jnp.concatenate(pieces, axis=1),
                preferred_element_type=F32,
            ).astype(BF16)
            for e in range(experts):
                xs_ref[e, part * rows : (part + 1) * rows, :] = picked[e * rows : (e + 1) * rows, :]

    @pl.when((expert == 0) & (chunk == pl.num_programs(0) - 1))
    def _():
        total = jnp.sum(jnp.transpose(sq_ref[...]), axis=0, keepdims=True)
        scale_ref[...] = jnp.broadcast_to(lax.rsqrt(total / width + 1e-06), scale_ref.shape)

    both = jnp.dot(
        xs_ref[expert],
        jnp.concatenate([wg_ref[0], wu_ref[0]], axis=1),
        preferred_element_type=F32,
    )

    @pl.when(chunk == 0)
    def _():
        acc_ref[expert] = both

    @pl.when(chunk > 0)
    def _():
        acc_ref[expert] += both

    @pl.when(chunk == pl.num_programs(0) - 1)
    def _():
        hidden_units = wg_ref.shape[2]
        for part in range(parts):
            window = slice(part * span, (part + 1) * span)
            hits = hits_of(slot_ref[pl.ds(expert, 1), window], rows)
            scale = jnp.sum(
                jnp.where(hits, scale_ref[0:1, window], 0.0), axis=1, keepdims=True
            )
            weight = jnp.sum(
                jnp.where(hits, weight_ref[pl.ds(expert, 1), window], 0.0), axis=1, keepdims=True
            )
            both_part = acc_ref[expert, part * rows : (part + 1) * rows, :]
            gate = both_part[:, :hidden_units] * scale
            upper = both_part[:, hidden_units:] * scale
            act = gate / (1.0 + jnp.exp(-gate)) * upper * weight
            act_ref[expert, part * rows : (part + 1) * rows, :] = act.astype(BF16)


def gate_up(slots, weights, x, invgain, w_gate, w_up, rows, per_chunk):
    experts, width, hidden_units = w_gate.shape
    blocks, tokens, lanes = x.shape
    parts = tokens // (PAIR * 128)
    depth = per_chunk * lanes
    return pl.pallas_call(
        functools.partial(gate_up_kernel, experts, rows, width),
        grid=(blocks // per_chunk, experts),
        in_specs=[
            pl.BlockSpec((experts, tokens), lambda k, e: (0, 0)),
            pl.BlockSpec((experts, tokens), lambda k, e: (0, 0)),
            pl.BlockSpec((per_chunk, tokens, lanes), lambda k, e: (k, 0, 0)),
            pl.BlockSpec((per_chunk, lanes), lambda k, e: (k, 0)),
            pl.BlockSpec((1, depth, hidden_units), lambda k, e: (e, k, 0)),
            pl.BlockSpec((1, depth, hidden_units), lambda k, e: (e, k, 0)),
        ],
        out_specs=pl.BlockSpec((experts, parts * rows, hidden_units), lambda k, e: (0, 0, 0)),
        out_shape=jax.ShapeDtypeStruct((experts, parts * rows, hidden_units), BF16),
        scratch_shapes=[
            pltpu.VMEM((experts, parts * rows, depth), BF16),
            pltpu.VMEM((experts, parts * rows, 2 * hidden_units), F32),
            pltpu.VMEM((tokens, lanes), F32),
            pltpu.VMEM((8, tokens), F32),
        ],
        compiler_params=pltpu.CompilerParams(
            vmem_limit_bytes=VMEM_BYTES, dimension_semantics=("arbitrary", "arbitrary")
        ),
        cost_estimate=pl.CostEstimate(
            flops=2 * experts * parts * rows * width * 2 * hidden_units,
            bytes_accessed=4 * experts * width * hidden_units + 2 * x.size,
            transcendentals=0,
        ),
        name="gate_up",
    )(slots, weights, x, invgain, w_gate, w_up)


def down_kernel(rows, slot_ref, act_ref, wd_ref, out_ref, ys_ref):
    expert = pl.program_id(1)
    experts, all_rows, _ = act_ref.shape
    parts = all_rows // rows
    span = PAIR * 128
    result = jnp.dot(act_ref[expert], wd_ref[0], preferred_element_type=F32).astype(BF16)
    for part in range(parts):
        ys_ref[part, expert] = result[part * rows : (part + 1) * rows, :]

    @pl.when(expert == experts - 1)
    def _():
        for part in range(parts):
            window = slice(part * span, (part + 1) * span)
            hits = jnp.concatenate(
                [hits_of(slot_ref[e : e + 1, window], rows) for e in range(experts)], axis=0
            )
            spread = jnp.transpose(hits.astype(F32)).astype(BF16)
            picked = ys_ref[part].reshape(experts * rows, ys_ref.shape[3])
            mixed = jnp.dot(spread, picked, preferred_element_type=F32).astype(BF16)
            for i in range(PAIR):
                out_ref[part * PAIR + i, 0] = mixed[i * 128 : (i + 1) * 128, :]


def down(slots, act, w_down, rows, groups, members):
    experts, hidden_units, width = w_down.shape
    tokens = slots.shape[1]
    cols = width // members
    parts = act.shape[1] // rows
    return pl.pallas_call(
        functools.partial(down_kernel, rows),
        grid=(members, experts),
        in_specs=[
            pl.BlockSpec((experts, tokens), lambda c, e: (0, 0)),
            pl.BlockSpec(act.shape, lambda c, e: (0, 0, 0)),
            pl.BlockSpec((1, hidden_units, cols), lambda c, e: (e, 0, c)),
        ],
        out_specs=pl.BlockSpec((groups, 1, tokens // groups, cols), lambda c, e: (0, c, 0, 0)),
        out_shape=jax.ShapeDtypeStruct((groups, members, tokens // groups, cols), BF16),
        scratch_shapes=[pltpu.VMEM((parts, experts, rows, cols), BF16)],
        compiler_params=pltpu.CompilerParams(
            vmem_limit_bytes=VMEM_BYTES, dimension_semantics=("arbitrary", "arbitrary")
        ),
        cost_estimate=pl.CostEstimate(
            flops=2 * experts * parts * rows * width * hidden_units,
            bytes_accessed=2 * experts * width * hidden_units + 2 * tokens * width,
            transcendentals=0,
        ),
        name="down_mix",
    )(slots, act, w_down)


def route_tables(route_ids, route_weights, group, experts):
    rows_here = route_ids.shape[0]
    shares = route_weights / jnp.sum(route_weights, axis=-1, keepdims=True)
    ids = lax.all_gather(route_ids, "expert", axis=0, tiled=True)
    shares = lax.all_gather(shares, "expert", axis=0, tiled=True)
    tokens = ids.shape[0]
    own = group * experts + jnp.arange(experts, dtype=jnp.int32)
    match = ids.T[None, :, :] == own[:, None, None]
    named = jnp.any(match, axis=1)
    weights = jnp.sum(jnp.where(match, shares.T[None, :, :], 0.0), axis=1)
    span = PAIR * rows_here
    order = jnp.arange(span)
    earlier = (order[:, None] < order[None, :]).astype(BF16)
    rank = jnp.dot(
        named.astype(BF16).reshape(experts * tokens // span, span),
        earlier,
        preferred_element_type=F32,
    )
    slots = jnp.where(named, rank.reshape(experts, tokens).astype(jnp.int32), -1)
    return slots, weights


def per_device_tokens(
    attn_heads, out_proj, residual, norm_gain, route_ids, route_weights, w_gate, w_up, w_down
):
    groups, members = lax.axis_size("expert"), lax.axis_size("tensor")
    group, member = lax.axis_index("expert"), lax.axis_index("tensor")
    here, width = residual.shape
    experts = w_gate.shape[0]
    tokens = groups * here
    lanes = width // (groups * members)
    rows = -(-PAIR * CAP // 16) * 16

    slots, weights = route_tables(route_ids, route_weights, group, experts)

    own_cols = lax.dynamic_index_in_dim(
        residual.reshape(here, groups, members, lanes), member, 2, keepdims=False
    )
    moved = lax.all_to_all(
        jnp.transpose(own_cols, (1, 0, 2)), "expert", split_axis=0, concat_axis=0, tiled=True
    ).reshape(tokens, lanes)

    heads = lax.all_gather(attn_heads, "expert", axis=0, tiled=True)
    part = jnp.dot(heads, out_proj, preferred_element_type=F32).astype(BF16)
    part = jnp.transpose(part.reshape(tokens, members, lanes), (1, 0, 2))
    attn_out = lax.psum_scatter(part, "tensor", scatter_dimension=0, tiled=True)[0]
    hidden = moved.astype(F32) + attn_out.astype(F32)
    gain = lax.dynamic_index_in_dim(
        norm_gain.reshape(groups * members, lanes), group * members + member, 0, keepdims=True
    )
    x = lax.all_gather((hidden * gain).astype(BF16), ("expert", "tensor"), axis=0)

    invgain = (1.0 / norm_gain).reshape(groups * members, lanes)
    act = gate_up(slots, weights, x, invgain, w_gate, w_up, rows, per_chunk=8)
    mixed = down(slots, act, w_down, rows, groups, members)
    cols = width // members
    mixture = lax.psum_scatter(
        mixed.reshape(groups * members, here, cols),
        ("expert", "tensor"),
        scatter_dimension=0,
        tiled=True,
    )[0]
    per_member = groups
    own = lax.dynamic_slice(
        x, (member * per_member, group * here, 0), (per_member, here, lanes)
    ).astype(F32)
    own_invgain = lax.dynamic_slice(invgain, (member * per_member, 0), (per_member, lanes))
    own_hidden = jnp.transpose(own * own_invgain[:, None, :], (1, 0, 2)).reshape(here, cols)
    return (own_hidden + mixture.astype(F32)).astype(BF16)


def solution(mesh):
    groups, members = mesh.shape["expert"], mesh.shape["tensor"]
    placed = (
        P("expert", "tensor"),
        P("tensor", "expert"),
        P("expert", None),
        P(),
        P("expert", None),
        P("expert", None),
        P("expert", None, "tensor"),
        P("expert", None, "tensor"),
        P("expert", "tensor", None),
    )

    def run(*arrays):
        tokens, width = arrays[2].shape
        whole_tokens = tokens <= EXPERTS * CAP and width == groups * members * LANES
        body = per_device_tokens if whole_tokens else per_device_slots
        return jax.shard_map(
            body, mesh=mesh, in_specs=placed, out_specs=P("expert", "tensor"), check_vma=False
        )(*arrays)

    return run
```

time: 699 us -> 415 us (0.59); the launches traced: 690 us -> 413 us
  blocking collectives: 212 us -> 61.6 us
  matrix products: 86.6 us -> 4.02 us
  Pallas kernels: 0 us -> 75.8 us
  local copies, waits for them, and re-layouts: 69.6 us -> 18.2 us
  waiting for transfers between devices: 275 us -> 232 us
  other arithmetic: 27.5 us -> 4.45 us
    all_to_all x1 -> x0, blocking collectives: 212 us -> none  [per_device(): lax.all_to_all(buffer, 'expert', split_axis=0, concat_axis=0, tiled=True)]
    dot_general x5 -> x2, matrix products: 86.6 us -> 4.02 us  [the longest x1 3.87 us: per_device_tokens(): part = jnp.dot(heads, out_proj, preferred_element_type=F32).astype(BF16)]
    reduce_scatter x1 -> x2, waiting for transfers between devices: 77.1 us -> 154 us  [the longest x1 145 us: per_device_tokens(): lax.psum_scatter(mixed.reshape(groups * members, here, cols), ('expert',...]
    pallas_call x0 -> x2, Pallas kernels: none -> 75.8 us  [the longest x1 41.5 us: gate_up(): pl.pallas_call(functools.partial(gate_up_kernel, experts, rows, width), g...]
    all_gather x0 -> x2, blocking collectives: none -> 61.6 us  [the longest x1 30.9 us: route_tables(): shares = lax.all_gather(shares, 'expert', axis=0, tiled=True)]
    all_to_all x1, waiting for transfers between devices: 53.4 us -> 8.44 us  [per_device_tokens(): lax.all_to_all(jnp.transpose(own_cols, (1, 0, 2)), 'expert', split_axis=0...]
    all_gather x1 -> x2, waiting for transfers between devices: 111 us -> 68.9 us  [the longest x1 54.2 us: per_device_tokens(): heads = lax.all_gather(attn_heads, 'expert', axis=0, tiled=True)]
    psum x1 -> x0, waiting for transfers between devices: 32.5 us -> none  [per_device(): lax.psum(heads_out.astype(jnp.bfloat16), 'tensor').astype(jnp.float32)]
  transfers between devices with their start and end apart: 4 -> 5, of which waited for: 4 -> 5; matrix products, arithmetic and copies ran while one was open for 3% -> 2% of each run, Pallas kernels for 0% -> 0%
where the time goes in v1:
time: 415 us; the launch traced here: 413 us
  waiting for transfers between devices  232 us (56%)
  Pallas kernels  75.8 us (18%)
  blocking collectives  61.6 us (15%)
  local copies, waits for them, and re-layouts  18.2 us (4%)
  between operations  13.3 us (3%)
  other arithmetic  4.45 us (1%)
    reduce_scatter x1, waiting for transfers between devices, per_device_tokens(): lax.psum_scatter(mixed.reshape(groups * members, here, cols), ('expert',...  145 us
    all_gather x1, waiting for transfers between devices, per_device_tokens(): heads = lax.all_gather(attn_heads, 'expert', axis=0, tiled=True)  54.2 us
    pallas_call x1, Pallas kernels, gate_up(): pl.pallas_call(functools.partial(gate_up_kernel, experts, rows, width), g...  41.5 us
    pallas_call x1, Pallas kernels, down(): pl.pallas_call(functools.partial(down_kernel, rows), grid=(members, exper...  34.3 us
    all_gather x1, blocking collectives, route_tables(): shares = lax.all_gather(shares, 'expert', axis=0, tiled=True)  30.9 us
    all_gather x1, blocking collectives, route_tables(): ids = lax.all_gather(route_ids, 'expert', axis=0, tiled=True)  30.7 us
    all_gather x1, waiting for transfers between devices, per_device_tokens(): lax.all_gather((hidden * gain).astype(BF16), ('expert', 'tensor'), axis=0)  14.7 us
    reshape x1, local copies, waits for them, and re-layouts, per_device_tokens(): mixed.reshape(groups * members, here, cols)  12 us
  transfers between devices with their start and end apart: 5, of which 5 were waited for; matrix products, arithmetic and copies ran while one was open for 2% of the time, Pallas kernels for 0%

profile of v1, /device:TPU:0, one launch (start us, length us, event | category | flops | bytes accessed | tf_op | source)
XLA Modules:
  0.0 413.3 jit_solution(13757591928099862833)
XLA Ops:
  6.5 0.0 copy-start
  6.5 0.0 copy-start.2
  6.5 0.0 copy-start.4
  6.5 0.0 copy-start.5
  6.5 0.0 copy-start.3
  6.5 0.0 all-gather.3.cloned.1.call-start
  6.6 0.7 all-gather.3.cloned.1.call-update
  7.3 0.0 reduce-scatter.3.cloned.1.call-start
  7.3 54.2 %all-gather.3.cloned.1.call-done = bf16[1024,1024]{1,0:T(8,128)(2,1)} async-done(((bf16[128,1024]{1,0:T(8,128)(2,1)}), bf16[1024,1024]{1,0:T(8,128)(2,1)}) %all-gather.3.cloned.1.call-update) | async-done | bytes 2097168 | tf_op jit(solution)/shard_map/all_gather | solution.py:280
  61.5 0.0 copy-done
  61.5 3.9 convolution_convert_fusion
  65.4 0.0 reduce-scatter.3.cloned.1.call-update
  65.4 0.0 copy-done.2
  65.4 0.8 reshape.52
  66.2 0.5 constant_dynamic-slice_fusion.3
  66.8 1.1 copy.33
  67.8 3.4 all-to-all-start
  71.2 0.0 all-gather.5.cloned.1.call-start
  71.3 0.0 copy-done.4
  71.3 8.4 %all-to-all-done = bf16[8,128,128]{1,2,0:T(8,128)(2,1)S(1)} async-done(((bf16[8,128,128]{1,2,0:T(8,128)(2,1)}), bf16[8,128,128]{1,2,0:T(8,128)(2,1)S(1)}, u32[]{:S(2)}, u32[]{:S(2)}) %all-to-all-start) | async-done | bytes 262176 | tf_op jit(solution)/shard_map/all_to_all | solution.py:276
  79.8 0.2 copy.28
  79.9 0.1 reshape.59
  80.0 8.9 %reduce-scatter.3.cloned.1.call-done = bf16[1,1024,128]{1,2,0:T(8,128)(2,1)} async-done(((bf16[4,1024,128]{1,2,0:T(8,128)(2,1)}), bf16[1,1024,128]{1,2,0:T(8,128)(2,1)}) %reduce-scatter.3.cloned.1.call-update) | async-done | bytes 262160 | tf_op jit(solution)/shard_map/reduce_scatter | solution.py:283
  88.9 1.0 multiply_convert_fusion
  90.0 0.8 copy.29
  90.8 0.0 all-gather.5.cloned.1.call-update
  90.9 0.0 reduce-scatter.5.cloned.1.call-start
  90.9 0.0 copy-done.5
  90.9 30.7 %all_gather.15 = s32[1024,8]{0,1:T(8,128)S(1)} all-gather(s32[128,8]{0,1:T(8,128)S(1)} %copy-done.5), channel_id=1, replica_groups=mesh['expert'=8,'tensor'=4] {'expert'}, dimensions={0}, use_global_device_ids=true | all-gather | bytes 36864 | tf_op jit(solution)/shard_map/all_gather | solution.py:241
  121.6 0.2 compare_reduce_fusion
  121.8 0.2 convolution_convert_fusion.1
  122.0 0.0 copy-done.3
  122.0 30.9 %all_gather.16 = f32[1024,8]{0,1:T(8,128)S(1)} all-gather(f32[128,8]{0,1:T(8,128)S(1)} %broadcast_divide_fusion), channel_id=1, replica_groups=mesh['expert'=8,'tensor'=4] {'expert'}, dimensions={0}, use_global_device_ids=true | all-gather | bytes 36864 | tf_op jit(solution)/shard_map/all_gather | solution.py:242
  152.9 0.7 fusion.1.weight_ref
  153.7 0.6 divide_bitcast_fusion.invgain_ref
  154.3 0.6 broadcast_select_fusion.slot_ref
  154.9 14.7 %all-gather.5.cloned.1.call-done.x_ref = bf16[32,1024,128]{2,1,0:T(8,128)(2,1)} async-done(((bf16[1,1024,128]{2,1,0:T(8,128)(2,1)}), bf16[32,1024,128]{2,1,0:T(8,128)(2,1)}) %all-gather.5.cloned.1.call-update) | async-done | bytes 8388624 | tf_op jit(solution)/shard_map/all_gather | solution.py:288
  169.6 41.5 %gate_up.1.act_ref = bf16[8,192,384]{2,1,0:T(8,128)(2,1)} custom-call(s32[8,1024]{1,0:T(8,128)} %broadcast_select_fusion.slot_ref, f32[8,1024]{1,0:T(8,128)} %fusion.1.weight_ref, bf16[32,1024,128]{2,1,0:T(8,128)(2,1)} %all-gather.5.cloned.1.call-done.x_ref, f32[32,128]{1,0:T(8,128)} %divide_bitcast_fusion.invgain_ref, bf16[8,4096,384]{2,1,0:T(8,128)(2,1)} %wg_ref.1, ...), custom_call_target="tpu_custom_call" | custom-call | flops 9663676416 | bytes 58720256 | tf_op jit(solution)/shard_map/gate_up/pallas_call | solution.py:156
  211.1 34.3 %down_mix.1 = bf16[8,4,128,1024]{3,2,1,0:T(8,128)(2,1)} custom-call(s32[8,1024]{1,0:T(8,128)} %broadcast_select_fusion.slot_ref, bf16[8,192,384]{2,1,0:T(8,128)(2,1)} %gate_up.1.act_ref, bf16[8,384,4096]{2,1,0:T(8,128)(2,1)} %wd_ref.1), custom_call_target="tpu_custom_call" | custom-call | flops 4831838208 | bytes 33554432 | tf_op jit(solution)/shard_map/down_mix/pallas_call | solution.py:215
  245.4 0.0 copy-start.1
  245.4 12.0 %copy.31 = bf16[32,128,1024]{1,2,0:T(8,128)(2,1)} copy(bf16[32,128,1024]{2,1,0:T(8,128)(2,1)} %bitcast.26) | data formatting | bytes 16777216 | tf_op jit(solution)/shard_map/reshape | solution.py:295
  257.4 0.0 reduce-scatter.5.cloned.1.call-update
  257.5 0.7 constant_dynamic-slice_fusion
  258.1 1.0 constant_dynamic-slice_fusion.1
  259.1 0.2 copy.34
  259.3 0.2 convert_multiply_fusion
  259.5 145.4 %reduce-scatter.5.cloned.1.call-done = bf16[1,128,1024]{1,2,0:T(8,128)(2,1)} async-done(((bf16[32,128,1024]{1,2,0:T(8,128)(2,1)}), bf16[1,128,1024]{1,2,0:T(8,128)(2,1)}) %reduce-scatter.5.cloned.1.call-update) | async-done | bytes 262160 | tf_op jit(solution)/shard_map/reduce_scatter | solution.py:294
  404.9 1.0 fusion
  405.9 0.9 copy.32
  406.8 0.0 copy-done.1
  (6 shorter events, 0.1 us)
Async XLA Ops:
  6.5 55.0 %copy-start = (bf16[1024,512]{1,0:T(8,128)(2,1)S(1)}, bf16[1024,512]{1,0:T(8,128)(2,1)}, u32[]{:S(2)}) copy-start(bf16[1024,512]{1,0:T(8,128)(2,1)} %param.10) | copy-start | bytes 3145732
  6.5 58.9 %copy-start.2 = (bf16[128,4096]{1,0:T(8,128)(2,1)S(1)}, bf16[128,4096]{1,0:T(8,128)(2,1)}, u32[]{:S(2)}) copy-start(bf16[128,4096]{1,0:T(8,128)(2,1)} %param.11) | copy-start | bytes 3145732
  6.5 64.8 %copy-start.4 = (f32[4096]{0:T(1024)S(1)}, f32[4096]{0:T(1024)}, u32[]{:S(2)}) copy-start(f32[4096]{0:T(1024)} %param.12) | copy-start | bytes 49156
  6.5 84.4 %copy-start.5 = (s32[128,8]{0,1:T(8,128)S(1)}, s32[128,8]{0,1:T(8,128)}, u32[]{:S(2)}) copy-start(s32[128,8]{0,1:T(8,128)} %param.13) | copy-start | bytes 12292
  6.5 115.5 %copy-start.3 = (f32[128,8]{0,1:T(8,128)S(1)}, f32[128,8]{0,1:T(8,128)}, u32[]{:S(2)}) copy-start(f32[128,8]{0,1:T(8,128)} %param.14) | copy-start | bytes 12292
  6.5 55.0 %all-gather.3.cloned.1.call-start = ((), (), s32[]{:S(2)}) async-start(), calls=%async_computation.3 | async-start | bytes 2359296 | tf_op jit(solution)/shard_map/all_gather | solution.py:280
  7.3 81.7 %reduce-scatter.3.cloned.1.call-start = ((), (), s32[]{:S(2)}) async-start(), calls=%async_computation.4 | async-start | bytes 1310720 | tf_op jit(solution)/shard_map/reduce_scatter | solution.py:283
  67.8 11.9 %all-to-all-start = ((bf16[8,128,128]{1,2,0:T(8,128)(2,1)}), bf16[8,128,128]{1,2,0:T(8,128)(2,1)S(1)}, u32[]{:S(2)}, u32[]{:S(2)}) async-start(bf16[8,128,128]{1,2,0:T(8,128)(2,1)} %bitcast.1), calls=%async_computation | async-start | bytes 524288 | tf_op jit(solution)/shard_map/all_to_all | solution.py:276
  71.2 98.4 %all-gather.5.cloned.1.call-start = ((), (), s32[]{:S(2)}) async-start(), calls=%async_computation.5 | async-start | bytes 8650752 | tf_op jit(solution)/shard_map/all_gather | solution.py:288
  90.9 314.0 %reduce-scatter.5.cloned.1.call-start = ((), (), s32[]{:S(2)}) async-start(), calls=%async_computation.6 | async-start | bytes 8650752 | tf_op jit(solution)/shard_map/reduce_scatter | solution.py:294
  245.4 161.4 %copy-start.1 = (bf16[1024,512]{1,0:T(8,128)(2,1)S(1)}, bf16[1024,512]{1,0:T(8,128)(2,1)}, u32[]{:S(2)}) copy-start(bf16[1024,512]{1,0:T(8,128)(2,1)} %param.10) | copy-start | bytes 3145732
Sparse Core Ops, SparseCore 0:
  9.5 51.9 all-gather.2
  65.5 23.3 reduce-scatter.2
  92.2 77.3 all-gather.4
  257.6 147.2 reduce-scatter.4

commit v2 on v1

--- a/solution.py
+++ b/solution.py
@@ -161,8 +161,12 @@
             pl.BlockSpec((experts, tokens), lambda k, e: (0, 0)),
             pl.BlockSpec((per_chunk, tokens, lanes), lambda k, e: (k, 0, 0)),
             pl.BlockSpec((per_chunk, lanes), lambda k, e: (k, 0)),
-            pl.BlockSpec((1, depth, hidden_units), lambda k, e: (e, k, 0)),
-            pl.BlockSpec((1, depth, hidden_units), lambda k, e: (e, k, 0)),
+            pl.BlockSpec(
+                (1, depth, hidden_units), lambda k, e: (e, k, 0)
+            ),
+            pl.BlockSpec(
+                (1, depth, hidden_units), lambda k, e: (e, k, 0)
+            ),
         ],
         out_specs=pl.BlockSpec((experts, parts * rows, hidden_units), lambda k, e: (0, 0, 0)),
         out_shape=jax.ShapeDtypeStruct((experts, parts * rows, hidden_units), BF16),
@@ -184,14 +188,18 @@
     )(slots, weights, x, invgain, w_gate, w_up)
 
 
-def down_kernel(rows, slot_ref, act_ref, wd_ref, out_ref, ys_ref):
-    expert = pl.program_id(1)
+def down_kernel(rows, place_ref, slot_ref, act_ref, wd0_ref, wd1_ref, *rest):
+    out_refs, ys_ref = rest[:-1], rest[-1]
+    out_cols = out_refs[0].shape[2]
+    expert = pl.program_id(0)
     experts, all_rows, _ = act_ref.shape
     parts = all_rows // rows
+    groups = parts * PAIR
     span = PAIR * 128
-    result = jnp.dot(act_ref[expert], wd_ref[0], preferred_element_type=F32).astype(BF16)
-    for part in range(parts):
-        ys_ref[part, expert] = result[part * rows : (part + 1) * rows, :]
+    for side, wd_ref in enumerate((wd0_ref, wd1_ref)):
+        result = jnp.dot(act_ref[expert], wd_ref[0], preferred_element_type=F32).astype(BF16)
+        for part in range(parts):
+            ys_ref[side, part, expert] = result[part * rows : (part + 1) * rows, :]
 
     @pl.when(expert == experts - 1)
     def _():
@@ -201,45 +209,133 @@
                 [hits_of(slot_ref[e : e + 1, window], rows) for e in range(experts)], axis=0
             )
             spread = jnp.transpose(hits.astype(F32)).astype(BF16)
-            picked = ys_ref[part].reshape(experts * rows, ys_ref.shape[3])
-            mixed = jnp.dot(spread, picked, preferred_element_type=F32).astype(BF16)
-            for i in range(PAIR):
-                out_ref[part * PAIR + i, 0] = mixed[i * 128 : (i + 1) * 128, :]
-
-
-def down(slots, act, w_down, rows, groups, members):
+            for side in range(2):
+                picked = ys_ref[side, part].reshape(experts * rows, ys_ref.shape[4])
+                mixed = jnp.dot(spread, picked, preferred_element_type=F32).astype(BF16)
+                for i in range(PAIR):
+                    target = place_ref[2 + side * groups + part * PAIR + i]
+                    for number, out_ref in enumerate(out_refs):
+                        out_ref[target] = mixed[
+                            i * 128 : (i + 1) * 128, number * out_cols : (number + 1) * out_cols
+                        ]
+
+
+def down(place, slots, act, w_down, rows, groups, cols, chunks):
     experts, hidden_units, width = w_down.shape
     tokens = slots.shape[1]
-    cols = width // members
     parts = act.shape[1] // rows
     return pl.pallas_call(
         functools.partial(down_kernel, rows),
-        grid=(members, experts),
-        in_specs=[
-            pl.BlockSpec((experts, tokens), lambda c, e: (0, 0)),
-            pl.BlockSpec(act.shape, lambda c, e: (0, 0, 0)),
-            pl.BlockSpec((1, hidden_units, cols), lambda c, e: (e, 0, c)),
-        ],
-        out_specs=pl.BlockSpec((groups, 1, tokens // groups, cols), lambda c, e: (0, c, 0, 0)),
-        out_shape=jax.ShapeDtypeStruct((groups, members, tokens // groups, cols), BF16),
-        scratch_shapes=[pltpu.VMEM((parts, experts, rows, cols), BF16)],
+        grid_spec=pltpu.PrefetchScalarGridSpec(
+            num_scalar_prefetch=1,
+            grid=(experts,),
+            in_specs=[
+                pl.BlockSpec((experts, tokens), lambda e, p: (0, 0)),
+                pl.BlockSpec(act.shape, lambda e, p: (0, 0, 0)),
+                pl.BlockSpec(
+                    (1, hidden_units, cols),
+                    lambda e, p: (e, 0, p[0])
+                ),
+                pl.BlockSpec(
+                    (1, hidden_units, cols),
+                    lambda e, p: (e, 0, p[1])
+                ),
+            ],
+            out_specs=[
+                pl.BlockSpec((2 * groups, tokens // groups, cols // chunks), lambda e, p: (0, 0, 0))
+            ]
+            * chunks,
+            scratch_shapes=[pltpu.VMEM((2, parts, experts, rows, cols), BF16)],
+        ),
+        out_shape=[jax.ShapeDtypeStruct((2 * groups, tokens // groups, cols // chunks), BF16)]
+        * chunks,
         compiler_params=pltpu.CompilerParams(
-            vmem_limit_bytes=VMEM_BYTES, dimension_semantics=("arbitrary", "arbitrary")
+            vmem_limit_bytes=VMEM_BYTES, dimension_semantics=("arbitrary",)
         ),
         cost_estimate=pl.CostEstimate(
-            flops=2 * experts * parts * rows * width * hidden_units,
-            bytes_accessed=2 * experts * width * hidden_units + 2 * tokens * width,
+            flops=8 * experts * parts * rows * cols * hidden_units,
+            bytes_accessed=4 * experts * cols * hidden_units + 4 * tokens * cols,
             transcendentals=0,
         ),
         name="down_mix",
-    )(slots, act, w_down)
+    )(place, slots, act, w_down, w_down)
+
+
+def flip(array, bits_of):
+    pairs = []
+    for index in range(32):
+        pairs.append((index, index ^ bits_of(index & 1)))
+    return lax.ppermute(array, ("expert", "tensor"), pairs)
+
+
+CORE, X, Y, ZLOW, ZHIGH = 1, 2, 4, 8, 16
+
+
+def first_axis(core):
+    return Y if core else X
+
+
+def last_axis(core):
+    return X if core else Y
+
+
+def halving_places(to_core, group, member, groups):
+    g = jnp.arange(groups, dtype=jnp.int32)[None, :]
+    y_kept = ((g & 1) == (group & 1)).astype(jnp.int32)
+    low_kept = (((g >> 1) & 1) == ((group >> 1) & 1)).astype(jnp.int32)
+    high_kept = ((g >> 2) == (group >> 2)).astype(jnp.int32)
+    x_kept = jnp.arange(2, dtype=jnp.int32)[:, None]
+    first = jnp.where(to_core == 0, x_kept, y_kept)
+    last = jnp.where(to_core == 0, y_kept, x_kept)
+    return (((first * 2 + low_kept) * 2 + high_kept) * 2 + last).reshape(-1)
+
+
+def total_of(terms):
+    total = terms[0].astype(F32)
+    for term in terms[1:]:
+        total = total + term.astype(F32)
+    return total
+
+
+HALVING = (first_axis, lambda core: ZLOW, lambda core: ZHIGH, last_axis)
+
+
+def after(value, earlier):
+    return lax.optimization_barrier((value, earlier))
+
+
+def sent_half(terms):
+    half = terms[0].shape[0] // 2
+    return total_of([term[:half] for term in terms]).astype(BF16), [term[half:] for term in terms]
+
+
+def reduce_chunks(makers):
+    chunks, arrived, first_sent = [None] * len(makers), {}, None
+    for tick in range(len(HALVING) + len(makers) - 1):
+        for index, maker in enumerate(makers):
+            stage = tick - index
+            if not 0 <= stage < len(HALVING):
+                continue
+            if stage == 0:
+                chunks[index] = maker(first_sent)
+            sent, rest = sent_half(chunks[index])
+            if index:
+                sent, _ = after(sent, arrived[index - 1, stage])
+            if stage == 0:
+                first_sent = sent
+            came = flip(sent, HALVING[stage])
+            arrived[index, stage] = came
+            chunks[index] = rest + [came]
+    return [total_of([term[0] for term in terms]) for terms in chunks]
 
 
 def route_tables(route_ids, route_weights, group, experts):
     rows_here = route_ids.shape[0]
     shares = route_weights / jnp.sum(route_weights, axis=-1, keepdims=True)
-    ids = lax.all_gather(route_ids, "expert", axis=0, tiled=True)
-    shares = lax.all_gather(shares, "expert", axis=0, tiled=True)
+    table = jnp.concatenate([route_ids.astype(F32), shares], axis=1)
+    table = lax.all_gather(table, "expert", axis=0, tiled=True)
+    ids = table[:, : route_ids.shape[1]].astype(jnp.int32)
+    shares = table[:, route_ids.shape[1] :]
     tokens = ids.shape[0]
     own = group * experts + jnp.arange(experts, dtype=jnp.int32)
     match = ids.T[None, :, :] == own[:, None, None]
@@ -280,6 +376,7 @@
     heads = lax.all_gather(attn_heads, "expert", axis=0, tiled=True)
     part = jnp.dot(heads, out_proj, preferred_element_type=F32).astype(BF16)
     part = jnp.transpose(part.reshape(tokens, members, lanes), (1, 0, 2))
+    part, slots, weights = lax.optimization_barrier((part, slots, weights))
     attn_out = lax.psum_scatter(part, "tensor", scatter_dimension=0, tiled=True)[0]
     hidden = moved.astype(F32) + attn_out.astype(F32)
     gain = lax.dynamic_index_in_dim(
@@ -288,22 +385,37 @@
     x = lax.all_gather((hidden * gain).astype(BF16), ("expert", "tensor"), axis=0)
 
     invgain = (1.0 / norm_gain).reshape(groups * members, lanes)
-    act = gate_up(slots, weights, x, invgain, w_gate, w_up, rows, per_chunk=8)
-    mixed = down(slots, act, w_down, rows, groups, members)
+    act = gate_up(slots, weights, x, invgain, w_gate, w_up, rows, per_chunk=16)
     cols = width // members
-    mixture = lax.psum_scatter(
-        mixed.reshape(groups * members, here, cols),
-        ("expert", "tensor"),
-        scatter_dimension=0,
-        tiled=True,
-    )[0]
+    x_side, core = member >> 1, member & 1
+
+    def columns_of(to_core, chunk, chunks):
+        sides = jnp.stack([1 - x_side, x_side])
+        blocks = (sides * 2 + to_core) * chunks + chunk
+        return jnp.concatenate([blocks, halving_places(to_core, group, member, groups)])
+
+    chunks = 2
+    chunk_cols = cols // chunks
+    other = down(
+        columns_of(1 - core, 0, 1), slots, act, w_down, rows, groups, cols, chunks
+    )
+    came = [flip(piece, lambda c: CORE) for piece in other]
+
+    def terms_of(chunk, earlier):
+        ready = act if earlier is None else after(act, earlier)[0]
+        place = columns_of(core, chunk, chunks)
+        (kept,) = down(place, slots, ready, w_down, rows, groups, chunk_cols, 1)
+        return [kept, came[chunk]]
+
+    sums = reduce_chunks([functools.partial(terms_of, chunk) for chunk in range(chunks)])
+    mixture = jnp.concatenate(sums, axis=1)
     per_member = groups
     own = lax.dynamic_slice(
         x, (member * per_member, group * here, 0), (per_member, here, lanes)
     ).astype(F32)
     own_invgain = lax.dynamic_slice(invgain, (member * per_member, 0), (per_member, lanes))
     own_hidden = jnp.transpose(own * own_invgain[:, None, :], (1, 0, 2)).reshape(here, cols)
-    return (own_hidden + mixture.astype(F32)).astype(BF16)
+    return (own_hidden + mixture).astype(BF16)
 
 
 def solution(mesh):
@@ -322,7 +434,7 @@
 
     def run(*arrays):
         tokens, width = arrays[2].shape
-        whole_tokens = tokens <= EXPERTS * CAP and width == groups * members * LANES
+        whole_tokens = (groups, members) == (8, 4) and width == groups * members * LANES
         body = per_device_tokens if whole_tokens else per_device_slots
         return jax.shard_map(
             body, mesh=mesh, in_specs=placed, out_specs=P("expert", "tensor"), check_vma=False

time: 415 us -> 310 us (0.75)
  waiting for transfers between devices: 232 us -> 149 us
  blocking collectives: 61.6 us -> 32.5 us
  other arithmetic: 4.45 us -> 24.1 us
  local copies, waits for them, and re-layouts: 18.2 us -> 4.38 us
  starting transfers between devices: 3.57 us -> 15.4 us
  Pallas kernels: 75.8 us -> 67 us
    reduce_scatter x1 -> x0, waiting for transfers between devices: 145 us -> none  [per_device_tokens(): lax.psum_scatter(mixed.reshape(groups * members, here, cols), ('expert',...]
    all_gather x1, waiting for transfers between devices: 14.7 us -> 77.2 us  [per_device_tokens(): lax.all_gather((hidden * gain).astype(BF16), ('expert', 'tensor'), axis=0)]
    all_gather x1, waiting for transfers between devices: 54.2 us -> 17.9 us  [per_device_tokens(): heads = lax.all_gather(attn_heads, 'expert', axis=0, tiled=True)]
    ppermute x0 -> x10, waiting for transfers between devices: none -> 35.6 us  [flip(): return lax.ppermute(array, ('expert', 'tensor'), pairs)]
    all_gather x2 -> x1, blocking collectives: 61.6 us -> 32.5 us  [route_tables(): table = lax.all_gather(table, 'expert', axis=0, tiled=True)]
    convert_element_type x1 -> x13, other arithmetic: 1.05 us -> 16.2 us  [the longest x8 13.8 us: sent_half(): total_of([term[:half] for term in terms]).astype(BF16)]
    reshape x1 -> x0, local copies, waits for them, and re-layouts: 12 us -> none  [per_device_tokens(): mixed.reshape(groups * members, here, cols)]
    ppermute x0 -> x10, starting transfers between devices: none -> 11.7 us  [flip(): return lax.ppermute(array, ('expert', 'tensor'), pairs)]
  transfers between devices with their start and end apart: 5 -> 14, of which waited for: 5 -> 9; matrix products, arithmetic and copies ran while one was open for 2% -> 8% of each run, Pallas kernels for 0% -> 7%
where the time goes in v2:
time: 310 us; the launch traced here: 309 us
  waiting for transfers between devices  149 us (48%)
  Pallas kernels  67 us (22%)
  blocking collectives  32.5 us (10%)
  other arithmetic  24.1 us (8%)
  starting transfers between devices  15.4 us (5%)
  between operations  13.4 us (4%)
  local copies, waits for them, and re-layouts  4.38 us (1%)
  matrix products  4.02 us (1%)
    all_gather x1, waiting for transfers between devices, per_device_tokens(): lax.all_gather((hidden * gain).astype(BF16), ('expert', 'tensor'), axis=0)  77.2 us
    ppermute x10, waiting for transfers between devices, flip(): return lax.ppermute(array, ('expert', 'tensor'), pairs)  35.6 us
    pallas_call x3, Pallas kernels, down(): pl.pallas_call(functools.partial(down_kernel, rows), grid_spec=pltpu.Pref...  35 us
    all_gather x1, blocking collectives, route_tables(): table = lax.all_gather(table, 'expert', axis=0, tiled=True)  32.5 us
    pallas_call x1, Pallas kernels, gate_up(): pl.pallas_call(functools.partial(gate_up_kernel, experts, rows, width), g...  32.1 us
    all_gather x1, waiting for transfers between devices, per_device_tokens(): heads = lax.all_gather(attn_heads, 'expert', axis=0, tiled=True)  17.9 us
    convert_element_type x8, other arithmetic, sent_half(): total_of([term[:half] for term in terms]).astype(BF16)  13.8 us
    ppermute x10, starting transfers between devices, flip(): return lax.ppermute(array, ('expert', 'tensor'), pairs)  11.7 us
  transfers between devices with their start and end apart: 14, of which 9 were waited for; matrix products, arithmetic and copies ran while one was open for 8% of the time, Pallas kernels for 7%

profile of v2, /device:TPU:0, one launch (start us, length us, event | category | flops | bytes accessed | tf_op | source)
XLA Modules:
  0.0 309.4 jit_solution(10125239798456112780)
XLA Ops:
  6.5 0.7 all-gather.3.cloned.1.call-update
  7.3 0.0 reduce-scatter.2.cloned.1.call-start
  7.3 0.7 convert_element_type.241
  8.0 0.7 reduce_sum.18
  8.7 0.7 broadcast_divide_fusion
  9.4 32.5 %all_gather.11 = f32[1024,16]{0,1:T(8,128)S(1)} all-gather(f32[128,16]{0,1:T(8,128)S(1)} %pad_maximum_fusion), channel_id=1, replica_groups=mesh['expert'=8,'tensor'=4] {'expert'}, dimensions={0}, use_global_device_ids=true | all-gather | bytes 73728 | tf_op jit(solution)/shard_map/all_gather | solution.py:336
  41.9 0.2 compare_reduce_fusion
  42.1 0.2 convolution_convert_fusion.1
  42.3 0.7 fusion.1.weight_ref
  43.0 0.6 broadcast_select_fusion.slot_ref
  43.6 17.9 %all-gather.3.cloned.1.call-done = bf16[1024,1024]{1,0:T(8,128)(2,1)} async-done(((bf16[128,1024]{1,0:T(8,128)(2,1)}), bf16[1024,1024]{1,0:T(8,128)(2,1)}) %all-gather.3.cloned.1.call-update) | async-done | bytes 2097168 | tf_op jit(solution)/shard_map/all_gather | solution.py:376
  61.6 3.9 %convolution_convert_fusion = bf16[1024,512]{0,1:T(8,128)(2,1)} fusion(bf16[1024,1024]{1,0:T(8,128)(2,1)} %all-gather.3.cloned.1.call-done, bf16[1024,512]{1,0:T(8,128)(2,1)S(1)} %copy-done), kind=kOutput, calls=%fused_computation.2 | convolution fusion | flops 1074266112 | bytes 4194304 | tf_op jit(solution)/shard_map/dot_general | solution.py:377
  65.4 0.0 reduce-scatter.2.cloned.1.call-update
  65.5 0.0 copy-start.8
  65.5 0.8 reshape.131
  66.3 0.5 constant_dynamic-slice_fusion.2
  66.8 1.1 copy.26
  67.9 3.4 %all-to-all-start = ((bf16[8,128,128]{1,2,0:T(8,128)(2,1)}), bf16[8,128,128]{1,2,0:T(8,128)(2,1)S(1)}, u32[]{:S(2)}, u32[]{:S(2)}) async-start(bf16[8,128,128]{1,2,0:T(8,128)(2,1)} %bitcast.1), calls=%async_computation | async-start | bytes 524288 | tf_op jit(solution)/shard_map/all_to_all | solution.py:372
  71.3 0.2 all-gather.5.cloned.1.call-start
  71.6 8.4 %all-to-all-done = bf16[8,128,128]{1,2,0:T(8,128)(2,1)S(1)} async-done(((bf16[8,128,128]{1,2,0:T(8,128)(2,1)}), bf16[8,128,128]{1,2,0:T(8,128)(2,1)S(1)}, u32[]{:S(2)}, u32[]{:S(2)}) %all-to-all-start) | async-done | bytes 262176 | tf_op jit(solution)/shard_map/all_to_all | solution.py:372
  80.0 0.2 copy.23
  80.1 0.1 reshape.137
  80.2 8.8 %reduce-scatter.2.cloned.1.call-done = bf16[1,1024,128]{1,2,0:T(8,128)(2,1)} async-done(((bf16[4,1024,128]{1,2,0:T(8,128)(2,1)}), bf16[1,1024,128]{1,2,0:T(8,128)(2,1)}) %reduce-scatter.2.cloned.1.call-update) | async-done | bytes 262160 | tf_op jit(solution)/shard_map/reduce_scatter | solution.py:380
  89.0 1.0 multiply_convert_fusion
  90.1 0.8 copy.24
  90.9 0.0 all-gather.5.cloned.1.call-update
  91.0 0.1 reshape.150
  91.1 0.1 reshape.151
  91.2 0.1 broadcast_add_fusion.1
  91.3 0.1 broadcast_add_fusion
  91.3 0.7 pad_add_fusion
  92.0 0.6 divide_bitcast_fusion.invgain_ref
  92.6 77.2 %all-gather.5.cloned.1.call-done.x_ref = bf16[32,1024,128]{2,1,0:T(8,128)(2,1)} async-done(((bf16[1,1024,128]{2,1,0:T(8,128)(2,1)}), bf16[32,1024,128]{2,1,0:T(8,128)(2,1)}) %all-gather.5.cloned.1.call-update) | async-done | bytes 8388624 | tf_op jit(solution)/shard_map/all_gather | solution.py:385
  169.8 32.1 %gate_up.1.act_ref = bf16[8,192,384]{2,1,0:T(8,128)(2,1)} custom-call(s32[8,1024]{1,0:T(8,128)} %broadcast_select_fusion.slot_ref, f32[8,1024]{1,0:T(8,128)} %fusion.1.weight_ref, bf16[32,1024,128]{2,1,0:T(8,128)(2,1)} %all-gather.5.cloned.1.call-done.x_ref, f32[32,128]{1,0:T(8,128)} %divide_bitcast_fusion.invgain_ref, bf16[8,4096,384]{2,1,0:T(8,128)(2,1)} %wg_ref.1, ...), custom_call_target="tpu_custom_call" | custom-call | flops 9663676416 | bytes 58720256 | tf_op jit(solution)/shard_map/gate_up/pallas_call | solution.py:156
  201.9 14.3 %down_mix.4 = (bf16[16,128,512]{2,1,0:T(8,128)(2,1)}, bf16[16,128,512]{2,1,0:T(8,128)(2,1)}) custom-call(s32[18]{0:T(128)} %get-tuple-element.33.place_ref, s32[8,1024]{1,0:T(8,128)} %broadcast_select_fusion.slot_ref, bf16[8,192,384]{2,1,0:T(8,128)(2,1)} %gate_up.1.act_ref, bf16[8,384,4096]{2,1,0:T(8,128)(2,1)} %wd1_ref.5, bf16[8,384,4096]{2,1,0:T(8,128)(2,1)} %wd1_ref.5), custom_call_target="tpu_custom_call" | custom-call | flops 4831838208 | bytes 16777216 | tf_op jit(solution)/shard_map/down_mix/pallas_call | solution.py:227
  216.1 0.3 collective-permute-start
  216.4 0.2 collective-permute-start.5
  216.7 10.3 %down_mix.3 = bf16[16,128,512]{2,1,0:T(8,128)(2,1)} custom-call(s32[18]{0:T(128)} %get-tuple-element.31.place_ref, s32[8,1024]{1,0:T(8,128)} %broadcast_select_fusion.slot_ref, bf16[8,192,384]{2,1,0:T(8,128)(2,1)} %gate_up.1.act_ref, bf16[8,384,4096]{2,1,0:T(8,128)(2,1)} %wd1_ref.5, bf16[8,384,4096]{2,1,0:T(8,128)(2,1)} %wd1_ref.5), custom_call_target="tpu_custom_call" | custom-call | flops 2415919104 | bytes 8388608 | tf_op jit(solution)/shard_map/down_mix/pallas_call | solution.py:227
  227.0 2.3 add_convert_fusion.1
  229.3 1.5 collective-permute-start.1
  230.8 10.4 %down_mix.5 = bf16[16,128,512]{2,1,0:T(8,128)(2,1)} custom-call(s32[18]{0:T(128)} %get-tuple-element.32.place_ref, s32[8,1024]{1,0:T(8,128)} %broadcast_select_fusion.slot_ref, bf16[8,192,384]{2,1,0:T(8,128)(2,1)} %gate_up.1.act_ref, bf16[8,384,4096]{2,1,0:T(8,128)(2,1)} %wd1_ref.5, bf16[8,384,4096]{2,1,0:T(8,128)(2,1)} %wd1_ref.5), custom_call_target="tpu_custom_call" | custom-call | flops 2415919104 | bytes 8388608 | tf_op jit(solution)/shard_map/down_mix/pallas_call | solution.py:227
  241.1 2.3 add_convert_fusion
  243.5 0.8 collective-permute-done.1
  244.3 1.4 collective-permute-start.6
  245.7 1.2 add_convert_fusion.3
  246.9 1.6 collective-permute-start.2
  248.5 10.6 %collective-permute-done.6 = bf16[8,128,512]{2,1,0:T(8,128)(2,1)S(1)} collective-permute-done((bf16[8,128,512]{2,1,0:T(8,128)(2,1)S(1)}, bf16[8,128,512]{2,1,0:T(8,128)(2,1)S(1)}, u32[]{:S(2)}, u32[]{:S(2)}) %collective-permute-start.6) | collective-permute-done | bytes 1048608 | tf_op jit(solution)/shard_map/ppermute | solution.py:268
  259.1 2.4 add_convert_fusion.2
  261.5 1.5 collective-permute-start.7
  263.0 1.8 add_convert_fusion.5
  264.8 0.9 collective-permute-start.3
  265.7 14.1 %collective-permute-done.7 = bf16[4,128,512]{2,1,0:T(8,128)(2,1)} collective-permute-done((bf16[4,128,512]{2,1,0:T(8,128)(2,1)}, bf16[4,128,512]{2,1,0:T(8,128)(2,1)}, u32[]{:S(2)}, u32[]{:S(2)}) %collective-permute-start.7) | collective-permute-done | bytes 524320 | tf_op jit(solution)/shard_map/ppermute | solution.py:268
  279.8 1.2 add_convert_fusion.4
  281.0 1.2 collective-permute-start.8
  282.2 0.7 constant_dynamic-slice_fusion
  282.9 1.3 add_convert_fusion.7
  284.1 1.5 collective-permute-start.4
  285.7 7.9 %collective-permute-done.8 = bf16[2,128,512]{2,1,0:T(8,128)(2,1)} collective-permute-done((bf16[2,128,512]{2,1,0:T(8,128)(2,1)S(1)}, bf16[2,128,512]{2,1,0:T(8,128)(2,1)}, u32[]{:S(2)}, u32[]{:S(2)}) %collective-permute-start.8) | collective-permute-done | bytes 262176 | tf_op jit(solution)/shard_map/ppermute | solution.py:268
  293.6 1.2 add_convert_fusion.6
  294.8 1.6 collective-permute-start.9
  296.4 1.2 add_bitcast_fusion.1
  297.6 2.3 collective-permute-done.9
  299.9 1.3 add_bitcast_fusion
  301.1 1.7 fusion
  (33 shorter events, 0.1 us)
Async XLA Ops:
  6.5 55.0 %copy-start = (bf16[1024,512]{1,0:T(8,128)(2,1)S(1)}, bf16[1024,512]{1,0:T(8,128)(2,1)}, u32[]{:S(2)}) copy-start(bf16[1024,512]{1,0:T(8,128)(2,1)} %param.10) | copy-start | bytes 3145732
  6.5 55.0 %all-gather.3.cloned.1.call-start = ((), (), s32[]{:S(2)}) async-start(), calls=%async_computation.2 | async-start | bytes 2359296 | tf_op jit(solution)/shard_map/all_gather | solution.py:376
  7.3 81.8 %reduce-scatter.2.cloned.1.call-start = ((), (), s32[]{:S(2)}) async-start(), calls=%async_computation.3 | async-start | bytes 1310720 | tf_op jit(solution)/shard_map/reduce_scatter | solution.py:380
  43.6 21.8 %copy-start.5 = (bf16[128,4096]{1,0:T(8,128)(2,1)S(1)}, bf16[128,4096]{1,0:T(8,128)(2,1)}, u32[]{:S(2)}) copy-start(bf16[128,4096]{1,0:T(8,128)(2,1)} %param.11) | copy-start | bytes 3145732
  65.5 6.1 %copy-start.8 = (f32[4096]{0:T(1024)S(1)}, f32[4096]{0:T(1024)}, u32[]{:S(2)}) copy-start(f32[4096]{0:T(1024)} %param.12) | copy-start | bytes 49156
  67.9 12.1 %all-to-all-start = ((bf16[8,128,128]{1,2,0:T(8,128)(2,1)}), bf16[8,128,128]{1,2,0:T(8,128)(2,1)S(1)}, u32[]{:S(2)}, u32[]{:S(2)}) async-start(bf16[8,128,128]{1,2,0:T(8,128)(2,1)} %bitcast.1), calls=%async_computation | async-start | bytes 524288 | tf_op jit(solution)/shard_map/all_to_all | solution.py:372
  71.3 98.5 %all-gather.5.cloned.1.call-start = ((), (), s32[]{:S(2)}) async-start(), calls=%async_computation.4 | async-start | bytes 8650752 | tf_op jit(solution)/shard_map/all_gather | solution.py:385
  216.1 10.8 %collective-permute-start = (bf16[16,128,512]{2,1,0:T(8,128)(2,1)}, bf16[16,128,512]{2,1,0:T(8,128)(2,1)S(1)}, u32[]{:S(2)}, u32[]{:S(2)}) collective-permute-start(bf16[16,128,512]{2,1,0:T(8,128)(2,1)} %get-tuple-element.18), channel_id=1, source_target_pairs={{0,1},{1,0},{2,3},{3,2},{4,5},{5,4},{6,7},{7,6},{8,9},{9,8},{10,11... | collective-permute-start | bytes 6291464 | tf_op jit(solution)/shard_map/ppermute | solution.py:268
  216.4 24.7 %collective-permute-start.5 = (bf16[16,128,512]{2,1,0:T(8,128)(2,1)}, bf16[16,128,512]{2,1,0:T(8,128)(2,1)S(1)}, u32[]{:S(2)}, u32[]{:S(2)}) collective-permute-start(bf16[16,128,512]{2,1,0:T(8,128)(2,1)} %get-tuple-element.20), channel_id=1, source_target_pairs={{0,1},{1,0},{2,3},{3,2},{4,5},{5,4},{6,7},{7,6},{8,9},{9,8},{10,11... | collective-permute-start | bytes 6291464 | tf_op jit(solution)/shard_map/ppermute | solution.py:268
  227.0 36.0 %copy-start.4 = (bf16[16,128,512]{2,1,0:T(8,128)(2,1)}, bf16[16,128,512]{2,1,0:T(8,128)(2,1)S(1)}, u32[]{:S(2)}) copy-start(bf16[16,128,512]{2,1,0:T(8,128)(2,1)S(1)} %collective-permute-done) | copy-start | bytes 6291460
  229.3 15.0 %collective-permute-start.1 = (bf16[8,128,512]{2,1,0:T(8,128)(2,1)S(1)}, bf16[8,128,512]{2,1,0:T(8,128)(2,1)}, u32[]{:S(2)}, u32[]{:S(2)}) collective-permute-start(bf16[8,128,512]{2,1,0:T(8,128)(2,1)S(1)} %add_convert_fusion.1), channel_id=1, source_target_pairs={{0,2},{1,5},{2,0},{3,7},{4,6},{5,1},{6,4},{7,3},{8,10},{9,13},{10,... | collective-permute-start | bytes 3145736 | tf_op jit(solution)/shard_map/ppermute | solution.py:268
  241.1 4.5 %copy-start.2 = (bf16[16,128,512]{2,1,0:T(8,128)(2,1)S(1)}, bf16[16,128,512]{2,1,0:T(8,128)(2,1)}, u32[]{:S(2)}) copy-start(bf16[16,128,512]{2,1,0:T(8,128)(2,1)} %down_mix.3) | copy-start | bytes 6291460
  241.1 17.9 %copy-start.3 = (bf16[16,128,512]{2,1,0:T(8,128)(2,1)}, bf16[16,128,512]{2,1,0:T(8,128)(2,1)S(1)}, u32[]{:S(2)}) copy-start(bf16[16,128,512]{2,1,0:T(8,128)(2,1)S(1)} %collective-permute-done.5) | copy-start | bytes 6291460
  244.3 14.8 %collective-permute-start.6 = (bf16[8,128,512]{2,1,0:T(8,128)(2,1)S(1)}, bf16[8,128,512]{2,1,0:T(8,128)(2,1)S(1)}, u32[]{:S(2)}, u32[]{:S(2)}) collective-permute-start(bf16[8,128,512]{2,1,0:T(8,128)(2,1)S(1)} %add_convert_fusion), channel_id=1, source_target_pairs={{0,2},{1,5},{2,0},{3,7},{4,6},{5,1},{6,4},{7,3},{8,10},{9,13},{10,... | collective-permute-start | bytes 3145736 | tf_op jit(solution)/shard_map/ppermute | solution.py:268
  246.9 14.6 %collective-permute-start.2 = (bf16[4,128,512]{2,1,0:T(8,128)(2,1)S(1)}, bf16[4,128,512]{2,1,0:T(8,128)(2,1)S(1)}, u32[]{:S(2)}, u32[]{:S(2)}) collective-permute-start(bf16[4,128,512]{2,1,0:T(8,128)(2,1)S(1)} %add_convert_fusion.3), channel_id=1, source_target_pairs={{0,8},{1,9},{2,10},{3,11},{4,12},{5,13},{6,14},{7,15},{8,0},{9,1},... | collective-permute-start | bytes 1572872 | tf_op jit(solution)/shard_map/ppermute | solution.py:268
  259.1 22.0 %copy-start.6 = (bf16[8,128,512]{2,1,0:T(8,128)(2,1)}, bf16[8,128,512]{2,1,0:T(8,128)(2,1)S(1)}, u32[]{:S(2)}) copy-start(bf16[8,128,512]{2,1,0:T(8,128)(2,1)S(1)} %collective-permute-done.6) | copy-start | bytes 3145732
  261.5 3.3 %copy-start.7 = (bf16[4,128,512]{2,1,0:T(8,128)(2,1)}, bf16[4,128,512]{2,1,0:T(8,128)(2,1)S(1)}, u32[]{:S(2)}) copy-start(bf16[4,128,512]{2,1,0:T(8,128)(2,1)S(1)} %collective-permute-done.2) | copy-start | bytes 1572868
  261.5 18.3 %collective-permute-start.7 = (bf16[4,128,512]{2,1,0:T(8,128)(2,1)}, bf16[4,128,512]{2,1,0:T(8,128)(2,1)}, u32[]{:S(2)}, u32[]{:S(2)}) collective-permute-start(bf16[4,128,512]{2,1,0:T(8,128)(2,1)} %add_convert_fusion.2), channel_id=1, source_target_pairs={{0,8},{1,9},{2,10},{3,11},{4,12},{5,13},{6,14},{7,15},{8,0},{9,1},... | collective-permute-start | bytes 1572872 | tf_op jit(solution)/shard_map/ppermute | solution.py:268
  264.8 16.3 %collective-permute-start.3 = (bf16[2,128,512]{2,1,0:T(8,128)(2,1)}, bf16[2,128,512]{2,1,0:T(8,128)(2,1)}, u32[]{:S(2)}, u32[]{:S(2)}) collective-permute-start(bf16[2,128,512]{2,1,0:T(8,128)(2,1)} %add_convert_fusion.5), channel_id=1, source_target_pairs={{0,16},{1,17},{2,18},{3,19},{4,20},{5,21},{6,22},{7,23},{8,24},{9,... | collective-permute-start | bytes 786440 | tf_op jit(solution)/shard_map/ppermute | solution.py:268
  281.0 12.5 %collective-permute-start.8 = (bf16[2,128,512]{2,1,0:T(8,128)(2,1)S(1)}, bf16[2,128,512]{2,1,0:T(8,128)(2,1)}, u32[]{:S(2)}, u32[]{:S(2)}) collective-permute-start(bf16[2,128,512]{2,1,0:T(8,128)(2,1)S(1)} %add_convert_fusion.4), channel_id=1, source_target_pairs={{0,16},{1,17},{2,18},{3,19},{4,20},{5,21},{6,22},{7,23},{8,24},{9,... | collective-permute-start | bytes 786440 | tf_op jit(solution)/shard_map/ppermute | solution.py:268
  282.9 20.0 %copy-start.1 = (bf16[1024,512]{1,0:T(8,128)(2,1)S(1)}, bf16[1024,512]{1,0:T(8,128)(2,1)}, u32[]{:S(2)}) copy-start(bf16[1024,512]{1,0:T(8,128)(2,1)} %param.10) | copy-start | bytes 3145732
  284.1 10.7 %collective-permute-start.4 = (bf16[1,128,512]{2,1,0:T(8,128)(2,1)S(1)}, bf16[1,128,512]{2,1,0:T(8,128)(2,1)S(1)}, u32[]{:S(2)}, u32[]{:S(2)}) collective-permute-start(bf16[1,128,512]{2,1,0:T(8,128)(2,1)S(1)} %add_convert_fusion.7), channel_id=1, source_target_pairs={{0,4},{1,3},{2,6},{3,1},{4,0},{5,7},{6,2},{7,5},{8,12},{9,11},{10,... | collective-permute-start | bytes 393224 | tf_op jit(solution)/shard_map/ppermute | solution.py:268
  294.8 5.0 %collective-permute-start.9 = (bf16[1,128,512]{2,1,0:T(8,128)(2,1)S(1)}, bf16[1,128,512]{2,1,0:T(8,128)(2,1)S(1)}, u32[]{:S(2)}, u32[]{:S(2)}) collective-permute-start(bf16[1,128,512]{2,1,0:T(8,128)(2,1)S(1)} %add_convert_fusion.6), channel_id=1, source_target_pairs={{0,4},{1,3},{2,6},{3,1},{4,0},{5,7},{6,2},{7,5},{8,12},{9,11},{10,... | collective-permute-start | bytes 393224 | tf_op jit(solution)/shard_map/ppermute | solution.py:268
Sparse Core Ops, SparseCore 0:
  9.5 52.0 all-gather.2
  65.6 23.3 reduce-scatter.1
  92.3 77.4 all-gather.4

commit v3 on v2

--- a/solution.py
+++ b/solution.py
@@ -13,7 +13,7 @@
 F32 = jnp.float32
 PAIR = 2
 LANES = 128
-VMEM_BYTES = 56 * 1024 * 1024
+HEAD_ORDER = (0, 2, 1, 3)
 
 
 def slot_places(ids, experts, capacity):
@@ -76,62 +76,149 @@
     return places == slot_row
 
 
+def project_kernel(member_ref, head_refs, weight_ref, send_ref, keep_ref):
+    core, x_side, z = member_ref[0], member_ref[1], member_ref[2]
+    result = jnp.dot(
+        jnp.concatenate([ref[...] for ref in head_refs], axis=0),
+        weight_ref[...],
+        preferred_element_type=F32,
+    ).astype(BF16)
+    here = head_refs[0].shape[0]
+    for to_x in range(2):
+        x_kept = (x_side == to_x).astype(jnp.int32)
+        for to_core in range(2):
+            start = (to_x * 2 + to_core) * LANES
+            for out_ref, wanted in ((keep_ref, core == to_core), (send_ref, core != to_core)):
+
+                @pl.when(wanted)
+                def _(out_ref=out_ref, x_kept=x_kept, start=start):
+                    for piece, z_bits in enumerate(HEAD_ORDER):
+                        out_ref[x_kept, z ^ z_bits] = result[
+                            piece * here : (piece + 1) * here, start : start + LANES
+                        ]
+
+
+def project(member_info, pieces, out_proj):
+    here = pieces[0].shape[0]
+    out = jax.ShapeDtypeStruct((2, len(pieces), here, LANES), BF16)
+    vmem = pl.BlockSpec(memory_space=pltpu.VMEM)
+
+    def kernel(member_ref, *refs):
+        project_kernel(member_ref, refs[:4], refs[4], refs[5], refs[6])
+
+    return pl.pallas_call(
+        kernel,
+        in_specs=[pl.BlockSpec(memory_space=pltpu.SMEM)] + [vmem] * 5,
+        out_specs=[vmem, vmem],
+        out_shape=[out, out],
+        compiler_params=pltpu.CompilerParams(vmem_limit_bytes=24 * 1024 * 1024),
+        cost_estimate=pl.CostEstimate(
+            flops=2 * 4 * here * out_proj.size,
+            bytes_accessed=2 * (out_proj.size + 5 * pieces[0].size),
+            transcendentals=0,
+        ),
+        name="project",
+    )(member_info, *pieces, out_proj)
+
+
 def gate_up_kernel(
-    experts, rows, width, slot_ref, weight_ref, x_ref, invgain_ref, wg_ref, wu_ref, act_ref,
-    xs_ref, acc_ref, sq_ref, scale_ref
+    experts, rows, width, info_ref, slot_ref, weight_ref, invgain_ref, x_refs, wg_ref, wu_ref,
+    act_ref, hidden_ref, xs_ref, acc_ref, sq_ref, scale_ref, hits_ref
 ):
-    chunk, expert = pl.program_id(0), pl.program_id(1)
-    blocks, tokens, lanes = x_ref.shape
-    span = PAIR * 128
-    parts = tokens // span
-
-    @pl.when(expert == 0)
+    expert, chunk = pl.program_id(0), pl.program_id(1)
+    arrays = len(x_refs) // 2
+    each, parts, here, lanes = x_refs[0].shape
+    blocks = arrays * each
+    span = 2 * here
+    member, z = info_ref[2 * blocks], info_ref[2 * blocks + 1]
+    depth = wg_ref.shape[1]
+
+    @pl.when((expert == 0) & (chunk == 0))
     def _():
-        @pl.when(chunk == 0)
-        def _():
-            sq_ref[...] = jnp.zeros_like(sq_ref)
-
+        sq_ref[...] = jnp.zeros_like(sq_ref)
         for part in range(parts):
-            window = slice(part * span, (part + 1) * span)
-            hits = jnp.concatenate(
-                [hits_of(slot_ref[e : e + 1, window], rows) for e in range(experts)], axis=0
-            )
-            pieces = [x_ref[b, window, :] for b in range(blocks)]
-            total = sq_ref[window, :]
-            for b in range(blocks):
-                value = pieces[b].astype(F32) * invgain_ref[b : b + 1, :]
-                total = total + value * value
-            sq_ref[window, :] = total
-            picked = jnp.dot(
-                hits.astype(F32).astype(BF16),
-                jnp.concatenate(pieces, axis=1),
-                preferred_element_type=F32,
-            ).astype(BF16)
             for e in range(experts):
-                xs_ref[e, part * rows : (part + 1) * rows, :] = picked[e * rows : (e + 1) * rows, :]
-
-    @pl.when((expert == 0) & (chunk == pl.num_programs(0) - 1))
-    def _():
-        total = jnp.sum(jnp.transpose(sq_ref[...]), axis=0, keepdims=True)
+                first = hits_of(slot_ref[e : e + 1, part * span : part * span + here], rows)
+                second = hits_of(
+                    slot_ref[e : e + 1, part * span + here : (part + 1) * span], rows
+                )
+                first = first.astype(F32).astype(BF16)
+                second = second.astype(F32).astype(BF16)
+                window = slice(e * rows, (e + 1) * rows)
+                hits_ref[0, part, window, :] = jnp.concatenate([first, second], axis=1)
+                hits_ref[1, part, window, :] = jnp.concatenate([second, first], axis=1)
+
+        def pair_of_blocks(low, carry):
+            for array in range(arrays):
+                own, other = x_refs[2 * array], x_refs[2 * array + 1]
+                swapped = info_ref[blocks + array * each + low]
+                places = (low, low + each // 2)
+                features = [info_ref[array * each + place] for place in places]
+                for place, feature in zip(places, features):
+                    invgain = invgain_ref[pl.ds(feature, 1), :]
+                    for part in range(parts):
+                        for half, ref in enumerate((own, other)):
+                            value = ref[place, part].astype(F32) * invgain
+                            sq_ref[swapped, part, half] += value * value
+
+                    @pl.when(feature >> 3 == member)
+                    def _(place=place, feature=feature, invgain=invgain):
+                        mine = jnp.where(
+                            swapped == 0, own[place, z].astype(F32), other[place, z].astype(F32)
+                        )
+                        column = pl.multiple_of((feature & 7) * lanes, lanes)
+                        hidden_ref[:, pl.ds(column, lanes)] = mine * invgain
+
+                for part in range(parts):
+                    both = jnp.concatenate(
+                        [
+                            jnp.concatenate([own[place, part], other[place, part]], axis=0)
+                            for place in places
+                        ],
+                        axis=1,
+                    )
+                    picked = jnp.dot(
+                        hits_ref[swapped, part], both, preferred_element_type=F32
+                    ).astype(BF16)
+                    for number, feature in enumerate(features):
+                        column = pl.multiple_of(feature * lanes, lanes)
+                        for e in range(experts):
+                            xs_ref[e, part * rows : (part + 1) * rows, pl.ds(column, lanes)] = (
+                                picked[
+                                    e * rows : (e + 1) * rows, number * lanes : (number + 1) * lanes
+                                ]
+                            )
+            return carry
+
+        lax.fori_loop(0, each // 2, pair_of_blocks, 0)
+        pieces = [
+            sq_ref[0, part, half] + sq_ref[1, part, 1 - half]
+            for part in range(parts)
+            for half in range(2)
+        ]
+        total = jnp.sum(
+            jnp.transpose(jnp.concatenate(pieces, axis=0)), axis=0, keepdims=True
+        )
         scale_ref[...] = jnp.broadcast_to(lax.rsqrt(total / width + 1e-06), scale_ref.shape)
 
     both = jnp.dot(
-        xs_ref[expert],
+        xs_ref[expert, :, pl.ds(pl.multiple_of(chunk * depth, depth), depth)],
         jnp.concatenate([wg_ref[0], wu_ref[0]], axis=1),
         preferred_element_type=F32,
     )
 
     @pl.when(chunk == 0)
     def _():
-        acc_ref[expert] = both
-
-    @pl.when(chunk > 0)
+        acc_ref[...] = both
+
+    @pl.when((chunk > 0) & (chunk < pl.num_programs(1) - 1))
     def _():
-        acc_ref[expert] += both
-
-    @pl.when(chunk == pl.num_programs(0) - 1)
+        acc_ref[...] += both
+
+    @pl.when(chunk == pl.num_programs(1) - 1)
     def _():
         hidden_units = wg_ref.shape[2]
+        summed = acc_ref[...] + both
         for part in range(parts):
             window = slice(part * span, (part + 1) * span)
             hits = hits_of(slot_ref[pl.ds(expert, 1), window], rows)
@@ -141,51 +228,65 @@
             weight = jnp.sum(
                 jnp.where(hits, weight_ref[pl.ds(expert, 1), window], 0.0), axis=1, keepdims=True
             )
-            both_part = acc_ref[expert, part * rows : (part + 1) * rows, :]
+            both_part = summed[part * rows : (part + 1) * rows, :]
             gate = both_part[:, :hidden_units] * scale
             upper = both_part[:, hidden_units:] * scale
             act = gate / (1.0 + jnp.exp(-gate)) * upper * weight
             act_ref[expert, part * rows : (part + 1) * rows, :] = act.astype(BF16)
 
 
-def gate_up(slots, weights, x, invgain, w_gate, w_up, rows, per_chunk):
+def gate_up(info, slots, weights, invgain, x, w_gate, w_up, rows, chunks):
     experts, width, hidden_units = w_gate.shape
-    blocks, tokens, lanes = x.shape
-    parts = tokens // (PAIR * 128)
-    depth = per_chunk * lanes
+    each, parts, here, lanes = x[0].shape
+    tokens = slots.shape[1]
+    members = width // (each * lanes)
+    depth = width // chunks
+
+    def kernel(info_ref, slot_ref, weight_ref, invgain_ref, *rest):
+        gate_up_kernel(
+            experts, rows, width, info_ref, slot_ref, weight_ref, invgain_ref,
+            rest[: len(x)], *rest[len(x) :]
+        )
+
+    def whole(shape):
+        return pl.BlockSpec(
+            shape, lambda e, k, info: (0,) * len(shape), pipeline_mode=pl.Buffered(1)
+        )
+
     return pl.pallas_call(
-        functools.partial(gate_up_kernel, experts, rows, width),
-        grid=(blocks // per_chunk, experts),
-        in_specs=[
-            pl.BlockSpec((experts, tokens), lambda k, e: (0, 0)),
-            pl.BlockSpec((experts, tokens), lambda k, e: (0, 0)),
-            pl.BlockSpec((per_chunk, tokens, lanes), lambda k, e: (k, 0, 0)),
-            pl.BlockSpec((per_chunk, lanes), lambda k, e: (k, 0)),
-            pl.BlockSpec(
-                (1, depth, hidden_units), lambda k, e: (e, k, 0)
-            ),
-            pl.BlockSpec(
-                (1, depth, hidden_units), lambda k, e: (e, k, 0)
-            ),
-        ],
-        out_specs=pl.BlockSpec((experts, parts * rows, hidden_units), lambda k, e: (0, 0, 0)),
-        out_shape=jax.ShapeDtypeStruct((experts, parts * rows, hidden_units), BF16),
-        scratch_shapes=[
-            pltpu.VMEM((experts, parts * rows, depth), BF16),
-            pltpu.VMEM((experts, parts * rows, 2 * hidden_units), F32),
-            pltpu.VMEM((tokens, lanes), F32),
-            pltpu.VMEM((8, tokens), F32),
+        kernel,
+        grid_spec=pltpu.PrefetchScalarGridSpec(
+            num_scalar_prefetch=1,
+            grid=(experts, chunks),
+            in_specs=[whole(slots.shape), whole(weights.shape), whole(invgain.shape)]
+            + [pl.BlockSpec(memory_space=pltpu.VMEM)] * len(x)
+            + [pl.BlockSpec((1, depth, hidden_units), lambda e, k, info: (e, k, 0))] * 2,
+            out_specs=[
+                pl.BlockSpec((experts, parts * rows, hidden_units), lambda e, k, info: (0, 0, 0)),
+                pl.BlockSpec((here, width // members), lambda e, k, info: (0, 0)),
+            ],
+            scratch_shapes=[
+                pltpu.VMEM((experts, parts * rows, width), BF16),
+                pltpu.VMEM((parts * rows, 2 * hidden_units), F32),
+                pltpu.VMEM((2, parts, 2, here, lanes), F32),
+                pltpu.VMEM((8, tokens), F32),
+                pltpu.VMEM((2, parts, experts * rows, 2 * here), BF16),
+            ],
+        ),
+        out_shape=[
+            jax.ShapeDtypeStruct((experts, parts * rows, hidden_units), BF16),
+            jax.ShapeDtypeStruct((here, width // members), F32),
         ],
         compiler_params=pltpu.CompilerParams(
-            vmem_limit_bytes=VMEM_BYTES, dimension_semantics=("arbitrary", "arbitrary")
+            vmem_limit_bytes=40 * 1024 * 1024, dimension_semantics=("arbitrary", "arbitrary")
         ),
         cost_estimate=pl.CostEstimate(
             flops=2 * experts * parts * rows * width * 2 * hidden_units,
-            bytes_accessed=4 * experts * width * hidden_units + 2 * x.size,
+            bytes_accessed=4 * experts * width * hidden_units + 2 * len(x) * x[0].size,
             transcendentals=0,
         ),
         name="gate_up",
-    )(slots, weights, x, invgain, w_gate, w_up)
+    )(info, slots, weights, invgain, *x, w_gate, w_up)
 
 
 def down_kernel(rows, place_ref, slot_ref, act_ref, wd0_ref, wd1_ref, *rest):
@@ -230,8 +331,8 @@
             num_scalar_prefetch=1,
             grid=(experts,),
             in_specs=[
-                pl.BlockSpec((experts, tokens), lambda e, p: (0, 0)),
-                pl.BlockSpec(act.shape, lambda e, p: (0, 0, 0)),
+                pl.BlockSpec(memory_space=pltpu.VMEM),
+                pl.BlockSpec(memory_space=pltpu.VMEM),
                 pl.BlockSpec(
                     (1, hidden_units, cols),
                     lambda e, p: (e, 0, p[0])
@@ -250,7 +351,7 @@
         out_shape=[jax.ShapeDtypeStruct((2 * groups, tokens // groups, cols // chunks), BF16)]
         * chunks,
         compiler_params=pltpu.CompilerParams(
-            vmem_limit_bytes=VMEM_BYTES, dimension_semantics=("arbitrary",)
+            vmem_limit_bytes=32 * 1024 * 1024, dimension_semantics=("arbitrary",)
         ),
         cost_estimate=pl.CostEstimate(
             flops=8 * experts * parts * rows * cols * hidden_units,
@@ -279,8 +380,13 @@
     return X if core else Y
 
 
-def halving_places(to_core, group, member, groups):
-    g = jnp.arange(groups, dtype=jnp.int32)[None, :]
+def own_order(groups, group):
+    order = jnp.arange(groups, dtype=jnp.int32)
+    return order ^ (group & 1)
+
+
+def halving_places(to_core, group, groups):
+    g = own_order(groups, group)[None, :]
     y_kept = ((g & 1) == (group & 1)).astype(jnp.int32)
     low_kept = (((g >> 1) & 1) == ((group >> 1) & 1)).astype(jnp.int32)
     high_kept = ((g >> 2) == (group >> 2)).astype(jnp.int32)
@@ -329,28 +435,84 @@
     return [total_of([term[0] for term in terms]) for terms in chunks]
 
 
-def route_tables(route_ids, route_weights, group, experts):
-    rows_here = route_ids.shape[0]
+def route_tables(route_ids, route_weights, group, experts, groups):
+    here, top = route_ids.shape
     shares = route_weights / jnp.sum(route_weights, axis=-1, keepdims=True)
-    table = jnp.concatenate([route_ids.astype(F32), shares], axis=1)
-    table = lax.all_gather(table, "expert", axis=0, tiled=True)
-    ids = table[:, : route_ids.shape[1]].astype(jnp.int32)
-    shares = table[:, route_ids.shape[1] :]
-    tokens = ids.shape[0]
+    table = jnp.concatenate([route_ids.astype(F32), shares], axis=1).T[None]
+    for bits in (ZHIGH, ZLOW, Y):
+        table = jnp.concatenate([table, flip(table, lambda core, bits=bits: bits)], axis=0)
+    apart = own_order(groups, group) ^ group
+    place = (apart >> 2) | (apart & 2) | ((apart & 1) << 2)
+    table = jnp.take(table, place, axis=0, mode="clip")
     own = group * experts + jnp.arange(experts, dtype=jnp.int32)
-    match = ids.T[None, :, :] == own[:, None, None]
-    named = jnp.any(match, axis=1)
-    weights = jnp.sum(jnp.where(match, shares.T[None, :, :], 0.0), axis=1)
-    span = PAIR * rows_here
+    ids = table[:, :top, :].astype(jnp.int32)
+    match = ids[None] == own[:, None, None, None]
+    named = jnp.any(match, axis=2)
+    weights = jnp.sum(jnp.where(match, table[None, :, top:, :], 0.0), axis=2)
+    span = PAIR * here
     order = jnp.arange(span)
     earlier = (order[:, None] < order[None, :]).astype(BF16)
     rank = jnp.dot(
-        named.astype(BF16).reshape(experts * tokens // span, span),
+        named.astype(BF16).reshape(experts * groups // PAIR, span),
         earlier,
         preferred_element_type=F32,
     )
-    slots = jnp.where(named, rank.reshape(experts, tokens).astype(jnp.int32), -1)
-    return slots, weights
+    slots = jnp.where(named, rank.reshape(named.shape).astype(jnp.int32), -1)
+    return slots.reshape(experts, groups * here), weights.reshape(experts, groups * here)
+
+
+def block_table(device, groups, member):
+    number = jnp.arange(32, dtype=jnp.int32)
+    array, place = number >> 3, number & 7
+    source_core = (device & 1) ^ (array >> 1)
+    first = jnp.where(source_core == 0, X, Y)
+    last = jnp.where(source_core == 0, Y, X)
+    feature = (
+        device
+        ^ (array >> 1)
+        ^ jnp.where(array & 1 == 1, first, 0)
+        ^ jnp.where(place & 1 == 1, last, 0)
+        ^ jnp.where(place & 2 == 2, ZHIGH, 0)
+        ^ jnp.where(place & 4 == 4, ZLOW, 0)
+    )
+    swapped = ((feature ^ device) >> 2) & 1
+    return jnp.concatenate([feature, swapped, jnp.stack([member, device >> 3])])
+
+
+def gather_chunks(starts):
+    stages = (last_axis, lambda core: ZHIGH, lambda core: ZLOW, first_axis)
+    held = [[start] for start in starts]
+    arrived = {}
+    for tick in range(len(stages) + len(starts) - 1):
+        for index in range(len(starts)):
+            stage = tick - index
+            if not 0 <= stage < len(stages):
+                continue
+            block = held[index][-1]
+            if index:
+                block, _ = after(block, arrived[index - 1, stage])
+            came = flip(block, stages[stage])
+            arrived[index, stage] = came
+            if stage < len(stages) - 1:
+                held[index].append(jnp.concatenate([block, came], axis=0))
+            else:
+                other = flip(block, lambda core: CORE)
+                held[index] = [block, came, other, flip(came, lambda core: CORE)]
+    return held
+
+
+def gather_heads(heads, beside):
+    def along(bits, piece):
+        return flip(piece, lambda core: bits)
+
+    high = along(ZHIGH, heads)
+    low = along(ZLOW, heads)
+    high, beside = after(high, beside)
+    both = along(ZLOW, high)
+    own = [heads, high, low, both]
+    other = [along(Y, piece) for piece in own]
+    own, _ = after(own, (other[0], other[1]))
+    return own, other, beside
 
 
 def per_device_tokens(
@@ -358,41 +520,52 @@
 ):
     groups, members = lax.axis_size("expert"), lax.axis_size("tensor")
     group, member = lax.axis_index("expert"), lax.axis_index("tensor")
+    device = group * members + member
     here, width = residual.shape
     experts = w_gate.shape[0]
-    tokens = groups * here
-    lanes = width // (groups * members)
     rows = -(-PAIR * CAP // 16) * 16
-
-    slots, weights = route_tables(route_ids, route_weights, group, experts)
+    x_side, core, y_side, z = member >> 1, member & 1, group & 1, group >> 1
 
     own_cols = lax.dynamic_index_in_dim(
-        residual.reshape(here, groups, members, lanes), member, 2, keepdims=False
+        residual.reshape(here, groups, members, LANES), member, 2, keepdims=False
     )
     moved = lax.all_to_all(
         jnp.transpose(own_cols, (1, 0, 2)), "expert", split_axis=0, concat_axis=0, tiled=True
-    ).reshape(tokens, lanes)
-
-    heads = lax.all_gather(attn_heads, "expert", axis=0, tiled=True)
-    part = jnp.dot(heads, out_proj, preferred_element_type=F32).astype(BF16)
-    part = jnp.transpose(part.reshape(tokens, members, lanes), (1, 0, 2))
-    part, slots, weights = lax.optimization_barrier((part, slots, weights))
-    attn_out = lax.psum_scatter(part, "tensor", scatter_dimension=0, tiled=True)[0]
-    hidden = moved.astype(F32) + attn_out.astype(F32)
+    ).reshape(groups // 2, 2, here, LANES)
     gain = lax.dynamic_index_in_dim(
-        norm_gain.reshape(groups * members, lanes), group * members + member, 0, keepdims=True
-    )
-    x = lax.all_gather((hidden * gain).astype(BF16), ("expert", "tensor"), axis=0)
-
-    invgain = (1.0 / norm_gain).reshape(groups * members, lanes)
-    act = gate_up(slots, weights, x, invgain, w_gate, w_up, rows, per_chunk=16)
+        norm_gain.reshape(groups * members, LANES), device, 0, keepdims=False
+    )
+
+    member_info = jnp.stack([core, x_side, z])
+    slots, weights = route_tables(route_ids, route_weights, group, experts, groups)
+    starts = []
+    own_heads, other_heads, moved = gather_heads(attn_heads, moved)
+    for half, pieces in enumerate((own_heads, other_heads)):
+        if half:
+            (pieces, moved, gain), _ = after((pieces, moved, gain), (starts[0], slots, weights))
+        send, keep = project(member_info, pieces, out_proj)
+        came = flip(send, lambda c: CORE)
+        to_x = (keep[0].astype(F32) + came[0].astype(F32)).astype(BF16)
+        if not half:
+            to_x, _ = after(to_x, other_heads[2])
+        from_x = flip(to_x, lambda c: X)
+        hidden = lax.dynamic_index_in_dim(moved, y_side ^ half, 1, keepdims=False).astype(F32)
+        hidden = hidden + total_of([keep[1], came[1], from_x])
+        starts.append((hidden * gain).astype(BF16)[None])
+
+    own_x, other_x = gather_chunks(starts)
+    x = [piece for pair in zip(own_x, other_x) for piece in pair]
+    invgain = (1.0 / norm_gain).reshape(groups * members, LANES)
+    act, own_hidden = gate_up(
+        block_table(device, groups, member), slots, weights, invgain, x, w_gate, w_up, rows, 2
+    )
+
     cols = width // members
-    x_side, core = member >> 1, member & 1
 
     def columns_of(to_core, chunk, chunks):
         sides = jnp.stack([1 - x_side, x_side])
         blocks = (sides * 2 + to_core) * chunks + chunk
-        return jnp.concatenate([blocks, halving_places(to_core, group, member, groups)])
+        return jnp.concatenate([blocks, halving_places(to_core, group, groups)])
 
     chunks = 2
     chunk_cols = cols // chunks
@@ -409,12 +582,6 @@
 
     sums = reduce_chunks([functools.partial(terms_of, chunk) for chunk in range(chunks)])
     mixture = jnp.concatenate(sums, axis=1)
-    per_member = groups
-    own = lax.dynamic_slice(
-        x, (member * per_member, group * here, 0), (per_member, here, lanes)
-    ).astype(F32)
-    own_invgain = lax.dynamic_slice(invgain, (member * per_member, 0), (per_member, lanes))
-    own_hidden = jnp.transpose(own * own_invgain[:, None, :], (1, 0, 2)).reshape(here, cols)
     return (own_hidden + mixture).astype(BF16)
 
 

time: 310 us -> 254 us (0.82)
  blocking collectives: 32.5 us -> 0 us
  waiting for transfers between devices: 149 us -> 119 us
  starting transfers between devices: 15.4 us -> 40.2 us
  between operations: 13.4 us -> 0.41 us
  other arithmetic: 24.1 us -> 17.9 us
  matrix products: 4.02 us -> 0.15 us
  Pallas kernels: 67 us -> 70.5 us
    all_gather x2 -> x0, waiting for transfers between devices: 95.1 us -> none  [the longest x1 77.2 us: per_device_tokens(): lax.all_gather((hidden * gain).astype(BF16), ('expert', 'tensor'), axis=0)]
    ppermute x10 -> x36, waiting for transfers between devices: 35.6 us -> 114 us  [flip(): return lax.ppermute(array, ('expert', 'tensor'), pairs)]
    all_gather x1 -> x0, blocking collectives: 32.5 us -> none  [route_tables(): table = lax.all_gather(table, 'expert', axis=0, tiled=True)]
    ppermute x10 -> x36, starting transfers between devices: 11.7 us -> 36.1 us  [flip(): return lax.ppermute(array, ('expert', 'tensor'), pairs)]
    reduce_scatter x1 -> x0, waiting for transfers between devices: 8.82 us -> none  [per_device_tokens(): lax.psum_scatter(part, 'tensor', scatter_dimension=0, tiled=True)[0]]
    pallas_call x1 -> x3, Pallas kernels: 32.1 us -> 39.9 us  [the longest x1 37.3 us: gate_up(): pl.pallas_call(kernel, grid_spec=pltpu.PrefetchScalarGridSpec(num_scalar_...]
    pallas_call x3, Pallas kernels: 35 us -> 30.5 us  [down(): pl.pallas_call(functools.partial(down_kernel, rows), grid_spec=pltpu.Pref...]
    convert_element_type x8, other arithmetic: 13.8 us -> 9.71 us  [sent_half(): total_of([term[:half] for term in terms]).astype(BF16)]
  transfers between devices with their start and end apart: 14 -> 37, of which waited for: 9 -> 21; matrix products, arithmetic and copies ran while one was open for 8% -> 8% of each run, Pallas kernels for 7% -> 7%
where the time goes in v3:
time: 254 us; the launch traced here: 253 us
  waiting for transfers between devices  119 us (47%)
  Pallas kernels  70.5 us (28%)
  starting transfers between devices  40.2 us (16%)
  other arithmetic  17.9 us (7%)
  local copies, waits for them, and re-layouts  5.47 us (2%)
    ppermute x36, waiting for transfers between devices, flip(): return lax.ppermute(array, ('expert', 'tensor'), pairs)  114 us
    pallas_call x1, Pallas kernels, gate_up(): pl.pallas_call(kernel, grid_spec=pltpu.PrefetchScalarGridSpec(num_scalar_...  37.3 us
    ppermute x36, starting transfers between devices, flip(): return lax.ppermute(array, ('expert', 'tensor'), pairs)  36.1 us
    pallas_call x3, Pallas kernels, down(): pl.pallas_call(functools.partial(down_kernel, rows), grid_spec=pltpu.Pref...  30.5 us
    convert_element_type x8, other arithmetic, sent_half(): total_of([term[:half] for term in terms]).astype(BF16)  9.71 us
  transfers between devices with their start and end apart: 37, of which 21 were waited for; matrix products, arithmetic and copies ran while one was open for 8% of the time, Pallas kernels for 7%

profile of v3, /device:TPU:0, one launch (start us, length us, event | category | flops | bytes accessed | tf_op | source)
XLA Modules:
  0.0 253.2 jit_solution(3500563717802667510)
XLA Ops:
  0.0 3.1 %collective-permute-start.4 = (bf16[128,1024]{1,0:T(8,128)(2,1)}, bf16[128,1024]{1,0:T(8,128)(2,1)S(1)}, u32[]{:S(2)}, u32[]{:S(2)}) collective-permute-start(bf16[128,1024]{1,0:T(8,128)(2,1)} %refs_0_), channel_id=1, source_target_pairs={{0,8},{1,9},{2,10},{3,11},{4,12},{5,13},{6,14},{7,15},{8,0},{9,1},... | collective-permute-start | bytes 786440 | tf_op jit(solution)/shard_map/ppermute | solution.py:369
  3.1 2.6 %collective-permute-start.3 = (bf16[128,1024]{1,0:T(8,128)(2,1)}, bf16[128,1024]{1,0:T(8,128)(2,1)S(1)}, u32[]{:S(2)}, u32[]{:S(2)}) collective-permute-start(bf16[128,1024]{1,0:T(8,128)(2,1)} %refs_0_), channel_id=1, source_target_pairs={{0,16},{1,17},{2,18},{3,19},{4,20},{5,21},{6,22},{7,23},{8,24},{9,... | collective-permute-start | bytes 786440 | tf_op jit(solution)/shard_map/ppermute | solution.py:369
  5.7 1.5 collective-permute-start.6
  7.2 0.7 reduce_sum.18
  8.6 0.7 convert_element_type.280
  9.6 1.6 copy.23
  11.3 0.9 copy.25
  12.1 4.0 %all-to-all-start = ((bf16[8,128,128]{2,1,0:T(8,128)(2,1)}), bf16[8,128,128]{2,1,0:T(8,128)(2,1)}, u32[]{:S(2)}, u32[]{:S(2)}) async-start(bf16[8,128,128]{2,1,0:T(8,128)(2,1)} %copy.25), calls=%async_computation | async-start | bytes 524288 | tf_op jit(solution)/shard_map/all_to_all | solution.py:532
  16.2 1.9 collective-permute-done
  18.1 1.7 collective-permute-start.1
  19.9 4.6 %all-to-all-done = bf16[8,128,128]{2,1,0:T(8,128)(2,1)} async-done(((bf16[8,128,128]{2,1,0:T(8,128)(2,1)}), bf16[8,128,128]{2,1,0:T(8,128)(2,1)}, u32[]{:S(2)}, u32[]{:S(2)}) %all-to-all-start) | async-done | bytes 262176 | tf_op jit(solution)/shard_map/all_to_all | solution.py:532
  24.5 1.4 collective-permute-start.7
  25.9 1.6 collective-permute-start.2
  27.6 3.6 %collective-permute-done.2 = f32[4,16,128]{2,1,0:T(8,128)S(1)} collective-permute-done((f32[4,16,128]{2,1,0:T(8,128)S(1)}, f32[4,16,128]{2,1,0:T(8,128)S(1)}, u32[]{:S(2)}, u32[]{:S(2)}) %collective-permute-start.2) | collective-permute-done | bytes 32800 | tf_op jit(solution)/shard_map/ppermute | solution.py:369
  32.2 1.3 project.2
  33.8 1.0 collective-permute-start.9
  35.2 7.4 %collective-permute-done.9.refs_2_ = bf16[128,1024]{1,0:T(8,128)(2,1)S(1)} collective-permute-done((bf16[128,1024]{1,0:T(8,128)(2,1)S(1)}, bf16[128,1024]{1,0:T(8,128)(2,1)S(1)}, u32[]{:S(2)}, u32[]{:S(2)}) %collective-permute-start.9) | collective-permute-done | bytes 262176 | tf_op jit(solution)/shard_map/ppermute | solution.py:369
  42.6 1.5 collective-permute-start.10
  44.1 1.0 collective-permute-start.14
  45.3 2.4 collective-permute-done.10
  47.7 1.1 fusion.8
  48.7 1.0 collective-permute-start.11
  49.8 2.0 collective-permute-done.14.refs_3_
  51.8 1.3 project.3
  53.8 2.2 collective-permute-start.12
  56.1 1.6 collective-permute-start.16
  57.6 10.9 %collective-permute-done.12 = bf16[2,4,128,128]{3,2,1,0:T(8,128)(2,1)S(1)} collective-permute-done((bf16[2,4,128,128]{3,2,1,0:T(8,128)(2,1)S(1)}, bf16[2,4,128,128]{3,2,1,0:T(8,128)(2,1)S(1)}, u32[]{:S(2)}, u32[]{:S(2)}) %collective-permute-start.12) | collective-permute-done | bytes 262176 | tf_op jit(solution)/shard_map/ppermute | solution.py:369
  68.9 1.0 fusion.9
  69.8 0.9 collective-permute-start.17
  70.7 4.2 %collective-permute-done.17 = bf16[1,4,128,128]{3,2,1,0:T(8,128)(2,1)S(1)} collective-permute-done((bf16[1,4,128,128]{3,2,1,0:T(8,128)(2,1)S(1)}, bf16[1,4,128,128]{3,2,1,0:T(8,128)(2,1)S(1)}, u32[]{:S(2)}, u32[]{:S(2)}) %collective-permute-start.17) | collective-permute-done | bytes 131104 | tf_op jit(solution)/shard_map/ppermute | solution.py:369
  74.9 3.4 %collective-permute-start.18 = (bf16[2,4,128,128]{3,2,1,0:T(8,128)(2,1)S(1)}, bf16[2,4,128,128]{3,2,1,0:T(8,128)(2,1)S(1)}, u32[]{:S(2)}, u32[]{:S(2)}) collective-permute-start(bf16[2,4,128,128]{3,2,1,0:T(8,128)(2,1)S(1)} %pad_maximum_fusion.5), channel_id=1, source_target_pairs={{0,16},{1,17},{2,18},{3,19},{4,20},{5,21},{6,22},{7,23},{8,24},{9,... | collective-permute-start | bytes 786440 | tf_op jit(solution)/shard_map/ppermute | solution.py:369
  78.4 9.4 %collective-permute-done.13 = bf16[4,4,128,128]{3,2,1,0:T(8,128)(2,1)S(1)} collective-permute-done((bf16[4,4,128,128]{3,2,1,0:T(8,128)(2,1)S(1)}, bf16[4,4,128,128]{3,2,1,0:T(8,128)(2,1)S(1)}, u32[]{:S(2)}, u32[]{:S(2)}) %collective-permute-start.13) | collective-permute-done | bytes 524320 | tf_op jit(solution)/shard_map/ppermute | solution.py:369
  88.4 1.6 collective-permute-start.19
  90.0 11.5 %collective-permute-done.19 = bf16[4,4,128,128]{3,2,1,0:T(8,128)(2,1)S(1)} collective-permute-done((bf16[4,4,128,128]{3,2,1,0:T(8,128)(2,1)S(1)}, bf16[4,4,128,128]{3,2,1,0:T(8,128)(2,1)S(1)}, u32[]{:S(2)}, u32[]{:S(2)}) %collective-permute-start.19) | collective-permute-done | bytes 524320 | tf_op jit(solution)/shard_map/ppermute | solution.py:369
  101.6 1.0 collective-permute-done.20.rest_2_
  103.7 1.0 copy-done.1
  104.6 12.9 %collective-permute-done.21.rest_3_ = bf16[8,4,128,128]{3,2,1,0:T(8,128)(2,1)} collective-permute-done((bf16[8,4,128,128]{3,2,1,0:T(8,128)(2,1)S(1)}, bf16[8,4,128,128]{3,2,1,0:T(8,128)(2,1)}, u32[]{:S(2)}, u32[]{:S(2)}) %collective-permute-start.21) | collective-permute-done | bytes 1048608 | tf_op jit(solution)/shard_map/ppermute | solution.py:369
  118.0 2.6 %collective-permute-done.25.rest_7_ = bf16[8,4,128,128]{3,2,1,0:T(8,128)(2,1)} collective-permute-done((bf16[8,4,128,128]{3,2,1,0:T(8,128)(2,1)}, bf16[8,4,128,128]{3,2,1,0:T(8,128)(2,1)}, u32[]{:S(2)}, u32[]{:S(2)}) %collective-permute-start.25) | collective-permute-done | bytes 1048608 | tf_op jit(solution)/shard_map/ppermute | solution.py:369
  120.6 1.2 copy-done.2
  121.8 37.3 %gate_up.1 = (bf16[8,192,384]{2,1,0:T(8,128)(2,1)S(1)}, f32[128,1024]{1,0:T(8,128)S(1)}) custom-call(s32[66]{0:T(128)S(1)} %pad_add_fusion.info_ref, s32[8,1024]{1,0:T(8,128)S(1)} %bitcast_select_fusion.slot_ref, f32[8,1024]{1,0:T(8,128)S(1)} %bitcast.61, f32[32,128]{1,0:T(8,128)S(1)} %divide_bitcast_fusion.invgain_ref, ...), custom_call_target="tpu_custom_call" | custom-call | flops 9663676416 | bytes 58720256 | tf_op jit(solution)/shard_map/gate_up/pallas_call | solution.py:256
  159.1 13.7 %down_mix.4 = (bf16[16,128,512]{2,1,0:T(8,128)(2,1)}, bf16[16,128,512]{2,1,0:T(8,128)(2,1)}) custom-call(s32[18]{0:T(128)S(1)} %pad_add_fusion.3.place_ref, s32[8,1024]{1,0:T(8,128)S(1)} %bitcast_select_fusion.slot_ref, bf16[8,192,384]{2,1,0:T(8,128)(2,1)S(1)} %get-tuple-element.59.act_ref, bf16[8,384,4096]{2,1,0:T(8,128)(2,1)} %wd1_ref.5, ...), custom_call_target="tpu_custom_call" | custom-call | flops 4831838208 | bytes 16777216 | tf_op jit(solution)/shard_map/down_mix/pallas_call | solution.py:328
  173.6 8.4 %down_mix.3 = bf16[16,128,512]{2,1,0:T(8,128)(2,1)S(1)} custom-call(s32[18]{0:T(128)S(1)} %get-tuple-element.71.place_ref, s32[8,1024]{1,0:T(8,128)S(1)} %bitcast_select_fusion.slot_ref, bf16[8,192,384]{2,1,0:T(8,128)(2,1)S(1)} %get-tuple-element.59.act_ref, bf16[8,384,4096]{2,1,0:T(8,128)(2,1)} %wd1_ref.5, bf16[8,384,4096]{2,1,0:T(8,128)(2,1)} %wd1_ref.5), custom_call_target="tpu_custom_call" | custom-call | flops 2415919104 | bytes 8388608 | tf_op jit(solution)/shard_map/down_mix/pallas_call | solution.py:328
  182.0 1.5 add_convert_fusion.1
  184.1 8.4 %down_mix.5 = bf16[16,128,512]{2,1,0:T(8,128)(2,1)S(1)} custom-call(s32[18]{0:T(128)S(1)} %get-tuple-element.72.place_ref, s32[8,1024]{1,0:T(8,128)S(1)} %bitcast_select_fusion.slot_ref, bf16[8,192,384]{2,1,0:T(8,128)(2,1)S(1)} %get-tuple-element.59.act_ref, bf16[8,384,4096]{2,1,0:T(8,128)(2,1)} %wd1_ref.5, bf16[8,384,4096]{2,1,0:T(8,128)(2,1)} %wd1_ref.5), custom_call_target="tpu_custom_call" | custom-call | flops 2415919104 | bytes 8388608 | tf_op jit(solution)/shard_map/down_mix/pallas_call | solution.py:328
  192.5 1.5 add_convert_fusion
  194.1 4.3 %collective-permute-done.27 = bf16[8,128,512]{2,1,0:T(8,128)(2,1)S(1)} collective-permute-done((bf16[8,128,512]{2,1,0:T(8,128)(2,1)S(1)}, bf16[8,128,512]{2,1,0:T(8,128)(2,1)S(1)}, u32[]{:S(2)}, u32[]{:S(2)}) %collective-permute-start.27) | collective-permute-done | bytes 1048608 | tf_op jit(solution)/shard_map/ppermute | solution.py:369
  198.9 1.2 add_convert_fusion.3
  200.1 0.9 collective-permute-start.28
  201.0 12.2 %collective-permute-done.32 = bf16[8,128,512]{2,1,0:T(8,128)(2,1)S(1)} collective-permute-done((bf16[8,128,512]{2,1,0:T(8,128)(2,1)S(1)}, bf16[8,128,512]{2,1,0:T(8,128)(2,1)S(1)}, u32[]{:S(2)}, u32[]{:S(2)}) %collective-permute-start.32) | collective-permute-done | bytes 1048608 | tf_op jit(solution)/shard_map/ppermute | solution.py:369
  213.2 1.2 add_convert_fusion.2
  214.5 0.8 collective-permute-start.33
  215.3 1.1 add_convert_fusion.5
  216.4 1.7 collective-permute-start.29
  218.1 14.3 %collective-permute-done.33 = bf16[4,128,512]{2,1,0:T(8,128)(2,1)S(1)} collective-permute-done((bf16[4,128,512]{2,1,0:T(8,128)(2,1)S(1)}, bf16[4,128,512]{2,1,0:T(8,128)(2,1)S(1)}, u32[]{:S(2)}, u32[]{:S(2)}) %collective-permute-start.33) | collective-permute-done | bytes 524320 | tf_op jit(solution)/shard_map/ppermute | solution.py:369
  232.4 1.1 add_convert_fusion.4
  234.1 1.0 add_convert_fusion.7
  235.0 0.7 collective-permute-start.30
  235.8 9.6 %collective-permute-done.34 = bf16[2,128,512]{2,1,0:T(8,128)(2,1)S(1)} collective-permute-done((bf16[2,128,512]{2,1,0:T(8,128)(2,1)S(1)}, bf16[2,128,512]{2,1,0:T(8,128)(2,1)S(1)}, u32[]{:S(2)}, u32[]{:S(2)}) %collective-permute-start.34) | collective-permute-done | bytes 262176 | tf_op jit(solution)/shard_map/ppermute | solution.py:369
  245.4 1.0 add_convert_fusion.6
  246.4 1.3 collective-permute-start.35
  247.6 1.0 add_bitcast_fusion.1
  248.6 2.8 %collective-permute-done.35 = bf16[1,128,512]{2,1,0:T(8,128)(2,1)S(1)} collective-permute-done((bf16[1,128,512]{2,1,0:T(8,128)(2,1)S(1)}, bf16[1,128,512]{2,1,0:T(8,128)(2,1)S(1)}, u32[]{:S(2)}, u32[]{:S(2)}) %collective-permute-start.35) | collective-permute-done | bytes 131104 | tf_op jit(solution)/shard_map/ppermute | solution.py:369
  251.4 1.0 add_bitcast_fusion
  252.4 0.8 fusion
  (89 shorter events, 8.6 us)
Async XLA Ops:
  0.0 32.2 %copy-start.5 = (bf16[128,1024]{1,0:T(8,128)(2,1)S(1)}, bf16[128,1024]{1,0:T(8,128)(2,1)}, u32[]{:S(2)}) copy-start(bf16[128,1024]{1,0:T(8,128)(2,1)} %refs_0_) | copy-start | bytes 786436
  0.0 19.9 %copy-start.7 = (f32[4096]{0:T(1024)S(1)}, f32[4096]{0:T(1024)}, u32[]{:S(2)}) copy-start(f32[4096]{0:T(1024)} %param.12) | copy-start | bytes 49156
  0.0 32.2 %copy-start = (bf16[1024,512]{1,0:T(8,128)(2,1)S(1)}, bf16[1024,512]{1,0:T(8,128)(2,1)}, u32[]{:S(2)}) copy-start(bf16[1024,512]{1,0:T(8,128)(2,1)} %refs_4_.3) | copy-start | bytes 3145732
  0.0 31.7 %collective-permute-start.4 = (bf16[128,1024]{1,0:T(8,128)(2,1)}, bf16[128,1024]{1,0:T(8,128)(2,1)S(1)}, u32[]{:S(2)}, u32[]{:S(2)}) collective-permute-start(bf16[128,1024]{1,0:T(8,128)(2,1)} %refs_0_), channel_id=1, source_target_pairs={{0,8},{1,9},{2,10},{3,11},{4,12},{5,13},{6,14},{7,15},{8,0},{9,1},... | collective-permute-start | bytes 786440 | tf_op jit(solution)/shard_map/ppermute | solution.py:369
  3.1 16.8 %collective-permute-start.3 = (bf16[128,1024]{1,0:T(8,128)(2,1)}, bf16[128,1024]{1,0:T(8,128)(2,1)S(1)}, u32[]{:S(2)}, u32[]{:S(2)}) collective-permute-start(bf16[128,1024]{1,0:T(8,128)(2,1)} %refs_0_), channel_id=1, source_target_pairs={{0,16},{1,17},{2,18},{3,19},{4,20},{5,21},{6,22},{7,23},{8,24},{9,... | collective-permute-start | bytes 786440 | tf_op jit(solution)/shard_map/ppermute | solution.py:369
  5.7 26.1 %collective-permute-start.6 = (bf16[128,1024]{1,0:T(8,128)(2,1)}, bf16[128,1024]{1,0:T(8,128)(2,1)S(1)}, u32[]{:S(2)}, u32[]{:S(2)}) collective-permute-start(bf16[128,1024]{1,0:T(8,128)(2,1)} %refs_0_), channel_id=1, source_target_pairs={{0,4},{1,5},{2,6},{3,7},{4,0},{5,1},{6,2},{7,3},{8,12},{9,13},{10,... | collective-permute-start | bytes 786440 | tf_op jit(solution)/shard_map/ppermute | solution.py:369
  9.3 8.8 %collective-permute-start = (f32[1,16,128]{2,1,0:T(8,128)S(1)}, f32[1,16,128]{2,1,0:T(8,128)S(1)}, u32[]{:S(2)}, u32[]{:S(2)}) collective-permute-start(f32[1,16,128]{2,1,0:T(8,128)S(1)} %maximum_bitcast_fusion), channel_id=1, source_target_pairs={{0,16},{1,17},{2,18},{3,19},{4,20},{5,21},{6,22},{7,23},{8,24},{9,... | collective-permute-start | bytes 24584 | tf_op jit(solution)/shard_map/ppermute | solution.py:369
  12.1 12.3 %all-to-all-start = ((bf16[8,128,128]{2,1,0:T(8,128)(2,1)}), bf16[8,128,128]{2,1,0:T(8,128)(2,1)}, u32[]{:S(2)}, u32[]{:S(2)}) async-start(bf16[8,128,128]{2,1,0:T(8,128)(2,1)} %copy.25), calls=%async_computation | async-start | bytes 524288 | tf_op jit(solution)/shard_map/all_to_all | solution.py:532
  18.1 7.8 %collective-permute-start.1 = (f32[2,16,128]{2,1,0:T(8,128)S(1)}, f32[2,16,128]{2,1,0:T(8,128)S(1)}, u32[]{:S(2)}, u32[]{:S(2)}) collective-permute-start(f32[2,16,128]{2,1,0:T(8,128)S(1)} %pad_maximum_fusion.8), channel_id=1, source_target_pairs={{0,8},{1,9},{2,10},{3,11},{4,12},{5,13},{6,14},{7,15},{8,0},{9,1},... | collective-permute-start | bytes 49160 | tf_op jit(solution)/shard_map/ppermute | solution.py:369
  24.5 7.3 %collective-permute-start.7 = (bf16[128,1024]{1,0:T(8,128)(2,1)S(1)}, bf16[128,1024]{1,0:T(8,128)(2,1)S(1)}, u32[]{:S(2)}, u32[]{:S(2)}) collective-permute-start(bf16[128,1024]{1,0:T(8,128)(2,1)S(1)} %collective-permute-done.3.refs_1_), channel_id=1, source_target_pairs={{0,4},{1,5},{2,6},{3,7},{4,0},{5,1},{6,2},{7,3},{8,12},{9,13},{10,... | collective-permute-start | bytes 786440 | tf_op jit(solution)/shard_map/ppermute | solution.py:369
  25.8 6.4 %collective-permute-start.5 = (bf16[128,1024]{1,0:T(8,128)(2,1)S(1)}, bf16[128,1024]{1,0:T(8,128)(2,1)S(1)}, u32[]{:S(2)}, u32[]{:S(2)}) collective-permute-start(bf16[128,1024]{1,0:T(8,128)(2,1)S(1)} %collective-permute-done.3.refs_1_), channel_id=1, source_target_pairs={{0,8},{1,9},{2,10},{3,11},{4,12},{5,13},{6,14},{7,15},{8,0},{9,1},... | collective-permute-start | bytes 786440 | tf_op jit(solution)/shard_map/ppermute | solution.py:369
  25.9 5.2 %collective-permute-start.2 = (f32[4,16,128]{2,1,0:T(8,128)S(1)}, f32[4,16,128]{2,1,0:T(8,128)S(1)}, u32[]{:S(2)}, u32[]{:S(2)}) collective-permute-start(f32[4,16,128]{2,1,0:T(8,128)S(1)} %pad_maximum_fusion.7), channel_id=1, source_target_pairs={{0,4},{1,5},{2,6},{3,7},{4,0},{5,1},{6,2},{7,3},{8,12},{9,13},{10,... | collective-permute-start | bytes 98312 | tf_op jit(solution)/shard_map/ppermute | solution.py:369
  33.5 1.6 collective-permute-start.8
  33.8 8.8 %collective-permute-start.9 = (bf16[128,1024]{1,0:T(8,128)(2,1)S(1)}, bf16[128,1024]{1,0:T(8,128)(2,1)S(1)}, u32[]{:S(2)}, u32[]{:S(2)}) collective-permute-start(bf16[128,1024]{1,0:T(8,128)(2,1)S(1)} %collective-permute-done.4.refs_2_), channel_id=1, source_target_pairs={{0,4},{1,5},{2,6},{3,7},{4,0},{5,1},{6,2},{7,3},{8,12},{9,13},{10,... | collective-permute-start | bytes 786440 | tf_op jit(solution)/shard_map/ppermute | solution.py:369
  35.1 8.9 %copy-start.6 = (bf16[2,4,128,128]{3,2,1,0:T(8,128)(2,1)}, bf16[2,4,128,128]{3,2,1,0:T(8,128)(2,1)S(1)}, u32[]{:S(2)}) copy-start(bf16[2,4,128,128]{3,2,1,0:T(8,128)(2,1)S(1)} %collective-permute-done.8) | copy-start | bytes 786436
  42.6 5.1 %collective-permute-start.10 = (bf16[4,128,128]{2,1,0:T(8,128)(2,1)S(1)}, bf16[4,128,128]{2,1,0:T(8,128)(2,1)S(1)}, u32[]{:S(2)}, u32[]{:S(2)}) collective-permute-start(bf16[4,128,128]{2,1,0:T(8,128)(2,1)S(1)} %fusion.6), channel_id=1, source_target_pairs={{0,2},{1,3},{2,0},{3,1},{4,6},{5,7},{6,4},{7,5},{8,10},{9,11},{10,... | collective-permute-start | bytes 393224 | tf_op jit(solution)/shard_map/ppermute | solution.py:369
  44.1 7.7 %collective-permute-start.14 = (bf16[128,1024]{1,0:T(8,128)(2,1)S(1)}, bf16[128,1024]{1,0:T(8,128)(2,1)S(1)}, u32[]{:S(2)}, u32[]{:S(2)}) collective-permute-start(bf16[128,1024]{1,0:T(8,128)(2,1)S(1)} %collective-permute-done.5.refs_3_), channel_id=1, source_target_pairs={{0,4},{1,5},{2,6},{3,7},{4,0},{5,1},{6,2},{7,3},{8,12},{9,13},{10,... | collective-permute-start | bytes 786440 | tf_op jit(solution)/shard_map/ppermute | solution.py:369
  48.7 5.0 %collective-permute-start.11 = (bf16[1,4,128,128]{3,2,1,0:T(8,128)(2,1)S(1)}, bf16[1,4,128,128]{3,2,1,0:T(8,128)(2,1)S(1)}, u32[]{:S(2)}, u32[]{:S(2)}) collective-permute-start(bf16[1,4,128,128]{3,2,1,0:T(8,128)(2,1)S(1)} %fusion.8), channel_id=1, source_target_pairs={{0,4},{1,3},{2,6},{3,1},{4,0},{5,7},{6,2},{7,5},{8,12},{9,11},{10,... | collective-permute-start | bytes 393224 | tf_op jit(solution)/shard_map/ppermute | solution.py:369
  53.1 2.9 %collective-permute-start.15 = (bf16[2,4,128,128]{3,2,1,0:T(8,128)(2,1)S(1)}, bf16[2,4,128,128]{3,2,1,0:T(8,128)(2,1)S(1)}, u32[]{:S(2)}, u32[]{:S(2)}) collective-permute-start(bf16[2,4,128,128]{3,2,1,0:T(8,128)(2,1)S(1)} %get-tuple-element.50), channel_id=1, source_target_pairs={{0,1},{1,0},{2,3},{3,2},{4,5},{5,4},{6,7},{7,6},{8,9},{9,8},{10,11... | collective-permute-start | bytes 786440 | tf_op jit(solution)/shard_map/ppermute | solution.py:369
  53.8 14.7 %collective-permute-start.12 = (bf16[2,4,128,128]{3,2,1,0:T(8,128)(2,1)S(1)}, bf16[2,4,128,128]{3,2,1,0:T(8,128)(2,1)S(1)}, u32[]{:S(2)}, u32[]{:S(2)}) collective-permute-start(bf16[2,4,128,128]{3,2,1,0:T(8,128)(2,1)S(1)} %pad_maximum_fusion.4), channel_id=1, source_target_pairs={{0,16},{1,17},{2,18},{3,19},{4,20},{5,21},{6,22},{7,23},{8,24},{9,... | collective-permute-start | bytes 786440 | tf_op jit(solution)/shard_map/ppermute | solution.py:369
  56.1 12.8 %collective-permute-start.16 = (bf16[4,128,128]{2,1,0:T(8,128)(2,1)S(1)}, bf16[4,128,128]{2,1,0:T(8,128)(2,1)S(1)}, u32[]{:S(2)}, u32[]{:S(2)}) collective-permute-start(bf16[4,128,128]{2,1,0:T(8,128)(2,1)S(1)} %fusion.7), channel_id=1, source_target_pairs={{0,2},{1,3},{2,0},{3,1},{4,6},{5,7},{6,4},{7,5},{8,10},{9,11},{10,... | collective-permute-start | bytes 393224 | tf_op jit(solution)/shard_map/ppermute | solution.py:369
  68.6 19.1 %collective-permute-start.13 = (bf16[4,4,128,128]{3,2,1,0:T(8,128)(2,1)S(1)}, bf16[4,4,128,128]{3,2,1,0:T(8,128)(2,1)S(1)}, u32[]{:S(2)}, u32[]{:S(2)}) collective-permute-start(bf16[4,4,128,128]{3,2,1,0:T(8,128)(2,1)S(1)} %pad_maximum_fusion.2), channel_id=1, source_target_pairs={{0,8},{1,9},{2,10},{3,11},{4,12},{5,13},{6,14},{7,15},{8,0},{9,1},... | collective-permute-start | bytes 1572872 | tf_op jit(solution)/shard_map/ppermute | solution.py:369
  69.8 5.0 %collective-permute-start.17 = (bf16[1,4,128,128]{3,2,1,0:T(8,128)(2,1)S(1)}, bf16[1,4,128,128]{3,2,1,0:T(8,128)(2,1)S(1)}, u32[]{:S(2)}, u32[]{:S(2)}) collective-permute-start(bf16[1,4,128,128]{3,2,1,0:T(8,128)(2,1)S(1)} %fusion.9), channel_id=1, source_target_pairs={{0,4},{1,3},{2,6},{3,1},{4,0},{5,7},{6,2},{7,5},{8,12},{9,11},{10,... | collective-permute-start | bytes 393224 | tf_op jit(solution)/shard_map/ppermute | solution.py:369
  74.9 13.5 %collective-permute-start.18 = (bf16[2,4,128,128]{3,2,1,0:T(8,128)(2,1)S(1)}, bf16[2,4,128,128]{3,2,1,0:T(8,128)(2,1)S(1)}, u32[]{:S(2)}, u32[]{:S(2)}) collective-permute-start(bf16[2,4,128,128]{3,2,1,0:T(8,128)(2,1)S(1)} %pad_maximum_fusion.5), channel_id=1, source_target_pairs={{0,16},{1,17},{2,18},{3,19},{4,20},{5,21},{6,22},{7,23},{8,24},{9,... | collective-permute-start | bytes 786440 | tf_op jit(solution)/shard_map/ppermute | solution.py:369
  87.8 14.9 %collective-permute-start.20 = (bf16[8,4,128,128]{3,2,1,0:T(8,128)(2,1)S(1)}, bf16[8,4,128,128]{3,2,1,0:T(8,128)(2,1)S(1)}, u32[]{:S(2)}, u32[]{:S(2)}) collective-permute-start(bf16[8,4,128,128]{3,2,1,0:T(8,128)(2,1)S(1)} %pad_maximum_fusion.rest_0_), channel_id=1, source_target_pairs={{0,2},{1,5},{2,0},{3,7},{4,6},{5,1},{6,4},{7,3},{8,10},{9,13},{10,... | collective-permute-start | bytes 3145736 | tf_op jit(solution)/shard_map/ppermute | solution.py:369
  88.4 13.1 %collective-permute-start.19 = (bf16[4,4,128,128]{3,2,1,0:T(8,128)(2,1)S(1)}, bf16[4,4,128,128]{3,2,1,0:T(8,128)(2,1)S(1)}, u32[]{:S(2)}, u32[]{:S(2)}) collective-permute-start(bf16[4,4,128,128]{3,2,1,0:T(8,128)(2,1)S(1)} %pad_maximum_fusion.3), channel_id=1, source_target_pairs={{0,8},{1,9},{2,10},{3,11},{4,12},{5,13},{6,14},{7,15},{8,0},{9,1},... | collective-permute-start | bytes 1572872 | tf_op jit(solution)/shard_map/ppermute | solution.py:369
  102.7 14.9 %collective-permute-start.21 = (bf16[8,4,128,128]{3,2,1,0:T(8,128)(2,1)S(1)}, bf16[8,4,128,128]{3,2,1,0:T(8,128)(2,1)}, u32[]{:S(2)}, u32[]{:S(2)}) collective-permute-start(bf16[8,4,128,128]{3,2,1,0:T(8,128)(2,1)S(1)} %pad_maximum_fusion.1.rest_1_), channel_id=1, source_target_pairs={{0,2},{1,5},{2,0},{3,7},{4,6},{5,1},{6,4},{7,3},{8,10},{9,13},{10,... | collective-permute-start | bytes 3145736 | tf_op jit(solution)/shard_map/ppermute | solution.py:369
  103.2 14.8 %collective-permute-start.22 = (bf16[8,4,128,128]{3,2,1,0:T(8,128)(2,1)S(1)}, bf16[8,4,128,128]{3,2,1,0:T(8,128)(2,1)}, u32[]{:S(2)}, u32[]{:S(2)}) collective-permute-start(bf16[8,4,128,128]{3,2,1,0:T(8,128)(2,1)S(1)} %pad_maximum_fusion.rest_0_), channel_id=1, source_target_pairs={{0,1},{1,0},{2,3},{3,2},{4,5},{5,4},{6,7},{7,6},{8,9},{9,8},{10,11... | collective-permute-start | bytes 3145736 | tf_op jit(solution)/shard_map/ppermute | solution.py:369
  103.2 14.8 %collective-permute-start.23 = (bf16[8,4,128,128]{3,2,1,0:T(8,128)(2,1)S(1)}, bf16[8,4,128,128]{3,2,1,0:T(8,128)(2,1)}, u32[]{:S(2)}, u32[]{:S(2)}) collective-permute-start(bf16[8,4,128,128]{3,2,1,0:T(8,128)(2,1)S(1)} %pad_maximum_fusion.1.rest_1_), channel_id=1, source_target_pairs={{0,1},{1,0},{2,3},{3,2},{4,5},{5,4},{6,7},{7,6},{8,9},{9,8},{10,11... | collective-permute-start | bytes 3145736 | tf_op jit(solution)/shard_map/ppermute | solution.py:369
  103.7 14.3 %collective-permute-start.24 = (bf16[8,4,128,128]{3,2,1,0:T(8,128)(2,1)S(1)}, bf16[8,4,128,128]{3,2,1,0:T(8,128)(2,1)}, u32[]{:S(2)}, u32[]{:S(2)}) collective-permute-start(bf16[8,4,128,128]{3,2,1,0:T(8,128)(2,1)S(1)} %collective-permute-done.20.rest_2_), channel_id=1, source_target_pairs={{0,1},{1,0},{2,3},{3,2},{4,5},{5,4},{6,7},{7,6},{8,9},{9,8},{10,11... | collective-permute-start | bytes 3145736 | tf_op jit(solution)/shard_map/ppermute | solution.py:369
  103.7 1.0 copy-start.1
  117.6 3.0 %collective-permute-start.25 = (bf16[8,4,128,128]{3,2,1,0:T(8,128)(2,1)}, bf16[8,4,128,128]{3,2,1,0:T(8,128)(2,1)}, u32[]{:S(2)}, u32[]{:S(2)}) collective-permute-start(bf16[8,4,128,128]{3,2,1,0:T(8,128)(2,1)} %collective-permute-done.21.rest_3_), channel_id=1, source_target_pairs={{0,1},{1,0},{2,3},{3,2},{4,5},{5,4},{6,7},{7,6},{8,9},{9,8},{10,11... | collective-permute-start | bytes 3145736 | tf_op jit(solution)/shard_map/ppermute | solution.py:369
  120.6 1.2 copy-start.2
  159.1 13.7 %copy-start.3 = (f32[128,1024]{1,0:T(8,128)}, f32[128,1024]{1,0:T(8,128)S(1)}, u32[]{:S(2)}) copy-start(f32[128,1024]{1,0:T(8,128)S(1)} %get-tuple-element.56) | copy-start | bytes 1572868
  172.8 9.2 %collective-permute-start.26 = (bf16[16,128,512]{2,1,0:T(8,128)(2,1)}, bf16[16,128,512]{2,1,0:T(8,128)(2,1)}, u32[]{:S(2)}, u32[]{:S(2)}) collective-permute-start(bf16[16,128,512]{2,1,0:T(8,128)(2,1)} %get-tuple-element.58), channel_id=1, source_target_pairs={{0,1},{1,0},{2,3},{3,2},{4,5},{5,4},{6,7},{7,6},{8,9},{9,8},{10,11... | collective-permute-start | bytes 6291464 | tf_op jit(solution)/shard_map/ppermute | solution.py:369
  173.0 19.5 %collective-permute-start.31 = (bf16[16,128,512]{2,1,0:T(8,128)(2,1)}, bf16[16,128,512]{2,1,0:T(8,128)(2,1)}, u32[]{:S(2)}, u32[]{:S(2)}) collective-permute-start(bf16[16,128,512]{2,1,0:T(8,128)(2,1)} %get-tuple-element.60), channel_id=1, source_target_pairs={{0,1},{1,0},{2,3},{3,2},{4,5},{5,4},{6,7},{7,6},{8,9},{9,8},{10,11... | collective-permute-start | bytes 6291464 | tf_op jit(solution)/shard_map/ppermute | solution.py:369
  183.5 14.9 %collective-permute-start.27 = (bf16[8,128,512]{2,1,0:T(8,128)(2,1)S(1)}, bf16[8,128,512]{2,1,0:T(8,128)(2,1)S(1)}, u32[]{:S(2)}, u32[]{:S(2)}) collective-permute-start(bf16[8,128,512]{2,1,0:T(8,128)(2,1)S(1)} %add_convert_fusion.1), channel_id=1, source_target_pairs={{0,2},{1,5},{2,0},{3,7},{4,6},{5,1},{6,4},{7,3},{8,10},{9,13},{10,... | collective-permute-start | bytes 3145736 | tf_op jit(solution)/shard_map/ppermute | solution.py:369
  198.4 14.8 %collective-permute-start.32 = (bf16[8,128,512]{2,1,0:T(8,128)(2,1)S(1)}, bf16[8,128,512]{2,1,0:T(8,128)(2,1)S(1)}, u32[]{:S(2)}, u32[]{:S(2)}) collective-permute-start(bf16[8,128,512]{2,1,0:T(8,128)(2,1)S(1)} %add_convert_fusion), channel_id=1, source_target_pairs={{0,2},{1,5},{2,0},{3,7},{4,6},{5,1},{6,4},{7,3},{8,10},{9,13},{10,... | collective-permute-start | bytes 3145736 | tf_op jit(solution)/shard_map/ppermute | solution.py:369
  200.1 14.3 %collective-permute-start.28 = (bf16[4,128,512]{2,1,0:T(8,128)(2,1)S(1)}, bf16[4,128,512]{2,1,0:T(8,128)(2,1)S(1)}, u32[]{:S(2)}, u32[]{:S(2)}) collective-permute-start(bf16[4,128,512]{2,1,0:T(8,128)(2,1)S(1)} %add_convert_fusion.3), channel_id=1, source_target_pairs={{0,8},{1,9},{2,10},{3,11},{4,12},{5,13},{6,14},{7,15},{8,0},{9,1},... | collective-permute-start | bytes 1572872 | tf_op jit(solution)/shard_map/ppermute | solution.py:369
  214.5 17.9 %collective-permute-start.33 = (bf16[4,128,512]{2,1,0:T(8,128)(2,1)S(1)}, bf16[4,128,512]{2,1,0:T(8,128)(2,1)S(1)}, u32[]{:S(2)}, u32[]{:S(2)}) collective-permute-start(bf16[4,128,512]{2,1,0:T(8,128)(2,1)S(1)} %add_convert_fusion.2), channel_id=1, source_target_pairs={{0,8},{1,9},{2,10},{3,11},{4,12},{5,13},{6,14},{7,15},{8,0},{9,1},... | collective-permute-start | bytes 1572872 | tf_op jit(solution)/shard_map/ppermute | solution.py:369
  216.4 17.1 %collective-permute-start.29 = (bf16[2,128,512]{2,1,0:T(8,128)(2,1)S(1)}, bf16[2,128,512]{2,1,0:T(8,128)(2,1)S(1)}, u32[]{:S(2)}, u32[]{:S(2)}) collective-permute-start(bf16[2,128,512]{2,1,0:T(8,128)(2,1)S(1)} %add_convert_fusion.5), channel_id=1, source_target_pairs={{0,16},{1,17},{2,18},{3,19},{4,20},{5,21},{6,22},{7,23},{8,24},{9,... | collective-permute-start | bytes 786440 | tf_op jit(solution)/shard_map/ppermute | solution.py:369
  233.5 18.9 %copy-start.4 = (f32[128,1024]{1,0:T(8,128)S(1)}, f32[128,1024]{1,0:T(8,128)}, u32[]{:S(2)}) copy-start(f32[128,1024]{1,0:T(8,128)} %copy-done.3) | copy-start | bytes 1572868
  233.5 11.8 %collective-permute-start.34 = (bf16[2,128,512]{2,1,0:T(8,128)(2,1)S(1)}, bf16[2,128,512]{2,1,0:T(8,128)(2,1)S(1)}, u32[]{:S(2)}, u32[]{:S(2)}) collective-permute-start(bf16[2,128,512]{2,1,0:T(8,128)(2,1)S(1)} %add_convert_fusion.4), channel_id=1, source_target_pairs={{0,16},{1,17},{2,18},{3,19},{4,20},{5,21},{6,22},{7,23},{8,24},{9,... | collective-permute-start | bytes 786440 | tf_op jit(solution)/shard_map/ppermute | solution.py:369
  235.0 11.3 %collective-permute-start.30 = (bf16[1,128,512]{2,1,0:T(8,128)(2,1)S(1)}, bf16[1,128,512]{2,1,0:T(8,128)(2,1)S(1)}, u32[]{:S(2)}, u32[]{:S(2)}) collective-permute-start(bf16[1,128,512]{2,1,0:T(8,128)(2,1)S(1)} %add_convert_fusion.7), channel_id=1, source_target_pairs={{0,4},{1,3},{2,6},{3,1},{4,0},{5,7},{6,2},{7,5},{8,12},{9,11},{10,... | collective-permute-start | bytes 393224 | tf_op jit(solution)/shard_map/ppermute | solution.py:369
  246.4 5.0 %collective-permute-start.35 = (bf16[1,128,512]{2,1,0:T(8,128)(2,1)S(1)}, bf16[1,128,512]{2,1,0:T(8,128)(2,1)S(1)}, u32[]{:S(2)}, u32[]{:S(2)}) collective-permute-start(bf16[1,128,512]{2,1,0:T(8,128)(2,1)S(1)} %add_convert_fusion.6), channel_id=1, source_target_pairs={{0,4},{1,3},{2,6},{3,1},{4,0},{5,7},{6,2},{7,5},{8,12},{9,11},{10,... | collective-permute-start | bytes 393224 | tf_op jit(solution)/shard_map/ppermute | solution.py:369

commit v4 on v3

--- a/solution.py
+++ b/solution.py
@@ -123,17 +123,16 @@
 
 def gate_up_kernel(
     experts, rows, width, info_ref, slot_ref, weight_ref, invgain_ref, x_refs, wg_ref, wu_ref,
-    act_ref, hidden_ref, xs_ref, acc_ref, sq_ref, scale_ref, hits_ref
+    act_ref, hidden_ref, spread_ref, xs_ref, sq_ref, scale_ref, hits_ref
 ):
-    expert, chunk = pl.program_id(0), pl.program_id(1)
+    expert = pl.program_id(0)
     arrays = len(x_refs) // 2
     each, parts, here, lanes = x_refs[0].shape
     blocks = arrays * each
     span = 2 * here
     member, z = info_ref[2 * blocks], info_ref[2 * blocks + 1]
-    depth = wg_ref.shape[1]
-
-    @pl.when((expert == 0) & (chunk == 0))
+
+    @pl.when(expert == 0)
     def _():
         sq_ref[...] = jnp.zeros_like(sq_ref)
         for part in range(parts):
@@ -147,6 +146,7 @@
                 window = slice(e * rows, (e + 1) * rows)
                 hits_ref[0, part, window, :] = jnp.concatenate([first, second], axis=1)
                 hits_ref[1, part, window, :] = jnp.concatenate([second, first], axis=1)
+            spread_ref[part] = jnp.transpose(hits_ref[0, part].astype(F32)).astype(BF16)
 
         def pair_of_blocks(low, carry):
             for array in range(arrays):
@@ -160,14 +160,6 @@
                         for half, ref in enumerate((own, other)):
                             value = ref[place, part].astype(F32) * invgain
                             sq_ref[swapped, part, half] += value * value
-
-                    @pl.when(feature >> 3 == member)
-                    def _(place=place, feature=feature, invgain=invgain):
-                        mine = jnp.where(
-                            swapped == 0, own[place, z].astype(F32), other[place, z].astype(F32)
-                        )
-                        column = pl.multiple_of((feature & 7) * lanes, lanes)
-                        hidden_ref[:, pl.ds(column, lanes)] = mine * invgain
 
                 for part in range(parts):
                     both = jnp.concatenate(
@@ -191,6 +183,25 @@
             return carry
 
         lax.fori_loop(0, each // 2, pair_of_blocks, 0)
+
+        def own_block(place, carry):
+            for array in range(arrays):
+                feature = info_ref[array * each + place]
+
+                @pl.when(feature >> 3 == member)
+                def _(array=array, feature=feature):
+                    own, other = x_refs[2 * array], x_refs[2 * array + 1]
+                    mine = jnp.where(
+                        info_ref[blocks + array * each + place] == 0,
+                        own[place, z].astype(F32),
+                        other[place, z].astype(F32),
+                    )
+                    column = pl.multiple_of((feature & 7) * lanes, lanes)
+                    hidden_ref[:, pl.ds(column, lanes)] = mine * invgain_ref[pl.ds(feature, 1), :]
+
+            return carry
+
+        lax.fori_loop(0, each, own_block, 0)
         pieces = [
             sq_ref[0, part, half] + sq_ref[1, part, 1 - half]
             for part in range(parts)
@@ -201,46 +212,31 @@
         )
         scale_ref[...] = jnp.broadcast_to(lax.rsqrt(total / width + 1e-06), scale_ref.shape)
 
-    both = jnp.dot(
-        xs_ref[expert, :, pl.ds(pl.multiple_of(chunk * depth, depth), depth)],
+    summed = jnp.dot(
+        xs_ref[expert],
         jnp.concatenate([wg_ref[0], wu_ref[0]], axis=1),
         preferred_element_type=F32,
     )
-
-    @pl.when(chunk == 0)
-    def _():
-        acc_ref[...] = both
-
-    @pl.when((chunk > 0) & (chunk < pl.num_programs(1) - 1))
-    def _():
-        acc_ref[...] += both
-
-    @pl.when(chunk == pl.num_programs(1) - 1)
-    def _():
-        hidden_units = wg_ref.shape[2]
-        summed = acc_ref[...] + both
-        for part in range(parts):
-            window = slice(part * span, (part + 1) * span)
-            hits = hits_of(slot_ref[pl.ds(expert, 1), window], rows)
-            scale = jnp.sum(
-                jnp.where(hits, scale_ref[0:1, window], 0.0), axis=1, keepdims=True
-            )
-            weight = jnp.sum(
-                jnp.where(hits, weight_ref[pl.ds(expert, 1), window], 0.0), axis=1, keepdims=True
-            )
-            both_part = summed[part * rows : (part + 1) * rows, :]
-            gate = both_part[:, :hidden_units] * scale
-            upper = both_part[:, hidden_units:] * scale
-            act = gate / (1.0 + jnp.exp(-gate)) * upper * weight
-            act_ref[expert, part * rows : (part + 1) * rows, :] = act.astype(BF16)
-
-
-def gate_up(info, slots, weights, invgain, x, w_gate, w_up, rows, chunks):
+    hidden_units = wg_ref.shape[2]
+    for part in range(parts):
+        window = slice(part * span, (part + 1) * span)
+        hits = hits_of(slot_ref[pl.ds(expert, 1), window], rows)
+        scale = jnp.sum(jnp.where(hits, scale_ref[0:1, window], 0.0), axis=1, keepdims=True)
+        weight = jnp.sum(
+            jnp.where(hits, weight_ref[pl.ds(expert, 1), window], 0.0), axis=1, keepdims=True
+        )
+        both_part = summed[part * rows : (part + 1) * rows, :]
+        gate = both_part[:, :hidden_units] * scale
+        upper = both_part[:, hidden_units:] * scale
+        act = gate / (1.0 + jnp.exp(-gate)) * upper * weight
+        act_ref[expert, part * rows : (part + 1) * rows, :] = act.astype(BF16)
+
+
+def gate_up(info, slots, weights, invgain, x, w_gate, w_up, rows):
     experts, width, hidden_units = w_gate.shape
     each, parts, here, lanes = x[0].shape
     tokens = slots.shape[1]
     members = width // (each * lanes)
-    depth = width // chunks
 
     def kernel(info_ref, slot_ref, weight_ref, invgain_ref, *rest):
         gate_up_kernel(
@@ -250,24 +246,24 @@
 
     def whole(shape):
         return pl.BlockSpec(
-            shape, lambda e, k, info: (0,) * len(shape), pipeline_mode=pl.Buffered(1)
+            shape, lambda e, info: (0,) * len(shape), pipeline_mode=pl.Buffered(1)
         )
 
     return pl.pallas_call(
         kernel,
         grid_spec=pltpu.PrefetchScalarGridSpec(
             num_scalar_prefetch=1,
-            grid=(experts, chunks),
+            grid=(experts,),
             in_specs=[whole(slots.shape), whole(weights.shape), whole(invgain.shape)]
             + [pl.BlockSpec(memory_space=pltpu.VMEM)] * len(x)
-            + [pl.BlockSpec((1, depth, hidden_units), lambda e, k, info: (e, k, 0))] * 2,
+            + [pl.BlockSpec((1, width, hidden_units), lambda e, info: (e, 0, 0))] * 2,
             out_specs=[
-                pl.BlockSpec((experts, parts * rows, hidden_units), lambda e, k, info: (0, 0, 0)),
-                pl.BlockSpec((here, width // members), lambda e, k, info: (0, 0)),
+                pl.BlockSpec(memory_space=pltpu.VMEM),
+                pl.BlockSpec(memory_space=pltpu.VMEM),
+                pl.BlockSpec(memory_space=pltpu.VMEM),
             ],
             scratch_shapes=[
                 pltpu.VMEM((experts, parts * rows, width), BF16),
-                pltpu.VMEM((parts * rows, 2 * hidden_units), F32),
                 pltpu.VMEM((2, parts, 2, here, lanes), F32),
                 pltpu.VMEM((8, tokens), F32),
                 pltpu.VMEM((2, parts, experts * rows, 2 * here), BF16),
@@ -276,9 +272,10 @@
         out_shape=[
             jax.ShapeDtypeStruct((experts, parts * rows, hidden_units), BF16),
             jax.ShapeDtypeStruct((here, width // members), F32),
+            jax.ShapeDtypeStruct((parts, 2 * here, experts * rows), BF16),
         ],
         compiler_params=pltpu.CompilerParams(
-            vmem_limit_bytes=40 * 1024 * 1024, dimension_semantics=("arbitrary", "arbitrary")
+            vmem_limit_bytes=44 * 1024 * 1024, dimension_semantics=("arbitrary",)
         ),
         cost_estimate=pl.CostEstimate(
             flops=2 * experts * parts * rows * width * 2 * hidden_units,
@@ -289,30 +286,31 @@
     )(info, slots, weights, invgain, *x, w_gate, w_up)
 
 
-def down_kernel(rows, place_ref, slot_ref, act_ref, wd0_ref, wd1_ref, *rest):
+def down_kernel(rows, place_ref, spread_ref, act_ref, wd0_ref, wd1_ref, *rest):
     out_refs, ys_ref = rest[:-1], rest[-1]
     out_cols = out_refs[0].shape[2]
-    expert = pl.program_id(0)
+    step = pl.program_id(0)
     experts, all_rows, _ = act_ref.shape
+    per_step = wd0_ref.shape[0]
     parts = all_rows // rows
     groups = parts * PAIR
-    span = PAIR * 128
-    for side, wd_ref in enumerate((wd0_ref, wd1_ref)):
-        result = jnp.dot(act_ref[expert], wd_ref[0], preferred_element_type=F32).astype(BF16)
-        for part in range(parts):
-            ys_ref[side, part, expert] = result[part * rows : (part + 1) * rows, :]
-
-    @pl.when(expert == experts - 1)
+    for number in range(per_step):
+        expert = step * per_step + number
+        for side, wd_ref in enumerate((wd0_ref, wd1_ref)):
+            result = jnp.dot(
+                act_ref[expert], wd_ref[number], preferred_element_type=F32
+            ).astype(BF16)
+            for part in range(parts):
+                ys_ref[side, part, expert] = result[part * rows : (part + 1) * rows, :]
+
+    @pl.when(step == pl.num_programs(0) - 1)
     def _():
         for part in range(parts):
-            window = slice(part * span, (part + 1) * span)
-            hits = jnp.concatenate(
-                [hits_of(slot_ref[e : e + 1, window], rows) for e in range(experts)], axis=0
-            )
-            spread = jnp.transpose(hits.astype(F32)).astype(BF16)
             for side in range(2):
                 picked = ys_ref[side, part].reshape(experts * rows, ys_ref.shape[4])
-                mixed = jnp.dot(spread, picked, preferred_element_type=F32).astype(BF16)
+                mixed = jnp.dot(
+                    spread_ref[part], picked, preferred_element_type=F32
+                ).astype(BF16)
                 for i in range(PAIR):
                     target = place_ref[2 + side * groups + part * PAIR + i]
                     for number, out_ref in enumerate(out_refs):
@@ -321,45 +319,36 @@
                         ]
 
 
-def down(place, slots, act, w_down, rows, groups, cols, chunks):
+def down(place, spread, act, w_down, rows, groups, cols, chunks, per_step=2):
     experts, hidden_units, width = w_down.shape
-    tokens = slots.shape[1]
-    parts = act.shape[1] // rows
+    parts, span, _ = spread.shape
+    here = parts * span // groups
+    out = jax.ShapeDtypeStruct((2 * groups, here, cols // chunks), BF16)
     return pl.pallas_call(
         functools.partial(down_kernel, rows),
         grid_spec=pltpu.PrefetchScalarGridSpec(
             num_scalar_prefetch=1,
-            grid=(experts,),
+            grid=(experts // per_step,),
             in_specs=[
                 pl.BlockSpec(memory_space=pltpu.VMEM),
                 pl.BlockSpec(memory_space=pltpu.VMEM),
-                pl.BlockSpec(
-                    (1, hidden_units, cols),
-                    lambda e, p: (e, 0, p[0])
-                ),
-                pl.BlockSpec(
-                    (1, hidden_units, cols),
-                    lambda e, p: (e, 0, p[1])
-                ),
+                pl.BlockSpec((per_step, hidden_units, cols), lambda e, p: (e, 0, p[0])),
+                pl.BlockSpec((per_step, hidden_units, cols), lambda e, p: (e, 0, p[1])),
             ],
-            out_specs=[
-                pl.BlockSpec((2 * groups, tokens // groups, cols // chunks), lambda e, p: (0, 0, 0))
-            ]
-            * chunks,
+            out_specs=[pl.BlockSpec(out.shape, lambda e, p: (0, 0, 0))] * chunks,
             scratch_shapes=[pltpu.VMEM((2, parts, experts, rows, cols), BF16)],
         ),
-        out_shape=[jax.ShapeDtypeStruct((2 * groups, tokens // groups, cols // chunks), BF16)]
-        * chunks,
+        out_shape=[out] * chunks,
         compiler_params=pltpu.CompilerParams(
-            vmem_limit_bytes=32 * 1024 * 1024, dimension_semantics=("arbitrary",)
+            vmem_limit_bytes=36 * 1024 * 1024, dimension_semantics=("arbitrary",)
         ),
         cost_estimate=pl.CostEstimate(
             flops=8 * experts * parts * rows * cols * hidden_units,
-            bytes_accessed=4 * experts * cols * hidden_units + 4 * tokens * cols,
+            bytes_accessed=4 * experts * cols * hidden_units + 4 * parts * span * cols,
             transcendentals=0,
         ),
         name="down_mix",
-    )(place, slots, act, w_down, w_down)
+    )(place, spread, act, w_down, w_down)
 
 
 def flip(array, bits_of):
@@ -479,19 +468,23 @@
     return jnp.concatenate([feature, swapped, jnp.stack([member, device >> 3])])
 
 
-def gather_chunks(starts):
+def gather_chunks(starts, beside):
     stages = (last_axis, lambda core: ZHIGH, lambda core: ZLOW, first_axis)
     held = [[start] for start in starts]
     arrived = {}
     for tick in range(len(stages) + len(starts) - 1):
-        for index in range(len(starts)):
+        for index in reversed(range(len(starts))):
             stage = tick - index
             if not 0 <= stage < len(stages):
                 continue
             block = held[index][-1]
             if index:
                 block, _ = after(block, arrived[index - 1, stage])
+            if stage == len(stages) - 1 and index == len(starts) - 1:
+                block, _ = after(block, beside)
             came = flip(block, stages[stage])
+            if stage == 1 and (index + 1, 0) in arrived:
+                came, _ = after(came, arrived[index + 1, 0])
             arrived[index, stage] = came
             if stage < len(stages) - 1:
                 held[index].append(jnp.concatenate([block, came], axis=0))
@@ -507,11 +500,10 @@
 
     high = along(ZHIGH, heads)
     low = along(ZLOW, heads)
-    high, beside = after(high, beside)
-    both = along(ZLOW, high)
+    both, beside = after(along(ZLOW, high), beside)
     own = [heads, high, low, both]
     other = [along(Y, piece) for piece in own]
-    own, _ = after(own, (other[0], other[1]))
+    own, _ = after(own, other[:3])
     return own, other, beside
 
 
@@ -537,27 +529,26 @@
     )
 
     member_info = jnp.stack([core, x_side, z])
-    slots, weights = route_tables(route_ids, route_weights, group, experts, groups)
     starts = []
     own_heads, other_heads, moved = gather_heads(attn_heads, moved)
     for half, pieces in enumerate((own_heads, other_heads)):
         if half:
-            (pieces, moved, gain), _ = after((pieces, moved, gain), (starts[0], slots, weights))
+            (pieces, moved, gain), _ = after((pieces, moved, gain), starts[0])
         send, keep = project(member_info, pieces, out_proj)
         came = flip(send, lambda c: CORE)
         to_x = (keep[0].astype(F32) + came[0].astype(F32)).astype(BF16)
-        if not half:
-            to_x, _ = after(to_x, other_heads[2])
         from_x = flip(to_x, lambda c: X)
         hidden = lax.dynamic_index_in_dim(moved, y_side ^ half, 1, keepdims=False).astype(F32)
         hidden = hidden + total_of([keep[1], came[1], from_x])
         starts.append((hidden * gain).astype(BF16)[None])
 
-    own_x, other_x = gather_chunks(starts)
+    route_ids, _ = after(route_ids, starts[1])
+    slots, weights = route_tables(route_ids, route_weights, group, experts, groups)
+    own_x, other_x = gather_chunks(starts, (slots, weights))
     x = [piece for pair in zip(own_x, other_x) for piece in pair]
     invgain = (1.0 / norm_gain).reshape(groups * members, LANES)
-    act, own_hidden = gate_up(
-        block_table(device, groups, member), slots, weights, invgain, x, w_gate, w_up, rows, 2
+    act, own_hidden, spread = gate_up(
+        block_table(device, groups, member), slots, weights, invgain, x, w_gate, w_up, rows
     )
 
     cols = width // members
@@ -570,14 +561,14 @@
     chunks = 2
     chunk_cols = cols // chunks
     other = down(
-        columns_of(1 - core, 0, 1), slots, act, w_down, rows, groups, cols, chunks
+        columns_of(1 - core, 0, 1), spread, act, w_down, rows, groups, cols, chunks
     )
     came = [flip(piece, lambda c: CORE) for piece in other]
 
     def terms_of(chunk, earlier):
         ready = act if earlier is None else after(act, earlier)[0]
         place = columns_of(core, chunk, chunks)
-        (kept,) = down(place, slots, ready, w_down, rows, groups, chunk_cols, 1)
+        (kept,) = down(place, spread, ready, w_down, rows, groups, chunk_cols, 1)
         return [kept, came[chunk]]
 
     sums = reduce_chunks([functools.partial(terms_of, chunk) for chunk in range(chunks)])

time: 254 us -> 250 us (0.984)
  waiting for transfers between devices: 119 us -> 134 us
  Pallas kernels: 70.5 us -> 59.7 us
  starting transfers between devices: 40.2 us -> 35.4 us
    ppermute x36, waiting for transfers between devices: 114 us -> 133 us  [flip(): return lax.ppermute(array, ('expert', 'tensor'), pairs)]
    pallas_call x3, Pallas kernels: 30.5 us -> 24.8 us  [down(): pl.pallas_call(functools.partial(down_kernel, rows), grid_spec=pltpu.Pref...]
    pallas_call x1, Pallas kernels: 37.3 us -> 32.3 us  [gate_up(): pl.pallas_call(kernel, grid_spec=pltpu.PrefetchScalarGridSpec(num_scalar_...]
    ppermute x36, starting transfers between devices: 36.1 us -> 32 us  [flip(): return lax.ppermute(array, ('expert', 'tensor'), pairs)]
    all_to_all x1, waiting for transfers between devices: 4.59 us -> 0.69 us  [per_device_tokens(): lax.all_to_all(jnp.transpose(own_cols, (1, 0, 2)), 'expert', split_axis=0...]
  transfers between devices with their start and end apart: 37 -> 37, of which waited for: 21 -> 24; matrix products, arithmetic and copies ran while one was open for 8% -> 7% of each run, Pallas kernels for 7% -> 5%
where the time goes in v4:
time: 250 us; the launch traced here: 249 us
  waiting for transfers between devices  134 us (54%)
  Pallas kernels  59.7 us (24%)
  starting transfers between devices  35.4 us (14%)
  other arithmetic  15.6 us (6%)
  local copies, waits for them, and re-layouts  4.55 us (2%)
    ppermute x36, waiting for transfers between devices, flip(): return lax.ppermute(array, ('expert', 'tensor'), pairs)  133 us
    pallas_call x1, Pallas kernels, gate_up(): pl.pallas_call(kernel, grid_spec=pltpu.PrefetchScalarGridSpec(num_scalar_...  32.3 us
    ppermute x36, starting transfers between devices, flip(): return lax.ppermute(array, ('expert', 'tensor'), pairs)  32 us
    pallas_call x3, Pallas kernels, down(): pl.pallas_call(functools.partial(down_kernel, rows), grid_spec=pltpu.Pref...  24.8 us
    convert_element_type x8, other arithmetic, sent_half(): total_of([term[:half] for term in terms]).astype(BF16)  9.72 us
  transfers between devices with their start and end apart: 37, of which 24 were waited for; matrix products, arithmetic and copies ran while one was open for 7% of the time, Pallas kernels for 5%

profile of v4, /device:TPU:0, one launch (start us, length us, event | category | flops | bytes accessed | tf_op | source)
XLA Modules:
  0.0 249.5 jit_solution(3828383293166841559)
XLA Ops:
  0.0 4.0 %collective-permute-start.1 = (bf16[128,1024]{1,0:T(8,128)(2,1)}, bf16[128,1024]{1,0:T(8,128)(2,1)S(1)}, u32[]{:S(2)}, u32[]{:S(2)}) collective-permute-start(bf16[128,1024]{1,0:T(8,128)(2,1)} %refs_0_), channel_id=1, source_target_pairs={{0,16},{1,17},{2,18},{3,19},{4,20},{5,21},{6,22},{7,23},{8,24},{9,... | collective-permute-start | bytes 786440 | tf_op jit(solution)/shard_map/ppermute | solution.py:358
  4.0 1.6 collective-permute-start.3
  5.6 1.6 copy.23
  7.3 0.9 copy.25
  8.1 3.4 %all-to-all-start = ((bf16[8,128,128]{2,1,0:T(8,128)(2,1)}), bf16[8,128,128]{2,1,0:T(8,128)(2,1)S(1)}, u32[]{:S(2)}, u32[]{:S(2)}) async-start(bf16[8,128,128]{2,1,0:T(8,128)(2,1)} %copy.25), calls=%async_computation | async-start | bytes 524288 | tf_op jit(solution)/shard_map/all_to_all | solution.py:524
  11.6 5.8 %collective-permute-done.1.refs_1_ = bf16[128,1024]{1,0:T(8,128)(2,1)S(1)} collective-permute-done((bf16[128,1024]{1,0:T(8,128)(2,1)}, bf16[128,1024]{1,0:T(8,128)(2,1)S(1)}, u32[]{:S(2)}, u32[]{:S(2)}) %collective-permute-start.1) | collective-permute-done | bytes 262176 | tf_op jit(solution)/shard_map/ppermute | solution.py:358
  17.5 1.9 collective-permute-start
  19.5 1.9 collective-permute-start.4
  21.5 0.7 all-to-all-done
  22.2 4.1 %collective-permute-done.5.refs_3_ = bf16[128,1024]{1,0:T(8,128)(2,1)S(1)} collective-permute-done((bf16[128,1024]{1,0:T(8,128)(2,1)S(1)}, bf16[128,1024]{1,0:T(8,128)(2,1)S(1)}, u32[]{:S(2)}, u32[]{:S(2)}) %collective-permute-start.5) | collective-permute-done | bytes 262176 | tf_op jit(solution)/shard_map/ppermute | solution.py:358
  26.4 0.7 collective-permute-done.refs_0_
  27.1 5.6 %collective-permute-done.2.refs_1_ = bf16[128,1024]{1,0:T(8,128)(2,1)S(1)} collective-permute-done((bf16[128,1024]{1,0:T(8,128)(2,1)S(1)}, bf16[128,1024]{1,0:T(8,128)(2,1)S(1)}, u32[]{:S(2)}, u32[]{:S(2)}) %collective-permute-start.2) | collective-permute-done | bytes 262176 | tf_op jit(solution)/shard_map/ppermute | solution.py:358
  32.7 5.1 %collective-permute-done.4.refs_2_ = bf16[128,1024]{1,0:T(8,128)(2,1)S(1)} collective-permute-done((bf16[128,1024]{1,0:T(8,128)(2,1)S(1)}, bf16[128,1024]{1,0:T(8,128)(2,1)S(1)}, u32[]{:S(2)}, u32[]{:S(2)}) %collective-permute-start.4) | collective-permute-done | bytes 262176 | tf_op jit(solution)/shard_map/ppermute | solution.py:358
  37.8 1.3 project.2
  39.2 1.5 collective-permute-done.7
  40.8 1.6 collective-permute-start.8
  42.3 0.8 collective-permute-start.6
  43.2 3.2 %collective-permute-done.8 = bf16[4,128,128]{2,1,0:T(8,128)(2,1)S(1)} collective-permute-done((bf16[4,128,128]{2,1,0:T(8,128)(2,1)S(1)}, bf16[4,128,128]{2,1,0:T(8,128)(2,1)S(1)}, u32[]{:S(2)}, u32[]{:S(2)}) %collective-permute-start.8) | collective-permute-done | bytes 131104 | tf_op jit(solution)/shard_map/ppermute | solution.py:358
  46.5 3.9 %collective-permute-done.6.refs_3_ = bf16[128,1024]{1,0:T(8,128)(2,1)S(1)} collective-permute-done((bf16[128,1024]{1,0:T(8,128)(2,1)S(1)}, bf16[128,1024]{1,0:T(8,128)(2,1)S(1)}, u32[]{:S(2)}, u32[]{:S(2)}) %collective-permute-start.6) | collective-permute-done | bytes 262176 | tf_op jit(solution)/shard_map/ppermute | solution.py:358
  50.4 1.3 project.3
  51.8 0.9 collective-permute-start.14
  52.7 0.6 collective-permute-done.9
  54.0 2.9 %collective-permute-done.14 = bf16[1,4,128,128]{3,2,1,0:T(8,128)(2,1)S(1)} collective-permute-done((bf16[1,4,128,128]{3,2,1,0:T(8,128)(2,1)S(1)}, bf16[1,4,128,128]{3,2,1,0:T(8,128)(2,1)S(1)}, u32[]{:S(2)}, u32[]{:S(2)}) %collective-permute-start.14) | collective-permute-done | bytes 131104 | tf_op jit(solution)/shard_map/ppermute | solution.py:358
  56.9 3.0 %collective-permute-start.15 = (bf16[2,4,128,128]{3,2,1,0:T(8,128)(2,1)S(1)}, bf16[2,4,128,128]{3,2,1,0:T(8,128)(2,1)S(1)}, u32[]{:S(2)}, u32[]{:S(2)}) collective-permute-start(bf16[2,4,128,128]{3,2,1,0:T(8,128)(2,1)S(1)} %pad_maximum_fusion.4), channel_id=1, source_target_pairs={{0,16},{1,17},{2,18},{3,19},{4,20},{5,21},{6,22},{7,23},{8,24},{9,... | collective-permute-start | bytes 786440 | tf_op jit(solution)/shard_map/ppermute | solution.py:358
  60.0 2.3 collective-permute-start.11
  62.3 1.1 collective-permute-start.16
  63.4 8.6 %collective-permute-done.11 = f32[1,16,128]{2,1,0:T(8,128)S(1)} collective-permute-done((f32[1,16,128]{2,1,0:T(8,128)S(1)}, f32[1,16,128]{2,1,0:T(8,128)S(1)}, u32[]{:S(2)}, u32[]{:S(2)}) %collective-permute-start.11) | collective-permute-done | bytes 8224 | tf_op jit(solution)/shard_map/ppermute | solution.py:358
  72.0 2.1 collective-permute-start.17
  74.1 1.8 collective-permute-done.12
  75.9 1.1 collective-permute-start.13
  77.0 2.8 %collective-permute-done.13 = f32[4,16,128]{2,1,0:T(8,128)S(1)} collective-permute-done((f32[4,16,128]{2,1,0:T(8,128)S(1)}, f32[4,16,128]{2,1,0:T(8,128)S(1)}, u32[]{:S(2)}, u32[]{:S(2)}) %collective-permute-start.13) | collective-permute-done | bytes 32800 | tf_op jit(solution)/shard_map/ppermute | solution.py:358
  80.4 1.3 collective-permute-start.18
  81.7 10.1 %collective-permute-done.17 = bf16[4,4,128,128]{3,2,1,0:T(8,128)(2,1)} collective-permute-done((bf16[4,4,128,128]{3,2,1,0:T(8,128)(2,1)S(1)}, bf16[4,4,128,128]{3,2,1,0:T(8,128)(2,1)}, u32[]{:S(2)}, u32[]{:S(2)}) %collective-permute-start.17) | collective-permute-done | bytes 524320 | tf_op jit(solution)/shard_map/ppermute | solution.py:358
  91.8 1.1 pad_maximum_fusion.rest_0_
  94.6 11.7 %collective-permute-done.19 = bf16[4,4,128,128]{3,2,1,0:T(8,128)(2,1)S(1)} collective-permute-done((bf16[4,4,128,128]{3,2,1,0:T(8,128)(2,1)S(1)}, bf16[4,4,128,128]{3,2,1,0:T(8,128)(2,1)S(1)}, u32[]{:S(2)}, u32[]{:S(2)}) %collective-permute-start.19) | collective-permute-done | bytes 524320 | tf_op jit(solution)/shard_map/ppermute | solution.py:358
  106.3 1.6 collective-permute-done.20.rest_2_
  108.9 13.9 %collective-permute-done.21.rest_3_ = bf16[8,4,128,128]{3,2,1,0:T(8,128)(2,1)} collective-permute-done((bf16[8,4,128,128]{3,2,1,0:T(8,128)(2,1)S(1)}, bf16[8,4,128,128]{3,2,1,0:T(8,128)(2,1)}, u32[]{:S(2)}, u32[]{:S(2)}) %collective-permute-start.21) | collective-permute-done | bytes 1048608 | tf_op jit(solution)/shard_map/ppermute | solution.py:358
  123.8 2.0 collective-permute-done.25.rest_7_
  125.8 32.3 %gate_up.1 = (bf16[8,192,384]{2,1,0:T(8,128)(2,1)}, f32[128,1024]{1,0:T(8,128)S(1)}, bf16[4,256,384]{2,1,0:T(8,128)(2,1)S(1)}) custom-call(s32[66]{0:T(128)S(1)} %pad_add_fusion.info_ref, s32[8,1024]{1,0:T(8,128)S(1)} %bitcast_select_fusion.slot_ref, f32[8,1024]{1,0:T(8,128)S(1)} %bitcast.61, f32[32,128]{1,0:T(8,128)S(1)} %divide_bitcast_fusion.invgain_ref, ...), custom_call_target="tpu_custom_call" | custom-call | flops 9663676416 | bytes 58720256 | tf_op jit(solution)/shard_map/gate_up/pallas_call | solution.py:252
  158.1 1.3 copy-done
  159.4 11.8 %down_mix.4 = (bf16[16,128,512]{2,1,0:T(8,128)(2,1)}, bf16[16,128,512]{2,1,0:T(8,128)(2,1)}) custom-call(s32[18]{0:T(128)S(1)} %pad_add_fusion.3.place_ref, bf16[4,256,384]{2,1,0:T(8,128)(2,1)S(1)} %get-tuple-element.62.spread_ref, bf16[8,192,384]{2,1,0:T(8,128)(2,1)S(1)} %copy-done, bf16[8,384,4096]{2,1,0:T(8,128)(2,1)} %wd1_ref.5, ...), custom_call_target="tpu_custom_call" | custom-call | flops 4831838208 | bytes 16777216 | tf_op jit(solution)/shard_map/down_mix/pallas_call | solution.py:327
  172.0 6.5 %down_mix.3 = bf16[16,128,512]{2,1,0:T(8,128)(2,1)S(1)} custom-call(s32[18]{0:T(128)S(1)} %get-tuple-element.77.place_ref, bf16[4,256,384]{2,1,0:T(8,128)(2,1)S(1)} %get-tuple-element.62.spread_ref, bf16[8,192,384]{2,1,0:T(8,128)(2,1)S(1)} %copy-done.1, bf16[8,384,4096]{2,1,0:T(8,128)(2,1)} %wd1_ref.5, bf16[8,384,4096]{2,1,0:T(8,128)(2,1)} %wd1_ref.5), custom_call_target="tpu_custom_call" | custom-call | flops 2415919104 | bytes 8388608 | tf_op jit(solution)/shard_map/down_mix/pallas_call | solution.py:327
  178.4 1.5 add_convert_fusion.1
  180.0 0.7 collective-permute-start.27
  180.7 6.5 %down_mix.5 = bf16[16,128,512]{2,1,0:T(8,128)(2,1)S(1)} custom-call(s32[18]{0:T(128)S(1)} %get-tuple-element.78.place_ref, bf16[4,256,384]{2,1,0:T(8,128)(2,1)S(1)} %get-tuple-element.62.spread_ref, bf16[8,192,384]{2,1,0:T(8,128)(2,1)S(1)} %copy-done.1, bf16[8,384,4096]{2,1,0:T(8,128)(2,1)} %wd1_ref.5, bf16[8,384,4096]{2,1,0:T(8,128)(2,1)} %wd1_ref.5), custom_call_target="tpu_custom_call" | custom-call | flops 2415919104 | bytes 8388608 | tf_op jit(solution)/shard_map/down_mix/pallas_call | solution.py:327
  187.1 1.5 add_convert_fusion
  188.7 6.2 %collective-permute-done.27 = bf16[8,128,512]{2,1,0:T(8,128)(2,1)S(1)} collective-permute-done((bf16[8,128,512]{2,1,0:T(8,128)(2,1)S(1)}, bf16[8,128,512]{2,1,0:T(8,128)(2,1)S(1)}, u32[]{:S(2)}, u32[]{:S(2)}) %collective-permute-start.27) | collective-permute-done | bytes 1048608 | tf_op jit(solution)/shard_map/ppermute | solution.py:358
  194.8 0.6 collective-permute-start.32
  195.4 1.3 add_convert_fusion.3
  196.8 12.8 %collective-permute-done.32 = bf16[8,128,512]{2,1,0:T(8,128)(2,1)S(1)} collective-permute-done((bf16[8,128,512]{2,1,0:T(8,128)(2,1)S(1)}, bf16[8,128,512]{2,1,0:T(8,128)(2,1)S(1)}, u32[]{:S(2)}, u32[]{:S(2)}) %collective-permute-start.32) | collective-permute-done | bytes 1048608 | tf_op jit(solution)/shard_map/ppermute | solution.py:358
  209.6 1.2 add_convert_fusion.2
  211.0 1.1 add_convert_fusion.5
  212.1 1.6 collective-permute-start.29
  213.6 15.3 %collective-permute-done.33 = bf16[4,128,512]{2,1,0:T(8,128)(2,1)S(1)} collective-permute-done((bf16[4,128,512]{2,1,0:T(8,128)(2,1)S(1)}, bf16[4,128,512]{2,1,0:T(8,128)(2,1)S(1)}, u32[]{:S(2)}, u32[]{:S(2)}) %collective-permute-start.33) | collective-permute-done | bytes 524320 | tf_op jit(solution)/shard_map/ppermute | solution.py:358
  228.9 1.1 add_convert_fusion.4
  230.1 1.0 add_convert_fusion.7
  231.1 0.9 collective-permute-start.30
  231.9 9.7 %collective-permute-done.34 = bf16[2,128,512]{2,1,0:T(8,128)(2,1)S(1)} collective-permute-done((bf16[2,128,512]{2,1,0:T(8,128)(2,1)S(1)}, bf16[2,128,512]{2,1,0:T(8,128)(2,1)S(1)}, u32[]{:S(2)}, u32[]{:S(2)}) %collective-permute-start.34) | collective-permute-done | bytes 262176 | tf_op jit(solution)/shard_map/ppermute | solution.py:358
  241.6 1.0 add_convert_fusion.6
  242.6 0.9 collective-permute-start.35
  243.5 1.0 add_bitcast_fusion.1
  244.5 3.2 %collective-permute-done.35 = bf16[1,128,512]{2,1,0:T(8,128)(2,1)S(1)} collective-permute-done((bf16[1,128,512]{2,1,0:T(8,128)(2,1)S(1)}, bf16[1,128,512]{2,1,0:T(8,128)(2,1)S(1)}, u32[]{:S(2)}, u32[]{:S(2)}) %collective-permute-start.35) | collective-permute-done | bytes 131104 | tf_op jit(solution)/shard_map/ppermute | solution.py:358
  247.7 1.0 add_bitcast_fusion
  248.7 0.8 fusion
  (89 shorter events, 6.8 us)
Async XLA Ops:
  0.0 17.5 %copy-start.3 = (bf16[128,1024]{1,0:T(8,128)(2,1)S(1)}, bf16[128,1024]{1,0:T(8,128)(2,1)}, u32[]{:S(2)}) copy-start(bf16[128,1024]{1,0:T(8,128)(2,1)} %refs_0_) | copy-start | bytes 786436
  0.0 37.8 %copy-start.2 = (bf16[1024,512]{1,0:T(8,128)(2,1)S(1)}, bf16[1024,512]{1,0:T(8,128)(2,1)}, u32[]{:S(2)}) copy-start(bf16[1024,512]{1,0:T(8,128)(2,1)} %refs_4_.3) | copy-start | bytes 3145732
  0.0 17.3 %collective-permute-start.1 = (bf16[128,1024]{1,0:T(8,128)(2,1)}, bf16[128,1024]{1,0:T(8,128)(2,1)S(1)}, u32[]{:S(2)}, u32[]{:S(2)}) collective-permute-start(bf16[128,1024]{1,0:T(8,128)(2,1)} %refs_0_), channel_id=1, source_target_pairs={{0,16},{1,17},{2,18},{3,19},{4,20},{5,21},{6,22},{7,23},{8,24},{9,... | collective-permute-start | bytes 786440 | tf_op jit(solution)/shard_map/ppermute | solution.py:358
  4.0 15.5 %collective-permute-start.3 = (bf16[128,1024]{1,0:T(8,128)(2,1)}, bf16[128,1024]{1,0:T(8,128)(2,1)S(1)}, u32[]{:S(2)}, u32[]{:S(2)}) collective-permute-start(bf16[128,1024]{1,0:T(8,128)(2,1)} %refs_0_), channel_id=1, source_target_pairs={{0,8},{1,9},{2,10},{3,11},{4,12},{5,13},{6,14},{7,15},{8,0},{9,1},... | collective-permute-start | bytes 786440 | tf_op jit(solution)/shard_map/ppermute | solution.py:358
  7.2 35.9 %copy-start.5 = (f32[4096]{0:T(1024)S(1)}, f32[4096]{0:T(1024)}, u32[]{:S(2)}) copy-start(f32[4096]{0:T(1024)} %param.12) | copy-start | bytes 49156
  8.1 14.1 %all-to-all-start = ((bf16[8,128,128]{2,1,0:T(8,128)(2,1)}), bf16[8,128,128]{2,1,0:T(8,128)(2,1)S(1)}, u32[]{:S(2)}, u32[]{:S(2)}) async-start(bf16[8,128,128]{2,1,0:T(8,128)(2,1)} %copy.25), calls=%async_computation | async-start | bytes 524288 | tf_op jit(solution)/shard_map/all_to_all | solution.py:524
  17.3 9.0 %collective-permute-start.5 = (bf16[128,1024]{1,0:T(8,128)(2,1)S(1)}, bf16[128,1024]{1,0:T(8,128)(2,1)S(1)}, u32[]{:S(2)}, u32[]{:S(2)}) collective-permute-start(bf16[128,1024]{1,0:T(8,128)(2,1)S(1)} %collective-permute-done.1.refs_1_), channel_id=1, source_target_pairs={{0,8},{1,9},{2,10},{3,11},{4,12},{5,13},{6,14},{7,15},{8,0},{9,1},... | collective-permute-start | bytes 786440 | tf_op jit(solution)/shard_map/ppermute | solution.py:358
  17.5 9.6 %collective-permute-start = (bf16[128,1024]{1,0:T(8,128)(2,1)S(1)}, bf16[128,1024]{1,0:T(8,128)(2,1)S(1)}, u32[]{:S(2)}, u32[]{:S(2)}) collective-permute-start(bf16[128,1024]{1,0:T(8,128)(2,1)S(1)} %copy-done.3), channel_id=1, source_target_pairs={{0,4},{1,5},{2,6},{3,7},{4,0},{5,1},{6,2},{7,3},{8,12},{9,13},{10,... | collective-permute-start | bytes 786440 | tf_op jit(solution)/shard_map/ppermute | solution.py:358
  19.4 13.3 %collective-permute-start.2 = (bf16[128,1024]{1,0:T(8,128)(2,1)S(1)}, bf16[128,1024]{1,0:T(8,128)(2,1)S(1)}, u32[]{:S(2)}, u32[]{:S(2)}) collective-permute-start(bf16[128,1024]{1,0:T(8,128)(2,1)S(1)} %collective-permute-done.1.refs_1_), channel_id=1, source_target_pairs={{0,4},{1,5},{2,6},{3,7},{4,0},{5,1},{6,2},{7,3},{8,12},{9,13},{10,... | collective-permute-start | bytes 786440 | tf_op jit(solution)/shard_map/ppermute | solution.py:358
  19.5 18.2 %collective-permute-start.4 = (bf16[128,1024]{1,0:T(8,128)(2,1)S(1)}, bf16[128,1024]{1,0:T(8,128)(2,1)S(1)}, u32[]{:S(2)}, u32[]{:S(2)}) collective-permute-start(bf16[128,1024]{1,0:T(8,128)(2,1)S(1)} %collective-permute-done.3.refs_2_), channel_id=1, source_target_pairs={{0,4},{1,5},{2,6},{3,7},{4,0},{5,1},{6,2},{7,3},{8,12},{9,13},{10,... | collective-permute-start | bytes 786440 | tf_op jit(solution)/shard_map/ppermute | solution.py:358
  39.1 12.7 %copy-start.4 = (f32[128,8]{0,1:T(8,128)S(1)}, f32[128,8]{0,1:T(8,128)}, u32[]{:S(2)}) copy-start(f32[128,8]{0,1:T(8,128)} %param.14) | copy-start | bytes 12292
  39.1 1.6 collective-permute-start.7
  40.8 5.6 %collective-permute-start.8 = (bf16[4,128,128]{2,1,0:T(8,128)(2,1)S(1)}, bf16[4,128,128]{2,1,0:T(8,128)(2,1)S(1)}, u32[]{:S(2)}, u32[]{:S(2)}) collective-permute-start(bf16[4,128,128]{2,1,0:T(8,128)(2,1)S(1)} %fusion.6), channel_id=1, source_target_pairs={{0,2},{1,3},{2,0},{3,1},{4,6},{5,7},{6,4},{7,5},{8,10},{9,11},{10,... | collective-permute-start | bytes 393224 | tf_op jit(solution)/shard_map/ppermute | solution.py:358
  42.3 8.1 %collective-permute-start.6 = (bf16[128,1024]{1,0:T(8,128)(2,1)S(1)}, bf16[128,1024]{1,0:T(8,128)(2,1)S(1)}, u32[]{:S(2)}, u32[]{:S(2)}) collective-permute-start(bf16[128,1024]{1,0:T(8,128)(2,1)S(1)} %collective-permute-done.5.refs_3_), channel_id=1, source_target_pairs={{0,4},{1,5},{2,6},{3,7},{4,0},{5,1},{6,2},{7,3},{8,12},{9,13},{10,... | collective-permute-start | bytes 786440 | tf_op jit(solution)/shard_map/ppermute | solution.py:358
  43.2 16.8 %copy-start.6 = (s32[128,8]{0,1:T(8,128)S(1)}, s32[128,8]{0,1:T(8,128)}, u32[]{:S(2)}) copy-start(s32[128,8]{0,1:T(8,128)} %param.13) | copy-start | bytes 12292
  51.7 1.6 collective-permute-start.9
  51.8 5.0 %collective-permute-start.14 = (bf16[1,4,128,128]{3,2,1,0:T(8,128)(2,1)S(1)}, bf16[1,4,128,128]{3,2,1,0:T(8,128)(2,1)S(1)}, u32[]{:S(2)}, u32[]{:S(2)}) collective-permute-start(bf16[1,4,128,128]{3,2,1,0:T(8,128)(2,1)S(1)} %fusion.8), channel_id=1, source_target_pairs={{0,4},{1,3},{2,6},{3,1},{4,0},{5,7},{6,2},{7,5},{8,12},{9,11},{10,... | collective-permute-start | bytes 393224 | tf_op jit(solution)/shard_map/ppermute | solution.py:358
  53.4 6.5 %collective-permute-start.10 = (bf16[4,128,128]{2,1,0:T(8,128)(2,1)S(1)}, bf16[4,128,128]{2,1,0:T(8,128)(2,1)S(1)}, u32[]{:S(2)}, u32[]{:S(2)}) collective-permute-start(bf16[4,128,128]{2,1,0:T(8,128)(2,1)S(1)} %fusion.7), channel_id=1, source_target_pairs={{0,2},{1,3},{2,0},{3,1},{4,6},{5,7},{6,4},{7,5},{8,10},{9,11},{10,... | collective-permute-start | bytes 393224 | tf_op jit(solution)/shard_map/ppermute | solution.py:358
  56.9 15.0 %collective-permute-start.15 = (bf16[2,4,128,128]{3,2,1,0:T(8,128)(2,1)S(1)}, bf16[2,4,128,128]{3,2,1,0:T(8,128)(2,1)S(1)}, u32[]{:S(2)}, u32[]{:S(2)}) collective-permute-start(bf16[2,4,128,128]{3,2,1,0:T(8,128)(2,1)S(1)} %pad_maximum_fusion.4), channel_id=1, source_target_pairs={{0,16},{1,17},{2,18},{3,19},{4,20},{5,21},{6,22},{7,23},{8,24},{9,... | collective-permute-start | bytes 786440 | tf_op jit(solution)/shard_map/ppermute | solution.py:358
  60.0 11.9 %collective-permute-start.11 = (f32[1,16,128]{2,1,0:T(8,128)S(1)}, f32[1,16,128]{2,1,0:T(8,128)S(1)}, u32[]{:S(2)}, u32[]{:S(2)}) collective-permute-start(f32[1,16,128]{2,1,0:T(8,128)S(1)} %maximum_bitcast_fusion), channel_id=1, source_target_pairs={{0,16},{1,17},{2,18},{3,19},{4,20},{5,21},{6,22},{7,23},{8,24},{9,... | collective-permute-start | bytes 24584 | tf_op jit(solution)/shard_map/ppermute | solution.py:358
  62.3 9.7 %collective-permute-start.16 = (bf16[1,4,128,128]{3,2,1,0:T(8,128)(2,1)S(1)}, bf16[1,4,128,128]{3,2,1,0:T(8,128)(2,1)S(1)}, u32[]{:S(2)}, u32[]{:S(2)}) collective-permute-start(bf16[1,4,128,128]{3,2,1,0:T(8,128)(2,1)S(1)} %fusion.9), channel_id=1, source_target_pairs={{0,4},{1,3},{2,6},{3,1},{4,0},{5,7},{6,2},{7,5},{8,12},{9,11},{10,... | collective-permute-start | bytes 393224 | tf_op jit(solution)/shard_map/ppermute | solution.py:358
  71.9 3.9 %collective-permute-start.12 = (f32[2,16,128]{2,1,0:T(8,128)S(1)}, f32[2,16,128]{2,1,0:T(8,128)S(1)}, u32[]{:S(2)}, u32[]{:S(2)}) collective-permute-start(f32[2,16,128]{2,1,0:T(8,128)S(1)} %pad_maximum_fusion.8), channel_id=1, source_target_pairs={{0,8},{1,9},{2,10},{3,11},{4,12},{5,13},{6,14},{7,15},{8,0},{9,1},... | collective-permute-start | bytes 49160 | tf_op jit(solution)/shard_map/ppermute | solution.py:358
  72.0 19.7 %collective-permute-start.17 = (bf16[4,4,128,128]{3,2,1,0:T(8,128)(2,1)S(1)}, bf16[4,4,128,128]{3,2,1,0:T(8,128)(2,1)}, u32[]{:S(2)}, u32[]{:S(2)}) collective-permute-start(bf16[4,4,128,128]{3,2,1,0:T(8,128)(2,1)S(1)} %pad_maximum_fusion.2), channel_id=1, source_target_pairs={{0,8},{1,9},{2,10},{3,11},{4,12},{5,13},{6,14},{7,15},{8,0},{9,1},... | collective-permute-start | bytes 1572872 | tf_op jit(solution)/shard_map/ppermute | solution.py:358
  75.9 3.9 %collective-permute-start.13 = (f32[4,16,128]{2,1,0:T(8,128)S(1)}, f32[4,16,128]{2,1,0:T(8,128)S(1)}, u32[]{:S(2)}, u32[]{:S(2)}) collective-permute-start(f32[4,16,128]{2,1,0:T(8,128)S(1)} %pad_maximum_fusion.7), channel_id=1, source_target_pairs={{0,4},{1,5},{2,6},{3,7},{4,0},{5,1},{6,2},{7,3},{8,12},{9,13},{10,... | collective-permute-start | bytes 98312 | tf_op jit(solution)/shard_map/ppermute | solution.py:358
  80.4 13.1 %collective-permute-start.18 = (bf16[2,4,128,128]{3,2,1,0:T(8,128)(2,1)S(1)}, bf16[2,4,128,128]{3,2,1,0:T(8,128)(2,1)S(1)}, u32[]{:S(2)}, u32[]{:S(2)}) collective-permute-start(bf16[2,4,128,128]{3,2,1,0:T(8,128)(2,1)S(1)} %pad_maximum_fusion.5), channel_id=1, source_target_pairs={{0,16},{1,17},{2,18},{3,19},{4,20},{5,21},{6,22},{7,23},{8,24},{9,... | collective-permute-start | bytes 786440 | tf_op jit(solution)/shard_map/ppermute | solution.py:358
  92.9 15.0 %collective-permute-start.20 = (bf16[8,4,128,128]{3,2,1,0:T(8,128)(2,1)S(1)}, bf16[8,4,128,128]{3,2,1,0:T(8,128)(2,1)}, u32[]{:S(2)}, u32[]{:S(2)}) collective-permute-start(bf16[8,4,128,128]{3,2,1,0:T(8,128)(2,1)S(1)} %pad_maximum_fusion.rest_0_), channel_id=1, source_target_pairs={{0,2},{1,5},{2,0},{3,7},{4,6},{5,1},{6,4},{7,3},{8,10},{9,13},{10,... | collective-permute-start | bytes 3145736 | tf_op jit(solution)/shard_map/ppermute | solution.py:358
  93.6 12.6 %collective-permute-start.19 = (bf16[4,4,128,128]{3,2,1,0:T(8,128)(2,1)S(1)}, bf16[4,4,128,128]{3,2,1,0:T(8,128)(2,1)S(1)}, u32[]{:S(2)}, u32[]{:S(2)}) collective-permute-start(bf16[4,4,128,128]{3,2,1,0:T(8,128)(2,1)S(1)} %pad_maximum_fusion.3), channel_id=1, source_target_pairs={{0,8},{1,9},{2,10},{3,11},{4,12},{5,13},{6,14},{7,15},{8,0},{9,1},... | collective-permute-start | bytes 1572872 | tf_op jit(solution)/shard_map/ppermute | solution.py:358
  107.9 14.9 %collective-permute-start.21 = (bf16[8,4,128,128]{3,2,1,0:T(8,128)(2,1)S(1)}, bf16[8,4,128,128]{3,2,1,0:T(8,128)(2,1)}, u32[]{:S(2)}, u32[]{:S(2)}) collective-permute-start(bf16[8,4,128,128]{3,2,1,0:T(8,128)(2,1)S(1)} %pad_maximum_fusion.1.rest_1_), channel_id=1, source_target_pairs={{0,2},{1,5},{2,0},{3,7},{4,6},{5,1},{6,4},{7,3},{8,10},{9,13},{10,... | collective-permute-start | bytes 3145736 | tf_op jit(solution)/shard_map/ppermute | solution.py:358
  108.4 15.3 %collective-permute-start.22 = (bf16[8,4,128,128]{3,2,1,0:T(8,128)(2,1)S(1)}, bf16[8,4,128,128]{3,2,1,0:T(8,128)(2,1)}, u32[]{:S(2)}, u32[]{:S(2)}) collective-permute-start(bf16[8,4,128,128]{3,2,1,0:T(8,128)(2,1)S(1)} %pad_maximum_fusion.rest_0_), channel_id=1, source_target_pairs={{0,1},{1,0},{2,3},{3,2},{4,5},{5,4},{6,7},{7,6},{8,9},{9,8},{10,11... | collective-permute-start | bytes 3145736 | tf_op jit(solution)/shard_map/ppermute | solution.py:358
  108.4 15.3 %collective-permute-start.23 = (bf16[8,4,128,128]{3,2,1,0:T(8,128)(2,1)S(1)}, bf16[8,4,128,128]{3,2,1,0:T(8,128)(2,1)}, u32[]{:S(2)}, u32[]{:S(2)}) collective-permute-start(bf16[8,4,128,128]{3,2,1,0:T(8,128)(2,1)S(1)} %pad_maximum_fusion.1.rest_1_), channel_id=1, source_target_pairs={{0,1},{1,0},{2,3},{3,2},{4,5},{5,4},{6,7},{7,6},{8,9},{9,8},{10,11... | collective-permute-start | bytes 3145736 | tf_op jit(solution)/shard_map/ppermute | solution.py:358
  108.9 14.8 %collective-permute-start.24 = (bf16[8,4,128,128]{3,2,1,0:T(8,128)(2,1)}, bf16[8,4,128,128]{3,2,1,0:T(8,128)(2,1)}, u32[]{:S(2)}, u32[]{:S(2)}) collective-permute-start(bf16[8,4,128,128]{3,2,1,0:T(8,128)(2,1)} %collective-permute-done.20.rest_2_), channel_id=1, source_target_pairs={{0,1},{1,0},{2,3},{3,2},{4,5},{5,4},{6,7},{7,6},{8,9},{9,8},{10,11... | collective-permute-start | bytes 3145736 | tf_op jit(solution)/shard_map/ppermute | solution.py:358
  122.8 3.0 %collective-permute-start.25 = (bf16[8,4,128,128]{3,2,1,0:T(8,128)(2,1)}, bf16[8,4,128,128]{3,2,1,0:T(8,128)(2,1)}, u32[]{:S(2)}, u32[]{:S(2)}) collective-permute-start(bf16[8,4,128,128]{3,2,1,0:T(8,128)(2,1)} %collective-permute-done.21.rest_3_), channel_id=1, source_target_pairs={{0,1},{1,0},{2,3},{3,2},{4,5},{5,4},{6,7},{7,6},{8,9},{9,8},{10,11... | collective-permute-start | bytes 3145736 | tf_op jit(solution)/shard_map/ppermute | solution.py:358
  158.1 1.3 copy-start
  159.4 12.4 %copy-start.7 = (s32[2,8]{1,0:T(2,128)S(1)}, s32[2,8]{1,0:T(2,128)}, u32[]{:S(2)}) copy-start(s32[2,8]{1,0:T(2,128)} %get-tuple-element.75) | copy-start | bytes 196
  159.4 12.6 %copy-start.1 = (bf16[8,192,384]{2,1,0:T(8,128)(2,1)S(1)}, bf16[8,192,384]{2,1,0:T(8,128)(2,1)}, u32[]{:S(2)}) copy-start(bf16[8,192,384]{2,1,0:T(8,128)(2,1)} %get-tuple-element.65.act_ref) | copy-start | bytes 3538948
  171.2 7.2 %collective-permute-start.26 = (bf16[16,128,512]{2,1,0:T(8,128)(2,1)}, bf16[16,128,512]{2,1,0:T(8,128)(2,1)}, u32[]{:S(2)}, u32[]{:S(2)}) collective-permute-start(bf16[16,128,512]{2,1,0:T(8,128)(2,1)} %get-tuple-element.64), channel_id=1, source_target_pairs={{0,1},{1,0},{2,3},{3,2},{4,5},{5,4},{6,7},{7,6},{8,9},{9,8},{10,11... | collective-permute-start | bytes 6291464 | tf_op jit(solution)/shard_map/ppermute | solution.py:358
  171.4 15.7 %collective-permute-start.31 = (bf16[16,128,512]{2,1,0:T(8,128)(2,1)}, bf16[16,128,512]{2,1,0:T(8,128)(2,1)}, u32[]{:S(2)}, u32[]{:S(2)}) collective-permute-start(bf16[16,128,512]{2,1,0:T(8,128)(2,1)} %get-tuple-element.66), channel_id=1, source_target_pairs={{0,1},{1,0},{2,3},{3,2},{4,5},{5,4},{6,7},{7,6},{8,9},{9,8},{10,11... | collective-permute-start | bytes 6291464 | tf_op jit(solution)/shard_map/ppermute | solution.py:358
  180.0 14.9 %collective-permute-start.27 = (bf16[8,128,512]{2,1,0:T(8,128)(2,1)S(1)}, bf16[8,128,512]{2,1,0:T(8,128)(2,1)S(1)}, u32[]{:S(2)}, u32[]{:S(2)}) collective-permute-start(bf16[8,128,512]{2,1,0:T(8,128)(2,1)S(1)} %add_convert_fusion.1), channel_id=1, source_target_pairs={{0,2},{1,5},{2,0},{3,7},{4,6},{5,1},{6,4},{7,3},{8,10},{9,13},{10,... | collective-permute-start | bytes 3145736 | tf_op jit(solution)/shard_map/ppermute | solution.py:358
  194.8 14.8 %collective-permute-start.32 = (bf16[8,128,512]{2,1,0:T(8,128)(2,1)S(1)}, bf16[8,128,512]{2,1,0:T(8,128)(2,1)S(1)}, u32[]{:S(2)}, u32[]{:S(2)}) collective-permute-start(bf16[8,128,512]{2,1,0:T(8,128)(2,1)S(1)} %add_convert_fusion), channel_id=1, source_target_pairs={{0,2},{1,5},{2,0},{3,7},{4,6},{5,1},{6,4},{7,3},{8,10},{9,13},{10,... | collective-permute-start | bytes 3145736 | tf_op jit(solution)/shard_map/ppermute | solution.py:358
  196.7 14.2 %collective-permute-start.28 = (bf16[4,128,512]{2,1,0:T(8,128)(2,1)S(1)}, bf16[4,128,512]{2,1,0:T(8,128)(2,1)S(1)}, u32[]{:S(2)}, u32[]{:S(2)}) collective-permute-start(bf16[4,128,512]{2,1,0:T(8,128)(2,1)S(1)} %add_convert_fusion.3), channel_id=1, source_target_pairs={{0,8},{1,9},{2,10},{3,11},{4,12},{5,13},{6,14},{7,15},{8,0},{9,1},... | collective-permute-start | bytes 1572872 | tf_op jit(solution)/shard_map/ppermute | solution.py:358
  210.9 18.0 %collective-permute-start.33 = (bf16[4,128,512]{2,1,0:T(8,128)(2,1)S(1)}, bf16[4,128,512]{2,1,0:T(8,128)(2,1)S(1)}, u32[]{:S(2)}, u32[]{:S(2)}) collective-permute-start(bf16[4,128,512]{2,1,0:T(8,128)(2,1)S(1)} %add_convert_fusion.2), channel_id=1, source_target_pairs={{0,8},{1,9},{2,10},{3,11},{4,12},{5,13},{6,14},{7,15},{8,0},{9,1},... | collective-permute-start | bytes 1572872 | tf_op jit(solution)/shard_map/ppermute | solution.py:358
  212.1 17.9 %collective-permute-start.29 = (bf16[2,128,512]{2,1,0:T(8,128)(2,1)S(1)}, bf16[2,128,512]{2,1,0:T(8,128)(2,1)S(1)}, u32[]{:S(2)}, u32[]{:S(2)}) collective-permute-start(bf16[2,128,512]{2,1,0:T(8,128)(2,1)S(1)} %add_convert_fusion.5), channel_id=1, source_target_pairs={{0,16},{1,17},{2,18},{3,19},{4,20},{5,21},{6,22},{7,23},{8,24},{9,... | collective-permute-start | bytes 786440 | tf_op jit(solution)/shard_map/ppermute | solution.py:358
  230.0 11.7 %collective-permute-start.34 = (bf16[2,128,512]{2,1,0:T(8,128)(2,1)S(1)}, bf16[2,128,512]{2,1,0:T(8,128)(2,1)S(1)}, u32[]{:S(2)}, u32[]{:S(2)}) collective-permute-start(bf16[2,128,512]{2,1,0:T(8,128)(2,1)S(1)} %add_convert_fusion.4), channel_id=1, source_target_pairs={{0,16},{1,17},{2,18},{3,19},{4,20},{5,21},{6,22},{7,23},{8,24},{9,... | collective-permute-start | bytes 786440 | tf_op jit(solution)/shard_map/ppermute | solution.py:358
  231.1 11.6 %collective-permute-start.30 = (bf16[1,128,512]{2,1,0:T(8,128)(2,1)S(1)}, bf16[1,128,512]{2,1,0:T(8,128)(2,1)S(1)}, u32[]{:S(2)}, u32[]{:S(2)}) collective-permute-start(bf16[1,128,512]{2,1,0:T(8,128)(2,1)S(1)} %add_convert_fusion.7), channel_id=1, source_target_pairs={{0,4},{1,3},{2,6},{3,1},{4,0},{5,7},{6,2},{7,5},{8,12},{9,11},{10,... | collective-permute-start | bytes 393224 | tf_op jit(solution)/shard_map/ppermute | solution.py:358
  242.6 5.0 %collective-permute-start.35 = (bf16[1,128,512]{2,1,0:T(8,128)(2,1)S(1)}, bf16[1,128,512]{2,1,0:T(8,128)(2,1)S(1)}, u32[]{:S(2)}, u32[]{:S(2)}) collective-permute-start(bf16[1,128,512]{2,1,0:T(8,128)(2,1)S(1)} %add_convert_fusion.6), channel_id=1, source_target_pairs={{0,4},{1,3},{2,6},{3,1},{4,0},{5,7},{6,2},{7,5},{8,12},{9,11},{10,... | collective-permute-start | bytes 393224 | tf_op jit(solution)/shard_map/ppermute | solution.py:358

commit v5 on v4

--- a/solution.py
+++ b/solution.py
@@ -78,47 +78,53 @@
 
 def project_kernel(member_ref, head_refs, weight_ref, send_ref, keep_ref):
     core, x_side, z = member_ref[0], member_ref[1], member_ref[2]
-    result = jnp.dot(
-        jnp.concatenate([ref[...] for ref in head_refs], axis=0),
-        weight_ref[...],
-        preferred_element_type=F32,
-    ).astype(BF16)
     here = head_refs[0].shape[0]
-    for to_x in range(2):
-        x_kept = (x_side == to_x).astype(jnp.int32)
-        for to_core in range(2):
-            start = (to_x * 2 + to_core) * LANES
-            for out_ref, wanted in ((keep_ref, core == to_core), (send_ref, core != to_core)):
-
-                @pl.when(wanted)
-                def _(out_ref=out_ref, x_kept=x_kept, start=start):
-                    for piece, z_bits in enumerate(HEAD_ORDER):
-                        out_ref[x_kept, z ^ z_bits] = result[
-                            piece * here : (piece + 1) * here, start : start + LANES
-                        ]
+    each = len(HEAD_ORDER)
+    for half in range(2):
+        result = jnp.dot(
+            jnp.concatenate([ref[...] for ref in head_refs[half * each : (half + 1) * each]]),
+            weight_ref[...],
+            preferred_element_type=F32,
+        ).astype(BF16)
+        for to_x in range(2):
+            x_kept = (x_side == to_x).astype(jnp.int32)
+            for to_core in range(2):
+                start = (to_x * 2 + to_core) * LANES
+                for out_ref, wanted in ((keep_ref, core == to_core), (send_ref, core != to_core)):
+
+                    @pl.when(wanted)
+                    def _(out_ref=out_ref, x_kept=x_kept, start=start, half=half, result=result):
+                        for piece, z_bits in enumerate(HEAD_ORDER):
+                            out_ref[x_kept, half, z ^ z_bits] = result[
+                                piece * here : (piece + 1) * here, start : start + LANES
+                            ]
 
 
 def project(member_info, pieces, out_proj):
     here = pieces[0].shape[0]
-    out = jax.ShapeDtypeStruct((2, len(pieces), here, LANES), BF16)
+    out = jax.ShapeDtypeStruct((2, 2, len(HEAD_ORDER), here, LANES), BF16)
     vmem = pl.BlockSpec(memory_space=pltpu.VMEM)
 
     def kernel(member_ref, *refs):
-        project_kernel(member_ref, refs[:4], refs[4], refs[5], refs[6])
+        project_kernel(member_ref, refs[: len(pieces)], *refs[len(pieces) :])
 
     return pl.pallas_call(
         kernel,
-        in_specs=[pl.BlockSpec(memory_space=pltpu.SMEM)] + [vmem] * 5,
+        in_specs=[pl.BlockSpec(memory_space=pltpu.SMEM)] + [vmem] * (len(pieces) + 1),
         out_specs=[vmem, vmem],
         out_shape=[out, out],
         compiler_params=pltpu.CompilerParams(vmem_limit_bytes=24 * 1024 * 1024),
         cost_estimate=pl.CostEstimate(
-            flops=2 * 4 * here * out_proj.size,
-            bytes_accessed=2 * (out_proj.size + 5 * pieces[0].size),
+            flops=2 * len(pieces) * here * out_proj.size,
+            bytes_accessed=2 * (out_proj.size + 2 * len(pieces) * pieces[0].size),
             transcendentals=0,
         ),
         name="project",
     )(member_info, *pieces, out_proj)
+
+
+def other_place(place):
+    return (place >> 1) | ((place & 1) << 2)
 
 
 def gate_up_kernel(
@@ -157,14 +163,16 @@
                 for place, feature in zip(places, features):
                     invgain = invgain_ref[pl.ds(feature, 1), :]
                     for part in range(parts):
-                        for half, ref in enumerate((own, other)):
-                            value = ref[place, part].astype(F32) * invgain
+                        for half, block in enumerate(
+                            (own[place, part], other[other_place(place), part])
+                        ):
+                            value = block.astype(F32) * invgain
                             sq_ref[swapped, part, half] += value * value
 
                 for part in range(parts):
                     both = jnp.concatenate(
                         [
-                            jnp.concatenate([own[place, part], other[place, part]], axis=0)
+                            jnp.concatenate([own[place, part], other[other_place(place), part]])
                             for place in places
                         ],
                         axis=1,
@@ -194,7 +202,7 @@
                     mine = jnp.where(
                         info_ref[blocks + array * each + place] == 0,
                         own[place, z].astype(F32),
-                        other[place, z].astype(F32),
+                        other[other_place(place), z].astype(F32),
                     )
                     column = pl.multiple_of((feature & 7) * lanes, lanes)
                     hidden_ref[:, pl.ds(column, lanes)] = mine * invgain_ref[pl.ds(feature, 1), :]
@@ -312,8 +320,9 @@
                     spread_ref[part], picked, preferred_element_type=F32
                 ).astype(BF16)
                 for i in range(PAIR):
-                    target = place_ref[2 + side * groups + part * PAIR + i]
                     for number, out_ref in enumerate(out_refs):
+                        block = (number * 2 + side) * groups + part * PAIR + i
+                        target = place_ref[2 + block]
                         out_ref[target] = mixed[
                             i * 128 : (i + 1) * 128, number * out_cols : (number + 1) * out_cols
                         ]
@@ -374,15 +383,29 @@
     return order ^ (group & 1)
 
 
-def halving_places(to_core, group, groups):
+HALVING = {
+    "first": first_axis,
+    "last": last_axis,
+    "low": lambda core: ZLOW,
+    "high": lambda core: ZHIGH,
+}
+ORDERS = (("first", "low", "high", "last"), ("first", "last", "low", "high"))
+
+
+def halving_places(to_core, group, groups, order):
     g = own_order(groups, group)[None, :]
     y_kept = ((g & 1) == (group & 1)).astype(jnp.int32)
-    low_kept = (((g >> 1) & 1) == ((group >> 1) & 1)).astype(jnp.int32)
-    high_kept = ((g >> 2) == (group >> 2)).astype(jnp.int32)
     x_kept = jnp.arange(2, dtype=jnp.int32)[:, None]
-    first = jnp.where(to_core == 0, x_kept, y_kept)
-    last = jnp.where(to_core == 0, y_kept, x_kept)
-    return (((first * 2 + low_kept) * 2 + high_kept) * 2 + last).reshape(-1)
+    kept = {
+        "first": jnp.where(to_core == 0, x_kept, y_kept),
+        "last": jnp.where(to_core == 0, y_kept, x_kept),
+        "low": (((g >> 1) & 1) == ((group >> 1) & 1)).astype(jnp.int32),
+        "high": ((g >> 2) == (group >> 2)).astype(jnp.int32),
+    }
+    place = 0
+    for axis in order:
+        place = place * 2 + kept[axis]
+    return place.reshape(-1)
 
 
 def total_of(terms):
@@ -392,36 +415,32 @@
     return total
 
 
-HALVING = (first_axis, lambda core: ZLOW, lambda core: ZHIGH, last_axis)
-
-
 def after(value, earlier):
     return lax.optimization_barrier((value, earlier))
 
 
-def sent_half(terms):
-    half = terms[0].shape[0] // 2
-    return total_of([term[:half] for term in terms]).astype(BF16), [term[half:] for term in terms]
-
-
 def reduce_chunks(makers):
-    chunks, arrived, first_sent = [None] * len(makers), {}, None
-    for tick in range(len(HALVING) + len(makers) - 1):
-        for index, maker in enumerate(makers):
-            stage = tick - index
-            if not 0 <= stage < len(HALVING):
-                continue
-            if stage == 0:
-                chunks[index] = maker(first_sent)
-            sent, rest = sent_half(chunks[index])
-            if index:
-                sent, _ = after(sent, arrived[index - 1, stage])
-            if stage == 0:
-                first_sent = sent
-            came = flip(sent, HALVING[stage])
-            arrived[index, stage] = came
-            chunks[index] = rest + [came]
-    return [total_of([term[0] for term in terms]) for terms in chunks]
+    terms, came = [None, None], {}
+
+    def exchange(chunk, stage, earlier=None):
+        half = terms[chunk][0].shape[0] // 2
+        sent = total_of([term[:half] for term in terms[chunk]]).astype(BF16)
+        if earlier is not None:
+            sent, _ = after(sent, earlier)
+        came[chunk, stage] = flip(sent, HALVING[ORDERS[chunk][stage]])
+        terms[chunk] = [term[half:] for term in terms[chunk]] + [came[chunk, stage]]
+        return sent
+
+    terms[0] = makers[0](None)
+    terms[1] = makers[1](exchange(0, 0))
+    exchange(1, 0, came[0, 0])
+    exchange(0, 1)
+    exchange(1, 1, came[0, 1])
+    exchange(0, 2)
+    exchange(1, 2)
+    exchange(0, 3, came[1, 2])
+    exchange(1, 3)
+    return [total_of([term[0] for term in chunk]) for chunk in terms]
 
 
 def route_tables(route_ids, route_weights, group, experts, groups):
@@ -468,43 +487,42 @@
     return jnp.concatenate([feature, swapped, jnp.stack([member, device >> 3])])
 
 
-def gather_chunks(starts, beside):
-    stages = (last_axis, lambda core: ZHIGH, lambda core: ZLOW, first_axis)
-    held = [[start] for start in starts]
-    arrived = {}
-    for tick in range(len(stages) + len(starts) - 1):
-        for index in reversed(range(len(starts))):
-            stage = tick - index
-            if not 0 <= stage < len(stages):
-                continue
-            block = held[index][-1]
-            if index:
-                block, _ = after(block, arrived[index - 1, stage])
-            if stage == len(stages) - 1 and index == len(starts) - 1:
-                block, _ = after(block, beside)
-            came = flip(block, stages[stage])
-            if stage == 1 and (index + 1, 0) in arrived:
-                came, _ = after(came, arrived[index + 1, 0])
-            arrived[index, stage] = came
-            if stage < len(stages) - 1:
-                held[index].append(jnp.concatenate([block, came], axis=0))
-            else:
-                other = flip(block, lambda core: CORE)
-                held[index] = [block, came, other, flip(came, lambda core: CORE)]
-    return held
-
-
-def gather_heads(heads, beside):
+def gather_blocks(first, second, make_beside):
+    def along(bits, block):
+        return flip(block, lambda core: bits)
+
+    def joined(held, came):
+        return jnp.concatenate([held, came], axis=0)
+
+    first_last = flip(first, last_axis)
+    second_high = along(ZHIGH, second)
+    second = joined(second, second_high)
+    second_low = along(ZLOW, second)
+    first, _ = after(joined(first, first_last), second_high)
+    beside = make_beside((first_last, second_high))
+    first_high = along(ZHIGH, first)
+    second = joined(second, second_low)
+    second_last = flip(second, last_axis)
+    first, _ = after(joined(first, first_high), second_low)
+    first_low = along(ZLOW, first)
+    second = joined(second, second_last)
+    second_first = flip(second, first_axis)
+    first, _ = after(joined(first, first_low), (second_last, beside))
+    first_first = flip(first, first_axis)
+    return [
+        [block, came, along(CORE, block), along(CORE, came)]
+        for block, came in ((first, first_first), (second, second_first))
+    ] + [beside]
+
+
+def gather_heads(heads):
     def along(bits, piece):
         return flip(piece, lambda core: bits)
 
     high = along(ZHIGH, heads)
     low = along(ZLOW, heads)
-    both, beside = after(along(ZLOW, high), beside)
-    own = [heads, high, low, both]
-    other = [along(Y, piece) for piece in own]
-    own, _ = after(own, other[:3])
-    return own, other, beside
+    own = [heads, high, low, along(ZLOW, high)]
+    return own + [along(Y, piece) for piece in own]
 
 
 def per_device_tokens(
@@ -529,22 +547,21 @@
     )
 
     member_info = jnp.stack([core, x_side, z])
+    pieces, moved = after(gather_heads(attn_heads), moved)
+    send, keep = project(member_info, pieces, out_proj)
+    came = flip(send, lambda c: CORE)
+    from_x = flip(total_of([keep[0], came[0]]).astype(BF16), lambda c: X)
     starts = []
-    own_heads, other_heads, moved = gather_heads(attn_heads, moved)
-    for half, pieces in enumerate((own_heads, other_heads)):
-        if half:
-            (pieces, moved, gain), _ = after((pieces, moved, gain), starts[0])
-        send, keep = project(member_info, pieces, out_proj)
-        came = flip(send, lambda c: CORE)
-        to_x = (keep[0].astype(F32) + came[0].astype(F32)).astype(BF16)
-        from_x = flip(to_x, lambda c: X)
+    for half in range(2):
         hidden = lax.dynamic_index_in_dim(moved, y_side ^ half, 1, keepdims=False).astype(F32)
-        hidden = hidden + total_of([keep[1], came[1], from_x])
+        hidden = hidden + total_of([keep[1, half], came[1, half], from_x[half]])
         starts.append((hidden * gain).astype(BF16)[None])
 
-    route_ids, _ = after(route_ids, starts[1])
-    slots, weights = route_tables(route_ids, route_weights, group, experts, groups)
-    own_x, other_x = gather_chunks(starts, (slots, weights))
+    def tables(earlier):
+        ids, _ = after(route_ids, earlier)
+        return route_tables(ids, route_weights, group, experts, groups)
+
+    own_x, other_x, (slots, weights) = gather_blocks(*starts, tables)
     x = [piece for pair in zip(own_x, other_x) for piece in pair]
     invgain = (1.0 / norm_gain).reshape(groups * members, LANES)
     act, own_hidden, spread = gate_up(
@@ -553,21 +570,22 @@
 
     cols = width // members
 
-    def columns_of(to_core, chunk, chunks):
+    def columns_of(to_core, chunk, chunks, orders):
         sides = jnp.stack([1 - x_side, x_side])
         blocks = (sides * 2 + to_core) * chunks + chunk
-        return jnp.concatenate([blocks, halving_places(to_core, group, groups)])
-
-    chunks = 2
+        places = [halving_places(to_core, group, groups, order) for order in orders]
+        return jnp.concatenate([blocks] + places)
+
+    chunks = len(ORDERS)
     chunk_cols = cols // chunks
     other = down(
-        columns_of(1 - core, 0, 1), spread, act, w_down, rows, groups, cols, chunks
+        columns_of(1 - core, 0, 1, ORDERS), spread, act, w_down, rows, groups, cols, chunks
     )
     came = [flip(piece, lambda c: CORE) for piece in other]
 
     def terms_of(chunk, earlier):
         ready = act if earlier is None else after(act, earlier)[0]
-        place = columns_of(core, chunk, chunks)
+        place = columns_of(core, chunk, chunks, ORDERS[chunk : chunk + 1])
         (kept,) = down(place, spread, ready, w_down, rows, groups, chunk_cols, 1)
         return [kept, came[chunk]]
 

time: 250 us -> 252 us (level)
  other arithmetic: 15.6 us -> 6.01 us
  waiting for transfers between devices: 134 us -> 142 us
  local copies, waits for them, and re-layouts: 4.55 us -> 10.6 us
  Pallas kernels: 59.7 us -> 57 us
    ppermute x36 -> x34, waiting for transfers between devices: 133 us -> 142 us  [flip(): return lax.ppermute(array, ('expert', 'tensor'), pairs)]
    convert_element_type x11, other arithmetic: 9.8 us -> 2.69 us  [the longest x8 1.48 us: exchange(): sent = total_of([term[:half] for term in terms[chunk]]).astype(BF16)]
    unnamed x18 -> x32, local copies, waits for them, and re-layouts: 2.92 us -> 8.61 us
    ppermute x36 -> x34, starting transfers between devices: 32 us -> 28.7 us  [flip(): return lax.ppermute(array, ('expert', 'tensor'), pairs)]
  transfers between devices with their start and end apart: 37 -> 35, of which waited for: 24 -> 22; matrix products, arithmetic and copies ran while one was open for 7% -> 3% of each run, Pallas kernels for 5% -> 5%
where the time goes in v5:
time: 252 us; the launch traced here: 250 us
  waiting for transfers between devices  142 us (56%)
  Pallas kernels  57 us (23%)
  starting transfers between devices  34.2 us (14%)
  local copies, waits for them, and re-layouts  10.6 us (4%)
  other arithmetic  6.01 us (2%)
    ppermute x34, waiting for transfers between devices, flip(): return lax.ppermute(array, ('expert', 'tensor'), pairs)  142 us
    pallas_call x1, Pallas kernels, gate_up(): pl.pallas_call(kernel, grid_spec=pltpu.PrefetchScalarGridSpec(num_scalar_...  32.1 us
    ppermute x34, starting transfers between devices, flip(): return lax.ppermute(array, ('expert', 'tensor'), pairs)  28.7 us
    pallas_call x3, Pallas kernels, down(): pl.pallas_call(functools.partial(down_kernel, rows), grid_spec=pltpu.Pref...  22.8 us
    unnamed x32, local copies, waits for them, and re-layouts  8.61 us
    all_to_all x1, starting transfers between devices, per_device_tokens(): lax.all_to_all(jnp.transpose(own_cols, (1, 0, 2)), 'expert', split_axis=0...  5.51 us
  transfers between devices with their start and end apart: 35, of which 22 were waited for; matrix products, arithmetic and copies ran while one was open for 3% of the time, Pallas kernels for 5%

profile of v5, /device:TPU:0, one launch (start us, length us, event | category | flops | bytes accessed | tf_op | source)
XLA Modules:
  0.0 250.2 jit_solution(17504647538369721310)
XLA Ops:
  0.0 4.0 %collective-permute-start = (bf16[128,1024]{1,0:T(8,128)(2,1)}, bf16[128,1024]{1,0:T(8,128)(2,1)S(1)}, u32[]{:S(2)}, u32[]{:S(2)}) collective-permute-start(bf16[128,1024]{1,0:T(8,128)(2,1)} %refs_0_), channel_id=1, source_target_pairs={{0,16},{1,17},{2,18},{3,19},{4,20},{5,21},{6,22},{7,23},{8,24},{9,... | collective-permute-start | bytes 786440 | tf_op jit(solution)/shard_map/ppermute | solution.py:367
  4.0 1.6 collective-permute-start.1
  5.6 1.6 copy.23
  7.2 9.1 %collective-permute-done.refs_1_ = bf16[128,1024]{1,0:T(8,128)(2,1)S(1)} collective-permute-done((bf16[128,1024]{1,0:T(8,128)(2,1)}, bf16[128,1024]{1,0:T(8,128)(2,1)S(1)}, u32[]{:S(2)}, u32[]{:S(2)}) %collective-permute-start) | collective-permute-done | bytes 262176 | tf_op jit(solution)/shard_map/ppermute | solution.py:367
  16.3 0.7 collective-permute-start.2
  17.0 0.9 copy.25
  17.9 5.5 %all-to-all-start = ((bf16[8,128,128]{2,1,0:T(8,128)(2,1)}), bf16[8,128,128]{2,1,0:T(8,128)(2,1)S(1)}, u32[]{:S(2)}, u32[]{:S(2)}) async-start(bf16[8,128,128]{2,1,0:T(8,128)(2,1)} %copy.25), calls=%async_computation | async-start | bytes 524288 | tf_op jit(solution)/shard_map/all_to_all | solution.py:542
  23.4 2.0 collective-permute-start.3
  25.5 2.0 collective-permute-start.5
  27.6 7.9 %collective-permute-done.3.refs_4_ = bf16[128,1024]{1,0:T(8,128)(2,1)S(1)} collective-permute-done((bf16[128,1024]{1,0:T(8,128)(2,1)S(1)}, bf16[128,1024]{1,0:T(8,128)(2,1)S(1)}, u32[]{:S(2)}, u32[]{:S(2)}) %collective-permute-start.3) | collective-permute-done | bytes 262176 | tf_op jit(solution)/shard_map/ppermute | solution.py:367
  35.5 5.6 %collective-permute-done.4.refs_5_ = bf16[128,1024]{1,0:T(8,128)(2,1)S(1)} collective-permute-done((bf16[128,1024]{1,0:T(8,128)(2,1)S(1)}, bf16[128,1024]{1,0:T(8,128)(2,1)S(1)}, u32[]{:S(2)}, u32[]{:S(2)}) %collective-permute-start.4) | collective-permute-done | bytes 262176 | tf_op jit(solution)/shard_map/ppermute | solution.py:367
  41.1 0.7 copy-done.3
  41.8 4.9 %collective-permute-done.5.refs_6_ = bf16[128,1024]{1,0:T(8,128)(2,1)S(1)} collective-permute-done((bf16[128,1024]{1,0:T(8,128)(2,1)S(1)}, bf16[128,1024]{1,0:T(8,128)(2,1)S(1)}, u32[]{:S(2)}, u32[]{:S(2)}) %collective-permute-start.5) | collective-permute-done | bytes 262176 | tf_op jit(solution)/shard_map/ppermute | solution.py:367
  46.7 0.7 copy-done.5
  47.4 3.5 %collective-permute-done.6.refs_7_ = bf16[128,1024]{1,0:T(8,128)(2,1)S(1)} collective-permute-done((bf16[128,1024]{1,0:T(8,128)(2,1)S(1)}, bf16[128,1024]{1,0:T(8,128)(2,1)S(1)}, u32[]{:S(2)}, u32[]{:S(2)}) %collective-permute-start.6) | collective-permute-done | bytes 262176 | tf_op jit(solution)/shard_map/ppermute | solution.py:367
  50.9 0.7 copy-done.7
  51.6 0.9 copy-done.4
  52.6 0.9 copy-done.6
  53.5 0.9 copy-done.8
  54.5 2.1 project.1
  56.7 1.9 collective-permute-done.7
  58.7 1.6 collective-permute-start.8
  60.3 6.8 %collective-permute-done.8 = bf16[2,4,128,128]{3,2,1,0:T(8,128)(2,1)S(1)} collective-permute-done((bf16[2,4,128,128]{3,2,1,0:T(8,128)(2,1)S(1)}, bf16[2,4,128,128]{3,2,1,0:T(8,128)(2,1)S(1)}, u32[]{:S(2)}, u32[]{:S(2)}) %collective-permute-start.8) | collective-permute-done | bytes 262176 | tf_op jit(solution)/shard_map/ppermute | solution.py:367
  67.1 1.1 fusion.4
  68.2 1.2 collective-permute-start.9
  69.4 2.0 collective-permute-start.10
  71.4 1.8 collective-permute-done.9
  73.2 4.7 %collective-permute-done.10 = bf16[1,4,128,128]{3,2,1,0:T(8,128)(2,1)S(1)} collective-permute-done((bf16[1,4,128,128]{3,2,1,0:T(8,128)(2,1)S(1)}, bf16[1,4,128,128]{3,2,1,0:T(8,128)(2,1)S(1)}, u32[]{:S(2)}, u32[]{:S(2)}) %collective-permute-start.10) | collective-permute-done | bytes 131104 | tf_op jit(solution)/shard_map/ppermute | solution.py:367
  78.0 4.5 %collective-permute-done.11 = f32[1,16,128]{2,1,0:T(8,128)S(1)} collective-permute-done((f32[1,16,128]{2,1,0:T(8,128)S(1)}, f32[1,16,128]{2,1,0:T(8,128)S(1)}, u32[]{:S(2)}, u32[]{:S(2)}) %collective-permute-start.11) | collective-permute-done | bytes 8224 | tf_op jit(solution)/shard_map/ppermute | solution.py:367
  82.5 0.9 collective-permute-start.12
  83.5 3.0 %collective-permute-start.14 = (bf16[2,4,128,128]{3,2,1,0:T(8,128)(2,1)S(1)}, bf16[2,4,128,128]{3,2,1,0:T(8,128)(2,1)S(1)}, u32[]{:S(2)}, u32[]{:S(2)}) collective-permute-start(bf16[2,4,128,128]{3,2,1,0:T(8,128)(2,1)S(1)} %pad_maximum_fusion.4), channel_id=1, source_target_pairs={{0,16},{1,17},{2,18},{3,19},{4,20},{5,21},{6,22},{7,23},{8,24},{9,... | collective-permute-start | bytes 786440 | tf_op jit(solution)/shard_map/ppermute | solution.py:367
  86.5 0.9 collective-permute-start.13
  87.4 0.4 collective-permute-start.15
  87.9 2.5 %collective-permute-done.13 = f32[4,16,128]{2,1,0:T(8,128)S(1)} collective-permute-done((f32[4,16,128]{2,1,0:T(8,128)S(1)}, f32[4,16,128]{2,1,0:T(8,128)S(1)}, u32[]{:S(2)}, u32[]{:S(2)}) %collective-permute-start.13) | collective-permute-done | bytes 32800 | tf_op jit(solution)/shard_map/ppermute | solution.py:367
  90.4 0.6 gather_fusion
  91.1 5.9 %collective-permute-done.14 = bf16[2,4,128,128]{3,2,1,0:T(8,128)(2,1)S(1)} collective-permute-done((bf16[2,4,128,128]{3,2,1,0:T(8,128)(2,1)S(1)}, bf16[2,4,128,128]{3,2,1,0:T(8,128)(2,1)S(1)}, u32[]{:S(2)}, u32[]{:S(2)}) %collective-permute-start.14) | collective-permute-done | bytes 262176 | tf_op jit(solution)/shard_map/ppermute | solution.py:367
  97.1 1.5 collective-permute-done.15
  98.6 0.3 collective-permute-start.16
  99.0 0.6 collective-permute-start.17
  99.9 11.0 %collective-permute-done.16 = bf16[4,4,128,128]{3,2,1,0:T(8,128)(2,1)S(1)} collective-permute-done((bf16[4,4,128,128]{3,2,1,0:T(8,128)(2,1)S(1)}, bf16[4,4,128,128]{3,2,1,0:T(8,128)(2,1)S(1)}, u32[]{:S(2)}, u32[]{:S(2)}) %collective-permute-start.16) | collective-permute-done | bytes 524320 | tf_op jit(solution)/shard_map/ppermute | solution.py:367
  111.1 0.7 copy-done.11
  111.8 1.1 pad_maximum_fusion.1.rest_1_
  113.0 1.3 collective-permute-start.19
  114.3 0.5 collective-permute-start.21
  114.8 11.0 %collective-permute-done.18.rest_2_ = bf16[8,4,128,128]{3,2,1,0:T(8,128)(2,1)S(1)} collective-permute-done((bf16[8,4,128,128]{3,2,1,0:T(8,128)(2,1)S(1)}, bf16[8,4,128,128]{3,2,1,0:T(8,128)(2,1)S(1)}, u32[]{:S(2)}, u32[]{:S(2)}) %collective-permute-start.18) | collective-permute-done | bytes 1048608 | tf_op jit(solution)/shard_map/ppermute | solution.py:367
  125.9 11.3 %collective-permute-done.19.rest_3_ = bf16[8,4,128,128]{3,2,1,0:T(8,128)(2,1)} collective-permute-done((bf16[8,4,128,128]{3,2,1,0:T(8,128)(2,1)S(1)}, bf16[8,4,128,128]{3,2,1,0:T(8,128)(2,1)}, u32[]{:S(2)}, u32[]{:S(2)}) %collective-permute-start.19) | collective-permute-done | bytes 1048608 | tf_op jit(solution)/shard_map/ppermute | solution.py:367
  138.0 2.2 collective-permute-done.23.rest_7_
  140.2 32.1 %gate_up.1 = (bf16[8,192,384]{2,1,0:T(8,128)(2,1)}, f32[128,1024]{1,0:T(8,128)S(1)}, bf16[4,256,384]{2,1,0:T(8,128)(2,1)S(1)}) custom-call(s32[66]{0:T(128)S(1)} %pad_add_fusion.info_ref, s32[8,1024]{1,0:T(8,128)S(1)} %bitcast_select_fusion.slot_ref, f32[8,1024]{1,0:T(8,128)S(1)} %bitcast.51, f32[32,128]{1,0:T(8,128)S(1)} %divide_bitcast_fusion.invgain_ref, ...), custom_call_target="tpu_custom_call" | custom-call | flops 9663676416 | bytes 58720256 | tf_op jit(solution)/shard_map/gate_up/pallas_call | solution.py:260
  172.3 1.3 copy-done
  173.6 9.9 %down_mix.4 = (bf16[16,128,512]{2,1,0:T(8,128)(2,1)S(1)}, bf16[16,128,512]{2,1,0:T(8,128)(2,1)S(1)}) custom-call(s32[34]{0:T(128)S(1)} %pad_add_fusion.3.place_ref, bf16[4,256,384]{2,1,0:T(8,128)(2,1)S(1)} %get-tuple-element.45.spread_ref, bf16[8,192,384]{2,1,0:T(8,128)(2,1)S(1)} %copy-done, bf16[8,384,4096]{2,1,0:T(8,128)(2,1)} %wd1_ref.5, ...), custom_call_target="tpu_custom_call" | custom-call | flops 4831838208 | bytes 16777216 | tf_op jit(solution)/shard_map/down_mix/pallas_call | solution.py:336
  183.6 0.4 collective-permute-start.28
  184.2 6.4 %down_mix.3 = bf16[16,128,512]{2,1,0:T(8,128)(2,1)S(1)} custom-call(s32[18]{0:T(128)S(1)} %pad_add_fusion.2.place_ref, bf16[4,256,384]{2,1,0:T(8,128)(2,1)S(1)} %get-tuple-element.45.spread_ref, bf16[8,192,384]{2,1,0:T(8,128)(2,1)S(1)} %copy-done, bf16[8,384,4096]{2,1,0:T(8,128)(2,1)} %wd1_ref.5, bf16[8,384,4096]{2,1,0:T(8,128)(2,1)} %wd1_ref.5), custom_call_target="tpu_custom_call" | custom-call | flops 2415919104 | bytes 8388608 | tf_op jit(solution)/shard_map/down_mix/pallas_call | solution.py:336
  190.7 0.3 add_convert_fusion.1
  191.2 6.4 %down_mix.5 = bf16[16,128,512]{2,1,0:T(8,128)(2,1)S(1)} custom-call(s32[18]{0:T(128)S(1)} %pad_add_fusion.4.place_ref, bf16[4,256,384]{2,1,0:T(8,128)(2,1)S(1)} %get-tuple-element.45.spread_ref, bf16[8,192,384]{2,1,0:T(8,128)(2,1)S(1)} %copy-done, bf16[8,384,4096]{2,1,0:T(8,128)(2,1)} %wd1_ref.5, bf16[8,384,4096]{2,1,0:T(8,128)(2,1)} %wd1_ref.5), custom_call_target="tpu_custom_call" | custom-call | flops 2415919104 | bytes 8388608 | tf_op jit(solution)/shard_map/down_mix/pallas_call | solution.py:336
  197.6 0.3 add_convert_fusion
  197.9 7.9 %collective-permute-done.25 = bf16[8,128,512]{2,1,0:T(8,128)(2,1)S(1)} collective-permute-done((bf16[8,128,512]{2,1,0:T(8,128)(2,1)S(1)}, bf16[8,128,512]{2,1,0:T(8,128)(2,1)S(1)}, u32[]{:S(2)}, u32[]{:S(2)}) %collective-permute-start.25) | collective-permute-done | bytes 1048608 | tf_op jit(solution)/shard_map/ppermute | solution.py:367
  206.4 14.3 %collective-permute-done.29 = bf16[8,128,512]{2,1,0:T(8,128)(2,1)S(1)} collective-permute-done((bf16[8,128,512]{2,1,0:T(8,128)(2,1)S(1)}, bf16[8,128,512]{2,1,0:T(8,128)(2,1)S(1)}, u32[]{:S(2)}, u32[]{:S(2)}) %collective-permute-start.29) | collective-permute-done | bytes 1048608 | tf_op jit(solution)/shard_map/ppermute | solution.py:367
  220.9 0.6 collective-permute-start.30
  221.5 8.6 %collective-permute-done.30 = bf16[4,128,512]{2,1,0:T(8,128)(2,1)S(1)} collective-permute-done((bf16[4,128,512]{2,1,0:T(8,128)(2,1)S(1)}, bf16[4,128,512]{2,1,0:T(8,128)(2,1)S(1)}, u32[]{:S(2)}, u32[]{:S(2)}) %collective-permute-start.30) | collective-permute-done | bytes 524320 | tf_op jit(solution)/shard_map/ppermute | solution.py:367
  230.6 2.1 collective-permute-start.27
  232.8 8.9 %collective-permute-done.31 = bf16[2,128,512]{2,1,0:T(8,128)(2,1)S(1)} collective-permute-done((bf16[2,128,512]{2,1,0:T(8,128)(2,1)S(1)}, bf16[2,128,512]{2,1,0:T(8,128)(2,1)S(1)}, u32[]{:S(2)}, u32[]{:S(2)}) %collective-permute-start.31) | collective-permute-done | bytes 262176 | tf_op jit(solution)/shard_map/ppermute | solution.py:367
  241.9 1.4 collective-permute-start.32
  243.3 5.9 %collective-permute-done.33 = bf16[1,128,512]{2,1,0:T(8,128)(2,1)S(1)} collective-permute-done((bf16[1,128,512]{2,1,0:T(8,128)(2,1)S(1)}, bf16[1,128,512]{2,1,0:T(8,128)(2,1)S(1)}, u32[]{:S(2)}, u32[]{:S(2)}) %collective-permute-start.33) | collective-permute-done | bytes 131104 | tf_op jit(solution)/shard_map/ppermute | solution.py:367
  249.5 0.8 fusion
  (104 shorter events, 4.4 us)
Async XLA Ops:
  0.0 23.4 %copy-start.2 = (bf16[128,1024]{1,0:T(8,128)(2,1)S(1)}, bf16[128,1024]{1,0:T(8,128)(2,1)}, u32[]{:S(2)}) copy-start(bf16[128,1024]{1,0:T(8,128)(2,1)} %refs_0_) | copy-start | bytes 786436
  0.0 51.6 %copy-start.1 = (bf16[1024,512]{1,0:T(8,128)(2,1)S(1)}, bf16[1024,512]{1,0:T(8,128)(2,1)}, u32[]{:S(2)}) copy-start(bf16[1024,512]{1,0:T(8,128)(2,1)} %refs_8_.1) | copy-start | bytes 3145732
  0.0 16.3 %collective-permute-start = (bf16[128,1024]{1,0:T(8,128)(2,1)}, bf16[128,1024]{1,0:T(8,128)(2,1)S(1)}, u32[]{:S(2)}, u32[]{:S(2)}) collective-permute-start(bf16[128,1024]{1,0:T(8,128)(2,1)} %refs_0_), channel_id=1, source_target_pairs={{0,16},{1,17},{2,18},{3,19},{4,20},{5,21},{6,22},{7,23},{8,24},{9,... | collective-permute-start | bytes 786440 | tf_op jit(solution)/shard_map/ppermute | solution.py:367
  4.0 21.4 %collective-permute-start.1 = (bf16[128,1024]{1,0:T(8,128)(2,1)}, bf16[128,1024]{1,0:T(8,128)(2,1)S(1)}, u32[]{:S(2)}, u32[]{:S(2)}) collective-permute-start(bf16[128,1024]{1,0:T(8,128)(2,1)} %refs_0_), channel_id=1, source_target_pairs={{0,8},{1,9},{2,10},{3,11},{4,12},{5,13},{6,14},{7,15},{8,0},{9,1},... | collective-permute-start | bytes 786440 | tf_op jit(solution)/shard_map/ppermute | solution.py:367
  16.3 11.1 %collective-permute-start.2 = (bf16[128,1024]{1,0:T(8,128)(2,1)S(1)}, bf16[128,1024]{1,0:T(8,128)(2,1)S(1)}, u32[]{:S(2)}, u32[]{:S(2)}) collective-permute-start(bf16[128,1024]{1,0:T(8,128)(2,1)S(1)} %collective-permute-done.refs_1_), channel_id=1, source_target_pairs={{0,8},{1,9},{2,10},{3,11},{4,12},{5,13},{6,14},{7,15},{8,0},{9,1},... | collective-permute-start | bytes 786440 | tf_op jit(solution)/shard_map/ppermute | solution.py:367
  17.9 17.6 %all-to-all-start = ((bf16[8,128,128]{2,1,0:T(8,128)(2,1)}), bf16[8,128,128]{2,1,0:T(8,128)(2,1)S(1)}, u32[]{:S(2)}, u32[]{:S(2)}) async-start(bf16[8,128,128]{2,1,0:T(8,128)(2,1)} %copy.25), calls=%async_computation | async-start | bytes 524288 | tf_op jit(solution)/shard_map/all_to_all | solution.py:542
  23.4 12.1 %collective-permute-start.3 = (bf16[128,1024]{1,0:T(8,128)(2,1)S(1)}, bf16[128,1024]{1,0:T(8,128)(2,1)S(1)}, u32[]{:S(2)}, u32[]{:S(2)}) collective-permute-start(bf16[128,1024]{1,0:T(8,128)(2,1)S(1)} %copy-done.2), channel_id=1, source_target_pairs={{0,4},{1,5},{2,6},{3,7},{4,0},{5,1},{6,2},{7,3},{8,12},{9,13},{10,... | collective-permute-start | bytes 786440 | tf_op jit(solution)/shard_map/ppermute | solution.py:367
  25.4 15.7 %collective-permute-start.4 = (bf16[128,1024]{1,0:T(8,128)(2,1)S(1)}, bf16[128,1024]{1,0:T(8,128)(2,1)S(1)}, u32[]{:S(2)}, u32[]{:S(2)}) collective-permute-start(bf16[128,1024]{1,0:T(8,128)(2,1)S(1)} %collective-permute-done.refs_1_), channel_id=1, source_target_pairs={{0,4},{1,5},{2,6},{3,7},{4,0},{5,1},{6,2},{7,3},{8,12},{9,13},{10,... | collective-permute-start | bytes 786440 | tf_op jit(solution)/shard_map/ppermute | solution.py:367
  25.5 21.2 %collective-permute-start.5 = (bf16[128,1024]{1,0:T(8,128)(2,1)S(1)}, bf16[128,1024]{1,0:T(8,128)(2,1)S(1)}, u32[]{:S(2)}, u32[]{:S(2)}) collective-permute-start(bf16[128,1024]{1,0:T(8,128)(2,1)S(1)} %collective-permute-done.1.refs_2_), channel_id=1, source_target_pairs={{0,4},{1,5},{2,6},{3,7},{4,0},{5,1},{6,2},{7,3},{8,12},{9,13},{10,... | collective-permute-start | bytes 786440 | tf_op jit(solution)/shard_map/ppermute | solution.py:367
  27.5 23.5 %collective-permute-start.6 = (bf16[128,1024]{1,0:T(8,128)(2,1)S(1)}, bf16[128,1024]{1,0:T(8,128)(2,1)S(1)}, u32[]{:S(2)}, u32[]{:S(2)}) collective-permute-start(bf16[128,1024]{1,0:T(8,128)(2,1)S(1)} %collective-permute-done.2.refs_3_), channel_id=1, source_target_pairs={{0,4},{1,5},{2,6},{3,7},{4,0},{5,1},{6,2},{7,3},{8,12},{9,13},{10,... | collective-permute-start | bytes 786440 | tf_op jit(solution)/shard_map/ppermute | solution.py:367
  35.5 15.4 %copy-start.9 = (bf16[8,128,128]{2,1,0:T(8,128)(2,1)}, bf16[8,128,128]{2,1,0:T(8,128)(2,1)S(1)}, u32[]{:S(2)}) copy-start(bf16[8,128,128]{2,1,0:T(8,128)(2,1)S(1)} %all-to-all-done) | copy-start | bytes 786436
  41.1 0.7 copy-start.3
  46.7 0.7 copy-start.5
  50.9 0.7 copy-start.7
  51.6 1.0 copy-start.4
  52.6 0.9 copy-start.6
  53.5 0.9 copy-start.8
  54.5 5.7 %copy-start.13 = (f32[4096]{0:T(1024)S(1)}, f32[4096]{0:T(1024)}, u32[]{:S(2)}) copy-start(f32[4096]{0:T(1024)} %param.12) | copy-start | bytes 49156
  54.5 5.7 %copy-start.12 = (f32[128,8]{0,1:T(8,128)S(1)}, f32[128,8]{0,1:T(8,128)}, u32[]{:S(2)}) copy-start(f32[128,8]{0,1:T(8,128)} %param.14) | copy-start | bytes 12292
  54.5 23.4 %copy-start.14 = (s32[128,8]{0,1:T(8,128)S(1)}, s32[128,8]{0,1:T(8,128)}, u32[]{:S(2)}) copy-start(s32[128,8]{0,1:T(8,128)} %param.13) | copy-start | bytes 12292
  56.6 2.0 collective-permute-start.7
  58.7 8.4 %collective-permute-start.8 = (bf16[2,4,128,128]{3,2,1,0:T(8,128)(2,1)S(1)}, bf16[2,4,128,128]{3,2,1,0:T(8,128)(2,1)S(1)}, u32[]{:S(2)}, u32[]{:S(2)}) collective-permute-start(bf16[2,4,128,128]{3,2,1,0:T(8,128)(2,1)S(1)} %fusion.2), channel_id=1, source_target_pairs={{0,2},{1,3},{2,0},{3,1},{4,6},{5,7},{6,4},{7,5},{8,10},{9,11},{10,... | collective-permute-start | bytes 786440 | tf_op jit(solution)/shard_map/ppermute | solution.py:367
  68.2 5.0 %collective-permute-start.9 = (bf16[1,4,128,128]{3,2,1,0:T(8,128)(2,1)S(1)}, bf16[1,4,128,128]{3,2,1,0:T(8,128)(2,1)S(1)}, u32[]{:S(2)}, u32[]{:S(2)}) collective-permute-start(bf16[1,4,128,128]{3,2,1,0:T(8,128)(2,1)S(1)} %get-tuple-element.56), channel_id=1, source_target_pairs={{0,4},{1,3},{2,6},{3,1},{4,0},{5,7},{6,2},{7,5},{8,12},{9,11},{10,... | collective-permute-start | bytes 393224 | tf_op jit(solution)/shard_map/ppermute | solution.py:367
  69.4 8.5 %collective-permute-start.10 = (bf16[1,4,128,128]{3,2,1,0:T(8,128)(2,1)S(1)}, bf16[1,4,128,128]{3,2,1,0:T(8,128)(2,1)S(1)}, u32[]{:S(2)}, u32[]{:S(2)}) collective-permute-start(bf16[1,4,128,128]{3,2,1,0:T(8,128)(2,1)S(1)} %get-tuple-element.55), channel_id=1, source_target_pairs={{0,16},{1,17},{2,18},{3,19},{4,20},{5,21},{6,22},{7,23},{8,24},{9,... | collective-permute-start | bytes 393224 | tf_op jit(solution)/shard_map/ppermute | solution.py:367
  77.9 4.6 %collective-permute-start.11 = (f32[1,16,128]{2,1,0:T(8,128)S(1)}, f32[1,16,128]{2,1,0:T(8,128)S(1)}, u32[]{:S(2)}, u32[]{:S(2)}) collective-permute-start(f32[1,16,128]{2,1,0:T(8,128)S(1)} %maximum_bitcast_fusion), channel_id=1, source_target_pairs={{0,16},{1,17},{2,18},{3,19},{4,20},{5,21},{6,22},{7,23},{8,24},{9,... | collective-permute-start | bytes 24584 | tf_op jit(solution)/shard_map/ppermute | solution.py:367
  82.5 3.9 %collective-permute-start.12 = (f32[2,16,128]{2,1,0:T(8,128)S(1)}, f32[2,16,128]{2,1,0:T(8,128)S(1)}, u32[]{:S(2)}, u32[]{:S(2)}) collective-permute-start(f32[2,16,128]{2,1,0:T(8,128)S(1)} %pad_maximum_fusion.8), channel_id=1, source_target_pairs={{0,8},{1,9},{2,10},{3,11},{4,12},{5,13},{6,14},{7,15},{8,0},{9,1},... | collective-permute-start | bytes 49160 | tf_op jit(solution)/shard_map/ppermute | solution.py:367
  83.5 13.6 %collective-permute-start.14 = (bf16[2,4,128,128]{3,2,1,0:T(8,128)(2,1)S(1)}, bf16[2,4,128,128]{3,2,1,0:T(8,128)(2,1)S(1)}, u32[]{:S(2)}, u32[]{:S(2)}) collective-permute-start(bf16[2,4,128,128]{3,2,1,0:T(8,128)(2,1)S(1)} %pad_maximum_fusion.4), channel_id=1, source_target_pairs={{0,16},{1,17},{2,18},{3,19},{4,20},{5,21},{6,22},{7,23},{8,24},{9,... | collective-permute-start | bytes 786440 | tf_op jit(solution)/shard_map/ppermute | solution.py:367
  86.5 3.9 %collective-permute-start.13 = (f32[4,16,128]{2,1,0:T(8,128)S(1)}, f32[4,16,128]{2,1,0:T(8,128)S(1)}, u32[]{:S(2)}, u32[]{:S(2)}) collective-permute-start(f32[4,16,128]{2,1,0:T(8,128)S(1)} %pad_maximum_fusion.7), channel_id=1, source_target_pairs={{0,4},{1,5},{2,6},{3,7},{4,0},{5,1},{6,2},{7,3},{8,12},{9,13},{10,... | collective-permute-start | bytes 98312 | tf_op jit(solution)/shard_map/ppermute | solution.py:367
  87.4 11.2 %collective-permute-start.15 = (bf16[2,4,128,128]{3,2,1,0:T(8,128)(2,1)S(1)}, bf16[2,4,128,128]{3,2,1,0:T(8,128)(2,1)S(1)}, u32[]{:S(2)}, u32[]{:S(2)}) collective-permute-start(bf16[2,4,128,128]{3,2,1,0:T(8,128)(2,1)S(1)} %pad_maximum_fusion.5), channel_id=1, source_target_pairs={{0,8},{1,9},{2,10},{3,11},{4,12},{5,13},{6,14},{7,15},{8,0},{9,1},... | collective-permute-start | bytes 786440 | tf_op jit(solution)/shard_map/ppermute | solution.py:367
  98.6 1.3 copy-start.10
  98.6 12.3 %collective-permute-start.16 = (bf16[4,4,128,128]{3,2,1,0:T(8,128)(2,1)S(1)}, bf16[4,4,128,128]{3,2,1,0:T(8,128)(2,1)S(1)}, u32[]{:S(2)}, u32[]{:S(2)}) collective-permute-start(bf16[4,4,128,128]{3,2,1,0:T(8,128)(2,1)S(1)} %pad_maximum_fusion.2), channel_id=1, source_target_pairs={{0,8},{1,9},{2,10},{3,11},{4,12},{5,13},{6,14},{7,15},{8,0},{9,1},... | collective-permute-start | bytes 1572872 | tf_op jit(solution)/shard_map/ppermute | solution.py:367
  99.0 12.0 %collective-permute-start.17 = (bf16[4,4,128,128]{3,2,1,0:T(8,128)(2,1)S(1)}, bf16[4,4,128,128]{3,2,1,0:T(8,128)(2,1)}, u32[]{:S(2)}, u32[]{:S(2)}) collective-permute-start(bf16[4,4,128,128]{3,2,1,0:T(8,128)(2,1)S(1)} %pad_maximum_fusion.3), channel_id=1, source_target_pairs={{0,4},{1,3},{2,6},{3,1},{4,0},{5,7},{6,2},{7,5},{8,12},{9,11},{10,... | collective-permute-start | bytes 1572872 | tf_op jit(solution)/shard_map/ppermute | solution.py:367
  110.9 1.0 copy-start.11
  111.0 14.9 %collective-permute-start.18 = (bf16[8,4,128,128]{3,2,1,0:T(8,128)(2,1)S(1)}, bf16[8,4,128,128]{3,2,1,0:T(8,128)(2,1)S(1)}, u32[]{:S(2)}, u32[]{:S(2)}) collective-permute-start(bf16[8,4,128,128]{3,2,1,0:T(8,128)(2,1)S(1)} %pad_maximum_fusion.rest_0_), channel_id=1, source_target_pairs={{0,2},{1,5},{2,0},{3,7},{4,6},{5,1},{6,4},{7,3},{8,10},{9,13},{10,... | collective-permute-start | bytes 3145736 | tf_op jit(solution)/shard_map/ppermute | solution.py:367
  113.0 24.2 %collective-permute-start.19 = (bf16[8,4,128,128]{3,2,1,0:T(8,128)(2,1)S(1)}, bf16[8,4,128,128]{3,2,1,0:T(8,128)(2,1)}, u32[]{:S(2)}, u32[]{:S(2)}) collective-permute-start(bf16[8,4,128,128]{3,2,1,0:T(8,128)(2,1)S(1)} %pad_maximum_fusion.1.rest_1_), channel_id=1, source_target_pairs={{0,2},{1,5},{2,0},{3,7},{4,6},{5,1},{6,4},{7,3},{8,10},{9,13},{10,... | collective-permute-start | bytes 3145736 | tf_op jit(solution)/shard_map/ppermute | solution.py:367
  114.3 23.7 %collective-permute-start.20 = (bf16[8,4,128,128]{3,2,1,0:T(8,128)(2,1)S(1)}, bf16[8,4,128,128]{3,2,1,0:T(8,128)(2,1)}, u32[]{:S(2)}, u32[]{:S(2)}) collective-permute-start(bf16[8,4,128,128]{3,2,1,0:T(8,128)(2,1)S(1)} %pad_maximum_fusion.rest_0_), channel_id=1, source_target_pairs={{0,1},{1,0},{2,3},{3,2},{4,5},{5,4},{6,7},{7,6},{8,9},{9,8},{10,11... | collective-permute-start | bytes 3145736 | tf_op jit(solution)/shard_map/ppermute | solution.py:367
  114.3 23.7 %collective-permute-start.21 = (bf16[8,4,128,128]{3,2,1,0:T(8,128)(2,1)S(1)}, bf16[8,4,128,128]{3,2,1,0:T(8,128)(2,1)}, u32[]{:S(2)}, u32[]{:S(2)}) collective-permute-start(bf16[8,4,128,128]{3,2,1,0:T(8,128)(2,1)S(1)} %pad_maximum_fusion.1.rest_1_), channel_id=1, source_target_pairs={{0,1},{1,0},{2,3},{3,2},{4,5},{5,4},{6,7},{7,6},{8,9},{9,8},{10,11... | collective-permute-start | bytes 3145736 | tf_op jit(solution)/shard_map/ppermute | solution.py:367
  125.8 12.2 %collective-permute-start.22 = (bf16[8,4,128,128]{3,2,1,0:T(8,128)(2,1)S(1)}, bf16[8,4,128,128]{3,2,1,0:T(8,128)(2,1)}, u32[]{:S(2)}, u32[]{:S(2)}) collective-permute-start(bf16[8,4,128,128]{3,2,1,0:T(8,128)(2,1)S(1)} %collective-permute-done.18.rest_2_), channel_id=1, source_target_pairs={{0,1},{1,0},{2,3},{3,2},{4,5},{5,4},{6,7},{7,6},{8,9},{9,8},{10,11... | collective-permute-start | bytes 3145736 | tf_op jit(solution)/shard_map/ppermute | solution.py:367
  137.2 3.0 %collective-permute-start.23 = (bf16[8,4,128,128]{3,2,1,0:T(8,128)(2,1)}, bf16[8,4,128,128]{3,2,1,0:T(8,128)(2,1)}, u32[]{:S(2)}, u32[]{:S(2)}) collective-permute-start(bf16[8,4,128,128]{3,2,1,0:T(8,128)(2,1)} %collective-permute-done.19.rest_3_), channel_id=1, source_target_pairs={{0,1},{1,0},{2,3},{3,2},{4,5},{5,4},{6,7},{7,6},{8,9},{9,8},{10,11... | collective-permute-start | bytes 3145736 | tf_op jit(solution)/shard_map/ppermute | solution.py:367
  172.3 1.3 copy-start
  183.5 7.2 %collective-permute-start.24 = (bf16[16,128,512]{2,1,0:T(8,128)(2,1)S(1)}, bf16[16,128,512]{2,1,0:T(8,128)(2,1)S(1)}, u32[]{:S(2)}, u32[]{:S(2)}) collective-permute-start(bf16[16,128,512]{2,1,0:T(8,128)(2,1)S(1)} %get-tuple-element.47), channel_id=1, source_target_pairs={{0,1},{1,0},{2,3},{3,2},{4,5},{5,4},{6,7},{7,6},{8,9},{9,8},{10,11... | collective-permute-start | bytes 6291464 | tf_op jit(solution)/shard_map/ppermute | solution.py:367
  183.6 14.0 %collective-permute-start.28 = (bf16[16,128,512]{2,1,0:T(8,128)(2,1)S(1)}, bf16[16,128,512]{2,1,0:T(8,128)(2,1)S(1)}, u32[]{:S(2)}, u32[]{:S(2)}) collective-permute-start(bf16[16,128,512]{2,1,0:T(8,128)(2,1)S(1)} %get-tuple-element.49), channel_id=1, source_target_pairs={{0,1},{1,0},{2,3},{3,2},{4,5},{5,4},{6,7},{7,6},{8,9},{9,8},{10,11... | collective-permute-start | bytes 6291464 | tf_op jit(solution)/shard_map/ppermute | solution.py:367
  191.0 14.9 %collective-permute-start.25 = (bf16[8,128,512]{2,1,0:T(8,128)(2,1)S(1)}, bf16[8,128,512]{2,1,0:T(8,128)(2,1)S(1)}, u32[]{:S(2)}, u32[]{:S(2)}) collective-permute-start(bf16[8,128,512]{2,1,0:T(8,128)(2,1)S(1)} %add_convert_fusion.1), channel_id=1, source_target_pairs={{0,2},{1,5},{2,0},{3,7},{4,6},{5,1},{6,4},{7,3},{8,10},{9,13},{10,... | collective-permute-start | bytes 3145736 | tf_op jit(solution)/shard_map/ppermute | solution.py:367
  205.9 14.8 %collective-permute-start.29 = (bf16[8,128,512]{2,1,0:T(8,128)(2,1)S(1)}, bf16[8,128,512]{2,1,0:T(8,128)(2,1)S(1)}, u32[]{:S(2)}, u32[]{:S(2)}) collective-permute-start(bf16[8,128,512]{2,1,0:T(8,128)(2,1)S(1)} %add_convert_fusion), channel_id=1, source_target_pairs={{0,2},{1,5},{2,0},{3,7},{4,6},{5,1},{6,4},{7,3},{8,10},{9,13},{10,... | collective-permute-start | bytes 3145736 | tf_op jit(solution)/shard_map/ppermute | solution.py:367
  206.1 14.8 %collective-permute-start.26 = (bf16[4,128,512]{2,1,0:T(8,128)(2,1)S(1)}, bf16[4,128,512]{2,1,0:T(8,128)(2,1)S(1)}, u32[]{:S(2)}, u32[]{:S(2)}) collective-permute-start(bf16[4,128,512]{2,1,0:T(8,128)(2,1)S(1)} %add_convert_fusion.3), channel_id=1, source_target_pairs={{0,8},{1,9},{2,10},{3,11},{4,12},{5,13},{6,14},{7,15},{8,0},{9,1},... | collective-permute-start | bytes 1572872 | tf_op jit(solution)/shard_map/ppermute | solution.py:367
  220.9 9.2 %collective-permute-start.30 = (bf16[4,128,512]{2,1,0:T(8,128)(2,1)S(1)}, bf16[4,128,512]{2,1,0:T(8,128)(2,1)S(1)}, u32[]{:S(2)}, u32[]{:S(2)}) collective-permute-start(bf16[4,128,512]{2,1,0:T(8,128)(2,1)S(1)} %add_convert_fusion.2), channel_id=1, source_target_pairs={{0,4},{1,3},{2,6},{3,1},{4,0},{5,7},{6,2},{7,5},{8,12},{9,11},{10,... | collective-permute-start | bytes 1572872 | tf_op jit(solution)/shard_map/ppermute | solution.py:367
  230.3 11.4 %collective-permute-start.31 = (bf16[2,128,512]{2,1,0:T(8,128)(2,1)S(1)}, bf16[2,128,512]{2,1,0:T(8,128)(2,1)S(1)}, u32[]{:S(2)}, u32[]{:S(2)}) collective-permute-start(bf16[2,128,512]{2,1,0:T(8,128)(2,1)S(1)} %add_convert_fusion.4), channel_id=1, source_target_pairs={{0,8},{1,9},{2,10},{3,11},{4,12},{5,13},{6,14},{7,15},{8,0},{9,1},... | collective-permute-start | bytes 786440 | tf_op jit(solution)/shard_map/ppermute | solution.py:367
  230.6 11.2 %collective-permute-start.27 = (bf16[2,128,512]{2,1,0:T(8,128)(2,1)S(1)}, bf16[2,128,512]{2,1,0:T(8,128)(2,1)S(1)}, u32[]{:S(2)}, u32[]{:S(2)}) collective-permute-start(bf16[2,128,512]{2,1,0:T(8,128)(2,1)S(1)} %add_convert_fusion.5), channel_id=1, source_target_pairs={{0,16},{1,17},{2,18},{3,19},{4,20},{5,21},{6,22},{7,23},{8,24},{9,... | collective-permute-start | bytes 786440 | tf_op jit(solution)/shard_map/ppermute | solution.py:367
  241.8 7.5 %collective-permute-start.33 = (bf16[1,128,512]{2,1,0:T(8,128)(2,1)S(1)}, bf16[1,128,512]{2,1,0:T(8,128)(2,1)S(1)}, u32[]{:S(2)}, u32[]{:S(2)}) collective-permute-start(bf16[1,128,512]{2,1,0:T(8,128)(2,1)S(1)} %add_convert_fusion.7), channel_id=1, source_target_pairs={{0,16},{1,17},{2,18},{3,19},{4,20},{5,21},{6,22},{7,23},{8,24},{9,... | collective-permute-start | bytes 393224 | tf_op jit(solution)/shard_map/ppermute | solution.py:367
  241.9 7.4 %collective-permute-start.32 = (bf16[1,128,512]{2,1,0:T(8,128)(2,1)S(1)}, bf16[1,128,512]{2,1,0:T(8,128)(2,1)S(1)}, u32[]{:S(2)}, u32[]{:S(2)}) collective-permute-start(bf16[1,128,512]{2,1,0:T(8,128)(2,1)S(1)} %add_convert_fusion.8), channel_id=1, source_target_pairs={{0,4},{1,3},{2,6},{3,1},{4,0},{5,7},{6,2},{7,5},{8,12},{9,11},{10,... | collective-permute-start | bytes 393224 | tf_op jit(solution)/shard_map/ppermute | solution.py:367

commit v6 on v5

--- a/solution.py
+++ b/solution.py
@@ -13,7 +13,6 @@
 F32 = jnp.float32
 PAIR = 2
 LANES = 128
-HEAD_ORDER = (0, 2, 1, 3)
 
 
 def slot_places(ids, experts, capacity):
@@ -76,13 +75,14 @@
     return places == slot_row
 
 
-def project_kernel(member_ref, head_refs, weight_ref, send_ref, keep_ref):
-    core, x_side, z = member_ref[0], member_ref[1], member_ref[2]
-    here = head_refs[0].shape[0]
-    each = len(HEAD_ORDER)
-    for half in range(2):
+def project_kernel(info_ref, head_refs, weight_ref, send_ref, keep_ref):
+    core, x_side = info_ref[0], info_ref[1]
+    pieces = [ref.at[i] for ref in head_refs for i in range(ref.shape[0])]
+    here = pieces[0].shape[0]
+    each = len(pieces) // 2
+    for part in range(2):
         result = jnp.dot(
-            jnp.concatenate([ref[...] for ref in head_refs[half * each : (half + 1) * each]]),
+            jnp.concatenate([ref[...] for ref in pieces[part * each : (part + 1) * each]]),
             weight_ref[...],
             preferred_element_type=F32,
         ).astype(BF16)
@@ -93,20 +93,21 @@
                 for out_ref, wanted in ((keep_ref, core == to_core), (send_ref, core != to_core)):
 
                     @pl.when(wanted)
-                    def _(out_ref=out_ref, x_kept=x_kept, start=start, half=half, result=result):
-                        for piece, z_bits in enumerate(HEAD_ORDER):
-                            out_ref[x_kept, half, z ^ z_bits] = result[
+                    def _(out_ref=out_ref, x_kept=x_kept, start=start, part=part, result=result):
+                        for piece in range(each):
+                            out_ref[x_kept, info_ref[2 + part * each + piece]] = result[
                                 piece * here : (piece + 1) * here, start : start + LANES
                             ]
 
 
-def project(member_info, pieces, out_proj):
-    here = pieces[0].shape[0]
-    out = jax.ShapeDtypeStruct((2, 2, len(HEAD_ORDER), here, LANES), BF16)
+def project(info, pieces, out_proj):
+    here = pieces[0].shape[1]
+    groups = sum(piece.shape[0] for piece in pieces)
+    out = jax.ShapeDtypeStruct((2, groups, here, LANES), BF16)
     vmem = pl.BlockSpec(memory_space=pltpu.VMEM)
 
-    def kernel(member_ref, *refs):
-        project_kernel(member_ref, refs[: len(pieces)], *refs[len(pieces) :])
+    def kernel(info_ref, *refs):
+        project_kernel(info_ref, refs[: len(pieces)], *refs[len(pieces) :])
 
     return pl.pallas_call(
         kernel,
@@ -115,12 +116,12 @@
         out_shape=[out, out],
         compiler_params=pltpu.CompilerParams(vmem_limit_bytes=24 * 1024 * 1024),
         cost_estimate=pl.CostEstimate(
-            flops=2 * len(pieces) * here * out_proj.size,
-            bytes_accessed=2 * (out_proj.size + 2 * len(pieces) * pieces[0].size),
+            flops=2 * groups * here * out_proj.size,
+            bytes_accessed=2 * (out_proj.size + 2 * groups * pieces[0][0].size),
             transcendentals=0,
         ),
         name="project",
-    )(member_info, *pieces, out_proj)
+    )(info, *pieces, out_proj)
 
 
 def other_place(place):
@@ -283,7 +284,7 @@
             jax.ShapeDtypeStruct((parts, 2 * here, experts * rows), BF16),
         ],
         compiler_params=pltpu.CompilerParams(
-            vmem_limit_bytes=44 * 1024 * 1024, dimension_semantics=("arbitrary",)
+            vmem_limit_bytes=36 * 1024 * 1024, dimension_semantics=("arbitrary",)
         ),
         cost_estimate=pl.CostEstimate(
             flops=2 * experts * parts * rows * width * 2 * hidden_units,
@@ -437,21 +438,45 @@
     exchange(0, 1)
     exchange(1, 1, came[0, 1])
     exchange(0, 2)
-    exchange(1, 2)
+    exchange(1, 2, came[0, 2])
     exchange(0, 3, came[1, 2])
     exchange(1, 3)
     return [total_of([term[0] for term in chunk]) for chunk in terms]
 
 
-def route_tables(route_ids, route_weights, group, experts, groups):
-    here, top = route_ids.shape
+HEAD_STAGES = (
+    lambda core: ZHIGH if core else Y,
+    lambda core: ZLOW if core else ZHIGH,
+    lambda core: Y if core else ZLOW,
+)
+
+
+def head_bits(place, core):
+    bits = [(place >> stage) & 1 for stage in range(3)]
+    return jnp.where(
+        core == 0,
+        bits[0] | (bits[1] << 2) | (bits[2] << 1),
+        (bits[0] << 2) | (bits[1] << 1) | bits[2],
+    )
+
+
+def gather_heads(heads):
+    heads = heads[None]
+    for number, bits_of in enumerate(HEAD_STAGES):
+        came = flip(heads, bits_of)
+        if number == len(HEAD_STAGES) - 1:
+            return [heads, came]
+        heads = jnp.concatenate([heads, came], axis=0)
+
+
+def route_table(route_ids, route_weights):
     shares = route_weights / jnp.sum(route_weights, axis=-1, keepdims=True)
-    table = jnp.concatenate([route_ids.astype(F32), shares], axis=1).T[None]
-    for bits in (ZHIGH, ZLOW, Y):
-        table = jnp.concatenate([table, flip(table, lambda core, bits=bits: bits)], axis=0)
-    apart = own_order(groups, group) ^ group
-    place = (apart >> 2) | (apart & 2) | ((apart & 1) << 2)
-    table = jnp.take(table, place, axis=0, mode="clip")
+    return jnp.concatenate([route_ids.astype(F32), shares], axis=1).T
+
+
+def own_routes(table, group, experts):
+    groups, both, here = table.shape
+    top = both // 2
     own = group * experts + jnp.arange(experts, dtype=jnp.int32)
     ids = table[:, :top, :].astype(jnp.int32)
     match = ids[None] == own[:, None, None, None]
@@ -487,7 +512,7 @@
     return jnp.concatenate([feature, swapped, jnp.stack([member, device >> 3])])
 
 
-def gather_blocks(first, second, make_beside):
+def gather_blocks(first, second, make_table, own_tables):
     def along(bits, block):
         return flip(block, lambda core: bits)
 
@@ -496,33 +521,27 @@
 
     first_last = flip(first, last_axis)
     second_high = along(ZHIGH, second)
-    second = joined(second, second_high)
+    second, _ = after(joined(second, second_high), first_last)
     second_low = along(ZLOW, second)
     first, _ = after(joined(first, first_last), second_high)
-    beside = make_beside((first_last, second_high))
     first_high = along(ZHIGH, first)
+    table = make_table(second_high)
+    for bits in (ZHIGH, ZLOW, Y):
+        table = joined(table, along(bits, table))
     second = joined(second, second_low)
     second_last = flip(second, last_axis)
-    first, _ = after(joined(first, first_high), second_low)
+    first = joined(first, first_high)
     first_low = along(ZLOW, first)
     second = joined(second, second_last)
     second_first = flip(second, first_axis)
-    first, _ = after(joined(first, first_low), (second_last, beside))
+    first_low, _ = after(first_low, second)
+    beside = own_tables(table)
+    first, (second_first, beside) = after(joined(first, first_low), (second_first, beside))
     first_first = flip(first, first_axis)
     return [
         [block, came, along(CORE, block), along(CORE, came)]
         for block, came in ((first, first_first), (second, second_first))
     ] + [beside]
-
-
-def gather_heads(heads):
-    def along(bits, piece):
-        return flip(piece, lambda core: bits)
-
-    high = along(ZHIGH, heads)
-    low = along(ZLOW, heads)
-    own = [heads, high, low, along(ZLOW, high)]
-    return own + [along(Y, piece) for piece in own]
 
 
 def per_device_tokens(
@@ -534,7 +553,7 @@
     here, width = residual.shape
     experts = w_gate.shape[0]
     rows = -(-PAIR * CAP // 16) * 16
-    x_side, core, y_side, z = member >> 1, member & 1, group & 1, group >> 1
+    x_side, core, y_side = member >> 1, member & 1, group & 1
 
     own_cols = lax.dynamic_index_in_dim(
         residual.reshape(here, groups, members, LANES), member, 2, keepdims=False
@@ -546,22 +565,34 @@
         norm_gain.reshape(groups * members, LANES), device, 0, keepdims=False
     )
 
-    member_info = jnp.stack([core, x_side, z])
-    pieces, moved = after(gather_heads(attn_heads), moved)
-    send, keep = project(member_info, pieces, out_proj)
+    pieces = gather_heads(attn_heads)
+    numbers = jnp.arange(groups, dtype=jnp.int32)
+    arrival = (head_bits(numbers, core) ^ group) ^ y_side
+    info = jnp.concatenate(
+        [jnp.stack([core, x_side]), ((arrival & 1) << 2) | (arrival >> 1)]
+    )
+    info, moved = after(info, moved)
+    send, keep = project(info, pieces, out_proj)
     came = flip(send, lambda c: CORE)
     from_x = flip(total_of([keep[0], came[0]]).astype(BF16), lambda c: X)
     starts = []
+    each = groups // 2
     for half in range(2):
+        window = slice(half * each, (half + 1) * each)
         hidden = lax.dynamic_index_in_dim(moved, y_side ^ half, 1, keepdims=False).astype(F32)
-        hidden = hidden + total_of([keep[1, half], came[1, half], from_x[half]])
+        hidden = hidden + total_of([keep[1, window], came[1, window], from_x[window]])
         starts.append((hidden * gain).astype(BF16)[None])
 
-    def tables(earlier):
+    def make_table(earlier):
         ids, _ = after(route_ids, earlier)
-        return route_tables(ids, route_weights, group, experts, groups)
-
-    own_x, other_x, (slots, weights) = gather_blocks(*starts, tables)
+        return route_table(ids, route_weights)[None]
+
+    def own_tables(table):
+        apart = own_order(groups, group) ^ group
+        order = (apart >> 2) | (apart & 2) | ((apart & 1) << 2)
+        return own_routes(jnp.take(table, order, axis=0, mode="clip"), group, experts)
+
+    own_x, other_x, (slots, weights) = gather_blocks(*starts, make_table, own_tables)
     x = [piece for pair in zip(own_x, other_x) for piece in pair]
     invgain = (1.0 / norm_gain).reshape(groups * members, LANES)
     act, own_hidden, spread = gate_up(
@@ -584,9 +615,10 @@
     came = [flip(piece, lambda c: CORE) for piece in other]
 
     def terms_of(chunk, earlier):
-        ready = act if earlier is None else after(act, earlier)[0]
         place = columns_of(core, chunk, chunks, ORDERS[chunk : chunk + 1])
-        (kept,) = down(place, spread, ready, w_down, rows, groups, chunk_cols, 1)
+        if earlier is not None:
+            place, _ = after(place, earlier)
+        (kept,) = down(place, spread, act, w_down, rows, groups, chunk_cols, 1)
         return [kept, came[chunk]]
 
     sums = reduce_chunks([functools.partial(terms_of, chunk) for chunk in range(chunks)])

time: 252 us -> 234 us (0.929)
  waiting for transfers between devices: 142 us -> 130 us
  local copies, waits for them, and re-layouts: 10.6 us -> 3.79 us
    ppermute x34 -> x30, waiting for transfers between devices: 142 us -> 118 us  [flip(): return lax.ppermute(array, ('expert', 'tensor'), pairs)]
    all_to_all x1, waiting for transfers between devices: 0.01 us -> 12.7 us  [per_device_tokens(): lax.all_to_all(jnp.transpose(own_cols, (1, 0, 2)), 'expert', split_axis=0...]
    unnamed x32 -> x14, local copies, waits for them, and re-layouts: 8.61 us -> 1.75 us
    ppermute x34 -> x30, starting transfers between devices: 28.7 us -> 29.4 us  [flip(): return lax.ppermute(array, ('expert', 'tensor'), pairs)]
  transfers between devices with their start and end apart: 35 -> 31, of which waited for: 22 -> 19; matrix products, arithmetic and copies ran while one was open for 3% -> 3% of each run, Pallas kernels for 5% -> 6%
where the time goes in v6:
time: 234 us
  waiting for transfers between devices  130 us (56%)
  Pallas kernels  56.7 us (24%)
  starting transfers between devices  35.1 us (15%)
  other arithmetic  7.07 us (3%)
  local copies, waits for them, and re-layouts  3.79 us (2%)
    ppermute x30, waiting for transfers between devices, flip(): return lax.ppermute(array, ('expert', 'tensor'), pairs)  118 us
    pallas_call x1, Pallas kernels, gate_up(): pl.pallas_call(kernel, grid_spec=pltpu.PrefetchScalarGridSpec(num_scalar_...  31.1 us
    ppermute x30, starting transfers between devices, flip(): return lax.ppermute(array, ('expert', 'tensor'), pairs)  29.4 us
    pallas_call x3, Pallas kernels, down(): pl.pallas_call(functools.partial(down_kernel, rows), grid_spec=pltpu.Pref...  22.8 us
    all_to_all x1, waiting for transfers between devices, per_device_tokens(): lax.all_to_all(jnp.transpose(own_cols, (1, 0, 2)), 'expert', split_axis=0...  12.7 us
    all_to_all x1, starting transfers between devices, per_device_tokens(): lax.all_to_all(jnp.transpose(own_cols, (1, 0, 2)), 'expert', split_axis=0...  5.73 us
  transfers between devices with their start and end apart: 31, of which 19 were waited for; matrix products, arithmetic and copies ran while one was open for 3% of the time, Pallas kernels for 6%

profile of v6, /device:TPU:0, one launch (start us, length us, event | category | flops | bytes accessed | tf_op | source)
XLA Modules:
  0.0 233.5 jit_solution(2499057745669810478)
XLA Ops:
  0.0 3.0 %collective-permute-start = (bf16[1,128,1024]{2,1,0:T(8,128)(2,1)}, bf16[1,128,1024]{2,1,0:T(8,128)(2,1)S(1)}, u32[]{:S(2)}, u32[]{:S(2)}) collective-permute-start(bf16[1,128,1024]{2,1,0:T(8,128)(2,1)} %bitcast.62), channel_id=1, source_target_pairs={{0,4},{1,17},{2,6},{3,19},{4,0},{5,21},{6,2},{7,23},{8,12},{9,25},... | collective-permute-start | bytes 786440 | tf_op jit(solution)/shard_map/ppermute | solution.py:368
  3.0 4.6 %collective-permute-done = bf16[1,128,1024]{2,1,0:T(8,128)(2,1)S(1)} collective-permute-done((bf16[1,128,1024]{2,1,0:T(8,128)(2,1)}, bf16[1,128,1024]{2,1,0:T(8,128)(2,1)S(1)}, u32[]{:S(2)}, u32[]{:S(2)}) %collective-permute-start) | collective-permute-done | bytes 262176 | tf_op jit(solution)/shard_map/ppermute | solution.py:368
  7.5 1.0 pad_maximum_fusion.2
  8.5 3.2 %collective-permute-start.1 = (bf16[2,128,1024]{2,1,0:T(8,128)(2,1)S(1)}, bf16[2,128,1024]{2,1,0:T(8,128)(2,1)S(1)}, u32[]{:S(2)}, u32[]{:S(2)}) collective-permute-start(bf16[2,128,1024]{2,1,0:T(8,128)(2,1)S(1)} %pad_maximum_fusion.2), channel_id=1, source_target_pairs={{0,16},{1,9},{2,18},{3,11},{4,20},{5,13},{6,22},{7,15},{8,24},{9,1... | collective-permute-start | bytes 1572872 | tf_op jit(solution)/shard_map/ppermute | solution.py:368
  11.7 12.6 %collective-permute-done.1 = bf16[2,128,1024]{2,1,0:T(8,128)(2,1)S(1)} collective-permute-done((bf16[2,128,1024]{2,1,0:T(8,128)(2,1)S(1)}, bf16[2,128,1024]{2,1,0:T(8,128)(2,1)S(1)}, u32[]{:S(2)}, u32[]{:S(2)}) %collective-permute-start.1) | collective-permute-done | bytes 524320 | tf_op jit(solution)/shard_map/ppermute | solution.py:368
  24.3 1.1 pad_maximum_fusion.refs_0_
  25.4 1.2 collective-permute-start.2
  26.6 1.6 copy.23
  28.2 0.9 copy.25
  29.1 5.7 %all-to-all-start = ((bf16[8,128,128]{2,1,0:T(8,128)(2,1)}), bf16[8,128,128]{2,1,0:T(8,128)(2,1)S(1)}, u32[]{:S(2)}, u32[]{:S(2)}) async-start(bf16[8,128,128]{2,1,0:T(8,128)(2,1)} %copy.25), calls=%async_computation | async-start | bytes 524288 | tf_op jit(solution)/shard_map/all_to_all | solution.py:561
  34.9 12.7 %all-to-all-done = bf16[8,128,128]{2,1,0:T(8,128)(2,1)S(1)} async-done(((bf16[8,128,128]{2,1,0:T(8,128)(2,1)}), bf16[8,128,128]{2,1,0:T(8,128)(2,1)S(1)}, u32[]{:S(2)}, u32[]{:S(2)}) %all-to-all-start) | async-done | bytes 262176 | tf_op jit(solution)/shard_map/all_to_all | solution.py:561
  47.6 2.8 %project.1 = (bf16[2,8,128,128]{3,2,1,0:T(8,128)(2,1)S(1)}, bf16[2,8,128,128]{3,2,1,0:T(8,128)(2,1)S(1)}) custom-call(s32[10]{0:T(128)S(1)} %pad_add_fusion.1.info_ref, bf16[4,128,1024]{2,1,0:T(8,128)(2,1)S(1)} %pad_maximum_fusion.refs_0_, bf16[4,128,1024]{2,1,0:T(8,128)(2,1)} %collective-permute-done.2.refs_1_, bf16[1024,512]{1,0:T(8,128)(2,1)S(1)} %copy-done), custom_call_target="tpu_custom_call" | custom-call | flops 1073741824 | bytes 5242880 | tf_op jit(solution)/shard_map/project/pallas_call | solution.py:112
  50.5 1.9 collective-permute-done.3
  52.5 1.6 collective-permute-start.4
  54.1 6.8 %collective-permute-done.4 = bf16[8,128,128]{2,1,0:T(8,128)(2,1)S(1)} collective-permute-done((bf16[8,128,128]{2,1,0:T(8,128)(2,1)S(1)}, bf16[8,128,128]{2,1,0:T(8,128)(2,1)S(1)}, u32[]{:S(2)}, u32[]{:S(2)}) %collective-permute-start.4) | collective-permute-done | bytes 262176 | tf_op jit(solution)/shard_map/ppermute | solution.py:368
  60.9 0.2 fusion.8
  61.1 0.3 collective-permute-start.6
  61.3 0.4 collective-permute-start.5
  61.8 7.2 %collective-permute-done.6 = bf16[1,4,128,128]{3,2,1,0:T(8,128)(2,1)S(1)} collective-permute-done((bf16[1,4,128,128]{3,2,1,0:T(8,128)(2,1)S(1)}, bf16[1,4,128,128]{3,2,1,0:T(8,128)(2,1)S(1)}, u32[]{:S(2)}, u32[]{:S(2)}) %collective-permute-start.6) | collective-permute-done | bytes 131104 | tf_op jit(solution)/shard_map/ppermute | solution.py:368
  69.1 2.4 %collective-permute-start.12 = (f32[1,16,128]{2,1,0:T(8,128)S(1)}, f32[1,16,128]{2,1,0:T(8,128)S(1)}, u32[]{:S(2)}, u32[]{:S(2)}) collective-permute-start(f32[1,16,128]{2,1,0:T(8,128)S(1)} %maximum_bitcast_fusion), channel_id=1, source_target_pairs={{0,16},{1,17},{2,18},{3,19},{4,20},{5,21},{6,22},{7,23},{8,24},{9,... | collective-permute-start | bytes 24584 | tf_op jit(solution)/shard_map/ppermute | solution.py:368
  71.5 3.6 %collective-permute-done.12 = f32[1,16,128]{2,1,0:T(8,128)S(1)} collective-permute-done((f32[1,16,128]{2,1,0:T(8,128)S(1)}, f32[1,16,128]{2,1,0:T(8,128)S(1)}, u32[]{:S(2)}, u32[]{:S(2)}) %collective-permute-start.12) | collective-permute-done | bytes 8224 | tf_op jit(solution)/shard_map/ppermute | solution.py:368
  75.1 2.9 %collective-permute-start.13 = (f32[2,16,128]{2,1,0:T(8,128)S(1)}, f32[2,16,128]{2,1,0:T(8,128)S(1)}, u32[]{:S(2)}, u32[]{:S(2)}) collective-permute-start(f32[2,16,128]{2,1,0:T(8,128)S(1)} %pad_maximum_fusion.9), channel_id=1, source_target_pairs={{0,8},{1,9},{2,10},{3,11},{4,12},{5,13},{6,14},{7,15},{8,0},{9,1},... | collective-permute-start | bytes 49160 | tf_op jit(solution)/shard_map/ppermute | solution.py:368
  78.0 0.3 collective-permute-start.10
  78.4 1.3 collective-permute-done.13
  79.7 0.5 collective-permute-start.14
  80.3 2.1 collective-permute-start.7
  82.3 5.3 %collective-permute-done.14 = f32[4,16,128]{2,1,0:T(8,128)S(1)} collective-permute-done((f32[4,16,128]{2,1,0:T(8,128)S(1)}, f32[4,16,128]{2,1,0:T(8,128)S(1)}, u32[]{:S(2)}, u32[]{:S(2)}) %collective-permute-start.14) | collective-permute-done | bytes 32800 | tf_op jit(solution)/shard_map/ppermute | solution.py:368
  87.6 0.6 gather_fusion
  88.3 1.6 collective-permute-start.11
  89.9 3.2 %collective-permute-done.7 = bf16[2,4,128,128]{3,2,1,0:T(8,128)(2,1)S(1)} collective-permute-done((bf16[2,4,128,128]{3,2,1,0:T(8,128)(2,1)S(1)}, bf16[2,4,128,128]{3,2,1,0:T(8,128)(2,1)S(1)}, u32[]{:S(2)}, u32[]{:S(2)}) %collective-permute-start.7) | collective-permute-done | bytes 262176 | tf_op jit(solution)/shard_map/ppermute | solution.py:368
  93.2 0.2 compare_reduce_fusion
  93.4 0.2 convolution_convert_fusion
  93.6 0.1 fusion.1
  93.8 12.4 %collective-permute-done.8 = bf16[4,4,128,128]{3,2,1,0:T(8,128)(2,1)} collective-permute-done((bf16[4,4,128,128]{3,2,1,0:T(8,128)(2,1)S(1)}, bf16[4,4,128,128]{3,2,1,0:T(8,128)(2,1)}, u32[]{:S(2)}, u32[]{:S(2)}) %collective-permute-start.8) | collective-permute-done | bytes 524320 | tf_op jit(solution)/shard_map/ppermute | solution.py:368
  106.2 1.2 pad_maximum_fusion.1.rest_0_
  107.4 0.9 collective-permute-start.15
  108.4 0.5 collective-permute-start.16
  108.9 13.5 %collective-permute-done.15.rest_2_ = bf16[8,4,128,128]{3,2,1,0:T(8,128)(2,1)} collective-permute-done((bf16[8,4,128,128]{3,2,1,0:T(8,128)(2,1)S(1)}, bf16[8,4,128,128]{3,2,1,0:T(8,128)(2,1)}, u32[]{:S(2)}, u32[]{:S(2)}) %collective-permute-start.15) | collective-permute-done | bytes 1048608 | tf_op jit(solution)/shard_map/ppermute | solution.py:368
  123.2 2.2 collective-permute-done.18.rest_6_
  125.4 31.1 %gate_up.1 = (bf16[8,192,384]{2,1,0:T(8,128)(2,1)S(1)}, f32[128,1024]{1,0:T(8,128)S(1)}, bf16[4,256,384]{2,1,0:T(8,128)(2,1)S(1)}) custom-call(s32[66]{0:T(128)S(1)} %pad_add_fusion.info_ref, s32[8,1024]{1,0:T(8,128)S(1)} %bitcast_select_fusion.slot_ref, f32[8,1024]{1,0:T(8,128)S(1)} %bitcast.59, f32[32,128]{1,0:T(8,128)S(1)} %divide_bitcast_fusion.invgain_ref, ...), custom_call_target="tpu_custom_call" | custom-call | flops 9663676416 | bytes 58720256 | tf_op jit(solution)/shard_map/gate_up/pallas_call | solution.py:261
  156.5 9.9 %down_mix.4 = (bf16[16,128,512]{2,1,0:T(8,128)(2,1)S(1)}, bf16[16,128,512]{2,1,0:T(8,128)(2,1)S(1)}) custom-call(s32[34]{0:T(128)S(1)} %pad_add_fusion.3.place_ref, bf16[4,256,384]{2,1,0:T(8,128)(2,1)S(1)} %get-tuple-element.40.spread_ref, bf16[8,192,384]{2,1,0:T(8,128)(2,1)S(1)} %get-tuple-element.41.act_ref, bf16[8,384,4096]{2,1,0:T(8,128)(2,1)} %wd1_ref.5, ...), custom_call_target="tpu_custom_call" | custom-call | flops 4831838208 | bytes 16777216 | tf_op jit(solution)/shard_map/down_mix/pallas_call | solution.py:337
  166.5 0.5 collective-permute-start.24
  167.2 6.4 %down_mix.3 = bf16[16,128,512]{2,1,0:T(8,128)(2,1)S(1)} custom-call(s32[18]{0:T(128)S(1)} %pad_add_fusion.2.place_ref, bf16[4,256,384]{2,1,0:T(8,128)(2,1)S(1)} %get-tuple-element.40.spread_ref, bf16[8,192,384]{2,1,0:T(8,128)(2,1)S(1)} %get-tuple-element.41.act_ref, bf16[8,384,4096]{2,1,0:T(8,128)(2,1)} %wd1_ref.5, bf16[8,384,4096]{2,1,0:T(8,128)(2,1)} %wd1_ref.5), custom_call_target="tpu_custom_call" | custom-call | flops 2415919104 | bytes 8388608 | tf_op jit(solution)/shard_map/down_mix/pallas_call | solution.py:337
  173.6 0.3 add_convert_fusion.1
  173.9 0.9 collective-permute-start.21
  174.9 6.4 %down_mix.5 = bf16[16,128,512]{2,1,0:T(8,128)(2,1)S(1)} custom-call(s32[18]{0:T(128)S(1)} %pad_add_fusion.4.place_ref, bf16[4,256,384]{2,1,0:T(8,128)(2,1)S(1)} %get-tuple-element.40.spread_ref, bf16[8,192,384]{2,1,0:T(8,128)(2,1)S(1)} %get-tuple-element.41.act_ref, bf16[8,384,4096]{2,1,0:T(8,128)(2,1)} %wd1_ref.5, bf16[8,384,4096]{2,1,0:T(8,128)(2,1)} %wd1_ref.5), custom_call_target="tpu_custom_call" | custom-call | flops 2415919104 | bytes 8388608 | tf_op jit(solution)/shard_map/down_mix/pallas_call | solution.py:337
  181.3 0.3 add_convert_fusion
  181.7 7.1 %collective-permute-done.21 = bf16[8,128,512]{2,1,0:T(8,128)(2,1)S(1)} collective-permute-done((bf16[8,128,512]{2,1,0:T(8,128)(2,1)S(1)}, bf16[8,128,512]{2,1,0:T(8,128)(2,1)S(1)}, u32[]{:S(2)}, u32[]{:S(2)}) %collective-permute-start.21) | collective-permute-done | bytes 1048608 | tf_op jit(solution)/shard_map/ppermute | solution.py:368
  188.8 0.8 collective-permute-start.25
  189.6 0.2 add_convert_fusion.3
  189.8 0.3 collective-permute-start.22
  190.1 13.5 %collective-permute-done.25 = bf16[8,128,512]{2,1,0:T(8,128)(2,1)S(1)} collective-permute-done((bf16[8,128,512]{2,1,0:T(8,128)(2,1)S(1)}, bf16[8,128,512]{2,1,0:T(8,128)(2,1)S(1)}, u32[]{:S(2)}, u32[]{:S(2)}) %collective-permute-start.25) | collective-permute-done | bytes 1048608 | tf_op jit(solution)/shard_map/ppermute | solution.py:368
  203.6 0.2 add_convert_fusion.2
  203.8 1.8 collective-permute-start.26
  205.6 0.1 add_convert_fusion.5
  205.7 0.7 collective-permute-start.23
  206.5 6.6 %collective-permute-done.26 = bf16[4,128,512]{2,1,0:T(8,128)(2,1)S(1)} collective-permute-done((bf16[4,128,512]{2,1,0:T(8,128)(2,1)S(1)}, bf16[4,128,512]{2,1,0:T(8,128)(2,1)S(1)}, u32[]{:S(2)}, u32[]{:S(2)}) %collective-permute-start.26) | collective-permute-done | bytes 524320 | tf_op jit(solution)/shard_map/ppermute | solution.py:368
  213.1 0.1 add_convert_fusion.4
  213.2 4.3 %collective-permute-done.23 = bf16[2,128,512]{2,1,0:T(8,128)(2,1)S(1)} collective-permute-done((bf16[2,128,512]{2,1,0:T(8,128)(2,1)S(1)}, bf16[2,128,512]{2,1,0:T(8,128)(2,1)S(1)}, u32[]{:S(2)}, u32[]{:S(2)}) %collective-permute-start.23) | collective-permute-done | bytes 262176 | tf_op jit(solution)/shard_map/ppermute | solution.py:368
  217.5 7.4 %collective-permute-done.27 = bf16[2,128,512]{2,1,0:T(8,128)(2,1)S(1)} collective-permute-done((bf16[2,128,512]{2,1,0:T(8,128)(2,1)S(1)}, bf16[2,128,512]{2,1,0:T(8,128)(2,1)S(1)}, u32[]{:S(2)}, u32[]{:S(2)}) %collective-permute-start.27) | collective-permute-done | bytes 262176 | tf_op jit(solution)/shard_map/ppermute | solution.py:368
  225.1 0.6 collective-permute-start.29
  225.7 2.8 %collective-permute-start.28 = (bf16[1,128,512]{2,1,0:T(8,128)(2,1)S(1)}, bf16[1,128,512]{2,1,0:T(8,128)(2,1)S(1)}, u32[]{:S(2)}, u32[]{:S(2)}) collective-permute-start(bf16[1,128,512]{2,1,0:T(8,128)(2,1)S(1)} %add_convert_fusion.8), channel_id=1, source_target_pairs={{0,4},{1,3},{2,6},{3,1},{4,0},{5,7},{6,2},{7,5},{8,12},{9,11},{10,... | collective-permute-start | bytes 393224 | tf_op jit(solution)/shard_map/ppermute | solution.py:368
  228.5 4.1 %collective-permute-done.29 = bf16[1,128,512]{2,1,0:T(8,128)(2,1)S(1)} collective-permute-done((bf16[1,128,512]{2,1,0:T(8,128)(2,1)S(1)}, bf16[1,128,512]{2,1,0:T(8,128)(2,1)S(1)}, u32[]{:S(2)}, u32[]{:S(2)}) %collective-permute-start.29) | collective-permute-done | bytes 131104 | tf_op jit(solution)/shard_map/ppermute | solution.py:368
  232.7 0.8 fusion
  (81 shorter events, 2.5 us)
Async XLA Ops:
  0.0 7.5 %collective-permute-start = (bf16[1,128,1024]{2,1,0:T(8,128)(2,1)}, bf16[1,128,1024]{2,1,0:T(8,128)(2,1)S(1)}, u32[]{:S(2)}, u32[]{:S(2)}) collective-permute-start(bf16[1,128,1024]{2,1,0:T(8,128)(2,1)} %bitcast.62), channel_id=1, source_target_pairs={{0,4},{1,17},{2,6},{3,19},{4,0},{5,21},{6,2},{7,23},{8,12},{9,25},... | collective-permute-start | bytes 786440 | tf_op jit(solution)/shard_map/ppermute | solution.py:368
  8.5 15.8 %collective-permute-start.1 = (bf16[2,128,1024]{2,1,0:T(8,128)(2,1)S(1)}, bf16[2,128,1024]{2,1,0:T(8,128)(2,1)S(1)}, u32[]{:S(2)}, u32[]{:S(2)}) collective-permute-start(bf16[2,128,1024]{2,1,0:T(8,128)(2,1)S(1)} %pad_maximum_fusion.2), channel_id=1, source_target_pairs={{0,16},{1,9},{2,18},{3,11},{4,20},{5,13},{6,22},{7,15},{8,24},{9,1... | collective-permute-start | bytes 1572872 | tf_op jit(solution)/shard_map/ppermute | solution.py:368
  25.4 22.2 %copy-start = (bf16[1024,512]{1,0:T(8,128)(2,1)S(1)}, bf16[1024,512]{1,0:T(8,128)(2,1)}, u32[]{:S(2)}) copy-start(bf16[1024,512]{1,0:T(8,128)(2,1)} %refs_2_.1) | copy-start | bytes 3145732
  25.4 22.2 %collective-permute-start.2 = (bf16[4,128,1024]{2,1,0:T(8,128)(2,1)S(1)}, bf16[4,128,1024]{2,1,0:T(8,128)(2,1)}, u32[]{:S(2)}, u32[]{:S(2)}) collective-permute-start(bf16[4,128,1024]{2,1,0:T(8,128)(2,1)S(1)} %pad_maximum_fusion.refs_0_), channel_id=1, source_target_pairs={{0,8},{1,5},{2,10},{3,7},{4,12},{5,1},{6,14},{7,3},{8,0},{9,13},{1... | collective-permute-start | bytes 3145736 | tf_op jit(solution)/shard_map/ppermute | solution.py:368
  29.1 18.5 %all-to-all-start = ((bf16[8,128,128]{2,1,0:T(8,128)(2,1)}), bf16[8,128,128]{2,1,0:T(8,128)(2,1)S(1)}, u32[]{:S(2)}, u32[]{:S(2)}) async-start(bf16[8,128,128]{2,1,0:T(8,128)(2,1)} %copy.25), calls=%async_computation | async-start | bytes 524288 | tf_op jit(solution)/shard_map/all_to_all | solution.py:561
  47.6 6.5 %copy-start.3 = (f32[4096]{0:T(1024)S(1)}, f32[4096]{0:T(1024)}, u32[]{:S(2)}) copy-start(f32[4096]{0:T(1024)} %param.12) | copy-start | bytes 49156
  47.6 6.5 %copy-start.2 = (f32[128,8]{0,1:T(8,128)S(1)}, f32[128,8]{0,1:T(8,128)}, u32[]{:S(2)}) copy-start(f32[128,8]{0,1:T(8,128)} %param.14) | copy-start | bytes 12292
  50.4 18.6 %copy-start.4 = (s32[128,8]{0,1:T(8,128)S(1)}, s32[128,8]{0,1:T(8,128)}, u32[]{:S(2)}) copy-start(s32[128,8]{0,1:T(8,128)} %param.13) | copy-start | bytes 12292
  50.4 2.0 collective-permute-start.3
  52.5 8.4 %collective-permute-start.4 = (bf16[8,128,128]{2,1,0:T(8,128)(2,1)S(1)}, bf16[8,128,128]{2,1,0:T(8,128)(2,1)S(1)}, u32[]{:S(2)}, u32[]{:S(2)}) collective-permute-start(bf16[8,128,128]{2,1,0:T(8,128)(2,1)S(1)} %fusion.2), channel_id=1, source_target_pairs={{0,2},{1,3},{2,0},{3,1},{4,6},{5,7},{6,4},{7,5},{8,10},{9,11},{10,... | collective-permute-start | bytes 786440 | tf_op jit(solution)/shard_map/ppermute | solution.py:368
  61.1 7.9 %collective-permute-start.6 = (bf16[1,4,128,128]{3,2,1,0:T(8,128)(2,1)S(1)}, bf16[1,4,128,128]{3,2,1,0:T(8,128)(2,1)S(1)}, u32[]{:S(2)}, u32[]{:S(2)}) collective-permute-start(bf16[1,4,128,128]{3,2,1,0:T(8,128)(2,1)S(1)} %get-tuple-element.51), channel_id=1, source_target_pairs={{0,16},{1,17},{2,18},{3,19},{4,20},{5,21},{6,22},{7,23},{8,24},{9,... | collective-permute-start | bytes 393224 | tf_op jit(solution)/shard_map/ppermute | solution.py:368
  61.3 7.6 %collective-permute-start.5 = (bf16[1,4,128,128]{3,2,1,0:T(8,128)(2,1)S(1)}, bf16[1,4,128,128]{3,2,1,0:T(8,128)(2,1)S(1)}, u32[]{:S(2)}, u32[]{:S(2)}) collective-permute-start(bf16[1,4,128,128]{3,2,1,0:T(8,128)(2,1)S(1)} %get-tuple-element.52), channel_id=1, source_target_pairs={{0,4},{1,3},{2,6},{3,1},{4,0},{5,7},{6,2},{7,5},{8,12},{9,11},{10,... | collective-permute-start | bytes 393224 | tf_op jit(solution)/shard_map/ppermute | solution.py:368
  69.0 9.0 %collective-permute-start.9 = (bf16[2,4,128,128]{3,2,1,0:T(8,128)(2,1)S(1)}, bf16[2,4,128,128]{3,2,1,0:T(8,128)(2,1)S(1)}, u32[]{:S(2)}, u32[]{:S(2)}) collective-permute-start(bf16[2,4,128,128]{3,2,1,0:T(8,128)(2,1)S(1)} %pad_maximum_fusion.6), channel_id=1, source_target_pairs={{0,8},{1,9},{2,10},{3,11},{4,12},{5,13},{6,14},{7,15},{8,0},{9,1},... | collective-permute-start | bytes 786440 | tf_op jit(solution)/shard_map/ppermute | solution.py:368
  69.1 6.0 %collective-permute-start.12 = (f32[1,16,128]{2,1,0:T(8,128)S(1)}, f32[1,16,128]{2,1,0:T(8,128)S(1)}, u32[]{:S(2)}, u32[]{:S(2)}) collective-permute-start(f32[1,16,128]{2,1,0:T(8,128)S(1)} %maximum_bitcast_fusion), channel_id=1, source_target_pairs={{0,16},{1,17},{2,18},{3,19},{4,20},{5,21},{6,22},{7,23},{8,24},{9,... | collective-permute-start | bytes 24584 | tf_op jit(solution)/shard_map/ppermute | solution.py:368
  75.1 4.6 %collective-permute-start.13 = (f32[2,16,128]{2,1,0:T(8,128)S(1)}, f32[2,16,128]{2,1,0:T(8,128)S(1)}, u32[]{:S(2)}, u32[]{:S(2)}) collective-permute-start(f32[2,16,128]{2,1,0:T(8,128)S(1)} %pad_maximum_fusion.9), channel_id=1, source_target_pairs={{0,8},{1,9},{2,10},{3,11},{4,12},{5,13},{6,14},{7,15},{8,0},{9,1},... | collective-permute-start | bytes 49160 | tf_op jit(solution)/shard_map/ppermute | solution.py:368
  78.0 10.2 %collective-permute-start.10 = (bf16[4,4,128,128]{3,2,1,0:T(8,128)(2,1)S(1)}, bf16[4,4,128,128]{3,2,1,0:T(8,128)(2,1)S(1)}, u32[]{:S(2)}, u32[]{:S(2)}) collective-permute-start(bf16[4,4,128,128]{3,2,1,0:T(8,128)(2,1)S(1)} %pad_maximum_fusion.4), channel_id=1, source_target_pairs={{0,4},{1,3},{2,6},{3,1},{4,0},{5,7},{6,2},{7,5},{8,12},{9,11},{10,... | collective-permute-start | bytes 1572872 | tf_op jit(solution)/shard_map/ppermute | solution.py:368
  79.7 7.9 %collective-permute-start.14 = (f32[4,16,128]{2,1,0:T(8,128)S(1)}, f32[4,16,128]{2,1,0:T(8,128)S(1)}, u32[]{:S(2)}, u32[]{:S(2)}) collective-permute-start(f32[4,16,128]{2,1,0:T(8,128)S(1)} %pad_maximum_fusion.8), channel_id=1, source_target_pairs={{0,4},{1,5},{2,6},{3,7},{4,0},{5,1},{6,2},{7,3},{8,12},{9,13},{10,... | collective-permute-start | bytes 98312 | tf_op jit(solution)/shard_map/ppermute | solution.py:368
  80.3 12.8 %collective-permute-start.7 = (bf16[2,4,128,128]{3,2,1,0:T(8,128)(2,1)S(1)}, bf16[2,4,128,128]{3,2,1,0:T(8,128)(2,1)S(1)}, u32[]{:S(2)}, u32[]{:S(2)}) collective-permute-start(bf16[2,4,128,128]{3,2,1,0:T(8,128)(2,1)S(1)} %pad_maximum_fusion.5), channel_id=1, source_target_pairs={{0,16},{1,17},{2,18},{3,19},{4,20},{5,21},{6,22},{7,23},{8,24},{9,... | collective-permute-start | bytes 786440 | tf_op jit(solution)/shard_map/ppermute | solution.py:368
  88.3 19.1 %collective-permute-start.11 = (bf16[8,4,128,128]{3,2,1,0:T(8,128)(2,1)S(1)}, bf16[8,4,128,128]{3,2,1,0:T(8,128)(2,1)S(1)}, u32[]{:S(2)}, u32[]{:S(2)}) collective-permute-start(bf16[8,4,128,128]{3,2,1,0:T(8,128)(2,1)S(1)} %constant_dynamic-update-slice_fusion.rest_1_), channel_id=1, source_target_pairs={{0,2},{1,5},{2,0},{3,7},{4,6},{5,1},{6,4},{7,3},{8,10},{9,13},{10,... | collective-permute-start | bytes 3145736 | tf_op jit(solution)/shard_map/ppermute | solution.py:368
  93.1 0.7 copy-start.1
  93.1 13.1 %collective-permute-start.8 = (bf16[4,4,128,128]{3,2,1,0:T(8,128)(2,1)S(1)}, bf16[4,4,128,128]{3,2,1,0:T(8,128)(2,1)}, u32[]{:S(2)}, u32[]{:S(2)}) collective-permute-start(bf16[4,4,128,128]{3,2,1,0:T(8,128)(2,1)S(1)} %pad_maximum_fusion.3), channel_id=1, source_target_pairs={{0,8},{1,9},{2,10},{3,11},{4,12},{5,13},{6,14},{7,15},{8,0},{9,1},... | collective-permute-start | bytes 1572872 | tf_op jit(solution)/shard_map/ppermute | solution.py:368
  107.4 15.0 %collective-permute-start.15 = (bf16[8,4,128,128]{3,2,1,0:T(8,128)(2,1)S(1)}, bf16[8,4,128,128]{3,2,1,0:T(8,128)(2,1)}, u32[]{:S(2)}, u32[]{:S(2)}) collective-permute-start(bf16[8,4,128,128]{3,2,1,0:T(8,128)(2,1)S(1)} %pad_maximum_fusion.1.rest_0_), channel_id=1, source_target_pairs={{0,2},{1,5},{2,0},{3,7},{4,6},{5,1},{6,4},{7,3},{8,10},{9,13},{10,... | collective-permute-start | bytes 3145736 | tf_op jit(solution)/shard_map/ppermute | solution.py:368
  108.4 14.9 %collective-permute-start.17 = (bf16[8,4,128,128]{3,2,1,0:T(8,128)(2,1)S(1)}, bf16[8,4,128,128]{3,2,1,0:T(8,128)(2,1)}, u32[]{:S(2)}, u32[]{:S(2)}) collective-permute-start(bf16[8,4,128,128]{3,2,1,0:T(8,128)(2,1)S(1)} %constant_dynamic-update-slice_fusion.rest_1_), channel_id=1, source_target_pairs={{0,1},{1,0},{2,3},{3,2},{4,5},{5,4},{6,7},{7,6},{8,9},{9,8},{10,11... | collective-permute-start | bytes 3145736 | tf_op jit(solution)/shard_map/ppermute | solution.py:368
  108.4 14.9 %collective-permute-start.16 = (bf16[8,4,128,128]{3,2,1,0:T(8,128)(2,1)S(1)}, bf16[8,4,128,128]{3,2,1,0:T(8,128)(2,1)}, u32[]{:S(2)}, u32[]{:S(2)}) collective-permute-start(bf16[8,4,128,128]{3,2,1,0:T(8,128)(2,1)S(1)} %pad_maximum_fusion.1.rest_0_), channel_id=1, source_target_pairs={{0,1},{1,0},{2,3},{3,2},{4,5},{5,4},{6,7},{7,6},{8,9},{9,8},{10,11... | collective-permute-start | bytes 3145736 | tf_op jit(solution)/shard_map/ppermute | solution.py:368
  108.9 14.4 %collective-permute-start.19 = (bf16[8,4,128,128]{3,2,1,0:T(8,128)(2,1)S(1)}, bf16[8,4,128,128]{3,2,1,0:T(8,128)(2,1)}, u32[]{:S(2)}, u32[]{:S(2)}) collective-permute-start(bf16[8,4,128,128]{3,2,1,0:T(8,128)(2,1)S(1)} %collective-permute-done.11.rest_3_), channel_id=1, source_target_pairs={{0,1},{1,0},{2,3},{3,2},{4,5},{5,4},{6,7},{7,6},{8,9},{9,8},{10,11... | collective-permute-start | bytes 3145736 | tf_op jit(solution)/shard_map/ppermute | solution.py:368
  122.4 3.0 %collective-permute-start.18 = (bf16[8,4,128,128]{3,2,1,0:T(8,128)(2,1)}, bf16[8,4,128,128]{3,2,1,0:T(8,128)(2,1)}, u32[]{:S(2)}, u32[]{:S(2)}) collective-permute-start(bf16[8,4,128,128]{3,2,1,0:T(8,128)(2,1)} %collective-permute-done.15.rest_2_), channel_id=1, source_target_pairs={{0,1},{1,0},{2,3},{3,2},{4,5},{5,4},{6,7},{7,6},{8,9},{9,8},{10,11... | collective-permute-start | bytes 3145736 | tf_op jit(solution)/shard_map/ppermute | solution.py:368
  166.4 7.2 %collective-permute-start.20 = (bf16[16,128,512]{2,1,0:T(8,128)(2,1)S(1)}, bf16[16,128,512]{2,1,0:T(8,128)(2,1)S(1)}, u32[]{:S(2)}, u32[]{:S(2)}) collective-permute-start(bf16[16,128,512]{2,1,0:T(8,128)(2,1)S(1)} %get-tuple-element.42), channel_id=1, source_target_pairs={{0,1},{1,0},{2,3},{3,2},{4,5},{5,4},{6,7},{7,6},{8,9},{9,8},{10,11... | collective-permute-start | bytes 6291464 | tf_op jit(solution)/shard_map/ppermute | solution.py:368
  166.5 14.8 %collective-permute-start.24 = (bf16[16,128,512]{2,1,0:T(8,128)(2,1)S(1)}, bf16[16,128,512]{2,1,0:T(8,128)(2,1)S(1)}, u32[]{:S(2)}, u32[]{:S(2)}) collective-permute-start(bf16[16,128,512]{2,1,0:T(8,128)(2,1)S(1)} %get-tuple-element.44), channel_id=1, source_target_pairs={{0,1},{1,0},{2,3},{3,2},{4,5},{5,4},{6,7},{7,6},{8,9},{9,8},{10,11... | collective-permute-start | bytes 6291464 | tf_op jit(solution)/shard_map/ppermute | solution.py:368
  173.9 14.9 %collective-permute-start.21 = (bf16[8,128,512]{2,1,0:T(8,128)(2,1)S(1)}, bf16[8,128,512]{2,1,0:T(8,128)(2,1)S(1)}, u32[]{:S(2)}, u32[]{:S(2)}) collective-permute-start(bf16[8,128,512]{2,1,0:T(8,128)(2,1)S(1)} %add_convert_fusion.1), channel_id=1, source_target_pairs={{0,2},{1,5},{2,0},{3,7},{4,6},{5,1},{6,4},{7,3},{8,10},{9,13},{10,... | collective-permute-start | bytes 3145736 | tf_op jit(solution)/shard_map/ppermute | solution.py:368
  188.8 14.8 %collective-permute-start.25 = (bf16[8,128,512]{2,1,0:T(8,128)(2,1)S(1)}, bf16[8,128,512]{2,1,0:T(8,128)(2,1)S(1)}, u32[]{:S(2)}, u32[]{:S(2)}) collective-permute-start(bf16[8,128,512]{2,1,0:T(8,128)(2,1)S(1)} %add_convert_fusion), channel_id=1, source_target_pairs={{0,2},{1,5},{2,0},{3,7},{4,6},{5,1},{6,4},{7,3},{8,10},{9,13},{10,... | collective-permute-start | bytes 3145736 | tf_op jit(solution)/shard_map/ppermute | solution.py:368
  189.8 14.0 %collective-permute-start.22 = (bf16[4,128,512]{2,1,0:T(8,128)(2,1)S(1)}, bf16[4,128,512]{2,1,0:T(8,128)(2,1)S(1)}, u32[]{:S(2)}, u32[]{:S(2)}) collective-permute-start(bf16[4,128,512]{2,1,0:T(8,128)(2,1)S(1)} %add_convert_fusion.3), channel_id=1, source_target_pairs={{0,8},{1,9},{2,10},{3,11},{4,12},{5,13},{6,14},{7,15},{8,0},{9,1},... | collective-permute-start | bytes 1572872 | tf_op jit(solution)/shard_map/ppermute | solution.py:368
  203.8 9.2 %collective-permute-start.26 = (bf16[4,128,512]{2,1,0:T(8,128)(2,1)S(1)}, bf16[4,128,512]{2,1,0:T(8,128)(2,1)S(1)}, u32[]{:S(2)}, u32[]{:S(2)}) collective-permute-start(bf16[4,128,512]{2,1,0:T(8,128)(2,1)S(1)} %add_convert_fusion.2), channel_id=1, source_target_pairs={{0,4},{1,3},{2,6},{3,1},{4,0},{5,7},{6,2},{7,5},{8,12},{9,11},{10,... | collective-permute-start | bytes 1572872 | tf_op jit(solution)/shard_map/ppermute | solution.py:368
  205.7 11.8 %collective-permute-start.23 = (bf16[2,128,512]{2,1,0:T(8,128)(2,1)S(1)}, bf16[2,128,512]{2,1,0:T(8,128)(2,1)S(1)}, u32[]{:S(2)}, u32[]{:S(2)}) collective-permute-start(bf16[2,128,512]{2,1,0:T(8,128)(2,1)S(1)} %add_convert_fusion.5), channel_id=1, source_target_pairs={{0,16},{1,17},{2,18},{3,19},{4,20},{5,21},{6,22},{7,23},{8,24},{9,... | collective-permute-start | bytes 786440 | tf_op jit(solution)/shard_map/ppermute | solution.py:368
  217.5 7.4 %collective-permute-start.27 = (bf16[2,128,512]{2,1,0:T(8,128)(2,1)S(1)}, bf16[2,128,512]{2,1,0:T(8,128)(2,1)S(1)}, u32[]{:S(2)}, u32[]{:S(2)}) collective-permute-start(bf16[2,128,512]{2,1,0:T(8,128)(2,1)S(1)} %add_convert_fusion.4), channel_id=1, source_target_pairs={{0,8},{1,9},{2,10},{3,11},{4,12},{5,13},{6,14},{7,15},{8,0},{9,1},... | collective-permute-start | bytes 786440 | tf_op jit(solution)/shard_map/ppermute | solution.py:368
  225.1 7.5 %collective-permute-start.29 = (bf16[1,128,512]{2,1,0:T(8,128)(2,1)S(1)}, bf16[1,128,512]{2,1,0:T(8,128)(2,1)S(1)}, u32[]{:S(2)}, u32[]{:S(2)}) collective-permute-start(bf16[1,128,512]{2,1,0:T(8,128)(2,1)S(1)} %add_convert_fusion.7), channel_id=1, source_target_pairs={{0,16},{1,17},{2,18},{3,19},{4,20},{5,21},{6,22},{7,23},{8,24},{9,... | collective-permute-start | bytes 393224 | tf_op jit(solution)/shard_map/ppermute | solution.py:368
  225.7 6.9 %collective-permute-start.28 = (bf16[1,128,512]{2,1,0:T(8,128)(2,1)S(1)}, bf16[1,128,512]{2,1,0:T(8,128)(2,1)S(1)}, u32[]{:S(2)}, u32[]{:S(2)}) collective-permute-start(bf16[1,128,512]{2,1,0:T(8,128)(2,1)S(1)} %add_convert_fusion.8), channel_id=1, source_target_pairs={{0,4},{1,3},{2,6},{3,1},{4,0},{5,7},{6,2},{7,5},{8,12},{9,11},{10,... | collective-permute-start | bytes 393224 | tf_op jit(solution)/shard_map/ppermute | solution.py:368

commit v7 on v6

--- a/solution.py
+++ b/solution.py
@@ -460,12 +460,14 @@
     )
 
 
-def gather_heads(heads):
+def gather_heads(heads, beside):
     heads = heads[None]
     for number, bits_of in enumerate(HEAD_STAGES):
+        if number == len(HEAD_STAGES) - 1:
+            heads, beside = after(heads, beside)
         came = flip(heads, bits_of)
         if number == len(HEAD_STAGES) - 1:
-            return [heads, came]
+            return [heads, came], beside
         heads = jnp.concatenate([heads, came], axis=0)
 
 
@@ -525,10 +527,10 @@
     second_low = along(ZLOW, second)
     first, _ = after(joined(first, first_last), second_high)
     first_high = along(ZHIGH, first)
-    table = make_table(second_high)
+    table = make_table(first_high)
     for bits in (ZHIGH, ZLOW, Y):
         table = joined(table, along(bits, table))
-    second = joined(second, second_low)
+    second, first_high = after(joined(second, second_low), first_high)
     second_last = flip(second, last_axis)
     first = joined(first, first_high)
     first_low = along(ZLOW, first)
@@ -565,13 +567,12 @@
         norm_gain.reshape(groups * members, LANES), device, 0, keepdims=False
     )
 
-    pieces = gather_heads(attn_heads)
+    pieces, moved = gather_heads(attn_heads, moved)
     numbers = jnp.arange(groups, dtype=jnp.int32)
     arrival = (head_bits(numbers, core) ^ group) ^ y_side
     info = jnp.concatenate(
         [jnp.stack([core, x_side]), ((arrival & 1) << 2) | (arrival >> 1)]
     )
-    info, moved = after(info, moved)
     send, keep = project(info, pieces, out_proj)
     came = flip(send, lambda c: CORE)
     from_x = flip(total_of([keep[0], came[0]]).astype(BF16), lambda c: X)

time: 234 us -> 240 us (1.026)
  waiting for transfers between devices: 130 us -> 136 us
    ppermute x30, waiting for transfers between devices: 118 us -> 132 us  [flip(): return lax.ppermute(array, ('expert', 'tensor'), pairs)]
    all_to_all x1, waiting for transfers between devices: 12.7 us -> 3.88 us  [per_device_tokens(): lax.all_to_all(jnp.transpose(own_cols, (1, 0, 2)), 'expert', split_axis=0...]
  transfers between devices with their start and end apart: 31 -> 31, of which waited for: 19 -> 22; matrix products, arithmetic and copies ran while one was open for 3% -> 4% of each run, Pallas kernels for 6% -> 5%
where the time goes in v7:
time: 240 us
  waiting for transfers between devices  136 us (57%)
  Pallas kernels  56.7 us (24%)
  starting transfers between devices  35 us (15%)
  other arithmetic  7.95 us (3%)
  local copies, waits for them, and re-layouts  3.73 us (2%)
    ppermute x30, waiting for transfers between devices, flip(): return lax.ppermute(array, ('expert', 'tensor'), pairs)  132 us
    ppermute x30, starting transfers between devices, flip(): return lax.ppermute(array, ('expert', 'tensor'), pairs)  31.2 us
    pallas_call x1, Pallas kernels, gate_up(): pl.pallas_call(kernel, grid_spec=pltpu.PrefetchScalarGridSpec(num_scalar_...  31.1 us
    pallas_call x3, Pallas kernels, down(): pl.pallas_call(functools.partial(down_kernel, rows), grid_spec=pltpu.Pref...  22.8 us
  transfers between devices with their start and end apart: 31, of which 22 were waited for; matrix products, arithmetic and copies ran while one was open for 4% of the time, Pallas kernels for 5%

profile of v7, /device:TPU:0, one launch (start us, length us, event | category | flops | bytes accessed | tf_op | source)
XLA Modules:
  0.0 239.6 jit_solution(7281630982745387867)
XLA Ops:
  0.0 3.0 %collective-permute-start = (bf16[1,128,1024]{2,1,0:T(8,128)(2,1)}, bf16[1,128,1024]{2,1,0:T(8,128)(2,1)S(1)}, u32[]{:S(2)}, u32[]{:S(2)}) collective-permute-start(bf16[1,128,1024]{2,1,0:T(8,128)(2,1)} %bitcast.62), channel_id=1, source_target_pairs={{0,4},{1,17},{2,6},{3,19},{4,0},{5,21},{6,2},{7,23},{8,12},{9,25},... | collective-permute-start | bytes 786440 | tf_op jit(solution)/shard_map/ppermute | solution.py:368
  3.0 4.6 %collective-permute-done = bf16[1,128,1024]{2,1,0:T(8,128)(2,1)S(1)} collective-permute-done((bf16[1,128,1024]{2,1,0:T(8,128)(2,1)}, bf16[1,128,1024]{2,1,0:T(8,128)(2,1)S(1)}, u32[]{:S(2)}, u32[]{:S(2)}) %collective-permute-start) | collective-permute-done | bytes 262176 | tf_op jit(solution)/shard_map/ppermute | solution.py:368
  7.5 1.8 pad_maximum_fusion.2
  9.3 3.1 %collective-permute-start.1 = (bf16[2,128,1024]{2,1,0:T(8,128)(2,1)}, bf16[2,128,1024]{2,1,0:T(8,128)(2,1)}, u32[]{:S(2)}, u32[]{:S(2)}) collective-permute-start(bf16[2,128,1024]{2,1,0:T(8,128)(2,1)} %pad_maximum_fusion.2), channel_id=1, source_target_pairs={{0,16},{1,9},{2,18},{3,11},{4,20},{5,13},{6,22},{7,15},{8,24},{9,1... | collective-permute-start | bytes 1572872 | tf_op jit(solution)/shard_map/ppermute | solution.py:368
  12.4 1.6 copy.23
  14.1 0.9 copy.25
  14.9 3.8 %all-to-all-start = ((bf16[8,128,128]{2,1,0:T(8,128)(2,1)}), bf16[8,128,128]{2,1,0:T(8,128)(2,1)S(1)}, u32[]{:S(2)}, u32[]{:S(2)}) async-start(bf16[8,128,128]{2,1,0:T(8,128)(2,1)} %copy.25), calls=%async_computation | async-start | bytes 524288 | tf_op jit(solution)/shard_map/all_to_all | solution.py:563
  18.7 7.2 %collective-permute-done.1 = bf16[2,128,1024]{2,1,0:T(8,128)(2,1)} collective-permute-done((bf16[2,128,1024]{2,1,0:T(8,128)(2,1)}, bf16[2,128,1024]{2,1,0:T(8,128)(2,1)}, u32[]{:S(2)}, u32[]{:S(2)}) %collective-permute-start.1) | collective-permute-done | bytes 524320 | tf_op jit(solution)/shard_map/ppermute | solution.py:368
  26.0 1.1 pad_maximum_fusion.refs_0_
  27.1 3.9 %all-to-all-done = bf16[8,128,128]{2,1,0:T(8,128)(2,1)S(1)} async-done(((bf16[8,128,128]{2,1,0:T(8,128)(2,1)}), bf16[8,128,128]{2,1,0:T(8,128)(2,1)S(1)}, u32[]{:S(2)}, u32[]{:S(2)}) %all-to-all-start) | async-done | bytes 262176 | tf_op jit(solution)/shard_map/all_to_all | solution.py:563
  31.0 1.2 collective-permute-start.2
  32.3 13.6 %collective-permute-done.2.refs_1_ = bf16[4,128,1024]{2,1,0:T(8,128)(2,1)} collective-permute-done((bf16[4,128,1024]{2,1,0:T(8,128)(2,1)S(1)}, bf16[4,128,1024]{2,1,0:T(8,128)(2,1)}, u32[]{:S(2)}, u32[]{:S(2)}) %collective-permute-start.2) | collective-permute-done | bytes 1048608 | tf_op jit(solution)/shard_map/ppermute | solution.py:368
  45.9 2.8 %project.1 = (bf16[2,8,128,128]{3,2,1,0:T(8,128)(2,1)S(1)}, bf16[2,8,128,128]{3,2,1,0:T(8,128)(2,1)S(1)}) custom-call(s32[10]{0:T(128)S(1)} %pad_add_fusion.1.info_ref, bf16[4,128,1024]{2,1,0:T(8,128)(2,1)S(1)} %pad_maximum_fusion.refs_0_, bf16[4,128,1024]{2,1,0:T(8,128)(2,1)} %collective-permute-done.2.refs_1_, bf16[1024,512]{1,0:T(8,128)(2,1)S(1)} %copy-done), custom_call_target="tpu_custom_call" | custom-call | flops 1073741824 | bytes 5242880 | tf_op jit(solution)/shard_map/project/pallas_call | solution.py:112
  48.8 1.9 collective-permute-done.3
  50.8 1.9 collective-permute-start.4
  52.7 6.6 %collective-permute-done.4 = bf16[8,128,128]{2,1,0:T(8,128)(2,1)S(1)} collective-permute-done((bf16[8,128,128]{2,1,0:T(8,128)(2,1)S(1)}, bf16[8,128,128]{2,1,0:T(8,128)(2,1)S(1)}, u32[]{:S(2)}, u32[]{:S(2)}) %collective-permute-start.4) | collective-permute-done | bytes 262176 | tf_op jit(solution)/shard_map/ppermute | solution.py:368
  59.3 0.2 fusion.7
  59.4 3.6 %collective-permute-start.6 = (bf16[1,4,128,128]{3,2,1,0:T(8,128)(2,1)S(1)}, bf16[1,4,128,128]{3,2,1,0:T(8,128)(2,1)S(1)}, u32[]{:S(2)}, u32[]{:S(2)}) collective-permute-start(bf16[1,4,128,128]{3,2,1,0:T(8,128)(2,1)S(1)} %get-tuple-element.56), channel_id=1, source_target_pairs={{0,16},{1,17},{2,18},{3,19},{4,20},{5,21},{6,22},{7,23},{8,24},{9,... | collective-permute-start | bytes 393224 | tf_op jit(solution)/shard_map/ppermute | solution.py:368
  63.0 0.4 collective-permute-start.5
  63.4 5.4 %collective-permute-done.6 = bf16[1,4,128,128]{3,2,1,0:T(8,128)(2,1)S(1)} collective-permute-done((bf16[1,4,128,128]{3,2,1,0:T(8,128)(2,1)S(1)}, bf16[1,4,128,128]{3,2,1,0:T(8,128)(2,1)S(1)}, u32[]{:S(2)}, u32[]{:S(2)}) %collective-permute-start.6) | collective-permute-done | bytes 131104 | tf_op jit(solution)/shard_map/ppermute | solution.py:368
  68.8 0.2 collective-permute-start.7
  69.0 3.4 %collective-permute-start.8 = (bf16[2,4,128,128]{3,2,1,0:T(8,128)(2,1)S(1)}, bf16[2,4,128,128]{3,2,1,0:T(8,128)(2,1)S(1)}, u32[]{:S(2)}, u32[]{:S(2)}) collective-permute-start(bf16[2,4,128,128]{3,2,1,0:T(8,128)(2,1)S(1)} %pad_maximum_fusion.5), channel_id=1, source_target_pairs={{0,16},{1,17},{2,18},{3,19},{4,20},{5,21},{6,22},{7,23},{8,24},{9,... | collective-permute-start | bytes 786440 | tf_op jit(solution)/shard_map/ppermute | solution.py:368
  72.5 9.6 %collective-permute-done.7 = bf16[2,4,128,128]{3,2,1,0:T(8,128)(2,1)S(1)} collective-permute-done((bf16[2,4,128,128]{3,2,1,0:T(8,128)(2,1)S(1)}, bf16[2,4,128,128]{3,2,1,0:T(8,128)(2,1)S(1)}, u32[]{:S(2)}, u32[]{:S(2)}) %collective-permute-start.7) | collective-permute-done | bytes 262176 | tf_op jit(solution)/shard_map/ppermute | solution.py:368
  82.1 1.6 collective-permute-done.8
  83.7 1.5 collective-permute-start.10
  85.3 4.5 %collective-permute-done.12 = f32[1,16,128]{2,1,0:T(8,128)S(1)} collective-permute-done((f32[1,16,128]{2,1,0:T(8,128)S(1)}, f32[1,16,128]{2,1,0:T(8,128)S(1)}, u32[]{:S(2)}, u32[]{:S(2)}) %collective-permute-start.12) | collective-permute-done | bytes 8224 | tf_op jit(solution)/shard_map/ppermute | solution.py:368
  89.8 0.3 collective-permute-start.13
  90.2 1.8 collective-permute-start.9
  91.9 1.8 collective-permute-done.13
  93.8 0.7 collective-permute-start.14
  94.5 1.4 collective-permute-start.11
  95.9 2.1 collective-permute-done.14
  98.1 0.6 gather_fusion
  98.7 0.2 compare_reduce_fusion
  98.9 0.2 convolution_convert_fusion
  99.2 2.1 collective-permute-done.9
  101.3 1.2 pad_maximum_fusion.1.rest_0_
  102.5 6.9 %collective-permute-done.11.rest_3_ = bf16[8,4,128,128]{3,2,1,0:T(8,128)(2,1)S(1)} collective-permute-done((bf16[8,4,128,128]{3,2,1,0:T(8,128)(2,1)S(1)}, bf16[8,4,128,128]{3,2,1,0:T(8,128)(2,1)S(1)}, u32[]{:S(2)}, u32[]{:S(2)}) %collective-permute-start.11) | collective-permute-done | bytes 1048608 | tf_op jit(solution)/shard_map/ppermute | solution.py:368
  109.4 1.4 collective-permute-start.15
  110.8 0.5 collective-permute-start.16
  111.3 12.9 %collective-permute-done.15.rest_2_ = bf16[8,4,128,128]{3,2,1,0:T(8,128)(2,1)} collective-permute-done((bf16[8,4,128,128]{3,2,1,0:T(8,128)(2,1)S(1)}, bf16[8,4,128,128]{3,2,1,0:T(8,128)(2,1)}, u32[]{:S(2)}, u32[]{:S(2)}) %collective-permute-start.15) | collective-permute-done | bytes 1048608 | tf_op jit(solution)/shard_map/ppermute | solution.py:368
  125.1 2.2 collective-permute-done.18.rest_6_
  127.3 31.1 %gate_up.1 = (bf16[8,192,384]{2,1,0:T(8,128)(2,1)S(1)}, f32[128,1024]{1,0:T(8,128)S(1)}, bf16[4,256,384]{2,1,0:T(8,128)(2,1)S(1)}) custom-call(s32[66]{0:T(128)S(1)} %pad_add_fusion.info_ref, s32[8,1024]{1,0:T(8,128)S(1)} %bitcast_select_fusion.slot_ref, f32[8,1024]{1,0:T(8,128)S(1)} %bitcast.59, f32[32,128]{1,0:T(8,128)S(1)} %divide_bitcast_fusion.invgain_ref, ...), custom_call_target="tpu_custom_call" | custom-call | flops 9663676416 | bytes 58720256 | tf_op jit(solution)/shard_map/gate_up/pallas_call | solution.py:261
  158.4 9.9 %down_mix.4 = (bf16[16,128,512]{2,1,0:T(8,128)(2,1)S(1)}, bf16[16,128,512]{2,1,0:T(8,128)(2,1)S(1)}) custom-call(s32[34]{0:T(128)S(1)} %pad_add_fusion.3.place_ref, bf16[4,256,384]{2,1,0:T(8,128)(2,1)S(1)} %get-tuple-element.44.spread_ref, bf16[8,192,384]{2,1,0:T(8,128)(2,1)S(1)} %get-tuple-element.45.act_ref, bf16[8,384,4096]{2,1,0:T(8,128)(2,1)} %wd1_ref.5, ...), custom_call_target="tpu_custom_call" | custom-call | flops 4831838208 | bytes 16777216 | tf_op jit(solution)/shard_map/down_mix/pallas_call | solution.py:337
  168.4 0.5 collective-permute-start.24
  169.0 6.4 %down_mix.3 = bf16[16,128,512]{2,1,0:T(8,128)(2,1)S(1)} custom-call(s32[18]{0:T(128)S(1)} %pad_add_fusion.2.place_ref, bf16[4,256,384]{2,1,0:T(8,128)(2,1)S(1)} %get-tuple-element.44.spread_ref, bf16[8,192,384]{2,1,0:T(8,128)(2,1)S(1)} %get-tuple-element.45.act_ref, bf16[8,384,4096]{2,1,0:T(8,128)(2,1)} %wd1_ref.5, bf16[8,384,4096]{2,1,0:T(8,128)(2,1)} %wd1_ref.5), custom_call_target="tpu_custom_call" | custom-call | flops 2415919104 | bytes 8388608 | tf_op jit(solution)/shard_map/down_mix/pallas_call | solution.py:337
  175.5 0.3 add_convert_fusion.1
  175.8 1.4 collective-permute-start.21
  177.3 6.4 %down_mix.5 = bf16[16,128,512]{2,1,0:T(8,128)(2,1)S(1)} custom-call(s32[18]{0:T(128)S(1)} %pad_add_fusion.4.place_ref, bf16[4,256,384]{2,1,0:T(8,128)(2,1)S(1)} %get-tuple-element.44.spread_ref, bf16[8,192,384]{2,1,0:T(8,128)(2,1)S(1)} %get-tuple-element.45.act_ref, bf16[8,384,4096]{2,1,0:T(8,128)(2,1)} %wd1_ref.5, bf16[8,384,4096]{2,1,0:T(8,128)(2,1)} %wd1_ref.5), custom_call_target="tpu_custom_call" | custom-call | flops 2415919104 | bytes 8388608 | tf_op jit(solution)/shard_map/down_mix/pallas_call | solution.py:337
  183.7 0.3 add_convert_fusion
  184.0 6.6 %collective-permute-done.21 = bf16[8,128,512]{2,1,0:T(8,128)(2,1)S(1)} collective-permute-done((bf16[8,128,512]{2,1,0:T(8,128)(2,1)S(1)}, bf16[8,128,512]{2,1,0:T(8,128)(2,1)S(1)}, u32[]{:S(2)}, u32[]{:S(2)}) %collective-permute-start.21) | collective-permute-done | bytes 1048608 | tf_op jit(solution)/shard_map/ppermute | solution.py:368
  190.7 1.3 collective-permute-start.25
  192.0 0.2 add_convert_fusion.3
  192.2 0.2 collective-permute-start.22
  192.4 13.0 %collective-permute-done.25 = bf16[8,128,512]{2,1,0:T(8,128)(2,1)S(1)} collective-permute-done((bf16[8,128,512]{2,1,0:T(8,128)(2,1)S(1)}, bf16[8,128,512]{2,1,0:T(8,128)(2,1)S(1)}, u32[]{:S(2)}, u32[]{:S(2)}) %collective-permute-start.25) | collective-permute-done | bytes 1048608 | tf_op jit(solution)/shard_map/ppermute | solution.py:368
  205.5 0.2 add_convert_fusion.2
  205.7 1.8 collective-permute-start.26
  207.6 0.7 collective-permute-start.23
  208.3 6.6 %collective-permute-done.26 = bf16[4,128,512]{2,1,0:T(8,128)(2,1)S(1)} collective-permute-done((bf16[4,128,512]{2,1,0:T(8,128)(2,1)S(1)}, bf16[4,128,512]{2,1,0:T(8,128)(2,1)S(1)}, u32[]{:S(2)}, u32[]{:S(2)}) %collective-permute-start.26) | collective-permute-done | bytes 524320 | tf_op jit(solution)/shard_map/ppermute | solution.py:368
  215.1 6.9 %collective-permute-done.23 = bf16[2,128,512]{2,1,0:T(8,128)(2,1)S(1)} collective-permute-done((bf16[2,128,512]{2,1,0:T(8,128)(2,1)S(1)}, bf16[2,128,512]{2,1,0:T(8,128)(2,1)S(1)}, u32[]{:S(2)}, u32[]{:S(2)}) %collective-permute-start.23) | collective-permute-done | bytes 262176 | tf_op jit(solution)/shard_map/ppermute | solution.py:368
  221.9 8.2 %collective-permute-done.27 = bf16[2,128,512]{2,1,0:T(8,128)(2,1)S(1)} collective-permute-done((bf16[2,128,512]{2,1,0:T(8,128)(2,1)S(1)}, bf16[2,128,512]{2,1,0:T(8,128)(2,1)S(1)}, u32[]{:S(2)}, u32[]{:S(2)}) %collective-permute-start.27) | collective-permute-done | bytes 262176 | tf_op jit(solution)/shard_map/ppermute | solution.py:368
  230.4 0.6 collective-permute-start.28
  231.1 7.5 %collective-permute-done.29 = bf16[1,128,512]{2,1,0:T(8,128)(2,1)S(1)} collective-permute-done((bf16[1,128,512]{2,1,0:T(8,128)(2,1)S(1)}, bf16[1,128,512]{2,1,0:T(8,128)(2,1)S(1)}, u32[]{:S(2)}, u32[]{:S(2)}) %collective-permute-start.29) | collective-permute-done | bytes 131104 | tf_op jit(solution)/shard_map/ppermute | solution.py:368
  238.8 0.8 fusion
  (82 shorter events, 2.8 us)
Async XLA Ops:
  0.0 7.5 %collective-permute-start = (bf16[1,128,1024]{2,1,0:T(8,128)(2,1)}, bf16[1,128,1024]{2,1,0:T(8,128)(2,1)S(1)}, u32[]{:S(2)}, u32[]{:S(2)}) collective-permute-start(bf16[1,128,1024]{2,1,0:T(8,128)(2,1)} %bitcast.62), channel_id=1, source_target_pairs={{0,4},{1,17},{2,6},{3,19},{4,0},{5,21},{6,2},{7,23},{8,12},{9,25},... | collective-permute-start | bytes 786440 | tf_op jit(solution)/shard_map/ppermute | solution.py:368
  9.3 16.7 %copy-start.1 = (bf16[128,1024]{1,0:T(8,128)(2,1)S(1)}, bf16[128,1024]{1,0:T(8,128)(2,1)}, u32[]{:S(2)}) copy-start(bf16[128,1024]{1,0:T(8,128)(2,1)} %param.9) | copy-start | bytes 786436
  9.3 16.7 %collective-permute-start.1 = (bf16[2,128,1024]{2,1,0:T(8,128)(2,1)}, bf16[2,128,1024]{2,1,0:T(8,128)(2,1)}, u32[]{:S(2)}, u32[]{:S(2)}) collective-permute-start(bf16[2,128,1024]{2,1,0:T(8,128)(2,1)} %pad_maximum_fusion.2), channel_id=1, source_target_pairs={{0,16},{1,9},{2,18},{3,11},{4,20},{5,13},{6,22},{7,15},{8,24},{9,1... | collective-permute-start | bytes 1572872 | tf_op jit(solution)/shard_map/ppermute | solution.py:368
  14.0 31.9 %copy-start = (bf16[1024,512]{1,0:T(8,128)(2,1)S(1)}, bf16[1024,512]{1,0:T(8,128)(2,1)}, u32[]{:S(2)}) copy-start(bf16[1024,512]{1,0:T(8,128)(2,1)} %refs_2_.1) | copy-start | bytes 3145732
  14.9 16.1 %all-to-all-start = ((bf16[8,128,128]{2,1,0:T(8,128)(2,1)}), bf16[8,128,128]{2,1,0:T(8,128)(2,1)S(1)}, u32[]{:S(2)}, u32[]{:S(2)}) async-start(bf16[8,128,128]{2,1,0:T(8,128)(2,1)} %copy.25), calls=%async_computation | async-start | bytes 524288 | tf_op jit(solution)/shard_map/all_to_all | solution.py:563
  31.0 14.9 %collective-permute-start.2 = (bf16[4,128,1024]{2,1,0:T(8,128)(2,1)S(1)}, bf16[4,128,1024]{2,1,0:T(8,128)(2,1)}, u32[]{:S(2)}, u32[]{:S(2)}) collective-permute-start(bf16[4,128,1024]{2,1,0:T(8,128)(2,1)S(1)} %pad_maximum_fusion.refs_0_), channel_id=1, source_target_pairs={{0,8},{1,5},{2,10},{3,7},{4,12},{5,1},{6,14},{7,3},{8,0},{9,13},{1... | collective-permute-start | bytes 3145736 | tf_op jit(solution)/shard_map/ppermute | solution.py:368
  32.3 20.4 %copy-start.3 = (f32[128,8]{0,1:T(8,128)S(1)}, f32[128,8]{0,1:T(8,128)}, u32[]{:S(2)}) copy-start(f32[128,8]{0,1:T(8,128)} %param.14) | copy-start | bytes 12292
  32.3 20.4 %copy-start.4 = (f32[4096]{0:T(1024)S(1)}, f32[4096]{0:T(1024)}, u32[]{:S(2)}) copy-start(f32[4096]{0:T(1024)} %param.12) | copy-start | bytes 49156
  48.7 2.0 collective-permute-start.3
  50.7 34.5 %copy-start.5 = (s32[128,8]{0,1:T(8,128)S(1)}, s32[128,8]{0,1:T(8,128)}, u32[]{:S(2)}) copy-start(s32[128,8]{0,1:T(8,128)} %param.13) | copy-start | bytes 12292
  50.8 8.5 %collective-permute-start.4 = (bf16[8,128,128]{2,1,0:T(8,128)(2,1)S(1)}, bf16[8,128,128]{2,1,0:T(8,128)(2,1)S(1)}, u32[]{:S(2)}, u32[]{:S(2)}) collective-permute-start(bf16[8,128,128]{2,1,0:T(8,128)(2,1)S(1)} %fusion.2), channel_id=1, source_target_pairs={{0,2},{1,3},{2,0},{3,1},{4,6},{5,7},{6,4},{7,5},{8,10},{9,11},{10,... | collective-permute-start | bytes 786440 | tf_op jit(solution)/shard_map/ppermute | solution.py:368
  59.4 9.3 %collective-permute-start.6 = (bf16[1,4,128,128]{3,2,1,0:T(8,128)(2,1)S(1)}, bf16[1,4,128,128]{3,2,1,0:T(8,128)(2,1)S(1)}, u32[]{:S(2)}, u32[]{:S(2)}) collective-permute-start(bf16[1,4,128,128]{3,2,1,0:T(8,128)(2,1)S(1)} %get-tuple-element.56), channel_id=1, source_target_pairs={{0,16},{1,17},{2,18},{3,19},{4,20},{5,21},{6,22},{7,23},{8,24},{9,... | collective-permute-start | bytes 393224 | tf_op jit(solution)/shard_map/ppermute | solution.py:368
  63.0 5.8 %collective-permute-start.5 = (bf16[1,4,128,128]{3,2,1,0:T(8,128)(2,1)S(1)}, bf16[1,4,128,128]{3,2,1,0:T(8,128)(2,1)S(1)}, u32[]{:S(2)}, u32[]{:S(2)}) collective-permute-start(bf16[1,4,128,128]{3,2,1,0:T(8,128)(2,1)S(1)} %get-tuple-element.55), channel_id=1, source_target_pairs={{0,4},{1,3},{2,6},{3,1},{4,0},{5,7},{6,2},{7,5},{8,12},{9,11},{10,... | collective-permute-start | bytes 393224 | tf_op jit(solution)/shard_map/ppermute | solution.py:368
  68.8 13.2 %collective-permute-start.7 = (bf16[2,4,128,128]{3,2,1,0:T(8,128)(2,1)S(1)}, bf16[2,4,128,128]{3,2,1,0:T(8,128)(2,1)S(1)}, u32[]{:S(2)}, u32[]{:S(2)}) collective-permute-start(bf16[2,4,128,128]{3,2,1,0:T(8,128)(2,1)S(1)} %pad_maximum_fusion.6), channel_id=1, source_target_pairs={{0,8},{1,9},{2,10},{3,11},{4,12},{5,13},{6,14},{7,15},{8,0},{9,1},... | collective-permute-start | bytes 786440 | tf_op jit(solution)/shard_map/ppermute | solution.py:368
  69.0 14.6 %collective-permute-start.8 = (bf16[2,4,128,128]{3,2,1,0:T(8,128)(2,1)S(1)}, bf16[2,4,128,128]{3,2,1,0:T(8,128)(2,1)S(1)}, u32[]{:S(2)}, u32[]{:S(2)}) collective-permute-start(bf16[2,4,128,128]{3,2,1,0:T(8,128)(2,1)S(1)} %pad_maximum_fusion.5), channel_id=1, source_target_pairs={{0,16},{1,17},{2,18},{3,19},{4,20},{5,21},{6,22},{7,23},{8,24},{9,... | collective-permute-start | bytes 786440 | tf_op jit(solution)/shard_map/ppermute | solution.py:368
  83.7 10.7 %copy-start.2 = (bf16[2,4,128,128]{3,2,1,0:T(8,128)(2,1)}, bf16[2,4,128,128]{3,2,1,0:T(8,128)(2,1)S(1)}, u32[]{:S(2)}) copy-start(bf16[2,4,128,128]{3,2,1,0:T(8,128)(2,1)S(1)} %collective-permute-done.8) | copy-start | bytes 786436
  83.7 10.7 %collective-permute-start.10 = (bf16[4,4,128,128]{3,2,1,0:T(8,128)(2,1)S(1)}, bf16[4,4,128,128]{3,2,1,0:T(8,128)(2,1)S(1)}, u32[]{:S(2)}, u32[]{:S(2)}) collective-permute-start(bf16[4,4,128,128]{3,2,1,0:T(8,128)(2,1)S(1)} %pad_maximum_fusion.3), channel_id=1, source_target_pairs={{0,4},{1,3},{2,6},{3,1},{4,0},{5,7},{6,2},{7,5},{8,12},{9,11},{10,... | collective-permute-start | bytes 1572872 | tf_op jit(solution)/shard_map/ppermute | solution.py:368
  85.2 4.6 %collective-permute-start.12 = (f32[1,16,128]{2,1,0:T(8,128)S(1)}, f32[1,16,128]{2,1,0:T(8,128)S(1)}, u32[]{:S(2)}, u32[]{:S(2)}) collective-permute-start(f32[1,16,128]{2,1,0:T(8,128)S(1)} %maximum_bitcast_fusion), channel_id=1, source_target_pairs={{0,16},{1,17},{2,18},{3,19},{4,20},{5,21},{6,22},{7,23},{8,24},{9,... | collective-permute-start | bytes 24584 | tf_op jit(solution)/shard_map/ppermute | solution.py:368
  89.8 4.0 %collective-permute-start.13 = (f32[2,16,128]{2,1,0:T(8,128)S(1)}, f32[2,16,128]{2,1,0:T(8,128)S(1)}, u32[]{:S(2)}, u32[]{:S(2)}) collective-permute-start(f32[2,16,128]{2,1,0:T(8,128)S(1)} %pad_maximum_fusion.9), channel_id=1, source_target_pairs={{0,8},{1,9},{2,10},{3,11},{4,12},{5,13},{6,14},{7,15},{8,0},{9,1},... | collective-permute-start | bytes 49160 | tf_op jit(solution)/shard_map/ppermute | solution.py:368
  90.2 11.1 %collective-permute-start.9 = (bf16[4,4,128,128]{3,2,1,0:T(8,128)(2,1)S(1)}, bf16[4,4,128,128]{3,2,1,0:T(8,128)(2,1)}, u32[]{:S(2)}, u32[]{:S(2)}) collective-permute-start(bf16[4,4,128,128]{3,2,1,0:T(8,128)(2,1)S(1)} %pad_maximum_fusion.4), channel_id=1, source_target_pairs={{0,8},{1,9},{2,10},{3,11},{4,12},{5,13},{6,14},{7,15},{8,0},{9,1},... | collective-permute-start | bytes 1572872 | tf_op jit(solution)/shard_map/ppermute | solution.py:368
  93.8 4.3 %collective-permute-start.14 = (f32[4,16,128]{2,1,0:T(8,128)S(1)}, f32[4,16,128]{2,1,0:T(8,128)S(1)}, u32[]{:S(2)}, u32[]{:S(2)}) collective-permute-start(f32[4,16,128]{2,1,0:T(8,128)S(1)} %pad_maximum_fusion.8), channel_id=1, source_target_pairs={{0,4},{1,5},{2,6},{3,7},{4,0},{5,1},{6,2},{7,3},{8,12},{9,13},{10,... | collective-permute-start | bytes 98312 | tf_op jit(solution)/shard_map/ppermute | solution.py:368
  94.5 14.9 %collective-permute-start.11 = (bf16[8,4,128,128]{3,2,1,0:T(8,128)(2,1)S(1)}, bf16[8,4,128,128]{3,2,1,0:T(8,128)(2,1)S(1)}, u32[]{:S(2)}, u32[]{:S(2)}) collective-permute-start(bf16[8,4,128,128]{3,2,1,0:T(8,128)(2,1)S(1)} %constant_dynamic-update-slice_fusion.rest_1_), channel_id=1, source_target_pairs={{0,2},{1,5},{2,0},{3,7},{4,6},{5,1},{6,4},{7,3},{8,10},{9,13},{10,... | collective-permute-start | bytes 3145736 | tf_op jit(solution)/shard_map/ppermute | solution.py:368
  109.4 14.9 %collective-permute-start.15 = (bf16[8,4,128,128]{3,2,1,0:T(8,128)(2,1)S(1)}, bf16[8,4,128,128]{3,2,1,0:T(8,128)(2,1)}, u32[]{:S(2)}, u32[]{:S(2)}) collective-permute-start(bf16[8,4,128,128]{3,2,1,0:T(8,128)(2,1)S(1)} %pad_maximum_fusion.1.rest_0_), channel_id=1, source_target_pairs={{0,2},{1,5},{2,0},{3,7},{4,6},{5,1},{6,4},{7,3},{8,10},{9,13},{10,... | collective-permute-start | bytes 3145736 | tf_op jit(solution)/shard_map/ppermute | solution.py:368
  110.8 14.3 %collective-permute-start.17 = (bf16[8,4,128,128]{3,2,1,0:T(8,128)(2,1)S(1)}, bf16[8,4,128,128]{3,2,1,0:T(8,128)(2,1)}, u32[]{:S(2)}, u32[]{:S(2)}) collective-permute-start(bf16[8,4,128,128]{3,2,1,0:T(8,128)(2,1)S(1)} %constant_dynamic-update-slice_fusion.rest_1_), channel_id=1, source_target_pairs={{0,1},{1,0},{2,3},{3,2},{4,5},{5,4},{6,7},{7,6},{8,9},{9,8},{10,11... | collective-permute-start | bytes 3145736 | tf_op jit(solution)/shard_map/ppermute | solution.py:368
  110.8 14.3 %collective-permute-start.16 = (bf16[8,4,128,128]{3,2,1,0:T(8,128)(2,1)S(1)}, bf16[8,4,128,128]{3,2,1,0:T(8,128)(2,1)}, u32[]{:S(2)}, u32[]{:S(2)}) collective-permute-start(bf16[8,4,128,128]{3,2,1,0:T(8,128)(2,1)S(1)} %pad_maximum_fusion.1.rest_0_), channel_id=1, source_target_pairs={{0,1},{1,0},{2,3},{3,2},{4,5},{5,4},{6,7},{7,6},{8,9},{9,8},{10,11... | collective-permute-start | bytes 3145736 | tf_op jit(solution)/shard_map/ppermute | solution.py:368
  111.3 13.8 %collective-permute-start.19 = (bf16[8,4,128,128]{3,2,1,0:T(8,128)(2,1)S(1)}, bf16[8,4,128,128]{3,2,1,0:T(8,128)(2,1)}, u32[]{:S(2)}, u32[]{:S(2)}) collective-permute-start(bf16[8,4,128,128]{3,2,1,0:T(8,128)(2,1)S(1)} %collective-permute-done.11.rest_3_), channel_id=1, source_target_pairs={{0,1},{1,0},{2,3},{3,2},{4,5},{5,4},{6,7},{7,6},{8,9},{9,8},{10,11... | collective-permute-start | bytes 3145736 | tf_op jit(solution)/shard_map/ppermute | solution.py:368
  124.3 3.0 %collective-permute-start.18 = (bf16[8,4,128,128]{3,2,1,0:T(8,128)(2,1)}, bf16[8,4,128,128]{3,2,1,0:T(8,128)(2,1)}, u32[]{:S(2)}, u32[]{:S(2)}) collective-permute-start(bf16[8,4,128,128]{3,2,1,0:T(8,128)(2,1)} %collective-permute-done.15.rest_2_), channel_id=1, source_target_pairs={{0,1},{1,0},{2,3},{3,2},{4,5},{5,4},{6,7},{7,6},{8,9},{9,8},{10,11... | collective-permute-start | bytes 3145736 | tf_op jit(solution)/shard_map/ppermute | solution.py:368
  168.3 7.2 %collective-permute-start.20 = (bf16[16,128,512]{2,1,0:T(8,128)(2,1)S(1)}, bf16[16,128,512]{2,1,0:T(8,128)(2,1)S(1)}, u32[]{:S(2)}, u32[]{:S(2)}) collective-permute-start(bf16[16,128,512]{2,1,0:T(8,128)(2,1)S(1)} %get-tuple-element.46), channel_id=1, source_target_pairs={{0,1},{1,0},{2,3},{3,2},{4,5},{5,4},{6,7},{7,6},{8,9},{9,8},{10,11... | collective-permute-start | bytes 6291464 | tf_op jit(solution)/shard_map/ppermute | solution.py:368
  168.4 15.3 %collective-permute-start.24 = (bf16[16,128,512]{2,1,0:T(8,128)(2,1)S(1)}, bf16[16,128,512]{2,1,0:T(8,128)(2,1)S(1)}, u32[]{:S(2)}, u32[]{:S(2)}) collective-permute-start(bf16[16,128,512]{2,1,0:T(8,128)(2,1)S(1)} %get-tuple-element.48), channel_id=1, source_target_pairs={{0,1},{1,0},{2,3},{3,2},{4,5},{5,4},{6,7},{7,6},{8,9},{9,8},{10,11... | collective-permute-start | bytes 6291464 | tf_op jit(solution)/shard_map/ppermute | solution.py:368
  175.8 14.9 %collective-permute-start.21 = (bf16[8,128,512]{2,1,0:T(8,128)(2,1)S(1)}, bf16[8,128,512]{2,1,0:T(8,128)(2,1)S(1)}, u32[]{:S(2)}, u32[]{:S(2)}) collective-permute-start(bf16[8,128,512]{2,1,0:T(8,128)(2,1)S(1)} %add_convert_fusion.1), channel_id=1, source_target_pairs={{0,2},{1,5},{2,0},{3,7},{4,6},{5,1},{6,4},{7,3},{8,10},{9,13},{10,... | collective-permute-start | bytes 3145736 | tf_op jit(solution)/shard_map/ppermute | solution.py:368
  190.7 14.8 %collective-permute-start.25 = (bf16[8,128,512]{2,1,0:T(8,128)(2,1)S(1)}, bf16[8,128,512]{2,1,0:T(8,128)(2,1)S(1)}, u32[]{:S(2)}, u32[]{:S(2)}) collective-permute-start(bf16[8,128,512]{2,1,0:T(8,128)(2,1)S(1)} %add_convert_fusion), channel_id=1, source_target_pairs={{0,2},{1,5},{2,0},{3,7},{4,6},{5,1},{6,4},{7,3},{8,10},{9,13},{10,... | collective-permute-start | bytes 3145736 | tf_op jit(solution)/shard_map/ppermute | solution.py:368
  192.2 13.5 %collective-permute-start.22 = (bf16[4,128,512]{2,1,0:T(8,128)(2,1)S(1)}, bf16[4,128,512]{2,1,0:T(8,128)(2,1)S(1)}, u32[]{:S(2)}, u32[]{:S(2)}) collective-permute-start(bf16[4,128,512]{2,1,0:T(8,128)(2,1)S(1)} %add_convert_fusion.3), channel_id=1, source_target_pairs={{0,8},{1,9},{2,10},{3,11},{4,12},{5,13},{6,14},{7,15},{8,0},{9,1},... | collective-permute-start | bytes 1572872 | tf_op jit(solution)/shard_map/ppermute | solution.py:368
  205.7 9.2 %collective-permute-start.26 = (bf16[4,128,512]{2,1,0:T(8,128)(2,1)S(1)}, bf16[4,128,512]{2,1,0:T(8,128)(2,1)S(1)}, u32[]{:S(2)}, u32[]{:S(2)}) collective-permute-start(bf16[4,128,512]{2,1,0:T(8,128)(2,1)S(1)} %add_convert_fusion.2), channel_id=1, source_target_pairs={{0,4},{1,3},{2,6},{3,1},{4,0},{5,7},{6,2},{7,5},{8,12},{9,11},{10,... | collective-permute-start | bytes 1572872 | tf_op jit(solution)/shard_map/ppermute | solution.py:368
  207.6 14.3 %collective-permute-start.23 = (bf16[2,128,512]{2,1,0:T(8,128)(2,1)S(1)}, bf16[2,128,512]{2,1,0:T(8,128)(2,1)S(1)}, u32[]{:S(2)}, u32[]{:S(2)}) collective-permute-start(bf16[2,128,512]{2,1,0:T(8,128)(2,1)S(1)} %add_convert_fusion.5), channel_id=1, source_target_pairs={{0,16},{1,17},{2,18},{3,19},{4,20},{5,21},{6,22},{7,23},{8,24},{9,... | collective-permute-start | bytes 786440 | tf_op jit(solution)/shard_map/ppermute | solution.py:368
  221.9 8.2 %collective-permute-start.27 = (bf16[2,128,512]{2,1,0:T(8,128)(2,1)S(1)}, bf16[2,128,512]{2,1,0:T(8,128)(2,1)S(1)}, u32[]{:S(2)}, u32[]{:S(2)}) collective-permute-start(bf16[2,128,512]{2,1,0:T(8,128)(2,1)S(1)} %add_convert_fusion.4), channel_id=1, source_target_pairs={{0,8},{1,9},{2,10},{3,11},{4,12},{5,13},{6,14},{7,15},{8,0},{9,1},... | collective-permute-start | bytes 786440 | tf_op jit(solution)/shard_map/ppermute | solution.py:368
  230.2 8.3 %collective-permute-start.29 = (bf16[1,128,512]{2,1,0:T(8,128)(2,1)S(1)}, bf16[1,128,512]{2,1,0:T(8,128)(2,1)S(1)}, u32[]{:S(2)}, u32[]{:S(2)}) collective-permute-start(bf16[1,128,512]{2,1,0:T(8,128)(2,1)S(1)} %add_convert_fusion.7), channel_id=1, source_target_pairs={{0,16},{1,17},{2,18},{3,19},{4,20},{5,21},{6,22},{7,23},{8,24},{9,... | collective-permute-start | bytes 393224 | tf_op jit(solution)/shard_map/ppermute | solution.py:368
  230.4 8.3 %collective-permute-start.28 = (bf16[1,128,512]{2,1,0:T(8,128)(2,1)S(1)}, bf16[1,128,512]{2,1,0:T(8,128)(2,1)S(1)}, u32[]{:S(2)}, u32[]{:S(2)}) collective-permute-start(bf16[1,128,512]{2,1,0:T(8,128)(2,1)S(1)} %add_convert_fusion.8), channel_id=1, source_target_pairs={{0,4},{1,3},{2,6},{3,1},{4,0},{5,7},{6,2},{7,5},{8,12},{9,11},{10,... | collective-permute-start | bytes 393224 | tf_op jit(solution)/shard_map/ppermute | solution.py:368

commit v8 on v7

--- a/solution.py
+++ b/solution.py
@@ -434,7 +434,7 @@
 
     terms[0] = makers[0](None)
     terms[1] = makers[1](exchange(0, 0))
-    exchange(1, 0, came[0, 0])
+    exchange(1, 0)
     exchange(0, 1)
     exchange(1, 1, came[0, 1])
     exchange(0, 2)
@@ -471,19 +471,49 @@
         heads = jnp.concatenate([heads, came], axis=0)
 
 
-def route_table(route_ids, route_weights):
-    shares = route_weights / jnp.sum(route_weights, axis=-1, keepdims=True)
-    return jnp.concatenate([route_ids.astype(F32), shares], axis=1).T
+def pack_kernel(member_ref, residual_ref, ids_ref, weights_ref, out_ref):
+    groups, rows, lanes = out_ref.shape
+    here, width = residual_ref.shape
+    each = width // groups
+    rest = weights_ref[...] / jnp.sum(weights_ref[...], axis=0, keepdims=True)
+    parts = [ids_ref[...].astype(F32)]
+    for _ in range(3):
+        part = rest.astype(BF16).astype(F32)
+        parts.append(part)
+        rest = rest - part
+    table = jnp.concatenate(parts, axis=0).astype(BF16)
+    for group in range(groups):
+        column = pl.multiple_of(group * each + member_ref[0] * lanes, lanes)
+        out_ref[group, :here, :] = residual_ref[:, pl.ds(column, lanes)]
+        out_ref[group, here:, :] = table
+
+
+def pack(member, residual, route_ids, route_weights, groups):
+    here, top = route_ids.shape
+    vmem = pl.BlockSpec(memory_space=pltpu.VMEM)
+    return pl.pallas_call(
+        pack_kernel,
+        in_specs=[pl.BlockSpec(memory_space=pltpu.SMEM), vmem, vmem, vmem],
+        out_specs=vmem,
+        out_shape=jax.ShapeDtypeStruct((groups, here + 4 * top, LANES), BF16),
+        compiler_params=pltpu.CompilerParams(vmem_limit_bytes=16 * 1024 * 1024),
+        cost_estimate=pl.CostEstimate(
+            flops=0, bytes_accessed=3 * residual.size, transcendentals=0
+        ),
+        name="pack",
+    )(member.reshape(1), residual, route_ids.T, route_weights.T)
 
 
 def own_routes(table, group, experts):
-    groups, both, here = table.shape
-    top = both // 2
+    groups, rows, here = table.shape
+    top = rows // 4
     own = group * experts + jnp.arange(experts, dtype=jnp.int32)
-    ids = table[:, :top, :].astype(jnp.int32)
+    table = table.astype(F32).reshape(groups, 4, top, here)
+    ids = table[:, 0].astype(jnp.int32)
     match = ids[None] == own[:, None, None, None]
     named = jnp.any(match, axis=2)
-    weights = jnp.sum(jnp.where(match, table[None, :, top:, :], 0.0), axis=2)
+    shares = table[:, 1] + table[:, 2] + table[:, 3]
+    weights = jnp.sum(jnp.where(match, shares[None], 0.0), axis=2)
     span = PAIR * here
     order = jnp.arange(span)
     earlier = (order[:, None] < order[None, :]).astype(BF16)
@@ -514,7 +544,7 @@
     return jnp.concatenate([feature, swapped, jnp.stack([member, device >> 3])])
 
 
-def gather_blocks(first, second, make_table, own_tables):
+def gather_blocks(first, second):
     def along(bits, block):
         return flip(block, lambda core: bits)
 
@@ -527,9 +557,6 @@
     second_low = along(ZLOW, second)
     first, _ = after(joined(first, first_last), second_high)
     first_high = along(ZHIGH, first)
-    table = make_table(first_high)
-    for bits in (ZHIGH, ZLOW, Y):
-        table = joined(table, along(bits, table))
     second, first_high = after(joined(second, second_low), first_high)
     second_last = flip(second, last_axis)
     first = joined(first, first_high)
@@ -537,13 +564,12 @@
     second = joined(second, second_last)
     second_first = flip(second, first_axis)
     first_low, _ = after(first_low, second)
-    beside = own_tables(table)
-    first, (second_first, beside) = after(joined(first, first_low), (second_first, beside))
+    first = joined(first, first_low)
     first_first = flip(first, first_axis)
     return [
         [block, came, along(CORE, block), along(CORE, came)]
         for block, came in ((first, first_first), (second, second_first))
-    ] + [beside]
+    ]
 
 
 def per_device_tokens(
@@ -557,12 +583,13 @@
     rows = -(-PAIR * CAP // 16) * 16
     x_side, core, y_side = member >> 1, member & 1, group & 1
 
-    own_cols = lax.dynamic_index_in_dim(
-        residual.reshape(here, groups, members, LANES), member, 2, keepdims=False
-    )
     moved = lax.all_to_all(
-        jnp.transpose(own_cols, (1, 0, 2)), "expert", split_axis=0, concat_axis=0, tiled=True
-    ).reshape(groups // 2, 2, here, LANES)
+        pack(member, residual, route_ids, route_weights, groups),
+        "expert",
+        split_axis=0,
+        concat_axis=0,
+        tiled=True,
+    )
     gain = lax.dynamic_index_in_dim(
         norm_gain.reshape(groups * members, LANES), device, 0, keepdims=False
     )
@@ -573,6 +600,10 @@
     info = jnp.concatenate(
         [jnp.stack([core, x_side]), ((arrival & 1) << 2) | (arrival >> 1)]
     )
+    table = jnp.take(moved[:, here:], own_order(groups, group), axis=0, mode="clip")
+    moved = moved[:, :here].reshape(groups // 2, 2, here, LANES)
+    slots, weights = own_routes(table, group, experts)
+    info, (slots, weights) = after(info, (slots, weights))
     send, keep = project(info, pieces, out_proj)
     came = flip(send, lambda c: CORE)
     from_x = flip(total_of([keep[0], came[0]]).astype(BF16), lambda c: X)
@@ -584,16 +615,7 @@
         hidden = hidden + total_of([keep[1, window], came[1, window], from_x[window]])
         starts.append((hidden * gain).astype(BF16)[None])
 
-    def make_table(earlier):
-        ids, _ = after(route_ids, earlier)
-        return route_table(ids, route_weights)[None]
-
-    def own_tables(table):
-        apart = own_order(groups, group) ^ group
-        order = (apart >> 2) | (apart & 2) | ((apart & 1) << 2)
-        return own_routes(jnp.take(table, order, axis=0, mode="clip"), group, experts)
-
-    own_x, other_x, (slots, weights) = gather_blocks(*starts, make_table, own_tables)
+    own_x, other_x = gather_blocks(*starts)
     x = [piece for pair in zip(own_x, other_x) for piece in pair]
     invgain = (1.0 / norm_gain).reshape(groups * members, LANES)
     act, own_hidden, spread = gate_up(

time: 240 us -> 233 us (0.971)
  waiting for transfers between devices: 136 us -> 126 us
  starting transfers between devices: 35 us -> 39.7 us
  other arithmetic: 7.95 us -> 4.92 us
    ppermute x30 -> x27, waiting for transfers between devices: 132 us -> 119 us  [flip(): return lax.ppermute(array, ('expert', 'tensor'), pairs)]
    ppermute x30 -> x27, starting transfers between devices: 31.2 us -> 35.8 us  [flip(): return lax.ppermute(array, ('expert', 'tensor'), pairs)]
    all_to_all x1, waiting for transfers between devices: 3.88 us -> 6.93 us  [per_device_tokens(): lax.all_to_all(pack(member, residual, route_ids, route_weights, groups),...]
  transfers between devices with their start and end apart: 31 -> 28, of which waited for: 22 -> 22; matrix products, arithmetic and copies ran while one was open for 4% -> 2% of each run, Pallas kernels for 5% -> 6%
where the time goes in v8:
time: 233 us
  waiting for transfers between devices  126 us (54%)
  Pallas kernels  57.6 us (25%)
  starting transfers between devices  39.7 us (17%)
  other arithmetic  4.92 us (2%)
  local copies, waits for them, and re-layouts  3.98 us (2%)
    ppermute x27, waiting for transfers between devices, flip(): return lax.ppermute(array, ('expert', 'tensor'), pairs)  119 us
    ppermute x27, starting transfers between devices, flip(): return lax.ppermute(array, ('expert', 'tensor'), pairs)  35.8 us
    pallas_call x1, Pallas kernels, gate_up(): pl.pallas_call(kernel, grid_spec=pltpu.PrefetchScalarGridSpec(num_scalar_...  31.1 us
    pallas_call x3, Pallas kernels, down(): pl.pallas_call(functools.partial(down_kernel, rows), grid_spec=pltpu.Pref...  22.9 us
    all_to_all x1, waiting for transfers between devices, per_device_tokens(): lax.all_to_all(pack(member, residual, route_ids, route_weights, groups),...  6.93 us
  transfers between devices with their start and end apart: 28, of which 22 were waited for; matrix products, arithmetic and copies ran while one was open for 2% of the time, Pallas kernels for 6%

profile of v8, /device:TPU:0, one launch (start us, length us, event | category | flops | bytes accessed | tf_op | source)
XLA Modules:
  0.0 232.9 jit_solution(5492261721583074608)
XLA Ops:
  0.0 3.0 %collective-permute-start = (bf16[1,128,1024]{2,1,0:T(8,128)(2,1)}, bf16[1,128,1024]{2,1,0:T(8,128)(2,1)S(1)}, u32[]{:S(2)}, u32[]{:S(2)}) collective-permute-start(bf16[1,128,1024]{2,1,0:T(8,128)(2,1)} %bitcast.67), channel_id=1, source_target_pairs={{0,4},{1,17},{2,6},{3,19},{4,0},{5,21},{6,2},{7,23},{8,12},{9,25},... | collective-permute-start | bytes 786440 | tf_op jit(solution)/shard_map/ppermute | solution.py:368
  3.0 4.6 %collective-permute-done = bf16[1,128,1024]{2,1,0:T(8,128)(2,1)S(1)} collective-permute-done((bf16[1,128,1024]{2,1,0:T(8,128)(2,1)}, bf16[1,128,1024]{2,1,0:T(8,128)(2,1)S(1)}, u32[]{:S(2)}, u32[]{:S(2)}) %collective-permute-start) | collective-permute-done | bytes 262176 | tf_op jit(solution)/shard_map/ppermute | solution.py:368
  7.6 1.0 pad_maximum_fusion.1
  8.6 3.1 %collective-permute-start.1 = (bf16[2,128,1024]{2,1,0:T(8,128)(2,1)S(1)}, bf16[2,128,1024]{2,1,0:T(8,128)(2,1)S(1)}, u32[]{:S(2)}, u32[]{:S(2)}) collective-permute-start(bf16[2,128,1024]{2,1,0:T(8,128)(2,1)S(1)} %pad_maximum_fusion.1), channel_id=1, source_target_pairs={{0,16},{1,9},{2,18},{3,11},{4,20},{5,13},{6,22},{7,15},{8,24},{9,1... | collective-permute-start | bytes 1572872 | tf_op jit(solution)/shard_map/ppermute | solution.py:368
  11.7 1.2 copy-done
  12.9 0.7 copy-done.1
  13.6 0.7 copy-done.2
  14.3 0.8 pack.1
  15.1 3.9 %all-to-all-start = ((bf16[8,160,128]{2,1,0:T(8,128)(2,1)}), bf16[8,160,128]{2,1,0:T(8,128)(2,1)S(1)}, u32[]{:S(2)}, u32[]{:S(2)}) async-start(bf16[8,160,128]{2,1,0:T(8,128)(2,1)} %pack.1), calls=%async_computation | async-start | bytes 655360 | tf_op jit(solution)/shard_map/all_to_all | solution.py:586
  19.1 5.2 %collective-permute-done.1 = bf16[2,128,1024]{2,1,0:T(8,128)(2,1)S(1)} collective-permute-done((bf16[2,128,1024]{2,1,0:T(8,128)(2,1)S(1)}, bf16[2,128,1024]{2,1,0:T(8,128)(2,1)S(1)}, u32[]{:S(2)}, u32[]{:S(2)}) %collective-permute-start.1) | collective-permute-done | bytes 524320 | tf_op jit(solution)/shard_map/ppermute | solution.py:368
  24.4 6.9 %all-to-all-done = bf16[8,160,128]{2,1,0:T(8,128)(2,1)S(1)} async-done(((bf16[8,160,128]{2,1,0:T(8,128)(2,1)}), bf16[8,160,128]{2,1,0:T(8,128)(2,1)S(1)}, u32[]{:S(2)}, u32[]{:S(2)}) %all-to-all-start) | async-done | bytes 327712 | tf_op jit(solution)/shard_map/all_to_all | solution.py:586
  31.4 1.3 collective-permute-start.2
  32.8 0.6 gather_fusion
  33.4 0.2 compare_reduce_fusion
  33.9 12.3 %collective-permute-done.2.refs_1_ = bf16[4,128,1024]{2,1,0:T(8,128)(2,1)} collective-permute-done((bf16[4,128,1024]{2,1,0:T(8,128)(2,1)S(1)}, bf16[4,128,1024]{2,1,0:T(8,128)(2,1)}, u32[]{:S(2)}, u32[]{:S(2)}) %collective-permute-start.2) | collective-permute-done | bytes 1048608 | tf_op jit(solution)/shard_map/ppermute | solution.py:368
  46.3 2.8 %project.1 = (bf16[2,8,128,128]{3,2,1,0:T(8,128)(2,1)S(1)}, bf16[2,8,128,128]{3,2,1,0:T(8,128)(2,1)S(1)}) custom-call(s32[10]{0:T(128)S(1)} %pad_add_fusion.1.info_ref, bf16[4,128,1024]{2,1,0:T(8,128)(2,1)S(1)} %pad_maximum_fusion.refs_0_, bf16[4,128,1024]{2,1,0:T(8,128)(2,1)} %collective-permute-done.2.refs_1_, bf16[1024,512]{1,0:T(8,128)(2,1)S(1)} %copy-done.3), custom_call_target="tpu_custom_call" | custom-call | flops 1073741824 | bytes 5242880 | tf_op jit(solution)/shard_map/project/pallas_call | solution.py:112
  49.2 1.9 collective-permute-done.3
  51.1 2.0 collective-permute-start.4
  53.2 6.6 %collective-permute-done.4 = bf16[8,128,128]{2,1,0:T(8,128)(2,1)S(1)} collective-permute-done((bf16[8,128,128]{2,1,0:T(8,128)(2,1)S(1)}, bf16[8,128,128]{2,1,0:T(8,128)(2,1)S(1)}, u32[]{:S(2)}, u32[]{:S(2)}) %collective-permute-start.4) | collective-permute-done | bytes 262176 | tf_op jit(solution)/shard_map/ppermute | solution.py:368
  59.8 0.2 fusion.8
  59.9 3.5 %collective-permute-start.6 = (bf16[1,4,128,128]{3,2,1,0:T(8,128)(2,1)S(1)}, bf16[1,4,128,128]{3,2,1,0:T(8,128)(2,1)S(1)}, u32[]{:S(2)}, u32[]{:S(2)}) collective-permute-start(bf16[1,4,128,128]{3,2,1,0:T(8,128)(2,1)S(1)} %get-tuple-element.49), channel_id=1, source_target_pairs={{0,16},{1,17},{2,18},{3,19},{4,20},{5,21},{6,22},{7,23},{8,24},{9,... | collective-permute-start | bytes 393224 | tf_op jit(solution)/shard_map/ppermute | solution.py:368
  63.4 0.4 collective-permute-start.5
  63.8 5.3 %collective-permute-done.6 = bf16[1,4,128,128]{3,2,1,0:T(8,128)(2,1)S(1)} collective-permute-done((bf16[1,4,128,128]{3,2,1,0:T(8,128)(2,1)S(1)}, bf16[1,4,128,128]{3,2,1,0:T(8,128)(2,1)S(1)}, u32[]{:S(2)}, u32[]{:S(2)}) %collective-permute-start.6) | collective-permute-done | bytes 131104 | tf_op jit(solution)/shard_map/ppermute | solution.py:368
  69.2 0.3 collective-permute-start.7
  69.5 3.4 %collective-permute-start.8 = (bf16[2,4,128,128]{3,2,1,0:T(8,128)(2,1)S(1)}, bf16[2,4,128,128]{3,2,1,0:T(8,128)(2,1)S(1)}, u32[]{:S(2)}, u32[]{:S(2)}) collective-permute-start(bf16[2,4,128,128]{3,2,1,0:T(8,128)(2,1)S(1)} %pad_maximum_fusion.4), channel_id=1, source_target_pairs={{0,16},{1,17},{2,18},{3,19},{4,20},{5,21},{6,22},{7,23},{8,24},{9,... | collective-permute-start | bytes 786440 | tf_op jit(solution)/shard_map/ppermute | solution.py:368
  73.0 9.4 %collective-permute-done.7 = bf16[2,4,128,128]{3,2,1,0:T(8,128)(2,1)S(1)} collective-permute-done((bf16[2,4,128,128]{3,2,1,0:T(8,128)(2,1)S(1)}, bf16[2,4,128,128]{3,2,1,0:T(8,128)(2,1)S(1)}, u32[]{:S(2)}, u32[]{:S(2)}) %collective-permute-start.7) | collective-permute-done | bytes 262176 | tf_op jit(solution)/shard_map/ppermute | solution.py:368
  82.4 1.8 collective-permute-done.8
  84.3 1.4 collective-permute-start.10
  85.7 0.3 collective-permute-start.9
  86.1 7.3 %collective-permute-done.10 = bf16[4,4,128,128]{3,2,1,0:T(8,128)(2,1)S(1)} collective-permute-done((bf16[4,4,128,128]{3,2,1,0:T(8,128)(2,1)S(1)}, bf16[4,4,128,128]{3,2,1,0:T(8,128)(2,1)S(1)}, u32[]{:S(2)}, u32[]{:S(2)}) %collective-permute-start.10) | collective-permute-done | bytes 524320 | tf_op jit(solution)/shard_map/ppermute | solution.py:368
  93.5 3.2 %collective-permute-done.9 = bf16[4,4,128,128]{3,2,1,0:T(8,128)(2,1)S(1)} collective-permute-done((bf16[4,4,128,128]{3,2,1,0:T(8,128)(2,1)S(1)}, bf16[4,4,128,128]{3,2,1,0:T(8,128)(2,1)S(1)}, u32[]{:S(2)}, u32[]{:S(2)}) %collective-permute-start.9) | collective-permute-done | bytes 524320 | tf_op jit(solution)/shard_map/ppermute | solution.py:368
  96.7 0.6 collective-permute-start.11
  97.3 1.5 collective-permute-start.12
  98.8 0.5 collective-permute-start.14
  99.4 12.3 %collective-permute-done.11.rest_2_ = bf16[8,4,128,128]{3,2,1,0:T(8,128)(2,1)S(1)} collective-permute-done((bf16[8,4,128,128]{3,2,1,0:T(8,128)(2,1)S(1)}, bf16[8,4,128,128]{3,2,1,0:T(8,128)(2,1)S(1)}, u32[]{:S(2)}, u32[]{:S(2)}) %collective-permute-start.11) | collective-permute-done | bytes 1048608 | tf_op jit(solution)/shard_map/ppermute | solution.py:368
  111.6 11.3 %collective-permute-done.12.rest_3_ = bf16[8,4,128,128]{3,2,1,0:T(8,128)(2,1)} collective-permute-done((bf16[8,4,128,128]{3,2,1,0:T(8,128)(2,1)S(1)}, bf16[8,4,128,128]{3,2,1,0:T(8,128)(2,1)}, u32[]{:S(2)}, u32[]{:S(2)}) %collective-permute-start.12) | collective-permute-done | bytes 1048608 | tf_op jit(solution)/shard_map/ppermute | solution.py:368
  123.8 2.2 collective-permute-done.16.rest_7_
  126.0 31.1 %gate_up.1 = (bf16[8,192,384]{2,1,0:T(8,128)(2,1)S(1)}, f32[128,1024]{1,0:T(8,128)S(1)}, bf16[4,256,384]{2,1,0:T(8,128)(2,1)S(1)}) custom-call(s32[66]{0:T(128)S(1)} %pad_add_fusion.info_ref, s32[8,1024]{1,0:T(8,128)S(1)} %bitcast_select_fusion.slot_ref, f32[8,1024]{1,0:T(8,128)S(1)} %bitcast.63, f32[32,128]{1,0:T(8,128)S(1)} %divide_bitcast_fusion.invgain_ref, ...), custom_call_target="tpu_custom_call" | custom-call | flops 9663676416 | bytes 58720256 | tf_op jit(solution)/shard_map/gate_up/pallas_call | solution.py:261
  157.0 10.0 %down_mix.4 = (bf16[16,128,512]{2,1,0:T(8,128)(2,1)S(1)}, bf16[16,128,512]{2,1,0:T(8,128)(2,1)S(1)}) custom-call(s32[34]{0:T(128)S(1)} %pad_add_fusion.3.place_ref, bf16[4,256,384]{2,1,0:T(8,128)(2,1)S(1)} %get-tuple-element.39.spread_ref, bf16[8,192,384]{2,1,0:T(8,128)(2,1)S(1)} %get-tuple-element.40.act_ref, bf16[8,384,4096]{2,1,0:T(8,128)(2,1)} %wd1_ref.5, ...), custom_call_target="tpu_custom_call" | custom-call | flops 4831838208 | bytes 16777216 | tf_op jit(solution)/shard_map/down_mix/pallas_call | solution.py:337
  167.0 0.2 collective-permute-start.17
  167.2 0.4 collective-permute-start.21
  167.8 6.5 %down_mix.3 = bf16[16,128,512]{2,1,0:T(8,128)(2,1)S(1)} custom-call(s32[18]{0:T(128)S(1)} %pad_add_fusion.2.place_ref, bf16[4,256,384]{2,1,0:T(8,128)(2,1)S(1)} %get-tuple-element.39.spread_ref, bf16[8,192,384]{2,1,0:T(8,128)(2,1)S(1)} %get-tuple-element.40.act_ref, bf16[8,384,4096]{2,1,0:T(8,128)(2,1)} %wd1_ref.5, bf16[8,384,4096]{2,1,0:T(8,128)(2,1)} %wd1_ref.5), custom_call_target="tpu_custom_call" | custom-call | flops 2415919104 | bytes 8388608 | tf_op jit(solution)/shard_map/down_mix/pallas_call | solution.py:337
  174.3 0.3 add_convert_fusion.1
  174.6 0.6 collective-permute-start.18
  175.2 6.5 %down_mix.5 = bf16[16,128,512]{2,1,0:T(8,128)(2,1)S(1)} custom-call(s32[18]{0:T(128)S(1)} %pad_add_fusion.4.place_ref, bf16[4,256,384]{2,1,0:T(8,128)(2,1)S(1)} %get-tuple-element.39.spread_ref, bf16[8,192,384]{2,1,0:T(8,128)(2,1)S(1)} %get-tuple-element.40.act_ref, bf16[8,384,4096]{2,1,0:T(8,128)(2,1)} %wd1_ref.5, bf16[8,384,4096]{2,1,0:T(8,128)(2,1)} %wd1_ref.5), custom_call_target="tpu_custom_call" | custom-call | flops 2415919104 | bytes 8388608 | tf_op jit(solution)/shard_map/down_mix/pallas_call | solution.py:337
  181.7 0.3 add_convert_fusion
  182.0 1.6 collective-permute-start.22
  183.6 5.9 %collective-permute-done.18 = bf16[8,128,512]{2,1,0:T(8,128)(2,1)S(1)} collective-permute-done((bf16[8,128,512]{2,1,0:T(8,128)(2,1)S(1)}, bf16[8,128,512]{2,1,0:T(8,128)(2,1)S(1)}, u32[]{:S(2)}, u32[]{:S(2)}) %collective-permute-start.18) | collective-permute-done | bytes 1048608 | tf_op jit(solution)/shard_map/ppermute | solution.py:368
  189.5 0.2 add_convert_fusion.3
  189.7 1.7 collective-permute-start.19
  191.4 9.3 %collective-permute-done.22 = bf16[8,128,512]{2,1,0:T(8,128)(2,1)S(1)} collective-permute-done((bf16[8,128,512]{2,1,0:T(8,128)(2,1)S(1)}, bf16[8,128,512]{2,1,0:T(8,128)(2,1)S(1)}, u32[]{:S(2)}, u32[]{:S(2)}) %collective-permute-start.22) | collective-permute-done | bytes 1048608 | tf_op jit(solution)/shard_map/ppermute | solution.py:368
  200.7 0.2 add_convert_fusion.2
  201.0 2.0 collective-permute-done.19
  203.0 1.7 collective-permute-start.23
  204.9 2.6 %collective-permute-start.20 = (bf16[2,128,512]{2,1,0:T(8,128)(2,1)S(1)}, bf16[2,128,512]{2,1,0:T(8,128)(2,1)S(1)}, u32[]{:S(2)}, u32[]{:S(2)}) collective-permute-start(bf16[2,128,512]{2,1,0:T(8,128)(2,1)S(1)} %add_convert_fusion.5), channel_id=1, source_target_pairs={{0,16},{1,17},{2,18},{3,19},{4,20},{5,21},{6,22},{7,23},{8,24},{9,... | collective-permute-start | bytes 786440 | tf_op jit(solution)/shard_map/ppermute | solution.py:368
  207.4 4.7 %collective-permute-done.23 = bf16[4,128,512]{2,1,0:T(8,128)(2,1)S(1)} collective-permute-done((bf16[4,128,512]{2,1,0:T(8,128)(2,1)S(1)}, bf16[4,128,512]{2,1,0:T(8,128)(2,1)S(1)}, u32[]{:S(2)}, u32[]{:S(2)}) %collective-permute-start.23) | collective-permute-done | bytes 524320 | tf_op jit(solution)/shard_map/ppermute | solution.py:368
  212.3 4.4 %collective-permute-done.20 = bf16[2,128,512]{2,1,0:T(8,128)(2,1)S(1)} collective-permute-done((bf16[2,128,512]{2,1,0:T(8,128)(2,1)S(1)}, bf16[2,128,512]{2,1,0:T(8,128)(2,1)S(1)}, u32[]{:S(2)}, u32[]{:S(2)}) %collective-permute-start.20) | collective-permute-done | bytes 262176 | tf_op jit(solution)/shard_map/ppermute | solution.py:368
  216.7 0.6 collective-permute-start.24
  217.2 6.5 %collective-permute-done.24 = bf16[2,128,512]{2,1,0:T(8,128)(2,1)S(1)} collective-permute-done((bf16[2,128,512]{2,1,0:T(8,128)(2,1)S(1)}, bf16[2,128,512]{2,1,0:T(8,128)(2,1)S(1)}, u32[]{:S(2)}, u32[]{:S(2)}) %collective-permute-start.24) | collective-permute-done | bytes 262176 | tf_op jit(solution)/shard_map/ppermute | solution.py:368
  223.9 2.2 collective-permute-start.26
  226.1 2.9 %collective-permute-start.25 = (bf16[1,128,512]{2,1,0:T(8,128)(2,1)S(1)}, bf16[1,128,512]{2,1,0:T(8,128)(2,1)S(1)}, u32[]{:S(2)}, u32[]{:S(2)}) collective-permute-start(bf16[1,128,512]{2,1,0:T(8,128)(2,1)S(1)} %add_convert_fusion.8), channel_id=1, source_target_pairs={{0,4},{1,3},{2,6},{3,1},{4,0},{5,7},{6,2},{7,5},{8,12},{9,11},{10,... | collective-permute-start | bytes 393224 | tf_op jit(solution)/shard_map/ppermute | solution.py:368
  229.1 2.1 collective-permute-done.26
  231.3 0.7 collective-permute-done.25
  232.1 0.8 fusion
  (72 shorter events, 2.8 us)
Async XLA Ops:
  0.0 24.3 %copy-start.4 = (bf16[128,1024]{1,0:T(8,128)(2,1)S(1)}, bf16[128,1024]{1,0:T(8,128)(2,1)}, u32[]{:S(2)}) copy-start(bf16[128,1024]{1,0:T(8,128)(2,1)} %param.9) | copy-start | bytes 786436
  0.0 7.6 %collective-permute-start = (bf16[1,128,1024]{2,1,0:T(8,128)(2,1)}, bf16[1,128,1024]{2,1,0:T(8,128)(2,1)S(1)}, u32[]{:S(2)}, u32[]{:S(2)}) collective-permute-start(bf16[1,128,1024]{2,1,0:T(8,128)(2,1)} %bitcast.67), channel_id=1, source_target_pairs={{0,4},{1,17},{2,6},{3,19},{4,0},{5,21},{6,2},{7,23},{8,12},{9,25},... | collective-permute-start | bytes 786440 | tf_op jit(solution)/shard_map/ppermute | solution.py:368
  8.6 15.7 %collective-permute-start.1 = (bf16[2,128,1024]{2,1,0:T(8,128)(2,1)S(1)}, bf16[2,128,1024]{2,1,0:T(8,128)(2,1)S(1)}, u32[]{:S(2)}, u32[]{:S(2)}) collective-permute-start(bf16[2,128,1024]{2,1,0:T(8,128)(2,1)S(1)} %pad_maximum_fusion.1), channel_id=1, source_target_pairs={{0,16},{1,9},{2,18},{3,11},{4,20},{5,13},{6,22},{7,15},{8,24},{9,1... | collective-permute-start | bytes 1572872 | tf_op jit(solution)/shard_map/ppermute | solution.py:368
  11.7 1.2 copy-start
  12.9 0.7 copy-start.1
  13.6 0.7 copy-start.2
  15.1 31.2 %copy-start.3 = (bf16[1024,512]{1,0:T(8,128)(2,1)S(1)}, bf16[1024,512]{1,0:T(8,128)(2,1)}, u32[]{:S(2)}) copy-start(bf16[1024,512]{1,0:T(8,128)(2,1)} %refs_2_.1) | copy-start | bytes 3145732
  15.1 16.3 %all-to-all-start = ((bf16[8,160,128]{2,1,0:T(8,128)(2,1)}), bf16[8,160,128]{2,1,0:T(8,128)(2,1)S(1)}, u32[]{:S(2)}, u32[]{:S(2)}) async-start(bf16[8,160,128]{2,1,0:T(8,128)(2,1)} %pack.1), calls=%async_computation | async-start | bytes 655360 | tf_op jit(solution)/shard_map/all_to_all | solution.py:586
  31.4 14.9 %collective-permute-start.2 = (bf16[4,128,1024]{2,1,0:T(8,128)(2,1)S(1)}, bf16[4,128,1024]{2,1,0:T(8,128)(2,1)}, u32[]{:S(2)}, u32[]{:S(2)}) collective-permute-start(bf16[4,128,1024]{2,1,0:T(8,128)(2,1)S(1)} %pad_maximum_fusion.refs_0_), channel_id=1, source_target_pairs={{0,8},{1,5},{2,10},{3,7},{4,12},{5,1},{6,14},{7,3},{8,0},{9,13},{1... | collective-permute-start | bytes 3145736 | tf_op jit(solution)/shard_map/ppermute | solution.py:368
  33.9 19.2 %copy-start.5 = (f32[4096]{0:T(1024)S(1)}, f32[4096]{0:T(1024)}, u32[]{:S(2)}) copy-start(f32[4096]{0:T(1024)} %param.12) | copy-start | bytes 49156
  49.1 2.0 collective-permute-start.3
  51.1 8.6 %collective-permute-start.4 = (bf16[8,128,128]{2,1,0:T(8,128)(2,1)S(1)}, bf16[8,128,128]{2,1,0:T(8,128)(2,1)S(1)}, u32[]{:S(2)}, u32[]{:S(2)}) collective-permute-start(bf16[8,128,128]{2,1,0:T(8,128)(2,1)S(1)} %fusion.2), channel_id=1, source_target_pairs={{0,2},{1,3},{2,0},{3,1},{4,6},{5,7},{6,4},{7,5},{8,10},{9,11},{10,... | collective-permute-start | bytes 786440 | tf_op jit(solution)/shard_map/ppermute | solution.py:368
  59.9 9.3 %collective-permute-start.6 = (bf16[1,4,128,128]{3,2,1,0:T(8,128)(2,1)S(1)}, bf16[1,4,128,128]{3,2,1,0:T(8,128)(2,1)S(1)}, u32[]{:S(2)}, u32[]{:S(2)}) collective-permute-start(bf16[1,4,128,128]{3,2,1,0:T(8,128)(2,1)S(1)} %get-tuple-element.49), channel_id=1, source_target_pairs={{0,16},{1,17},{2,18},{3,19},{4,20},{5,21},{6,22},{7,23},{8,24},{9,... | collective-permute-start | bytes 393224 | tf_op jit(solution)/shard_map/ppermute | solution.py:368
  63.4 5.8 %collective-permute-start.5 = (bf16[1,4,128,128]{3,2,1,0:T(8,128)(2,1)S(1)}, bf16[1,4,128,128]{3,2,1,0:T(8,128)(2,1)S(1)}, u32[]{:S(2)}, u32[]{:S(2)}) collective-permute-start(bf16[1,4,128,128]{3,2,1,0:T(8,128)(2,1)S(1)} %get-tuple-element.50), channel_id=1, source_target_pairs={{0,4},{1,3},{2,6},{3,1},{4,0},{5,7},{6,2},{7,5},{8,12},{9,11},{10,... | collective-permute-start | bytes 393224 | tf_op jit(solution)/shard_map/ppermute | solution.py:368
  69.2 13.2 %collective-permute-start.7 = (bf16[2,4,128,128]{3,2,1,0:T(8,128)(2,1)S(1)}, bf16[2,4,128,128]{3,2,1,0:T(8,128)(2,1)S(1)}, u32[]{:S(2)}, u32[]{:S(2)}) collective-permute-start(bf16[2,4,128,128]{3,2,1,0:T(8,128)(2,1)S(1)} %pad_maximum_fusion.5), channel_id=1, source_target_pairs={{0,8},{1,9},{2,10},{3,11},{4,12},{5,13},{6,14},{7,15},{8,0},{9,1},... | collective-permute-start | bytes 786440 | tf_op jit(solution)/shard_map/ppermute | solution.py:368
  69.5 14.7 %collective-permute-start.8 = (bf16[2,4,128,128]{3,2,1,0:T(8,128)(2,1)S(1)}, bf16[2,4,128,128]{3,2,1,0:T(8,128)(2,1)S(1)}, u32[]{:S(2)}, u32[]{:S(2)}) collective-permute-start(bf16[2,4,128,128]{3,2,1,0:T(8,128)(2,1)S(1)} %pad_maximum_fusion.4), channel_id=1, source_target_pairs={{0,16},{1,17},{2,18},{3,19},{4,20},{5,21},{6,22},{7,23},{8,24},{9,... | collective-permute-start | bytes 786440 | tf_op jit(solution)/shard_map/ppermute | solution.py:368
  84.3 9.2 %collective-permute-start.10 = (bf16[4,4,128,128]{3,2,1,0:T(8,128)(2,1)S(1)}, bf16[4,4,128,128]{3,2,1,0:T(8,128)(2,1)S(1)}, u32[]{:S(2)}, u32[]{:S(2)}) collective-permute-start(bf16[4,4,128,128]{3,2,1,0:T(8,128)(2,1)S(1)} %pad_maximum_fusion.2), channel_id=1, source_target_pairs={{0,4},{1,3},{2,6},{3,1},{4,0},{5,7},{6,2},{7,5},{8,12},{9,11},{10,... | collective-permute-start | bytes 1572872 | tf_op jit(solution)/shard_map/ppermute | solution.py:368
  85.7 11.0 %collective-permute-start.9 = (bf16[4,4,128,128]{3,2,1,0:T(8,128)(2,1)S(1)}, bf16[4,4,128,128]{3,2,1,0:T(8,128)(2,1)S(1)}, u32[]{:S(2)}, u32[]{:S(2)}) collective-permute-start(bf16[4,4,128,128]{3,2,1,0:T(8,128)(2,1)S(1)} %pad_maximum_fusion.3), channel_id=1, source_target_pairs={{0,8},{1,9},{2,10},{3,11},{4,12},{5,13},{6,14},{7,15},{8,0},{9,1},... | collective-permute-start | bytes 1572872 | tf_op jit(solution)/shard_map/ppermute | solution.py:368
  96.7 14.9 %collective-permute-start.11 = (bf16[8,4,128,128]{3,2,1,0:T(8,128)(2,1)S(1)}, bf16[8,4,128,128]{3,2,1,0:T(8,128)(2,1)S(1)}, u32[]{:S(2)}, u32[]{:S(2)}) collective-permute-start(bf16[8,4,128,128]{3,2,1,0:T(8,128)(2,1)S(1)} %constant_dynamic-update-slice_fusion.2.rest_0_), channel_id=1, source_target_pairs={{0,2},{1,5},{2,0},{3,7},{4,6},{5,1},{6,4},{7,3},{8,10},{9,13},{10,... | collective-permute-start | bytes 3145736 | tf_op jit(solution)/shard_map/ppermute | solution.py:368
  97.3 25.6 %collective-permute-start.12 = (bf16[8,4,128,128]{3,2,1,0:T(8,128)(2,1)S(1)}, bf16[8,4,128,128]{3,2,1,0:T(8,128)(2,1)}, u32[]{:S(2)}, u32[]{:S(2)}) collective-permute-start(bf16[8,4,128,128]{3,2,1,0:T(8,128)(2,1)S(1)} %constant_dynamic-update-slice_fusion.rest_1_), channel_id=1, source_target_pairs={{0,2},{1,5},{2,0},{3,7},{4,6},{5,1},{6,4},{7,3},{8,10},{9,13},{10,... | collective-permute-start | bytes 3145736 | tf_op jit(solution)/shard_map/ppermute | solution.py:368
  98.8 24.9 %collective-permute-start.13 = (bf16[8,4,128,128]{3,2,1,0:T(8,128)(2,1)S(1)}, bf16[8,4,128,128]{3,2,1,0:T(8,128)(2,1)}, u32[]{:S(2)}, u32[]{:S(2)}) collective-permute-start(bf16[8,4,128,128]{3,2,1,0:T(8,128)(2,1)S(1)} %constant_dynamic-update-slice_fusion.2.rest_0_), channel_id=1, source_target_pairs={{0,1},{1,0},{2,3},{3,2},{4,5},{5,4},{6,7},{7,6},{8,9},{9,8},{10,11... | collective-permute-start | bytes 3145736 | tf_op jit(solution)/shard_map/ppermute | solution.py:368
  98.8 24.9 %collective-permute-start.14 = (bf16[8,4,128,128]{3,2,1,0:T(8,128)(2,1)S(1)}, bf16[8,4,128,128]{3,2,1,0:T(8,128)(2,1)}, u32[]{:S(2)}, u32[]{:S(2)}) collective-permute-start(bf16[8,4,128,128]{3,2,1,0:T(8,128)(2,1)S(1)} %constant_dynamic-update-slice_fusion.rest_1_), channel_id=1, source_target_pairs={{0,1},{1,0},{2,3},{3,2},{4,5},{5,4},{6,7},{7,6},{8,9},{9,8},{10,11... | collective-permute-start | bytes 3145736 | tf_op jit(solution)/shard_map/ppermute | solution.py:368
  111.6 12.2 %collective-permute-start.15 = (bf16[8,4,128,128]{3,2,1,0:T(8,128)(2,1)S(1)}, bf16[8,4,128,128]{3,2,1,0:T(8,128)(2,1)}, u32[]{:S(2)}, u32[]{:S(2)}) collective-permute-start(bf16[8,4,128,128]{3,2,1,0:T(8,128)(2,1)S(1)} %collective-permute-done.11.rest_2_), channel_id=1, source_target_pairs={{0,1},{1,0},{2,3},{3,2},{4,5},{5,4},{6,7},{7,6},{8,9},{9,8},{10,11... | collective-permute-start | bytes 3145736 | tf_op jit(solution)/shard_map/ppermute | solution.py:368
  123.0 3.0 %collective-permute-start.16 = (bf16[8,4,128,128]{3,2,1,0:T(8,128)(2,1)}, bf16[8,4,128,128]{3,2,1,0:T(8,128)(2,1)}, u32[]{:S(2)}, u32[]{:S(2)}) collective-permute-start(bf16[8,4,128,128]{3,2,1,0:T(8,128)(2,1)} %collective-permute-done.12.rest_3_), channel_id=1, source_target_pairs={{0,1},{1,0},{2,3},{3,2},{4,5},{5,4},{6,7},{7,6},{8,9},{9,8},{10,11... | collective-permute-start | bytes 3145736 | tf_op jit(solution)/shard_map/ppermute | solution.py:368
  167.0 7.3 %collective-permute-start.17 = (bf16[16,128,512]{2,1,0:T(8,128)(2,1)S(1)}, bf16[16,128,512]{2,1,0:T(8,128)(2,1)S(1)}, u32[]{:S(2)}, u32[]{:S(2)}) collective-permute-start(bf16[16,128,512]{2,1,0:T(8,128)(2,1)S(1)} %get-tuple-element.41), channel_id=1, source_target_pairs={{0,1},{1,0},{2,3},{3,2},{4,5},{5,4},{6,7},{7,6},{8,9},{9,8},{10,11... | collective-permute-start | bytes 6291464 | tf_op jit(solution)/shard_map/ppermute | solution.py:368
  167.2 14.5 %collective-permute-start.21 = (bf16[16,128,512]{2,1,0:T(8,128)(2,1)S(1)}, bf16[16,128,512]{2,1,0:T(8,128)(2,1)S(1)}, u32[]{:S(2)}, u32[]{:S(2)}) collective-permute-start(bf16[16,128,512]{2,1,0:T(8,128)(2,1)S(1)} %get-tuple-element.43), channel_id=1, source_target_pairs={{0,1},{1,0},{2,3},{3,2},{4,5},{5,4},{6,7},{7,6},{8,9},{9,8},{10,11... | collective-permute-start | bytes 6291464 | tf_op jit(solution)/shard_map/ppermute | solution.py:368
  174.6 14.9 %collective-permute-start.18 = (bf16[8,128,512]{2,1,0:T(8,128)(2,1)S(1)}, bf16[8,128,512]{2,1,0:T(8,128)(2,1)S(1)}, u32[]{:S(2)}, u32[]{:S(2)}) collective-permute-start(bf16[8,128,512]{2,1,0:T(8,128)(2,1)S(1)} %add_convert_fusion.1), channel_id=1, source_target_pairs={{0,2},{1,5},{2,0},{3,7},{4,6},{5,1},{6,4},{7,3},{8,10},{9,13},{10,... | collective-permute-start | bytes 3145736 | tf_op jit(solution)/shard_map/ppermute | solution.py:368
  182.0 18.7 %collective-permute-start.22 = (bf16[8,128,512]{2,1,0:T(8,128)(2,1)S(1)}, bf16[8,128,512]{2,1,0:T(8,128)(2,1)S(1)}, u32[]{:S(2)}, u32[]{:S(2)}) collective-permute-start(bf16[8,128,512]{2,1,0:T(8,128)(2,1)S(1)} %add_convert_fusion), channel_id=1, source_target_pairs={{0,2},{1,5},{2,0},{3,7},{4,6},{5,1},{6,4},{7,3},{8,10},{9,13},{10,... | collective-permute-start | bytes 3145736 | tf_op jit(solution)/shard_map/ppermute | solution.py:368
  189.7 13.3 %collective-permute-start.19 = (bf16[4,128,512]{2,1,0:T(8,128)(2,1)S(1)}, bf16[4,128,512]{2,1,0:T(8,128)(2,1)S(1)}, u32[]{:S(2)}, u32[]{:S(2)}) collective-permute-start(bf16[4,128,512]{2,1,0:T(8,128)(2,1)S(1)} %add_convert_fusion.3), channel_id=1, source_target_pairs={{0,8},{1,9},{2,10},{3,11},{4,12},{5,13},{6,14},{7,15},{8,0},{9,1},... | collective-permute-start | bytes 1572872 | tf_op jit(solution)/shard_map/ppermute | solution.py:368
  203.0 9.2 %collective-permute-start.23 = (bf16[4,128,512]{2,1,0:T(8,128)(2,1)S(1)}, bf16[4,128,512]{2,1,0:T(8,128)(2,1)S(1)}, u32[]{:S(2)}, u32[]{:S(2)}) collective-permute-start(bf16[4,128,512]{2,1,0:T(8,128)(2,1)S(1)} %add_convert_fusion.2), channel_id=1, source_target_pairs={{0,4},{1,3},{2,6},{3,1},{4,0},{5,7},{6,2},{7,5},{8,12},{9,11},{10,... | collective-permute-start | bytes 1572872 | tf_op jit(solution)/shard_map/ppermute | solution.py:368
  204.9 11.8 %collective-permute-start.20 = (bf16[2,128,512]{2,1,0:T(8,128)(2,1)S(1)}, bf16[2,128,512]{2,1,0:T(8,128)(2,1)S(1)}, u32[]{:S(2)}, u32[]{:S(2)}) collective-permute-start(bf16[2,128,512]{2,1,0:T(8,128)(2,1)S(1)} %add_convert_fusion.5), channel_id=1, source_target_pairs={{0,16},{1,17},{2,18},{3,19},{4,20},{5,21},{6,22},{7,23},{8,24},{9,... | collective-permute-start | bytes 786440 | tf_op jit(solution)/shard_map/ppermute | solution.py:368
  216.7 7.1 %collective-permute-start.24 = (bf16[2,128,512]{2,1,0:T(8,128)(2,1)S(1)}, bf16[2,128,512]{2,1,0:T(8,128)(2,1)S(1)}, u32[]{:S(2)}, u32[]{:S(2)}) collective-permute-start(bf16[2,128,512]{2,1,0:T(8,128)(2,1)S(1)} %add_convert_fusion.4), channel_id=1, source_target_pairs={{0,8},{1,9},{2,10},{3,11},{4,12},{5,13},{6,14},{7,15},{8,0},{9,1},... | collective-permute-start | bytes 786440 | tf_op jit(solution)/shard_map/ppermute | solution.py:368
  223.9 7.3 %collective-permute-start.26 = (bf16[1,128,512]{2,1,0:T(8,128)(2,1)S(1)}, bf16[1,128,512]{2,1,0:T(8,128)(2,1)S(1)}, u32[]{:S(2)}, u32[]{:S(2)}) collective-permute-start(bf16[1,128,512]{2,1,0:T(8,128)(2,1)S(1)} %add_convert_fusion.7), channel_id=1, source_target_pairs={{0,16},{1,17},{2,18},{3,19},{4,20},{5,21},{6,22},{7,23},{8,24},{9,... | collective-permute-start | bytes 393224 | tf_op jit(solution)/shard_map/ppermute | solution.py:368
  226.1 5.9 %collective-permute-start.25 = (bf16[1,128,512]{2,1,0:T(8,128)(2,1)S(1)}, bf16[1,128,512]{2,1,0:T(8,128)(2,1)S(1)}, u32[]{:S(2)}, u32[]{:S(2)}) collective-permute-start(bf16[1,128,512]{2,1,0:T(8,128)(2,1)S(1)} %add_convert_fusion.8), channel_id=1, source_target_pairs={{0,4},{1,3},{2,6},{3,1},{4,0},{5,7},{6,2},{7,5},{8,12},{9,11},{10,... | collective-permute-start | bytes 393224 | tf_op jit(solution)/shard_map/ppermute | solution.py:368

commit v9 on v8

--- a/solution.py
+++ b/solution.py
@@ -124,20 +124,26 @@
     )(info, *pieces, out_proj)
 
 
-def other_place(place):
-    return (place >> 1) | ((place & 1) << 2)
-
-
 def gate_up_kernel(
     experts, rows, width, info_ref, slot_ref, weight_ref, invgain_ref, x_refs, wg_ref, wu_ref,
     act_ref, hidden_ref, spread_ref, xs_ref, sq_ref, scale_ref, hits_ref
 ):
     expert = pl.program_id(0)
-    arrays = len(x_refs) // 2
-    each, parts, here, lanes = x_refs[0].shape
-    blocks = arrays * each
+    arrays = 4
+    own_refs = (x_refs[:arrays], x_refs[arrays : 2 * arrays])
+    other_refs = (x_refs[2 * arrays : 3 * arrays], x_refs[3 * arrays :])
+    parts, here, lanes = x_refs[0].shape[1:]
+    blocks = info_ref.shape[0] // 2 - 1
+    each = blocks // arrays
     span = 2 * here
     member, z = info_ref[2 * blocks], info_ref[2 * blocks + 1]
+
+    def block_at(array, last, high, low):
+        return (
+            array * each + low * 4 + high * 2 + last,
+            own_refs[low][array].at[high * 2 + last],
+            other_refs[last][array].at[low * 2 + high],
+        )
 
     @pl.when(expert == 0)
     def _():
@@ -155,62 +161,63 @@
                 hits_ref[1, part, window, :] = jnp.concatenate([second, first], axis=1)
             spread_ref[part] = jnp.transpose(hits_ref[0, part].astype(F32)).astype(BF16)
 
-        def pair_of_blocks(low, carry):
+        def pairs_of_blocks(high, carry):
             for array in range(arrays):
-                own, other = x_refs[2 * array], x_refs[2 * array + 1]
-                swapped = info_ref[blocks + array * each + low]
-                places = (low, low + each // 2)
-                features = [info_ref[array * each + place] for place in places]
-                for place, feature in zip(places, features):
-                    invgain = invgain_ref[pl.ds(feature, 1), :]
+                for last in range(2):
+                    pair = [block_at(array, last, high, low) for low in range(2)]
+                    swapped = info_ref[blocks + pair[0][0]]
+                    features = [info_ref[place] for place, _, _ in pair]
+                    for feature, (_, own, other) in zip(features, pair):
+                        invgain = invgain_ref[pl.ds(feature, 1), :]
+                        for part in range(parts):
+                            for half, block in enumerate((own, other)):
+                                value = block[part].astype(F32) * invgain
+                                sq_ref[swapped, part, half] += value * value
                     for part in range(parts):
-                        for half, block in enumerate(
-                            (own[place, part], other[other_place(place), part])
-                        ):
-                            value = block.astype(F32) * invgain
-                            sq_ref[swapped, part, half] += value * value
-
-                for part in range(parts):
-                    both = jnp.concatenate(
-                        [
-                            jnp.concatenate([own[place, part], other[other_place(place), part]])
-                            for place in places
-                        ],
-                        axis=1,
-                    )
-                    picked = jnp.dot(
-                        hits_ref[swapped, part], both, preferred_element_type=F32
-                    ).astype(BF16)
-                    for number, feature in enumerate(features):
-                        column = pl.multiple_of(feature * lanes, lanes)
-                        for e in range(experts):
-                            xs_ref[e, part * rows : (part + 1) * rows, pl.ds(column, lanes)] = (
-                                picked[
+                        both = jnp.concatenate(
+                            [
+                                jnp.concatenate([own[part], other[part]], axis=0)
+                                for _, own, other in pair
+                            ],
+                            axis=1,
+                        )
+                        picked = jnp.dot(
+                            hits_ref[swapped, part], both, preferred_element_type=F32
+                        ).astype(BF16)
+                        for number, feature in enumerate(features):
+                            column = pl.multiple_of(feature * lanes, lanes)
+                            for e in range(experts):
+                                xs_ref[
+                                    e, part * rows : (part + 1) * rows, pl.ds(column, lanes)
+                                ] = picked[
                                     e * rows : (e + 1) * rows, number * lanes : (number + 1) * lanes
                                 ]
+            return carry
+
+        lax.fori_loop(0, 2, pairs_of_blocks, 0)
+
+        def own_blocks(high, carry):
+            for array in range(arrays):
+                for last in range(2):
+                    for low in range(2):
+                        place, own, other = block_at(array, last, high, low)
+                        feature = info_ref[place]
+
+                        @pl.when(feature >> 3 == member)
+                        def _(place=place, feature=feature, own=own, other=other):
+                            mine = jnp.where(
+                                info_ref[blocks + place] == 0,
+                                own[z].astype(F32),
+                                other[z].astype(F32),
                             )
+                            column = pl.multiple_of((feature & 7) * lanes, lanes)
+                            hidden_ref[:, pl.ds(column, lanes)] = (
+                                mine * invgain_ref[pl.ds(feature, 1), :]
+                            )
+
             return carry
 
-        lax.fori_loop(0, each // 2, pair_of_blocks, 0)
-
-        def own_block(place, carry):
-            for array in range(arrays):
-                feature = info_ref[array * each + place]
-
-                @pl.when(feature >> 3 == member)
-                def _(array=array, feature=feature):
-                    own, other = x_refs[2 * array], x_refs[2 * array + 1]
-                    mine = jnp.where(
-                        info_ref[blocks + array * each + place] == 0,
-                        own[place, z].astype(F32),
-                        other[other_place(place), z].astype(F32),
-                    )
-                    column = pl.multiple_of((feature & 7) * lanes, lanes)
-                    hidden_ref[:, pl.ds(column, lanes)] = mine * invgain_ref[pl.ds(feature, 1), :]
-
-            return carry
-
-        lax.fori_loop(0, each, own_block, 0)
+        lax.fori_loop(0, 2, own_blocks, 0)
         pieces = [
             sq_ref[0, part, half] + sq_ref[1, part, 1 - half]
             for part in range(parts)
@@ -241,11 +248,10 @@
         act_ref[expert, part * rows : (part + 1) * rows, :] = act.astype(BF16)
 
 
-def gate_up(info, slots, weights, invgain, x, w_gate, w_up, rows):
+def gate_up(info, slots, weights, invgain, x, w_gate, w_up, rows, members):
     experts, width, hidden_units = w_gate.shape
-    each, parts, here, lanes = x[0].shape
+    parts, here, lanes = x[0].shape[1:]
     tokens = slots.shape[1]
-    members = width // (each * lanes)
 
     def kernel(info_ref, slot_ref, weight_ref, invgain_ref, *rest):
         gate_up_kernel(
@@ -421,26 +427,43 @@
 
 
 def reduce_chunks(makers):
-    terms, came = [None, None], {}
+    terms, sends, came = [None, None], [None, None], {}
+
+    def split_exchange(chunk):
+        whole = terms[chunk]
+        quarter = whole[0].shape[0] // 4
+        rows = [slice(i * quarter, (i + 1) * quarter) for i in range(4)]
+        bits_of = HALVING[ORDERS[chunk][0]]
+        early = total_of([term[rows[0]] for term in whole]).astype(BF16)
+        late = total_of([term[rows[1]] for term in whole]).astype(BF16)
+        early, late = after(early, late)
+        early_came = flip(early, bits_of)
+        late, early_came = after(late, early_came)
+        sends[chunk] = [term[rows[2]] for term in whole] + [early_came]
+        terms[chunk] = [term[rows[3]] for term in whole] + [flip(late, bits_of)]
 
     def exchange(chunk, stage, earlier=None):
-        half = terms[chunk][0].shape[0] // 2
-        sent = total_of([term[:half] for term in terms[chunk]]).astype(BF16)
+        if sends[chunk] is None:
+            half = terms[chunk][0].shape[0] // 2
+            sends[chunk] = [term[:half] for term in terms[chunk]]
+            terms[chunk] = [term[half:] for term in terms[chunk]]
+        sent = total_of(sends[chunk]).astype(BF16)
+        sends[chunk] = None
         if earlier is not None:
             sent, _ = after(sent, earlier)
         came[chunk, stage] = flip(sent, HALVING[ORDERS[chunk][stage]])
-        terms[chunk] = [term[half:] for term in terms[chunk]] + [came[chunk, stage]]
+        terms[chunk] = terms[chunk] + [came[chunk, stage]]
         return sent
 
     terms[0] = makers[0](None)
     terms[1] = makers[1](exchange(0, 0))
-    exchange(1, 0)
+    split_exchange(1)
     exchange(0, 1)
-    exchange(1, 1, came[0, 1])
+    exchange(1, 1)
     exchange(0, 2)
-    exchange(1, 2, came[0, 2])
-    exchange(0, 3, came[1, 2])
-    exchange(1, 3)
+    exchange(1, 2)
+    exchange(1, 3, came[0, 2])
+    exchange(0, 3)
     return [total_of([term[0] for term in chunk]) for chunk in terms]
 
 
@@ -461,14 +484,13 @@
 
 
 def gather_heads(heads, beside):
+    first, second, third = HEAD_STAGES
     heads = heads[None]
-    for number, bits_of in enumerate(HEAD_STAGES):
-        if number == len(HEAD_STAGES) - 1:
-            heads, beside = after(heads, beside)
-        came = flip(heads, bits_of)
-        if number == len(HEAD_STAGES) - 1:
-            return [heads, came], beside
-        heads = jnp.concatenate([heads, came], axis=0)
+    heads = jnp.concatenate([heads, flip(heads, first)], axis=0)
+    came = flip(heads, second)
+    early = flip(heads, third)
+    late, (early, beside) = after(came, (early, beside))
+    return [heads, came, early, flip(late, third)], beside
 
 
 def pack_kernel(member_ref, residual_ref, ids_ref, weights_ref, out_ref):
@@ -561,15 +583,18 @@
     second_last = flip(second, last_axis)
     first = joined(first, first_high)
     first_low = along(ZLOW, first)
-    second = joined(second, second_last)
-    second_first = flip(second, first_axis)
-    first_low, _ = after(first_low, second)
-    first = joined(first, first_low)
-    first_first = flip(first, first_axis)
-    return [
-        [block, came, along(CORE, block), along(CORE, came)]
-        for block, came in ((first, first_first), (second, second_first))
-    ]
+    halves = []
+    for early, late in ((first, first_low), (second, second_last)):
+        early_first = flip(early, first_axis)
+        late, early_first = after(late, early_first)
+        late_first = flip(late, first_axis)
+        halves.append(
+            [
+                [block, came, along(CORE, block), along(CORE, came)]
+                for block, came in ((early, early_first), (late, late_first))
+            ]
+        )
+    return halves
 
 
 def per_device_tokens(
@@ -615,11 +640,10 @@
         hidden = hidden + total_of([keep[1, window], came[1, window], from_x[window]])
         starts.append((hidden * gain).astype(BF16)[None])
 
-    own_x, other_x = gather_blocks(*starts)
-    x = [piece for pair in zip(own_x, other_x) for piece in pair]
+    x = [block for half in gather_blocks(*starts) for part in half for block in part]
     invgain = (1.0 / norm_gain).reshape(groups * members, LANES)
     act, own_hidden, spread = gate_up(
-        block_table(device, groups, member), slots, weights, invgain, x, w_gate, w_up, rows
+        block_table(device, groups, member), slots, weights, invgain, x, w_gate, w_up, rows, members
     )
 
     cols = width // members

time: 233 us -> 227 us (0.974)
  waiting for transfers between devices: 126 us -> 121 us
    ppermute x27 -> x35, waiting for transfers between devices: 119 us -> 115 us  [flip(): return lax.ppermute(array, ('expert', 'tensor'), pairs)]
    ppermute x27 -> x35, starting transfers between devices: 35.8 us -> 34.4 us  [flip(): return lax.ppermute(array, ('expert', 'tensor'), pairs)]
  transfers between devices with their start and end apart: 28 -> 36, of which waited for: 22 -> 19; matrix products, arithmetic and copies ran while one was open for 2% -> 1% of each run, Pallas kernels for 6% -> 6%
where the time goes in v9:
time: 227 us; the launch traced here: 226 us
  waiting for transfers between devices  121 us (53%)
  Pallas kernels  56.5 us (25%)
  starting transfers between devices  39.2 us (17%)
  local copies, waits for them, and re-layouts  4.84 us (2%)
  other arithmetic  3.82 us (2%)
    ppermute x35, waiting for transfers between devices, flip(): return lax.ppermute(array, ('expert', 'tensor'), pairs)  115 us
    ppermute x35, starting transfers between devices, flip(): return lax.ppermute(array, ('expert', 'tensor'), pairs)  34.4 us
    pallas_call x1, Pallas kernels, gate_up(): pl.pallas_call(kernel, grid_spec=pltpu.PrefetchScalarGridSpec(num_scalar_...  30.1 us
    pallas_call x3, Pallas kernels, down(): pl.pallas_call(functools.partial(down_kernel, rows), grid_spec=pltpu.Pref...  22.9 us
    all_to_all x1, waiting for transfers between devices, per_device_tokens(): lax.all_to_all(pack(member, residual, route_ids, route_weights, groups),...  6.35 us
    all_to_all x1, starting transfers between devices, per_device_tokens(): lax.all_to_all(pack(member, residual, route_ids, route_weights, groups),...  4.88 us
  transfers between devices with their start and end apart: 36, of which 19 were waited for; matrix products, arithmetic and copies ran while one was open for 1% of the time, Pallas kernels for 6%

profile of v9, /device:TPU:0, one launch (start us, length us, event | category | flops | bytes accessed | tf_op | source)
XLA Modules:
  0.0 226.1 jit_solution(2947734894275554409)
XLA Ops:
  0.0 3.0 %collective-permute-start = (bf16[1,128,1024]{2,1,0:T(8,128)(2,1)}, bf16[1,128,1024]{2,1,0:T(8,128)(2,1)S(1)}, u32[]{:S(2)}, u32[]{:S(2)}) collective-permute-start(bf16[1,128,1024]{2,1,0:T(8,128)(2,1)} %bitcast.67), channel_id=1, source_target_pairs={{0,4},{1,17},{2,6},{3,19},{4,0},{5,21},{6,2},{7,23},{8,12},{9,25},... | collective-permute-start | bytes 786440 | tf_op jit(solution)/shard_map/ppermute | solution.py:374
  3.0 1.2 copy-done
  4.2 0.7 copy-done.1
  4.9 0.7 copy-done.2
  5.6 0.8 pack.1
  6.4 4.9 %all-to-all-start = ((bf16[8,160,128]{2,1,0:T(8,128)(2,1)}), bf16[8,160,128]{2,1,0:T(8,128)(2,1)S(1)}, u32[]{:S(2)}, u32[]{:S(2)}) async-start(bf16[8,160,128]{2,1,0:T(8,128)(2,1)} %pack.1), calls=%async_computation | async-start | bytes 655360 | tf_op jit(solution)/shard_map/all_to_all | solution.py:611
  11.3 2.1 collective-permute-start.2
  13.4 2.4 %collective-permute-start.1 = (bf16[2,128,1024]{2,1,0:T(8,128)(2,1)S(1)}, bf16[2,128,1024]{2,1,0:T(8,128)(2,1)S(1)}, u32[]{:S(2)}, u32[]{:S(2)}) collective-permute-start(bf16[2,128,1024]{2,1,0:T(8,128)(2,1)S(1)} %pad_maximum_fusion.refs_0_), channel_id=1, source_target_pairs={{0,16},{1,9},{2,18},{3,11},{4,20},{5,13},{6,22},{7,15},{8,24},{9,1... | collective-permute-start | bytes 1572872 | tf_op jit(solution)/shard_map/ppermute | solution.py:374
  15.9 6.4 %all-to-all-done = bf16[8,160,128]{2,1,0:T(8,128)(2,1)S(1)} async-done(((bf16[8,160,128]{2,1,0:T(8,128)(2,1)}), bf16[8,160,128]{2,1,0:T(8,128)(2,1)S(1)}, u32[]{:S(2)}, u32[]{:S(2)}) %all-to-all-start) | async-done | bytes 327712 | tf_op jit(solution)/shard_map/all_to_all | solution.py:611
  22.2 13.7 %collective-permute-done.2.refs_2_ = bf16[2,128,1024]{2,1,0:T(8,128)(2,1)S(1)} collective-permute-done((bf16[2,128,1024]{2,1,0:T(8,128)(2,1)S(1)}, bf16[2,128,1024]{2,1,0:T(8,128)(2,1)S(1)}, u32[]{:S(2)}, u32[]{:S(2)}) %collective-permute-start.2) | collective-permute-done | bytes 524320 | tf_op jit(solution)/shard_map/ppermute | solution.py:374
  36.0 0.6 gather_fusion
  36.6 1.9 collective-permute-start.3
  39.0 6.9 %collective-permute-done.3.refs_3_ = bf16[2,128,1024]{2,1,0:T(8,128)(2,1)} collective-permute-done((bf16[2,128,1024]{2,1,0:T(8,128)(2,1)S(1)}, bf16[2,128,1024]{2,1,0:T(8,128)(2,1)}, u32[]{:S(2)}, u32[]{:S(2)}) %collective-permute-start.3) | collective-permute-done | bytes 524320 | tf_op jit(solution)/shard_map/ppermute | solution.py:374
  45.9 1.0 copy-done.5
  47.0 2.6 %project.1 = (bf16[2,8,128,128]{3,2,1,0:T(8,128)(2,1)S(1)}, bf16[2,8,128,128]{3,2,1,0:T(8,128)(2,1)S(1)}) custom-call(s32[10]{0:T(128)S(1)} %pad_add_fusion.1.info_ref, bf16[2,128,1024]{2,1,0:T(8,128)(2,1)S(1)} %pad_maximum_fusion.refs_0_, bf16[2,128,1024]{2,1,0:T(8,128)(2,1)S(1)} %copy-done.5, bf16[2,128,1024]{2,1,0:T(8,128)(2,1)S(1)} %collective-permute-done.2.refs_2_, ...), custom_call_target="tpu_custom_call" | custom-call | flops 1073741824 | bytes 5242880 | tf_op jit(solution)/shard_map/project/pallas_call | solution.py:112
  49.7 1.9 collective-permute-done.4
  51.7 1.6 collective-permute-start.5
  53.3 6.8 %collective-permute-done.5 = bf16[8,128,128]{2,1,0:T(8,128)(2,1)S(1)} collective-permute-done((bf16[8,128,128]{2,1,0:T(8,128)(2,1)S(1)}, bf16[8,128,128]{2,1,0:T(8,128)(2,1)S(1)}, u32[]{:S(2)}, u32[]{:S(2)}) %collective-permute-start.5) | collective-permute-done | bytes 262176 | tf_op jit(solution)/shard_map/ppermute | solution.py:374
  60.1 0.2 fusion.8
  60.2 0.7 collective-permute-start.7
  61.0 1.7 collective-permute-start.6
  62.7 6.0 %collective-permute-done.7 = bf16[1,4,128,128]{3,2,1,0:T(8,128)(2,1)S(1)} collective-permute-done((bf16[1,4,128,128]{3,2,1,0:T(8,128)(2,1)S(1)}, bf16[1,4,128,128]{3,2,1,0:T(8,128)(2,1)S(1)}, u32[]{:S(2)}, u32[]{:S(2)}) %collective-permute-start.7) | collective-permute-done | bytes 131104 | tf_op jit(solution)/shard_map/ppermute | solution.py:374
  68.9 2.1 collective-permute-start.9
  71.1 8.6 %collective-permute-done.8 = bf16[2,4,128,128]{3,2,1,0:T(8,128)(2,1)S(1)} collective-permute-done((bf16[2,4,128,128]{3,2,1,0:T(8,128)(2,1)S(1)}, bf16[2,4,128,128]{3,2,1,0:T(8,128)(2,1)S(1)}, u32[]{:S(2)}, u32[]{:S(2)}) %collective-permute-start.8) | collective-permute-done | bytes 262176 | tf_op jit(solution)/shard_map/ppermute | solution.py:374
  79.7 3.1 %collective-permute-done.9 = bf16[2,4,128,128]{3,2,1,0:T(8,128)(2,1)S(1)} collective-permute-done((bf16[2,4,128,128]{3,2,1,0:T(8,128)(2,1)S(1)}, bf16[2,4,128,128]{3,2,1,0:T(8,128)(2,1)S(1)}, u32[]{:S(2)}, u32[]{:S(2)}) %collective-permute-start.9) | collective-permute-done | bytes 262176 | tf_op jit(solution)/shard_map/ppermute | solution.py:374
  82.8 1.6 collective-permute-start.11
  84.4 0.2 collective-permute-start.10
  84.6 0.5 collective-permute-start.18
  85.1 1.7 collective-permute-start.17
  87.1 10.4 %collective-permute-done.11.rest_1_ = bf16[4,4,128,128]{3,2,1,0:T(8,128)(2,1)S(1)} collective-permute-done((bf16[4,4,128,128]{3,2,1,0:T(8,128)(2,1)S(1)}, bf16[4,4,128,128]{3,2,1,0:T(8,128)(2,1)S(1)}, u32[]{:S(2)}, u32[]{:S(2)}) %collective-permute-start.11) | collective-permute-done | bytes 524320 | tf_op jit(solution)/shard_map/ppermute | solution.py:374
  97.5 0.5 collective-permute-start.13
  98.0 5.1 %collective-permute-done.18.rest_9_ = bf16[4,4,128,128]{3,2,1,0:T(8,128)(2,1)S(1)} collective-permute-done((bf16[4,4,128,128]{3,2,1,0:T(8,128)(2,1)S(1)}, bf16[4,4,128,128]{3,2,1,0:T(8,128)(2,1)S(1)}, u32[]{:S(2)}, u32[]{:S(2)}) %collective-permute-start.18) | collective-permute-done | bytes 524320 | tf_op jit(solution)/shard_map/ppermute | solution.py:374
  103.1 1.5 collective-permute-start.14
  104.6 0.5 collective-permute-start.21
  105.7 0.5 collective-permute-start.22
  106.2 6.1 %collective-permute-done.14.rest_5_ = bf16[4,4,128,128]{3,2,1,0:T(8,128)(2,1)} collective-permute-done((bf16[4,4,128,128]{3,2,1,0:T(8,128)(2,1)S(1)}, bf16[4,4,128,128]{3,2,1,0:T(8,128)(2,1)}, u32[]{:S(2)}, u32[]{:S(2)}) %collective-permute-start.14) | collective-permute-done | bytes 524320 | tf_op jit(solution)/shard_map/ppermute | solution.py:374
  112.4 5.6 %collective-permute-done.21.rest_13_ = bf16[4,4,128,128]{3,2,1,0:T(8,128)(2,1)} collective-permute-done((bf16[4,4,128,128]{3,2,1,0:T(8,128)(2,1)S(1)}, bf16[4,4,128,128]{3,2,1,0:T(8,128)(2,1)}, u32[]{:S(2)}, u32[]{:S(2)}) %collective-permute-start.21) | collective-permute-done | bytes 524320 | tf_op jit(solution)/shard_map/ppermute | solution.py:374
  118.1 2.0 collective-permute-done.23.rest_15_
  120.1 30.1 %gate_up.1 = (bf16[8,192,384]{2,1,0:T(8,128)(2,1)S(1)}, f32[128,1024]{1,0:T(8,128)S(1)}, bf16[4,256,384]{2,1,0:T(8,128)(2,1)S(1)}) custom-call(s32[66]{0:T(128)S(1)} %pad_add_fusion.info_ref, s32[8,1024]{1,0:T(8,128)S(1)} %bitcast_select_fusion.slot_ref, f32[8,1024]{1,0:T(8,128)S(1)} %bitcast.63, f32[32,128]{1,0:T(8,128)S(1)} %divide_bitcast_fusion.invgain_ref, ...), custom_call_target="tpu_custom_call" | custom-call | flops 9663676416 | bytes 58720256 | tf_op jit(solution)/shard_map/gate_up/pallas_call | solution.py:267
  150.3 10.0 %down_mix.4 = (bf16[16,128,512]{2,1,0:T(8,128)(2,1)S(1)}, bf16[16,128,512]{2,1,0:T(8,128)(2,1)S(1)}) custom-call(s32[34]{0:T(128)S(1)} %pad_add_fusion.3.place_ref, bf16[4,256,384]{2,1,0:T(8,128)(2,1)S(1)} %get-tuple-element.49.spread_ref, bf16[8,192,384]{2,1,0:T(8,128)(2,1)S(1)} %get-tuple-element.50.act_ref, bf16[8,384,4096]{2,1,0:T(8,128)(2,1)} %wd1_ref.5, ...), custom_call_target="tpu_custom_call" | custom-call | flops 4831838208 | bytes 16777216 | tf_op jit(solution)/shard_map/down_mix/pallas_call | solution.py:343
  160.2 0.2 collective-permute-start.24
  160.4 0.4 collective-permute-start.29
  161.0 6.5 %down_mix.3 = bf16[16,128,512]{2,1,0:T(8,128)(2,1)S(1)} custom-call(s32[18]{0:T(128)S(1)} %pad_add_fusion.2.place_ref, bf16[4,256,384]{2,1,0:T(8,128)(2,1)S(1)} %get-tuple-element.49.spread_ref, bf16[8,192,384]{2,1,0:T(8,128)(2,1)S(1)} %get-tuple-element.50.act_ref, bf16[8,384,4096]{2,1,0:T(8,128)(2,1)} %wd1_ref.5, bf16[8,384,4096]{2,1,0:T(8,128)(2,1)} %wd1_ref.5), custom_call_target="tpu_custom_call" | custom-call | flops 2415919104 | bytes 8388608 | tf_op jit(solution)/shard_map/down_mix/pallas_call | solution.py:343
  167.4 0.3 add_convert_fusion
  167.8 1.6 collective-permute-start.25
  169.4 6.5 %down_mix.5 = bf16[16,128,512]{2,1,0:T(8,128)(2,1)S(1)} custom-call(s32[18]{0:T(128)S(1)} %pad_add_fusion.4.place_ref, bf16[4,256,384]{2,1,0:T(8,128)(2,1)S(1)} %get-tuple-element.49.spread_ref, bf16[8,192,384]{2,1,0:T(8,128)(2,1)S(1)} %get-tuple-element.50.act_ref, bf16[8,384,4096]{2,1,0:T(8,128)(2,1)} %wd1_ref.5, bf16[8,384,4096]{2,1,0:T(8,128)(2,1)} %wd1_ref.5), custom_call_target="tpu_custom_call" | custom-call | flops 2415919104 | bytes 8388608 | tf_op jit(solution)/shard_map/down_mix/pallas_call | solution.py:343
  175.9 0.3 add_convert_fusion.2
  176.2 0.6 collective-permute-start.30
  176.8 11.4 %collective-permute-done.30 = bf16[4,128,512]{2,1,0:T(8,128)(2,1)S(1)} collective-permute-done((bf16[4,128,512]{2,1,0:T(8,128)(2,1)S(1)}, bf16[4,128,512]{2,1,0:T(8,128)(2,1)S(1)}, u32[]{:S(2)}, u32[]{:S(2)}) %collective-permute-start.30) | collective-permute-done | bytes 524320 | tf_op jit(solution)/shard_map/ppermute | solution.py:374
  188.3 0.2 add_convert_fusion.4
  188.5 0.4 collective-permute-start.26
  188.9 0.2 add_convert_fusion.1
  189.1 1.7 collective-permute-start.32
  190.8 1.5 collective-permute-start.31
  192.3 9.4 %collective-permute-done.26 = bf16[4,128,512]{2,1,0:T(8,128)(2,1)S(1)} collective-permute-done((bf16[4,128,512]{2,1,0:T(8,128)(2,1)S(1)}, bf16[4,128,512]{2,1,0:T(8,128)(2,1)S(1)}, u32[]{:S(2)}, u32[]{:S(2)}) %collective-permute-start.26) | collective-permute-done | bytes 524320 | tf_op jit(solution)/shard_map/ppermute | solution.py:374
  201.8 1.1 collective-permute-start.27
  202.9 0.3 collective-permute-done.32
  203.4 1.8 collective-permute-start.33
  205.1 9.7 %collective-permute-done.27 = bf16[2,128,512]{2,1,0:T(8,128)(2,1)S(1)} collective-permute-done((bf16[2,128,512]{2,1,0:T(8,128)(2,1)S(1)}, bf16[2,128,512]{2,1,0:T(8,128)(2,1)S(1)}, u32[]{:S(2)}, u32[]{:S(2)}) %collective-permute-start.27) | collective-permute-done | bytes 262176 | tf_op jit(solution)/shard_map/ppermute | solution.py:374
  214.9 1.7 collective-permute-start.28
  216.7 0.6 collective-permute-start.34
  217.3 2.7 %collective-permute-done.28 = bf16[1,128,512]{2,1,0:T(8,128)(2,1)S(1)} collective-permute-done((bf16[1,128,512]{2,1,0:T(8,128)(2,1)S(1)}, bf16[1,128,512]{2,1,0:T(8,128)(2,1)S(1)}, u32[]{:S(2)}, u32[]{:S(2)}) %collective-permute-start.28) | collective-permute-done | bytes 131104 | tf_op jit(solution)/shard_map/ppermute | solution.py:374
  220.0 5.2 %collective-permute-done.34 = bf16[1,128,512]{2,1,0:T(8,128)(2,1)S(1)} collective-permute-done((bf16[1,128,512]{2,1,0:T(8,128)(2,1)S(1)}, bf16[1,128,512]{2,1,0:T(8,128)(2,1)S(1)}, u32[]{:S(2)}, u32[]{:S(2)}) %collective-permute-start.34) | collective-permute-done | bytes 131104 | tf_op jit(solution)/shard_map/ppermute | solution.py:374
  225.3 0.8 fusion
  (87 shorter events, 2.9 us)
Async XLA Ops:
  0.0 11.3 %collective-permute-start = (bf16[1,128,1024]{2,1,0:T(8,128)(2,1)}, bf16[1,128,1024]{2,1,0:T(8,128)(2,1)S(1)}, u32[]{:S(2)}, u32[]{:S(2)}) collective-permute-start(bf16[1,128,1024]{2,1,0:T(8,128)(2,1)} %bitcast.67), channel_id=1, source_target_pairs={{0,4},{1,17},{2,6},{3,19},{4,0},{5,21},{6,2},{7,23},{8,12},{9,25},... | collective-permute-start | bytes 786440 | tf_op jit(solution)/shard_map/ppermute | solution.py:374
  3.0 1.2 copy-start
  4.2 0.7 copy-start.1
  4.9 0.7 copy-start.2
  5.6 5.7 %copy-start.6 = (bf16[128,1024]{1,0:T(8,128)(2,1)S(1)}, bf16[128,1024]{1,0:T(8,128)(2,1)}, u32[]{:S(2)}) copy-start(bf16[128,1024]{1,0:T(8,128)(2,1)} %param.9) | copy-start | bytes 786436
  5.6 40.4 %copy-start.3 = (bf16[1024,512]{1,0:T(8,128)(2,1)S(1)}, bf16[1024,512]{1,0:T(8,128)(2,1)}, u32[]{:S(2)}) copy-start(bf16[1024,512]{1,0:T(8,128)(2,1)} %refs_4_.1) | copy-start | bytes 3145732
  6.4 15.9 %all-to-all-start = ((bf16[8,160,128]{2,1,0:T(8,128)(2,1)}), bf16[8,160,128]{2,1,0:T(8,128)(2,1)S(1)}, u32[]{:S(2)}, u32[]{:S(2)}) async-start(bf16[8,160,128]{2,1,0:T(8,128)(2,1)} %pack.1), calls=%async_computation | async-start | bytes 655360 | tf_op jit(solution)/shard_map/all_to_all | solution.py:611
  11.3 24.6 %collective-permute-start.2 = (bf16[2,128,1024]{2,1,0:T(8,128)(2,1)S(1)}, bf16[2,128,1024]{2,1,0:T(8,128)(2,1)S(1)}, u32[]{:S(2)}, u32[]{:S(2)}) collective-permute-start(bf16[2,128,1024]{2,1,0:T(8,128)(2,1)S(1)} %pad_maximum_fusion.refs_0_), channel_id=1, source_target_pairs={{0,8},{1,5},{2,10},{3,7},{4,12},{5,1},{6,14},{7,3},{8,0},{9,13},{1... | collective-permute-start | bytes 1572872 | tf_op jit(solution)/shard_map/ppermute | solution.py:374
  13.4 22.6 %collective-permute-start.1 = (bf16[2,128,1024]{2,1,0:T(8,128)(2,1)S(1)}, bf16[2,128,1024]{2,1,0:T(8,128)(2,1)S(1)}, u32[]{:S(2)}, u32[]{:S(2)}) collective-permute-start(bf16[2,128,1024]{2,1,0:T(8,128)(2,1)S(1)} %pad_maximum_fusion.refs_0_), channel_id=1, source_target_pairs={{0,16},{1,9},{2,18},{3,11},{4,20},{5,13},{6,22},{7,15},{8,24},{9,1... | collective-permute-start | bytes 1572872 | tf_op jit(solution)/shard_map/ppermute | solution.py:374
  36.0 3.1 %copy-start.4 = (bf16[2,128,1024]{2,1,0:T(8,128)(2,1)}, bf16[2,128,1024]{2,1,0:T(8,128)(2,1)S(1)}, u32[]{:S(2)}) copy-start(bf16[2,128,1024]{2,1,0:T(8,128)(2,1)S(1)} %collective-permute-done.1.refs_1_) | copy-start | bytes 1572868
  36.6 9.4 %collective-permute-start.3 = (bf16[2,128,1024]{2,1,0:T(8,128)(2,1)S(1)}, bf16[2,128,1024]{2,1,0:T(8,128)(2,1)}, u32[]{:S(2)}, u32[]{:S(2)}) collective-permute-start(bf16[2,128,1024]{2,1,0:T(8,128)(2,1)S(1)} %collective-permute-done.1.refs_1_), channel_id=1, source_target_pairs={{0,8},{1,5},{2,10},{3,7},{4,12},{5,1},{6,14},{7,3},{8,0},{9,13},{1... | collective-permute-start | bytes 1572872 | tf_op jit(solution)/shard_map/ppermute | solution.py:374
  45.9 1.0 copy-start.5
  47.0 6.3 %copy-start.7 = (f32[4096]{0:T(1024)S(1)}, f32[4096]{0:T(1024)}, u32[]{:S(2)}) copy-start(f32[4096]{0:T(1024)} %param.12) | copy-start | bytes 49156
  49.6 2.0 collective-permute-start.4
  51.7 8.4 %collective-permute-start.5 = (bf16[8,128,128]{2,1,0:T(8,128)(2,1)S(1)}, bf16[8,128,128]{2,1,0:T(8,128)(2,1)S(1)}, u32[]{:S(2)}, u32[]{:S(2)}) collective-permute-start(bf16[8,128,128]{2,1,0:T(8,128)(2,1)S(1)} %fusion.2), channel_id=1, source_target_pairs={{0,2},{1,3},{2,0},{3,1},{4,6},{5,7},{6,4},{7,5},{8,10},{9,11},{10,... | collective-permute-start | bytes 786440 | tf_op jit(solution)/shard_map/ppermute | solution.py:374
  60.2 8.5 %collective-permute-start.7 = (bf16[1,4,128,128]{3,2,1,0:T(8,128)(2,1)S(1)}, bf16[1,4,128,128]{3,2,1,0:T(8,128)(2,1)S(1)}, u32[]{:S(2)}, u32[]{:S(2)}) collective-permute-start(bf16[1,4,128,128]{3,2,1,0:T(8,128)(2,1)S(1)} %get-tuple-element.63), channel_id=1, source_target_pairs={{0,16},{1,17},{2,18},{3,19},{4,20},{5,21},{6,22},{7,23},{8,24},{9,... | collective-permute-start | bytes 393224 | tf_op jit(solution)/shard_map/ppermute | solution.py:374
  61.0 7.8 %collective-permute-start.6 = (bf16[1,4,128,128]{3,2,1,0:T(8,128)(2,1)S(1)}, bf16[1,4,128,128]{3,2,1,0:T(8,128)(2,1)S(1)}, u32[]{:S(2)}, u32[]{:S(2)}) collective-permute-start(bf16[1,4,128,128]{3,2,1,0:T(8,128)(2,1)S(1)} %get-tuple-element.64), channel_id=1, source_target_pairs={{0,4},{1,3},{2,6},{3,1},{4,0},{5,7},{6,2},{7,5},{8,12},{9,11},{10,... | collective-permute-start | bytes 393224 | tf_op jit(solution)/shard_map/ppermute | solution.py:374
  68.8 10.8 %collective-permute-start.8 = (bf16[2,4,128,128]{3,2,1,0:T(8,128)(2,1)S(1)}, bf16[2,4,128,128]{3,2,1,0:T(8,128)(2,1)S(1)}, u32[]{:S(2)}, u32[]{:S(2)}) collective-permute-start(bf16[2,4,128,128]{3,2,1,0:T(8,128)(2,1)S(1)} %pad_maximum_fusion.3), channel_id=1, source_target_pairs={{0,8},{1,9},{2,10},{3,11},{4,12},{5,13},{6,14},{7,15},{8,0},{9,1},... | collective-permute-start | bytes 786440 | tf_op jit(solution)/shard_map/ppermute | solution.py:374
  68.9 13.9 %collective-permute-start.9 = (bf16[2,4,128,128]{3,2,1,0:T(8,128)(2,1)S(1)}, bf16[2,4,128,128]{3,2,1,0:T(8,128)(2,1)S(1)}, u32[]{:S(2)}, u32[]{:S(2)}) collective-permute-start(bf16[2,4,128,128]{3,2,1,0:T(8,128)(2,1)S(1)} %pad_maximum_fusion.2), channel_id=1, source_target_pairs={{0,16},{1,17},{2,18},{3,19},{4,20},{5,21},{6,22},{7,23},{8,24},{9,... | collective-permute-start | bytes 786440 | tf_op jit(solution)/shard_map/ppermute | solution.py:374
  82.8 14.7 %collective-permute-start.11 = (bf16[4,4,128,128]{3,2,1,0:T(8,128)(2,1)S(1)}, bf16[4,4,128,128]{3,2,1,0:T(8,128)(2,1)S(1)}, u32[]{:S(2)}, u32[]{:S(2)}) collective-permute-start(bf16[4,4,128,128]{3,2,1,0:T(8,128)(2,1)S(1)} %constant_dynamic-update-slice_fusion.rest_0_), channel_id=1, source_target_pairs={{0,2},{1,5},{2,0},{3,7},{4,6},{5,1},{6,4},{7,3},{8,10},{9,13},{10,... | collective-permute-start | bytes 1572872 | tf_op jit(solution)/shard_map/ppermute | solution.py:374
  84.4 13.1 %collective-permute-start.10 = (bf16[4,4,128,128]{3,2,1,0:T(8,128)(2,1)S(1)}, bf16[4,4,128,128]{3,2,1,0:T(8,128)(2,1)S(1)}, u32[]{:S(2)}, u32[]{:S(2)}) collective-permute-start(bf16[4,4,128,128]{3,2,1,0:T(8,128)(2,1)S(1)} %constant_dynamic-update-slice_fusion.rest_0_), channel_id=1, source_target_pairs={{0,8},{1,9},{2,10},{3,11},{4,12},{5,13},{6,14},{7,15},{8,0},{9,1},... | collective-permute-start | bytes 1572872 | tf_op jit(solution)/shard_map/ppermute | solution.py:374
  84.6 18.5 %collective-permute-start.18 = (bf16[4,4,128,128]{3,2,1,0:T(8,128)(2,1)S(1)}, bf16[4,4,128,128]{3,2,1,0:T(8,128)(2,1)S(1)}, u32[]{:S(2)}, u32[]{:S(2)}) collective-permute-start(bf16[4,4,128,128]{3,2,1,0:T(8,128)(2,1)S(1)} %pad_maximum_fusion.1.rest_8_), channel_id=1, source_target_pairs={{0,2},{1,5},{2,0},{3,7},{4,6},{5,1},{6,4},{7,3},{8,10},{9,13},{10,... | collective-permute-start | bytes 1572872 | tf_op jit(solution)/shard_map/ppermute | solution.py:374
  85.1 19.4 %collective-permute-start.17 = (bf16[4,4,128,128]{3,2,1,0:T(8,128)(2,1)S(1)}, bf16[4,4,128,128]{3,2,1,0:T(8,128)(2,1)S(1)}, u32[]{:S(2)}, u32[]{:S(2)}) collective-permute-start(bf16[4,4,128,128]{3,2,1,0:T(8,128)(2,1)S(1)} %pad_maximum_fusion.1.rest_8_), channel_id=1, source_target_pairs={{0,4},{1,3},{2,6},{3,1},{4,0},{5,7},{6,2},{7,5},{8,12},{9,11},{10,... | collective-permute-start | bytes 1572872 | tf_op jit(solution)/shard_map/ppermute | solution.py:374
  87.1 18.5 %collective-permute-start.12 = (bf16[4,4,128,128]{3,2,1,0:T(8,128)(2,1)S(1)}, bf16[4,4,128,128]{3,2,1,0:T(8,128)(2,1)}, u32[]{:S(2)}, u32[]{:S(2)}) collective-permute-start(bf16[4,4,128,128]{3,2,1,0:T(8,128)(2,1)S(1)} %constant_dynamic-update-slice_fusion.rest_0_), channel_id=1, source_target_pairs={{0,1},{1,0},{2,3},{3,2},{4,5},{5,4},{6,7},{7,6},{8,9},{9,8},{10,11... | collective-permute-start | bytes 1572872 | tf_op jit(solution)/shard_map/ppermute | solution.py:374
  97.5 8.2 %collective-permute-start.19 = (bf16[4,4,128,128]{3,2,1,0:T(8,128)(2,1)S(1)}, bf16[4,4,128,128]{3,2,1,0:T(8,128)(2,1)}, u32[]{:S(2)}, u32[]{:S(2)}) collective-permute-start(bf16[4,4,128,128]{3,2,1,0:T(8,128)(2,1)S(1)} %pad_maximum_fusion.1.rest_8_), channel_id=1, source_target_pairs={{0,1},{1,0},{2,3},{3,2},{4,5},{5,4},{6,7},{7,6},{8,9},{9,8},{10,11... | collective-permute-start | bytes 1572872 | tf_op jit(solution)/shard_map/ppermute | solution.py:374
  97.5 8.7 %collective-permute-start.13 = (bf16[4,4,128,128]{3,2,1,0:T(8,128)(2,1)S(1)}, bf16[4,4,128,128]{3,2,1,0:T(8,128)(2,1)}, u32[]{:S(2)}, u32[]{:S(2)}) collective-permute-start(bf16[4,4,128,128]{3,2,1,0:T(8,128)(2,1)S(1)} %collective-permute-done.11.rest_1_), channel_id=1, source_target_pairs={{0,1},{1,0},{2,3},{3,2},{4,5},{5,4},{6,7},{7,6},{8,9},{9,8},{10,11... | collective-permute-start | bytes 1572872 | tf_op jit(solution)/shard_map/ppermute | solution.py:374
  103.1 9.3 %collective-permute-start.14 = (bf16[4,4,128,128]{3,2,1,0:T(8,128)(2,1)S(1)}, bf16[4,4,128,128]{3,2,1,0:T(8,128)(2,1)}, u32[]{:S(2)}, u32[]{:S(2)}) collective-permute-start(bf16[4,4,128,128]{3,2,1,0:T(8,128)(2,1)S(1)} %collective-permute-done.10.rest_4_), channel_id=1, source_target_pairs={{0,2},{1,5},{2,0},{3,7},{4,6},{5,1},{6,4},{7,3},{8,10},{9,13},{10,... | collective-permute-start | bytes 1572872 | tf_op jit(solution)/shard_map/ppermute | solution.py:374
  104.6 13.4 %collective-permute-start.21 = (bf16[4,4,128,128]{3,2,1,0:T(8,128)(2,1)S(1)}, bf16[4,4,128,128]{3,2,1,0:T(8,128)(2,1)}, u32[]{:S(2)}, u32[]{:S(2)}) collective-permute-start(bf16[4,4,128,128]{3,2,1,0:T(8,128)(2,1)S(1)} %collective-permute-done.17.rest_12_), channel_id=1, source_target_pairs={{0,2},{1,5},{2,0},{3,7},{4,6},{5,1},{6,4},{7,3},{8,10},{9,13},{10,... | collective-permute-start | bytes 1572872 | tf_op jit(solution)/shard_map/ppermute | solution.py:374
  105.6 12.5 %collective-permute-start.15 = (bf16[4,4,128,128]{3,2,1,0:T(8,128)(2,1)S(1)}, bf16[4,4,128,128]{3,2,1,0:T(8,128)(2,1)S(1)}, u32[]{:S(2)}, u32[]{:S(2)}) collective-permute-start(bf16[4,4,128,128]{3,2,1,0:T(8,128)(2,1)S(1)} %collective-permute-done.10.rest_4_), channel_id=1, source_target_pairs={{0,1},{1,0},{2,3},{3,2},{4,5},{5,4},{6,7},{7,6},{8,9},{9,8},{10,11... | collective-permute-start | bytes 1572872 | tf_op jit(solution)/shard_map/ppermute | solution.py:374
  105.7 12.4 %collective-permute-start.22 = (bf16[4,4,128,128]{3,2,1,0:T(8,128)(2,1)S(1)}, bf16[4,4,128,128]{3,2,1,0:T(8,128)(2,1)S(1)}, u32[]{:S(2)}, u32[]{:S(2)}) collective-permute-start(bf16[4,4,128,128]{3,2,1,0:T(8,128)(2,1)S(1)} %collective-permute-done.17.rest_12_), channel_id=1, source_target_pairs={{0,1},{1,0},{2,3},{3,2},{4,5},{5,4},{6,7},{7,6},{8,9},{9,8},{10,11... | collective-permute-start | bytes 1572872 | tf_op jit(solution)/shard_map/ppermute | solution.py:374
  106.2 11.9 %collective-permute-start.20 = (bf16[4,4,128,128]{3,2,1,0:T(8,128)(2,1)S(1)}, bf16[4,4,128,128]{3,2,1,0:T(8,128)(2,1)S(1)}, u32[]{:S(2)}, u32[]{:S(2)}) collective-permute-start(bf16[4,4,128,128]{3,2,1,0:T(8,128)(2,1)S(1)} %collective-permute-done.18.rest_9_), channel_id=1, source_target_pairs={{0,1},{1,0},{2,3},{3,2},{4,5},{5,4},{6,7},{7,6},{8,9},{9,8},{10,11... | collective-permute-start | bytes 1572872 | tf_op jit(solution)/shard_map/ppermute | solution.py:374
  112.4 5.7 %collective-permute-start.16 = (bf16[4,4,128,128]{3,2,1,0:T(8,128)(2,1)}, bf16[4,4,128,128]{3,2,1,0:T(8,128)(2,1)S(1)}, u32[]{:S(2)}, u32[]{:S(2)}) collective-permute-start(bf16[4,4,128,128]{3,2,1,0:T(8,128)(2,1)} %collective-permute-done.14.rest_5_), channel_id=1, source_target_pairs={{0,1},{1,0},{2,3},{3,2},{4,5},{5,4},{6,7},{7,6},{8,9},{9,8},{10,11... | collective-permute-start | bytes 1572872 | tf_op jit(solution)/shard_map/ppermute | solution.py:374
  118.0 2.1 collective-permute-start.23
  160.2 7.2 %collective-permute-start.24 = (bf16[16,128,512]{2,1,0:T(8,128)(2,1)S(1)}, bf16[16,128,512]{2,1,0:T(8,128)(2,1)S(1)}, u32[]{:S(2)}, u32[]{:S(2)}) collective-permute-start(bf16[16,128,512]{2,1,0:T(8,128)(2,1)S(1)} %get-tuple-element.51), channel_id=1, source_target_pairs={{0,1},{1,0},{2,3},{3,2},{4,5},{5,4},{6,7},{7,6},{8,9},{9,8},{10,11... | collective-permute-start | bytes 6291464 | tf_op jit(solution)/shard_map/ppermute | solution.py:374
  160.4 15.5 %collective-permute-start.29 = (bf16[16,128,512]{2,1,0:T(8,128)(2,1)S(1)}, bf16[16,128,512]{2,1,0:T(8,128)(2,1)S(1)}, u32[]{:S(2)}, u32[]{:S(2)}) collective-permute-start(bf16[16,128,512]{2,1,0:T(8,128)(2,1)S(1)} %get-tuple-element.53), channel_id=1, source_target_pairs={{0,1},{1,0},{2,3},{3,2},{4,5},{5,4},{6,7},{7,6},{8,9},{9,8},{10,11... | collective-permute-start | bytes 6291464 | tf_op jit(solution)/shard_map/ppermute | solution.py:374
  167.8 20.5 %collective-permute-start.25 = (bf16[8,128,512]{2,1,0:T(8,128)(2,1)S(1)}, bf16[8,128,512]{2,1,0:T(8,128)(2,1)S(1)}, u32[]{:S(2)}, u32[]{:S(2)}) collective-permute-start(bf16[8,128,512]{2,1,0:T(8,128)(2,1)S(1)} %add_convert_fusion), channel_id=1, source_target_pairs={{0,2},{1,5},{2,0},{3,7},{4,6},{5,1},{6,4},{7,3},{8,10},{9,13},{10,... | collective-permute-start | bytes 3145736 | tf_op jit(solution)/shard_map/ppermute | solution.py:374
  176.2 12.0 %collective-permute-start.30 = (bf16[4,128,512]{2,1,0:T(8,128)(2,1)S(1)}, bf16[4,128,512]{2,1,0:T(8,128)(2,1)S(1)}, u32[]{:S(2)}, u32[]{:S(2)}) collective-permute-start(bf16[4,128,512]{2,1,0:T(8,128)(2,1)S(1)} %get-tuple-element.55), channel_id=1, source_target_pairs={{0,2},{1,5},{2,0},{3,7},{4,6},{5,1},{6,4},{7,3},{8,10},{9,13},{10,... | collective-permute-start | bytes 1572872 | tf_op jit(solution)/shard_map/ppermute | solution.py:374
  188.5 13.2 %collective-permute-start.26 = (bf16[4,128,512]{2,1,0:T(8,128)(2,1)S(1)}, bf16[4,128,512]{2,1,0:T(8,128)(2,1)S(1)}, u32[]{:S(2)}, u32[]{:S(2)}) collective-permute-start(bf16[4,128,512]{2,1,0:T(8,128)(2,1)S(1)} %add_convert_fusion.4), channel_id=1, source_target_pairs={{0,8},{1,9},{2,10},{3,11},{4,12},{5,13},{6,14},{7,15},{8,0},{9,1},... | collective-permute-start | bytes 1572872 | tf_op jit(solution)/shard_map/ppermute | solution.py:374
  189.1 14.1 %collective-permute-start.32 = (bf16[4,128,512]{2,1,0:T(8,128)(2,1)S(1)}, bf16[4,128,512]{2,1,0:T(8,128)(2,1)S(1)}, u32[]{:S(2)}, u32[]{:S(2)}) collective-permute-start(bf16[4,128,512]{2,1,0:T(8,128)(2,1)S(1)} %add_convert_fusion.1), channel_id=1, source_target_pairs={{0,4},{1,3},{2,6},{3,1},{4,0},{5,7},{6,2},{7,5},{8,12},{9,11},{10,... | collective-permute-start | bytes 1572872 | tf_op jit(solution)/shard_map/ppermute | solution.py:374
  190.8 12.4 %collective-permute-start.31 = (bf16[4,128,512]{2,1,0:T(8,128)(2,1)S(1)}, bf16[4,128,512]{2,1,0:T(8,128)(2,1)S(1)}, u32[]{:S(2)}, u32[]{:S(2)}) collective-permute-start(bf16[4,128,512]{2,1,0:T(8,128)(2,1)S(1)} %get-tuple-element.56), channel_id=1, source_target_pairs={{0,2},{1,5},{2,0},{3,7},{4,6},{5,1},{6,4},{7,3},{8,10},{9,13},{10,... | collective-permute-start | bytes 1572872 | tf_op jit(solution)/shard_map/ppermute | solution.py:374
  201.8 13.0 %collective-permute-start.27 = (bf16[2,128,512]{2,1,0:T(8,128)(2,1)S(1)}, bf16[2,128,512]{2,1,0:T(8,128)(2,1)S(1)}, u32[]{:S(2)}, u32[]{:S(2)}) collective-permute-start(bf16[2,128,512]{2,1,0:T(8,128)(2,1)S(1)} %add_convert_fusion.6), channel_id=1, source_target_pairs={{0,16},{1,17},{2,18},{3,19},{4,20},{5,21},{6,22},{7,23},{8,24},{9,... | collective-permute-start | bytes 786440 | tf_op jit(solution)/shard_map/ppermute | solution.py:374
  203.4 13.3 %collective-permute-start.33 = (bf16[2,128,512]{2,1,0:T(8,128)(2,1)S(1)}, bf16[2,128,512]{2,1,0:T(8,128)(2,1)S(1)}, u32[]{:S(2)}, u32[]{:S(2)}) collective-permute-start(bf16[2,128,512]{2,1,0:T(8,128)(2,1)S(1)} %add_convert_fusion.5), channel_id=1, source_target_pairs={{0,8},{1,9},{2,10},{3,11},{4,12},{5,13},{6,14},{7,15},{8,0},{9,1},... | collective-permute-start | bytes 786440 | tf_op jit(solution)/shard_map/ppermute | solution.py:374
  214.9 5.0 %collective-permute-start.28 = (bf16[1,128,512]{2,1,0:T(8,128)(2,1)S(1)}, bf16[1,128,512]{2,1,0:T(8,128)(2,1)S(1)}, u32[]{:S(2)}, u32[]{:S(2)}) collective-permute-start(bf16[1,128,512]{2,1,0:T(8,128)(2,1)S(1)} %add_convert_fusion.9), channel_id=1, source_target_pairs={{0,4},{1,3},{2,6},{3,1},{4,0},{5,7},{6,2},{7,5},{8,12},{9,11},{10,... | collective-permute-start | bytes 393224 | tf_op jit(solution)/shard_map/ppermute | solution.py:374
  216.7 8.5 %collective-permute-start.34 = (bf16[1,128,512]{2,1,0:T(8,128)(2,1)S(1)}, bf16[1,128,512]{2,1,0:T(8,128)(2,1)S(1)}, u32[]{:S(2)}, u32[]{:S(2)}) collective-permute-start(bf16[1,128,512]{2,1,0:T(8,128)(2,1)S(1)} %add_convert_fusion.8), channel_id=1, source_target_pairs={{0,16},{1,17},{2,18},{3,19},{4,20},{5,21},{6,22},{7,23},{8,24},{9,... | collective-permute-start | bytes 393224 | tf_op jit(solution)/shard_map/ppermute | solution.py:374

commit v10 on v9

--- a/solution.py
+++ b/solution.py
@@ -437,7 +437,7 @@
         early = total_of([term[rows[0]] for term in whole]).astype(BF16)
         late = total_of([term[rows[1]] for term in whole]).astype(BF16)
         early, late = after(early, late)
-        early_came = flip(early, bits_of)
+        early_came, _ = after(flip(early, bits_of), exchange(0, 1))
         late, early_came = after(late, early_came)
         sends[chunk] = [term[rows[2]] for term in whole] + [early_came]
         terms[chunk] = [term[rows[3]] for term in whole] + [flip(late, bits_of)]
@@ -458,7 +458,6 @@
     terms[0] = makers[0](None)
     terms[1] = makers[1](exchange(0, 0))
     split_exchange(1)
-    exchange(0, 1)
     exchange(1, 1)
     exchange(0, 2)
     exchange(1, 2)
@@ -468,8 +467,8 @@
 
 
 HEAD_STAGES = (
-    lambda core: ZHIGH if core else Y,
-    lambda core: ZLOW if core else ZHIGH,
+    lambda core: ZHIGH,
+    lambda core: ZLOW if core else Y,
     lambda core: Y if core else ZLOW,
 )
 
@@ -478,7 +477,7 @@
     bits = [(place >> stage) & 1 for stage in range(3)]
     return jnp.where(
         core == 0,
-        bits[0] | (bits[1] << 2) | (bits[2] << 1),
+        (bits[0] << 2) | bits[1] | (bits[2] << 1),
         (bits[0] << 2) | (bits[1] << 1) | bits[2],
     )
 

time: 227 us -> 225 us (level)
  starting transfers between devices: 39.2 us -> 36.1 us
    ppermute x35, waiting for transfers between devices: 115 us -> 122 us  [flip(): return lax.ppermute(array, ('expert', 'tensor'), pairs)]
    all_to_all x1, waiting for transfers between devices: 6.35 us -> 0.57 us  [per_device_tokens(): lax.all_to_all(pack(member, residual, route_ids, route_weights, groups),...]
  transfers between devices with their start and end apart: 36 -> 36, of which waited for: 19 -> 21; matrix products, arithmetic and copies ran while one was open for 1% -> 2% of each run, Pallas kernels for 6% -> 6%
where the time goes in v10:
time: 225 us
  waiting for transfers between devices  123 us (55%)
  Pallas kernels  56.5 us (25%)
  starting transfers between devices  36.1 us (16%)
  local copies, waits for them, and re-layouts  4.84 us (2%)
  other arithmetic  3.82 us (2%)
    ppermute x35, waiting for transfers between devices, flip(): return lax.ppermute(array, ('expert', 'tensor'), pairs)  122 us
    ppermute x35, starting transfers between devices, flip(): return lax.ppermute(array, ('expert', 'tensor'), pairs)  32.2 us
    pallas_call x1, Pallas kernels, gate_up(): pl.pallas_call(kernel, grid_spec=pltpu.PrefetchScalarGridSpec(num_scalar_...  30.1 us
    pallas_call x3, Pallas kernels, down(): pl.pallas_call(functools.partial(down_kernel, rows), grid_spec=pltpu.Pref...  22.9 us
  transfers between devices with their start and end apart: 36, of which 21 were waited for; matrix products, arithmetic and copies ran while one was open for 2% of the time, Pallas kernels for 6%

profile of v10, /device:TPU:0, one launch (start us, length us, event | category | flops | bytes accessed | tf_op | source)
XLA Modules:
  0.0 224.5 jit_solution(12698770515635676888)
XLA Ops:
  0.0 4.0 %collective-permute-start = (bf16[1,128,1024]{2,1,0:T(8,128)(2,1)}, bf16[1,128,1024]{2,1,0:T(8,128)(2,1)S(1)}, u32[]{:S(2)}, u32[]{:S(2)}) collective-permute-start(bf16[1,128,1024]{2,1,0:T(8,128)(2,1)} %bitcast.67), channel_id=1, source_target_pairs={{0,16},{1,17},{2,18},{3,19},{4,20},{5,21},{6,22},{7,23},{8,24},{9,... | collective-permute-start | bytes 786440 | tf_op jit(solution)/shard_map/ppermute | solution.py:374
  4.0 1.2 copy-done
  5.3 0.7 copy-done.1
  6.0 0.7 copy-done.2
  6.6 0.8 pack.1
  7.4 3.8 %all-to-all-start = ((bf16[8,160,128]{2,1,0:T(8,128)(2,1)}), bf16[8,160,128]{2,1,0:T(8,128)(2,1)S(1)}, u32[]{:S(2)}, u32[]{:S(2)}) async-start(bf16[8,160,128]{2,1,0:T(8,128)(2,1)} %pack.1), calls=%async_computation | async-start | bytes 655360 | tf_op jit(solution)/shard_map/all_to_all | solution.py:610
  11.3 9.3 %collective-permute-done = bf16[1,128,1024]{2,1,0:T(8,128)(2,1)S(1)} collective-permute-done((bf16[1,128,1024]{2,1,0:T(8,128)(2,1)}, bf16[1,128,1024]{2,1,0:T(8,128)(2,1)S(1)}, u32[]{:S(2)}, u32[]{:S(2)}) %collective-permute-start) | collective-permute-done | bytes 262176 | tf_op jit(solution)/shard_map/ppermute | solution.py:374
  20.8 1.9 collective-permute-start.1
  22.7 0.6 all-to-all-done
  23.3 11.2 %collective-permute-done.2.refs_2_ = bf16[2,128,1024]{2,1,0:T(8,128)(2,1)S(1)} collective-permute-done((bf16[2,128,1024]{2,1,0:T(8,128)(2,1)S(1)}, bf16[2,128,1024]{2,1,0:T(8,128)(2,1)S(1)}, u32[]{:S(2)}, u32[]{:S(2)}) %collective-permute-start.2) | collective-permute-done | bytes 524320 | tf_op jit(solution)/shard_map/ppermute | solution.py:374
  34.5 0.6 gather_fusion
  35.1 1.0 collective-permute-start.3
  36.6 7.8 %collective-permute-done.3.refs_3_ = bf16[2,128,1024]{2,1,0:T(8,128)(2,1)} collective-permute-done((bf16[2,128,1024]{2,1,0:T(8,128)(2,1)S(1)}, bf16[2,128,1024]{2,1,0:T(8,128)(2,1)}, u32[]{:S(2)}, u32[]{:S(2)}) %collective-permute-start.3) | collective-permute-done | bytes 524320 | tf_op jit(solution)/shard_map/ppermute | solution.py:374
  44.4 1.0 copy-done.5
  45.5 2.6 %project.1 = (bf16[2,8,128,128]{3,2,1,0:T(8,128)(2,1)S(1)}, bf16[2,8,128,128]{3,2,1,0:T(8,128)(2,1)S(1)}) custom-call(s32[10]{0:T(128)S(1)} %pad_add_fusion.1.info_ref, bf16[2,128,1024]{2,1,0:T(8,128)(2,1)S(1)} %pad_maximum_fusion.refs_0_, bf16[2,128,1024]{2,1,0:T(8,128)(2,1)S(1)} %copy-done.5, bf16[2,128,1024]{2,1,0:T(8,128)(2,1)S(1)} %collective-permute-done.2.refs_2_, ...), custom_call_target="tpu_custom_call" | custom-call | flops 1073741824 | bytes 5242880 | tf_op jit(solution)/shard_map/project/pallas_call | solution.py:112
  48.2 1.9 collective-permute-done.4
  50.2 1.6 collective-permute-start.5
  51.8 6.8 %collective-permute-done.5 = bf16[8,128,128]{2,1,0:T(8,128)(2,1)S(1)} collective-permute-done((bf16[8,128,128]{2,1,0:T(8,128)(2,1)S(1)}, bf16[8,128,128]{2,1,0:T(8,128)(2,1)S(1)}, u32[]{:S(2)}, u32[]{:S(2)}) %collective-permute-start.5) | collective-permute-done | bytes 262176 | tf_op jit(solution)/shard_map/ppermute | solution.py:374
  58.8 2.2 collective-permute-start.7
  61.0 1.4 collective-permute-start.6
  62.4 4.9 %collective-permute-done.7 = bf16[1,4,128,128]{3,2,1,0:T(8,128)(2,1)S(1)} collective-permute-done((bf16[1,4,128,128]{3,2,1,0:T(8,128)(2,1)S(1)}, bf16[1,4,128,128]{3,2,1,0:T(8,128)(2,1)S(1)}, u32[]{:S(2)}, u32[]{:S(2)}) %collective-permute-start.7) | collective-permute-done | bytes 131104 | tf_op jit(solution)/shard_map/ppermute | solution.py:374
  67.3 0.7 collective-permute-start.8
  68.0 3.1 %collective-permute-start.9 = (bf16[2,4,128,128]{3,2,1,0:T(8,128)(2,1)S(1)}, bf16[2,4,128,128]{3,2,1,0:T(8,128)(2,1)S(1)}, u32[]{:S(2)}, u32[]{:S(2)}) collective-permute-start(bf16[2,4,128,128]{3,2,1,0:T(8,128)(2,1)S(1)} %pad_maximum_fusion.2), channel_id=1, source_target_pairs={{0,16},{1,17},{2,18},{3,19},{4,20},{5,21},{6,22},{7,23},{8,24},{9,... | collective-permute-start | bytes 786440 | tf_op jit(solution)/shard_map/ppermute | solution.py:374
  71.1 8.7 %collective-permute-done.8 = bf16[2,4,128,128]{3,2,1,0:T(8,128)(2,1)S(1)} collective-permute-done((bf16[2,4,128,128]{3,2,1,0:T(8,128)(2,1)S(1)}, bf16[2,4,128,128]{3,2,1,0:T(8,128)(2,1)S(1)}, u32[]{:S(2)}, u32[]{:S(2)}) %collective-permute-start.8) | collective-permute-done | bytes 262176 | tf_op jit(solution)/shard_map/ppermute | solution.py:374
  79.9 2.9 %collective-permute-done.9 = bf16[2,4,128,128]{3,2,1,0:T(8,128)(2,1)S(1)} collective-permute-done((bf16[2,4,128,128]{3,2,1,0:T(8,128)(2,1)S(1)}, bf16[2,4,128,128]{3,2,1,0:T(8,128)(2,1)S(1)}, u32[]{:S(2)}, u32[]{:S(2)}) %collective-permute-start.9) | collective-permute-done | bytes 262176 | tf_op jit(solution)/shard_map/ppermute | solution.py:374
  82.8 1.6 collective-permute-start.11
  84.4 0.2 collective-permute-start.10
  84.6 0.5 collective-permute-start.18
  85.2 1.4 collective-permute-start.17
  86.7 10.7 %collective-permute-done.11.rest_1_ = bf16[4,4,128,128]{3,2,1,0:T(8,128)(2,1)S(1)} collective-permute-done((bf16[4,4,128,128]{3,2,1,0:T(8,128)(2,1)S(1)}, bf16[4,4,128,128]{3,2,1,0:T(8,128)(2,1)S(1)}, u32[]{:S(2)}, u32[]{:S(2)}) %collective-permute-start.11) | collective-permute-done | bytes 524320 | tf_op jit(solution)/shard_map/ppermute | solution.py:374
  97.4 0.5 collective-permute-start.13
  97.9 5.1 %collective-permute-done.18.rest_9_ = bf16[4,4,128,128]{3,2,1,0:T(8,128)(2,1)S(1)} collective-permute-done((bf16[4,4,128,128]{3,2,1,0:T(8,128)(2,1)S(1)}, bf16[4,4,128,128]{3,2,1,0:T(8,128)(2,1)S(1)}, u32[]{:S(2)}, u32[]{:S(2)}) %collective-permute-start.18) | collective-permute-done | bytes 524320 | tf_op jit(solution)/shard_map/ppermute | solution.py:374
  103.0 1.5 collective-permute-start.14
  104.5 0.5 collective-permute-start.21
  105.6 0.5 collective-permute-start.22
  106.2 6.1 %collective-permute-done.14.rest_5_ = bf16[4,4,128,128]{3,2,1,0:T(8,128)(2,1)} collective-permute-done((bf16[4,4,128,128]{3,2,1,0:T(8,128)(2,1)S(1)}, bf16[4,4,128,128]{3,2,1,0:T(8,128)(2,1)}, u32[]{:S(2)}, u32[]{:S(2)}) %collective-permute-start.14) | collective-permute-done | bytes 524320 | tf_op jit(solution)/shard_map/ppermute | solution.py:374
  112.3 5.6 %collective-permute-done.21.rest_13_ = bf16[4,4,128,128]{3,2,1,0:T(8,128)(2,1)} collective-permute-done((bf16[4,4,128,128]{3,2,1,0:T(8,128)(2,1)S(1)}, bf16[4,4,128,128]{3,2,1,0:T(8,128)(2,1)}, u32[]{:S(2)}, u32[]{:S(2)}) %collective-permute-start.21) | collective-permute-done | bytes 524320 | tf_op jit(solution)/shard_map/ppermute | solution.py:374
  118.1 2.0 collective-permute-done.23.rest_15_
  120.0 30.1 %gate_up.1 = (bf16[8,192,384]{2,1,0:T(8,128)(2,1)S(1)}, f32[128,1024]{1,0:T(8,128)S(1)}, bf16[4,256,384]{2,1,0:T(8,128)(2,1)S(1)}) custom-call(s32[66]{0:T(128)S(1)} %pad_add_fusion.info_ref, s32[8,1024]{1,0:T(8,128)S(1)} %bitcast_select_fusion.slot_ref, f32[8,1024]{1,0:T(8,128)S(1)} %bitcast.63, f32[32,128]{1,0:T(8,128)S(1)} %divide_bitcast_fusion.invgain_ref, ...), custom_call_target="tpu_custom_call" | custom-call | flops 9663676416 | bytes 58720256 | tf_op jit(solution)/shard_map/gate_up/pallas_call | solution.py:267
  150.2 10.0 %down_mix.4 = (bf16[16,128,512]{2,1,0:T(8,128)(2,1)S(1)}, bf16[16,128,512]{2,1,0:T(8,128)(2,1)S(1)}) custom-call(s32[34]{0:T(128)S(1)} %pad_add_fusion.3.place_ref, bf16[4,256,384]{2,1,0:T(8,128)(2,1)S(1)} %get-tuple-element.50.spread_ref, bf16[8,192,384]{2,1,0:T(8,128)(2,1)S(1)} %get-tuple-element.51.act_ref, bf16[8,384,4096]{2,1,0:T(8,128)(2,1)} %wd1_ref.5, ...), custom_call_target="tpu_custom_call" | custom-call | flops 4831838208 | bytes 16777216 | tf_op jit(solution)/shard_map/down_mix/pallas_call | solution.py:343
  160.2 0.2 collective-permute-start.24
  160.4 0.3 collective-permute-start.29
  160.9 6.5 %down_mix.3 = bf16[16,128,512]{2,1,0:T(8,128)(2,1)S(1)} custom-call(s32[18]{0:T(128)S(1)} %pad_add_fusion.2.place_ref, bf16[4,256,384]{2,1,0:T(8,128)(2,1)S(1)} %get-tuple-element.50.spread_ref, bf16[8,192,384]{2,1,0:T(8,128)(2,1)S(1)} %get-tuple-element.51.act_ref, bf16[8,384,4096]{2,1,0:T(8,128)(2,1)} %wd1_ref.5, bf16[8,384,4096]{2,1,0:T(8,128)(2,1)} %wd1_ref.5), custom_call_target="tpu_custom_call" | custom-call | flops 2415919104 | bytes 8388608 | tf_op jit(solution)/shard_map/down_mix/pallas_call | solution.py:343
  167.4 0.3 add_convert_fusion
  167.7 1.6 collective-permute-start.25
  169.4 6.5 %down_mix.5 = bf16[16,128,512]{2,1,0:T(8,128)(2,1)S(1)} custom-call(s32[18]{0:T(128)S(1)} %pad_add_fusion.4.place_ref, bf16[4,256,384]{2,1,0:T(8,128)(2,1)S(1)} %get-tuple-element.50.spread_ref, bf16[8,192,384]{2,1,0:T(8,128)(2,1)S(1)} %get-tuple-element.51.act_ref, bf16[8,384,4096]{2,1,0:T(8,128)(2,1)} %wd1_ref.5, bf16[8,384,4096]{2,1,0:T(8,128)(2,1)} %wd1_ref.5), custom_call_target="tpu_custom_call" | custom-call | flops 2415919104 | bytes 8388608 | tf_op jit(solution)/shard_map/down_mix/pallas_call | solution.py:343
  175.8 0.3 add_convert_fusion.2
  176.2 0.6 collective-permute-start.30
  176.8 5.8 %collective-permute-done.25 = bf16[8,128,512]{2,1,0:T(8,128)(2,1)S(1)} collective-permute-done((bf16[8,128,512]{2,1,0:T(8,128)(2,1)S(1)}, bf16[8,128,512]{2,1,0:T(8,128)(2,1)S(1)}, u32[]{:S(2)}, u32[]{:S(2)}) %collective-permute-start.25) | collective-permute-done | bytes 1048608 | tf_op jit(solution)/shard_map/ppermute | solution.py:374
  182.8 0.4 collective-permute-start.26
  183.2 5.0 %collective-permute-done.30 = bf16[4,128,512]{2,1,0:T(8,128)(2,1)S(1)} collective-permute-done((bf16[4,128,512]{2,1,0:T(8,128)(2,1)S(1)}, bf16[4,128,512]{2,1,0:T(8,128)(2,1)S(1)}, u32[]{:S(2)}, u32[]{:S(2)}) %collective-permute-start.30) | collective-permute-done | bytes 524320 | tf_op jit(solution)/shard_map/ppermute | solution.py:374
  188.2 0.2 add_convert_fusion.1
  188.4 1.5 collective-permute-start.32
  189.9 1.5 collective-permute-start.31
  191.4 4.6 %collective-permute-done.26 = bf16[4,128,512]{2,1,0:T(8,128)(2,1)S(1)} collective-permute-done((bf16[4,128,512]{2,1,0:T(8,128)(2,1)S(1)}, bf16[4,128,512]{2,1,0:T(8,128)(2,1)S(1)}, u32[]{:S(2)}, u32[]{:S(2)}) %collective-permute-start.26) | collective-permute-done | bytes 524320 | tf_op jit(solution)/shard_map/ppermute | solution.py:374
  196.1 1.0 collective-permute-start.27
  197.2 5.7 %collective-permute-done.32 = bf16[4,128,512]{2,1,0:T(8,128)(2,1)S(1)} collective-permute-done((bf16[4,128,512]{2,1,0:T(8,128)(2,1)S(1)}, bf16[4,128,512]{2,1,0:T(8,128)(2,1)S(1)}, u32[]{:S(2)}, u32[]{:S(2)}) %collective-permute-start.32) | collective-permute-done | bytes 524320 | tf_op jit(solution)/shard_map/ppermute | solution.py:374
  203.0 0.3 collective-permute-start.33
  203.3 5.9 %collective-permute-done.27 = bf16[2,128,512]{2,1,0:T(8,128)(2,1)S(1)} collective-permute-done((bf16[2,128,512]{2,1,0:T(8,128)(2,1)S(1)}, bf16[2,128,512]{2,1,0:T(8,128)(2,1)S(1)}, u32[]{:S(2)}, u32[]{:S(2)}) %collective-permute-start.27) | collective-permute-done | bytes 262176 | tf_op jit(solution)/shard_map/ppermute | solution.py:374
  209.2 1.4 collective-permute-start.28
  210.6 4.0 %collective-permute-done.33 = bf16[2,128,512]{2,1,0:T(8,128)(2,1)S(1)} collective-permute-done((bf16[2,128,512]{2,1,0:T(8,128)(2,1)S(1)}, bf16[2,128,512]{2,1,0:T(8,128)(2,1)S(1)}, u32[]{:S(2)}, u32[]{:S(2)}) %collective-permute-start.33) | collective-permute-done | bytes 262176 | tf_op jit(solution)/shard_map/ppermute | solution.py:374
  214.7 0.5 collective-permute-start.34
  215.4 8.3 %collective-permute-done.34 = bf16[1,128,512]{2,1,0:T(8,128)(2,1)S(1)} collective-permute-done((bf16[1,128,512]{2,1,0:T(8,128)(2,1)S(1)}, bf16[1,128,512]{2,1,0:T(8,128)(2,1)S(1)}, u32[]{:S(2)}, u32[]{:S(2)}) %collective-permute-start.34) | collective-permute-done | bytes 131104 | tf_op jit(solution)/shard_map/ppermute | solution.py:374
  223.8 0.8 fusion
  (87 shorter events, 3.3 us)
Async XLA Ops:
  0.0 20.6 %collective-permute-start = (bf16[1,128,1024]{2,1,0:T(8,128)(2,1)}, bf16[1,128,1024]{2,1,0:T(8,128)(2,1)S(1)}, u32[]{:S(2)}, u32[]{:S(2)}) collective-permute-start(bf16[1,128,1024]{2,1,0:T(8,128)(2,1)} %bitcast.67), channel_id=1, source_target_pairs={{0,16},{1,17},{2,18},{3,19},{4,20},{5,21},{6,22},{7,23},{8,24},{9,... | collective-permute-start | bytes 786440 | tf_op jit(solution)/shard_map/ppermute | solution.py:374
  4.0 1.2 copy-start
  5.3 0.7 copy-start.1
  6.0 0.7 copy-start.2
  6.6 13.9 %copy-start.6 = (bf16[128,1024]{1,0:T(8,128)(2,1)S(1)}, bf16[128,1024]{1,0:T(8,128)(2,1)}, u32[]{:S(2)}) copy-start(bf16[128,1024]{1,0:T(8,128)(2,1)} %param.9) | copy-start | bytes 786436
  6.6 37.8 %copy-start.3 = (bf16[1024,512]{1,0:T(8,128)(2,1)S(1)}, bf16[1024,512]{1,0:T(8,128)(2,1)}, u32[]{:S(2)}) copy-start(bf16[1024,512]{1,0:T(8,128)(2,1)} %refs_4_.1) | copy-start | bytes 3145732
  7.4 15.8 %all-to-all-start = ((bf16[8,160,128]{2,1,0:T(8,128)(2,1)}), bf16[8,160,128]{2,1,0:T(8,128)(2,1)S(1)}, u32[]{:S(2)}, u32[]{:S(2)}) async-start(bf16[8,160,128]{2,1,0:T(8,128)(2,1)} %pack.1), calls=%async_computation | async-start | bytes 655360 | tf_op jit(solution)/shard_map/all_to_all | solution.py:610
  20.6 13.9 %collective-permute-start.2 = (bf16[2,128,1024]{2,1,0:T(8,128)(2,1)S(1)}, bf16[2,128,1024]{2,1,0:T(8,128)(2,1)S(1)}, u32[]{:S(2)}, u32[]{:S(2)}) collective-permute-start(bf16[2,128,1024]{2,1,0:T(8,128)(2,1)S(1)} %pad_maximum_fusion.refs_0_), channel_id=1, source_target_pairs={{0,8},{1,5},{2,10},{3,7},{4,12},{5,1},{6,14},{7,3},{8,0},{9,13},{1... | collective-permute-start | bytes 1572872 | tf_op jit(solution)/shard_map/ppermute | solution.py:374
  20.8 13.7 %collective-permute-start.1 = (bf16[2,128,1024]{2,1,0:T(8,128)(2,1)S(1)}, bf16[2,128,1024]{2,1,0:T(8,128)(2,1)S(1)}, u32[]{:S(2)}, u32[]{:S(2)}) collective-permute-start(bf16[2,128,1024]{2,1,0:T(8,128)(2,1)S(1)} %pad_maximum_fusion.refs_0_), channel_id=1, source_target_pairs={{0,4},{1,9},{2,6},{3,11},{4,0},{5,13},{6,2},{7,15},{8,12},{9,1},{1... | collective-permute-start | bytes 1572872 | tf_op jit(solution)/shard_map/ppermute | solution.py:374
  34.5 2.1 copy-start.4
  35.1 9.4 %collective-permute-start.3 = (bf16[2,128,1024]{2,1,0:T(8,128)(2,1)S(1)}, bf16[2,128,1024]{2,1,0:T(8,128)(2,1)}, u32[]{:S(2)}, u32[]{:S(2)}) collective-permute-start(bf16[2,128,1024]{2,1,0:T(8,128)(2,1)S(1)} %collective-permute-done.1.refs_1_), channel_id=1, source_target_pairs={{0,8},{1,5},{2,10},{3,7},{4,12},{5,1},{6,14},{7,3},{8,0},{9,13},{1... | collective-permute-start | bytes 1572872 | tf_op jit(solution)/shard_map/ppermute | solution.py:374
  44.4 1.0 copy-start.5
  45.5 6.3 %copy-start.7 = (f32[4096]{0:T(1024)S(1)}, f32[4096]{0:T(1024)}, u32[]{:S(2)}) copy-start(f32[4096]{0:T(1024)} %param.12) | copy-start | bytes 49156
  48.1 2.0 collective-permute-start.4
  50.2 8.4 %collective-permute-start.5 = (bf16[8,128,128]{2,1,0:T(8,128)(2,1)S(1)}, bf16[8,128,128]{2,1,0:T(8,128)(2,1)S(1)}, u32[]{:S(2)}, u32[]{:S(2)}) collective-permute-start(bf16[8,128,128]{2,1,0:T(8,128)(2,1)S(1)} %fusion.2), channel_id=1, source_target_pairs={{0,2},{1,3},{2,0},{3,1},{4,6},{5,7},{6,4},{7,5},{8,10},{9,11},{10,... | collective-permute-start | bytes 786440 | tf_op jit(solution)/shard_map/ppermute | solution.py:374
  58.8 8.5 %collective-permute-start.7 = (bf16[1,4,128,128]{3,2,1,0:T(8,128)(2,1)S(1)}, bf16[1,4,128,128]{3,2,1,0:T(8,128)(2,1)S(1)}, u32[]{:S(2)}, u32[]{:S(2)}) collective-permute-start(bf16[1,4,128,128]{3,2,1,0:T(8,128)(2,1)S(1)} %get-tuple-element.65), channel_id=1, source_target_pairs={{0,16},{1,17},{2,18},{3,19},{4,20},{5,21},{6,22},{7,23},{8,24},{9,... | collective-permute-start | bytes 393224 | tf_op jit(solution)/shard_map/ppermute | solution.py:374
  61.0 6.3 %collective-permute-start.6 = (bf16[1,4,128,128]{3,2,1,0:T(8,128)(2,1)S(1)}, bf16[1,4,128,128]{3,2,1,0:T(8,128)(2,1)S(1)}, u32[]{:S(2)}, u32[]{:S(2)}) collective-permute-start(bf16[1,4,128,128]{3,2,1,0:T(8,128)(2,1)S(1)} %get-tuple-element.66), channel_id=1, source_target_pairs={{0,4},{1,3},{2,6},{3,1},{4,0},{5,7},{6,2},{7,5},{8,12},{9,11},{10,... | collective-permute-start | bytes 393224 | tf_op jit(solution)/shard_map/ppermute | solution.py:374
  67.3 12.5 %collective-permute-start.8 = (bf16[2,4,128,128]{3,2,1,0:T(8,128)(2,1)S(1)}, bf16[2,4,128,128]{3,2,1,0:T(8,128)(2,1)S(1)}, u32[]{:S(2)}, u32[]{:S(2)}) collective-permute-start(bf16[2,4,128,128]{3,2,1,0:T(8,128)(2,1)S(1)} %pad_maximum_fusion.3), channel_id=1, source_target_pairs={{0,8},{1,9},{2,10},{3,11},{4,12},{5,13},{6,14},{7,15},{8,0},{9,1},... | collective-permute-start | bytes 786440 | tf_op jit(solution)/shard_map/ppermute | solution.py:374
  68.0 14.8 %collective-permute-start.9 = (bf16[2,4,128,128]{3,2,1,0:T(8,128)(2,1)S(1)}, bf16[2,4,128,128]{3,2,1,0:T(8,128)(2,1)S(1)}, u32[]{:S(2)}, u32[]{:S(2)}) collective-permute-start(bf16[2,4,128,128]{3,2,1,0:T(8,128)(2,1)S(1)} %pad_maximum_fusion.2), channel_id=1, source_target_pairs={{0,16},{1,17},{2,18},{3,19},{4,20},{5,21},{6,22},{7,23},{8,24},{9,... | collective-permute-start | bytes 786440 | tf_op jit(solution)/shard_map/ppermute | solution.py:374
  82.8 14.6 %collective-permute-start.11 = (bf16[4,4,128,128]{3,2,1,0:T(8,128)(2,1)S(1)}, bf16[4,4,128,128]{3,2,1,0:T(8,128)(2,1)S(1)}, u32[]{:S(2)}, u32[]{:S(2)}) collective-permute-start(bf16[4,4,128,128]{3,2,1,0:T(8,128)(2,1)S(1)} %constant_dynamic-update-slice_fusion.rest_0_), channel_id=1, source_target_pairs={{0,2},{1,5},{2,0},{3,7},{4,6},{5,1},{6,4},{7,3},{8,10},{9,13},{10,... | collective-permute-start | bytes 1572872 | tf_op jit(solution)/shard_map/ppermute | solution.py:374
  84.4 13.0 %collective-permute-start.10 = (bf16[4,4,128,128]{3,2,1,0:T(8,128)(2,1)S(1)}, bf16[4,4,128,128]{3,2,1,0:T(8,128)(2,1)S(1)}, u32[]{:S(2)}, u32[]{:S(2)}) collective-permute-start(bf16[4,4,128,128]{3,2,1,0:T(8,128)(2,1)S(1)} %constant_dynamic-update-slice_fusion.rest_0_), channel_id=1, source_target_pairs={{0,8},{1,9},{2,10},{3,11},{4,12},{5,13},{6,14},{7,15},{8,0},{9,1},... | collective-permute-start | bytes 1572872 | tf_op jit(solution)/shard_map/ppermute | solution.py:374
  84.6 18.4 %collective-permute-start.18 = (bf16[4,4,128,128]{3,2,1,0:T(8,128)(2,1)S(1)}, bf16[4,4,128,128]{3,2,1,0:T(8,128)(2,1)S(1)}, u32[]{:S(2)}, u32[]{:S(2)}) collective-permute-start(bf16[4,4,128,128]{3,2,1,0:T(8,128)(2,1)S(1)} %pad_maximum_fusion.1.rest_8_), channel_id=1, source_target_pairs={{0,2},{1,5},{2,0},{3,7},{4,6},{5,1},{6,4},{7,3},{8,10},{9,13},{10,... | collective-permute-start | bytes 1572872 | tf_op jit(solution)/shard_map/ppermute | solution.py:374
  85.2 19.4 %collective-permute-start.17 = (bf16[4,4,128,128]{3,2,1,0:T(8,128)(2,1)S(1)}, bf16[4,4,128,128]{3,2,1,0:T(8,128)(2,1)S(1)}, u32[]{:S(2)}, u32[]{:S(2)}) collective-permute-start(bf16[4,4,128,128]{3,2,1,0:T(8,128)(2,1)S(1)} %pad_maximum_fusion.1.rest_8_), channel_id=1, source_target_pairs={{0,4},{1,3},{2,6},{3,1},{4,0},{5,7},{6,2},{7,5},{8,12},{9,11},{10,... | collective-permute-start | bytes 1572872 | tf_op jit(solution)/shard_map/ppermute | solution.py:374
  86.7 18.8 %collective-permute-start.12 = (bf16[4,4,128,128]{3,2,1,0:T(8,128)(2,1)S(1)}, bf16[4,4,128,128]{3,2,1,0:T(8,128)(2,1)}, u32[]{:S(2)}, u32[]{:S(2)}) collective-permute-start(bf16[4,4,128,128]{3,2,1,0:T(8,128)(2,1)S(1)} %constant_dynamic-update-slice_fusion.rest_0_), channel_id=1, source_target_pairs={{0,1},{1,0},{2,3},{3,2},{4,5},{5,4},{6,7},{7,6},{8,9},{9,8},{10,11... | collective-permute-start | bytes 1572872 | tf_op jit(solution)/shard_map/ppermute | solution.py:374
  97.4 8.2 %collective-permute-start.19 = (bf16[4,4,128,128]{3,2,1,0:T(8,128)(2,1)S(1)}, bf16[4,4,128,128]{3,2,1,0:T(8,128)(2,1)}, u32[]{:S(2)}, u32[]{:S(2)}) collective-permute-start(bf16[4,4,128,128]{3,2,1,0:T(8,128)(2,1)S(1)} %pad_maximum_fusion.1.rest_8_), channel_id=1, source_target_pairs={{0,1},{1,0},{2,3},{3,2},{4,5},{5,4},{6,7},{7,6},{8,9},{9,8},{10,11... | collective-permute-start | bytes 1572872 | tf_op jit(solution)/shard_map/ppermute | solution.py:374
  97.4 8.7 %collective-permute-start.13 = (bf16[4,4,128,128]{3,2,1,0:T(8,128)(2,1)S(1)}, bf16[4,4,128,128]{3,2,1,0:T(8,128)(2,1)}, u32[]{:S(2)}, u32[]{:S(2)}) collective-permute-start(bf16[4,4,128,128]{3,2,1,0:T(8,128)(2,1)S(1)} %collective-permute-done.11.rest_1_), channel_id=1, source_target_pairs={{0,1},{1,0},{2,3},{3,2},{4,5},{5,4},{6,7},{7,6},{8,9},{9,8},{10,11... | collective-permute-start | bytes 1572872 | tf_op jit(solution)/shard_map/ppermute | solution.py:374
  103.0 9.3 %collective-permute-start.14 = (bf16[4,4,128,128]{3,2,1,0:T(8,128)(2,1)S(1)}, bf16[4,4,128,128]{3,2,1,0:T(8,128)(2,1)}, u32[]{:S(2)}, u32[]{:S(2)}) collective-permute-start(bf16[4,4,128,128]{3,2,1,0:T(8,128)(2,1)S(1)} %collective-permute-done.10.rest_4_), channel_id=1, source_target_pairs={{0,2},{1,5},{2,0},{3,7},{4,6},{5,1},{6,4},{7,3},{8,10},{9,13},{10,... | collective-permute-start | bytes 1572872 | tf_op jit(solution)/shard_map/ppermute | solution.py:374
  104.5 13.4 %collective-permute-start.21 = (bf16[4,4,128,128]{3,2,1,0:T(8,128)(2,1)S(1)}, bf16[4,4,128,128]{3,2,1,0:T(8,128)(2,1)}, u32[]{:S(2)}, u32[]{:S(2)}) collective-permute-start(bf16[4,4,128,128]{3,2,1,0:T(8,128)(2,1)S(1)} %collective-permute-done.17.rest_12_), channel_id=1, source_target_pairs={{0,2},{1,5},{2,0},{3,7},{4,6},{5,1},{6,4},{7,3},{8,10},{9,13},{10,... | collective-permute-start | bytes 1572872 | tf_op jit(solution)/shard_map/ppermute | solution.py:374
  105.6 12.5 %collective-permute-start.15 = (bf16[4,4,128,128]{3,2,1,0:T(8,128)(2,1)S(1)}, bf16[4,4,128,128]{3,2,1,0:T(8,128)(2,1)S(1)}, u32[]{:S(2)}, u32[]{:S(2)}) collective-permute-start(bf16[4,4,128,128]{3,2,1,0:T(8,128)(2,1)S(1)} %collective-permute-done.10.rest_4_), channel_id=1, source_target_pairs={{0,1},{1,0},{2,3},{3,2},{4,5},{5,4},{6,7},{7,6},{8,9},{9,8},{10,11... | collective-permute-start | bytes 1572872 | tf_op jit(solution)/shard_map/ppermute | solution.py:374
  105.6 12.4 %collective-permute-start.22 = (bf16[4,4,128,128]{3,2,1,0:T(8,128)(2,1)S(1)}, bf16[4,4,128,128]{3,2,1,0:T(8,128)(2,1)S(1)}, u32[]{:S(2)}, u32[]{:S(2)}) collective-permute-start(bf16[4,4,128,128]{3,2,1,0:T(8,128)(2,1)S(1)} %collective-permute-done.17.rest_12_), channel_id=1, source_target_pairs={{0,1},{1,0},{2,3},{3,2},{4,5},{5,4},{6,7},{7,6},{8,9},{9,8},{10,11... | collective-permute-start | bytes 1572872 | tf_op jit(solution)/shard_map/ppermute | solution.py:374
  106.1 11.9 %collective-permute-start.20 = (bf16[4,4,128,128]{3,2,1,0:T(8,128)(2,1)S(1)}, bf16[4,4,128,128]{3,2,1,0:T(8,128)(2,1)S(1)}, u32[]{:S(2)}, u32[]{:S(2)}) collective-permute-start(bf16[4,4,128,128]{3,2,1,0:T(8,128)(2,1)S(1)} %collective-permute-done.18.rest_9_), channel_id=1, source_target_pairs={{0,1},{1,0},{2,3},{3,2},{4,5},{5,4},{6,7},{7,6},{8,9},{9,8},{10,11... | collective-permute-start | bytes 1572872 | tf_op jit(solution)/shard_map/ppermute | solution.py:374
  112.3 5.7 %collective-permute-start.16 = (bf16[4,4,128,128]{3,2,1,0:T(8,128)(2,1)}, bf16[4,4,128,128]{3,2,1,0:T(8,128)(2,1)S(1)}, u32[]{:S(2)}, u32[]{:S(2)}) collective-permute-start(bf16[4,4,128,128]{3,2,1,0:T(8,128)(2,1)} %collective-permute-done.14.rest_5_), channel_id=1, source_target_pairs={{0,1},{1,0},{2,3},{3,2},{4,5},{5,4},{6,7},{7,6},{8,9},{9,8},{10,11... | collective-permute-start | bytes 1572872 | tf_op jit(solution)/shard_map/ppermute | solution.py:374
  117.9 2.1 collective-permute-start.23
  160.2 7.2 %collective-permute-start.24 = (bf16[16,128,512]{2,1,0:T(8,128)(2,1)S(1)}, bf16[16,128,512]{2,1,0:T(8,128)(2,1)S(1)}, u32[]{:S(2)}, u32[]{:S(2)}) collective-permute-start(bf16[16,128,512]{2,1,0:T(8,128)(2,1)S(1)} %get-tuple-element.52), channel_id=1, source_target_pairs={{0,1},{1,0},{2,3},{3,2},{4,5},{5,4},{6,7},{7,6},{8,9},{9,8},{10,11... | collective-permute-start | bytes 6291464 | tf_op jit(solution)/shard_map/ppermute | solution.py:374
  160.4 15.4 %collective-permute-start.29 = (bf16[16,128,512]{2,1,0:T(8,128)(2,1)S(1)}, bf16[16,128,512]{2,1,0:T(8,128)(2,1)S(1)}, u32[]{:S(2)}, u32[]{:S(2)}) collective-permute-start(bf16[16,128,512]{2,1,0:T(8,128)(2,1)S(1)} %get-tuple-element.54), channel_id=1, source_target_pairs={{0,1},{1,0},{2,3},{3,2},{4,5},{5,4},{6,7},{7,6},{8,9},{9,8},{10,11... | collective-permute-start | bytes 6291464 | tf_op jit(solution)/shard_map/ppermute | solution.py:374
  167.7 14.9 %collective-permute-start.25 = (bf16[8,128,512]{2,1,0:T(8,128)(2,1)S(1)}, bf16[8,128,512]{2,1,0:T(8,128)(2,1)S(1)}, u32[]{:S(2)}, u32[]{:S(2)}) collective-permute-start(bf16[8,128,512]{2,1,0:T(8,128)(2,1)S(1)} %add_convert_fusion), channel_id=1, source_target_pairs={{0,2},{1,5},{2,0},{3,7},{4,6},{5,1},{6,4},{7,3},{8,10},{9,13},{10,... | collective-permute-start | bytes 3145736 | tf_op jit(solution)/shard_map/ppermute | solution.py:374
  176.2 12.0 %collective-permute-start.30 = (bf16[4,128,512]{2,1,0:T(8,128)(2,1)S(1)}, bf16[4,128,512]{2,1,0:T(8,128)(2,1)S(1)}, u32[]{:S(2)}, u32[]{:S(2)}) collective-permute-start(bf16[4,128,512]{2,1,0:T(8,128)(2,1)S(1)} %get-tuple-element.56), channel_id=1, source_target_pairs={{0,2},{1,5},{2,0},{3,7},{4,6},{5,1},{6,4},{7,3},{8,10},{9,13},{10,... | collective-permute-start | bytes 1572872 | tf_op jit(solution)/shard_map/ppermute | solution.py:374
  182.8 13.2 %collective-permute-start.26 = (bf16[4,128,512]{2,1,0:T(8,128)(2,1)S(1)}, bf16[4,128,512]{2,1,0:T(8,128)(2,1)S(1)}, u32[]{:S(2)}, u32[]{:S(2)}) collective-permute-start(bf16[4,128,512]{2,1,0:T(8,128)(2,1)S(1)} %add_convert_fusion.4), channel_id=1, source_target_pairs={{0,8},{1,9},{2,10},{3,11},{4,12},{5,13},{6,14},{7,15},{8,0},{9,1},... | collective-permute-start | bytes 1572872 | tf_op jit(solution)/shard_map/ppermute | solution.py:374
  188.4 14.4 %collective-permute-start.32 = (bf16[4,128,512]{2,1,0:T(8,128)(2,1)S(1)}, bf16[4,128,512]{2,1,0:T(8,128)(2,1)S(1)}, u32[]{:S(2)}, u32[]{:S(2)}) collective-permute-start(bf16[4,128,512]{2,1,0:T(8,128)(2,1)S(1)} %add_convert_fusion.1), channel_id=1, source_target_pairs={{0,4},{1,3},{2,6},{3,1},{4,0},{5,7},{6,2},{7,5},{8,12},{9,11},{10,... | collective-permute-start | bytes 1572872 | tf_op jit(solution)/shard_map/ppermute | solution.py:374
  189.9 13.0 %collective-permute-start.31 = (bf16[4,128,512]{2,1,0:T(8,128)(2,1)S(1)}, bf16[4,128,512]{2,1,0:T(8,128)(2,1)S(1)}, u32[]{:S(2)}, u32[]{:S(2)}) collective-permute-start(bf16[4,128,512]{2,1,0:T(8,128)(2,1)S(1)} %get-tuple-element.58), channel_id=1, source_target_pairs={{0,2},{1,5},{2,0},{3,7},{4,6},{5,1},{6,4},{7,3},{8,10},{9,13},{10,... | collective-permute-start | bytes 1572872 | tf_op jit(solution)/shard_map/ppermute | solution.py:374
  196.1 13.0 %collective-permute-start.27 = (bf16[2,128,512]{2,1,0:T(8,128)(2,1)S(1)}, bf16[2,128,512]{2,1,0:T(8,128)(2,1)S(1)}, u32[]{:S(2)}, u32[]{:S(2)}) collective-permute-start(bf16[2,128,512]{2,1,0:T(8,128)(2,1)S(1)} %add_convert_fusion.6), channel_id=1, source_target_pairs={{0,16},{1,17},{2,18},{3,19},{4,20},{5,21},{6,22},{7,23},{8,24},{9,... | collective-permute-start | bytes 786440 | tf_op jit(solution)/shard_map/ppermute | solution.py:374
  203.0 11.7 %collective-permute-start.33 = (bf16[2,128,512]{2,1,0:T(8,128)(2,1)S(1)}, bf16[2,128,512]{2,1,0:T(8,128)(2,1)S(1)}, u32[]{:S(2)}, u32[]{:S(2)}) collective-permute-start(bf16[2,128,512]{2,1,0:T(8,128)(2,1)S(1)} %add_convert_fusion.5), channel_id=1, source_target_pairs={{0,8},{1,9},{2,10},{3,11},{4,12},{5,13},{6,14},{7,15},{8,0},{9,1},... | collective-permute-start | bytes 786440 | tf_op jit(solution)/shard_map/ppermute | solution.py:374
  209.2 6.0 %collective-permute-start.28 = (bf16[1,128,512]{2,1,0:T(8,128)(2,1)S(1)}, bf16[1,128,512]{2,1,0:T(8,128)(2,1)S(1)}, u32[]{:S(2)}, u32[]{:S(2)}) collective-permute-start(bf16[1,128,512]{2,1,0:T(8,128)(2,1)S(1)} %add_convert_fusion.9), channel_id=1, source_target_pairs={{0,4},{1,3},{2,6},{3,1},{4,0},{5,7},{6,2},{7,5},{8,12},{9,11},{10,... | collective-permute-start | bytes 393224 | tf_op jit(solution)/shard_map/ppermute | solution.py:374
  214.7 8.9 %collective-permute-start.34 = (bf16[1,128,512]{2,1,0:T(8,128)(2,1)S(1)}, bf16[1,128,512]{2,1,0:T(8,128)(2,1)S(1)}, u32[]{:S(2)}, u32[]{:S(2)}) collective-permute-start(bf16[1,128,512]{2,1,0:T(8,128)(2,1)S(1)} %add_convert_fusion.8), channel_id=1, source_target_pairs={{0,16},{1,17},{2,18},{3,19},{4,20},{5,21},{6,22},{7,23},{8,24},{9,... | collective-permute-start | bytes 393224 | tf_op jit(solution)/shard_map/ppermute | solution.py:374

commit v11 on v10

--- a/solution.py
+++ b/solution.py
@@ -124,83 +124,139 @@
     )(info, *pieces, out_proj)
 
 
+ARRAYS = 4
+EARLY = (0, 2)
+REST = (1, 3)
+
+
+def block_at(x_refs, arrays, array, last, high, low):
+    count, number = len(arrays), arrays.index(array)
+    return (
+        array * 8 + low * 4 + high * 2 + last,
+        x_refs[low * count + number].at[high * 2 + last],
+        x_refs[(2 + last) * count + number].at[low * 2 + high],
+    )
+
+
+def dispatch_blocks(arrays, x_refs, info_ref, invgain_ref, hits_ref, sq_ref, xs_ref, column_of):
+    experts, all_rows, _ = xs_ref.shape
+    parts, here, lanes = x_refs[0].shape[1:]
+    rows = all_rows // parts
+    blocks = info_ref.shape[0] // 2 - 1
+
+    def pairs_of_blocks(high, carry):
+        for array in arrays:
+            for last in range(2):
+                pair = [block_at(x_refs, arrays, array, last, high, low) for low in range(2)]
+                swapped = info_ref[blocks + pair[0][0]]
+                for place, own, other in pair:
+                    invgain = invgain_ref[pl.ds(info_ref[place], 1), :]
+                    for part in range(parts):
+                        for half, block in enumerate((own, other)):
+                            value = block[part].astype(F32) * invgain
+                            sq_ref[swapped, part, half] += value * value
+                for part in range(parts):
+                    both = jnp.concatenate(
+                        [
+                            jnp.concatenate([own[part], other[part]], axis=0)
+                            for _, own, other in pair
+                        ],
+                        axis=1,
+                    )
+                    picked = jnp.dot(
+                        hits_ref[swapped, part], both, preferred_element_type=F32
+                    ).astype(BF16)
+                    for number, (place, _, _) in enumerate(pair):
+                        column = pl.multiple_of(column_of(place) * lanes, lanes)
+                        for e in range(experts):
+                            xs_ref[e, part * rows : (part + 1) * rows, pl.ds(column, lanes)] = (
+                                picked[
+                                    e * rows : (e + 1) * rows, number * lanes : (number + 1) * lanes
+                                ]
+                            )
+        return carry
+
+    lax.fori_loop(0, 2, pairs_of_blocks, 0)
+
+
+def early_kernel(
+    rows, info_ref, slot_ref, invgain_ref, x_refs, xs_ref, sq_ref, hits_ref, spread_ref
+):
+    experts = xs_ref.shape[0]
+    parts, here, lanes = x_refs[0].shape[1:]
+    span = 2 * here
+    sq_ref[...] = jnp.zeros_like(sq_ref)
+    for part in range(parts):
+        for e in range(experts):
+            first = hits_of(slot_ref[e : e + 1, part * span : part * span + here], rows)
+            second = hits_of(slot_ref[e : e + 1, part * span + here : (part + 1) * span], rows)
+            first = first.astype(F32).astype(BF16)
+            second = second.astype(F32).astype(BF16)
+            window = slice(e * rows, (e + 1) * rows)
+            hits_ref[0, part, window, :] = jnp.concatenate([first, second], axis=1)
+            hits_ref[1, part, window, :] = jnp.concatenate([second, first], axis=1)
+        spread_ref[part] = jnp.transpose(hits_ref[0, part].astype(F32)).astype(BF16)
+    dispatch_blocks(
+        EARLY, x_refs, info_ref, invgain_ref, hits_ref, sq_ref, xs_ref,
+        lambda place: (place >> 4) * 8 + (place & 7),
+    )
+
+
+def early_dispatch(info, slots, invgain, x, experts, rows):
+    parts, here, lanes = x[0].shape[1:]
+    vmem = pl.BlockSpec(memory_space=pltpu.VMEM)
+
+    def kernel(info_ref, slot_ref, invgain_ref, *rest):
+        early_kernel(rows, info_ref, slot_ref, invgain_ref, rest[: len(x)], *rest[len(x) :])
+
+    return pl.pallas_call(
+        kernel,
+        in_specs=[pl.BlockSpec(memory_space=pltpu.SMEM)] + [vmem] * (len(x) + 2),
+        out_specs=[vmem] * 4,
+        out_shape=[
+            jax.ShapeDtypeStruct((experts, parts * rows, 8 * len(EARLY) * lanes), BF16),
+            jax.ShapeDtypeStruct((2, parts, 2, here, lanes), F32),
+            jax.ShapeDtypeStruct((2, parts, experts * rows, 2 * here), BF16),
+            jax.ShapeDtypeStruct((parts, 2 * here, experts * rows), BF16),
+        ],
+        compiler_params=pltpu.CompilerParams(vmem_limit_bytes=24 * 1024 * 1024),
+        cost_estimate=pl.CostEstimate(
+            flops=4 * experts * rows * x[0].size * len(x) // 4,
+            bytes_accessed=4 * x[0].size * len(x),
+            transcendentals=0,
+        ),
+        name="early_dispatch",
+    )(info, slots, invgain, *x)
+
+
 def gate_up_kernel(
-    experts, rows, width, info_ref, slot_ref, weight_ref, invgain_ref, x_refs, wg_ref, wu_ref,
-    act_ref, hidden_ref, spread_ref, xs_ref, sq_ref, scale_ref, hits_ref
+    rows, width, info_ref, slot_ref, weight_ref, invgain_ref, early_ref, early_sq_ref, hits_ref,
+    x_refs, wg_ref, wu_ref, act_ref, hidden_ref, xs_ref, sq_ref, scale_ref
 ):
     expert = pl.program_id(0)
-    arrays = 4
-    own_refs = (x_refs[:arrays], x_refs[arrays : 2 * arrays])
-    other_refs = (x_refs[2 * arrays : 3 * arrays], x_refs[3 * arrays :])
+    experts = xs_ref.shape[0]
     parts, here, lanes = x_refs[0].shape[1:]
     blocks = info_ref.shape[0] // 2 - 1
-    each = blocks // arrays
     span = 2 * here
     member, z = info_ref[2 * blocks], info_ref[2 * blocks + 1]
-
-    def block_at(array, last, high, low):
-        return (
-            array * each + low * 4 + high * 2 + last,
-            own_refs[low][array].at[high * 2 + last],
-            other_refs[last][array].at[low * 2 + high],
-        )
+    everything = tuple(range(ARRAYS))
 
     @pl.when(expert == 0)
     def _():
-        sq_ref[...] = jnp.zeros_like(sq_ref)
-        for part in range(parts):
-            for e in range(experts):
-                first = hits_of(slot_ref[e : e + 1, part * span : part * span + here], rows)
-                second = hits_of(
-                    slot_ref[e : e + 1, part * span + here : (part + 1) * span], rows
-                )
-                first = first.astype(F32).astype(BF16)
-                second = second.astype(F32).astype(BF16)
-                window = slice(e * rows, (e + 1) * rows)
-                hits_ref[0, part, window, :] = jnp.concatenate([first, second], axis=1)
-                hits_ref[1, part, window, :] = jnp.concatenate([second, first], axis=1)
-            spread_ref[part] = jnp.transpose(hits_ref[0, part].astype(F32)).astype(BF16)
-
-        def pairs_of_blocks(high, carry):
-            for array in range(arrays):
-                for last in range(2):
-                    pair = [block_at(array, last, high, low) for low in range(2)]
-                    swapped = info_ref[blocks + pair[0][0]]
-                    features = [info_ref[place] for place, _, _ in pair]
-                    for feature, (_, own, other) in zip(features, pair):
-                        invgain = invgain_ref[pl.ds(feature, 1), :]
-                        for part in range(parts):
-                            for half, block in enumerate((own, other)):
-                                value = block[part].astype(F32) * invgain
-                                sq_ref[swapped, part, half] += value * value
-                    for part in range(parts):
-                        both = jnp.concatenate(
-                            [
-                                jnp.concatenate([own[part], other[part]], axis=0)
-                                for _, own, other in pair
-                            ],
-                            axis=1,
-                        )
-                        picked = jnp.dot(
-                            hits_ref[swapped, part], both, preferred_element_type=F32
-                        ).astype(BF16)
-                        for number, feature in enumerate(features):
-                            column = pl.multiple_of(feature * lanes, lanes)
-                            for e in range(experts):
-                                xs_ref[
-                                    e, part * rows : (part + 1) * rows, pl.ds(column, lanes)
-                                ] = picked[
-                                    e * rows : (e + 1) * rows, number * lanes : (number + 1) * lanes
-                                ]
-            return carry
-
-        lax.fori_loop(0, 2, pairs_of_blocks, 0)
+        sq_ref[...] = early_sq_ref[...]
+        rest = [
+            x_refs[part * ARRAYS + array] for part in range(len(x_refs) // ARRAYS) for array in REST
+        ]
+        dispatch_blocks(
+            REST, rest, info_ref, invgain_ref, hits_ref, sq_ref, xs_ref,
+            lambda place: info_ref[place],
+        )
 
         def own_blocks(high, carry):
-            for array in range(arrays):
+            for array in everything:
                 for last in range(2):
                     for low in range(2):
-                        place, own, other = block_at(array, last, high, low)
+                        place, own, other = block_at(x_refs, everything, array, last, high, low)
                         feature = info_ref[place]
 
                         @pl.when(feature >> 3 == member)
@@ -228,6 +284,14 @@
         )
         scale_ref[...] = jnp.broadcast_to(lax.rsqrt(total / width + 1e-06), scale_ref.shape)
 
+    def move(number, carry):
+        feature = info_ref[(number >> 3) * 16 + (number & 7)]
+        source = pl.multiple_of(number * lanes, lanes)
+        target = pl.multiple_of(feature * lanes, lanes)
+        xs_ref[expert, :, pl.ds(target, lanes)] = early_ref[0, :, pl.ds(source, lanes)]
+        return carry
+
+    lax.fori_loop(0, 8 * len(EARLY), move, 0)
     summed = jnp.dot(
         xs_ref[expert],
         jnp.concatenate([wg_ref[0], wu_ref[0]], axis=1),
@@ -248,16 +312,13 @@
         act_ref[expert, part * rows : (part + 1) * rows, :] = act.astype(BF16)
 
 
-def gate_up(info, slots, weights, invgain, x, w_gate, w_up, rows, members):
+def gate_up(info, slots, weights, invgain, early, x, w_gate, w_up, rows, members):
     experts, width, hidden_units = w_gate.shape
     parts, here, lanes = x[0].shape[1:]
     tokens = slots.shape[1]
 
-    def kernel(info_ref, slot_ref, weight_ref, invgain_ref, *rest):
-        gate_up_kernel(
-            experts, rows, width, info_ref, slot_ref, weight_ref, invgain_ref,
-            rest[: len(x)], *rest[len(x) :]
-        )
+    def kernel(*refs):
+        gate_up_kernel(rows, width, *refs[:7], refs[7 : 7 + len(x)], *refs[7 + len(x) :])
 
     def whole(shape):
         return pl.BlockSpec(
@@ -270,10 +331,10 @@
             num_scalar_prefetch=1,
             grid=(experts,),
             in_specs=[whole(slots.shape), whole(weights.shape), whole(invgain.shape)]
-            + [pl.BlockSpec(memory_space=pltpu.VMEM)] * len(x)
+            + [pl.BlockSpec((1,) + early[0].shape[1:], lambda e, info: (e, 0, 0))]
+            + [pl.BlockSpec(memory_space=pltpu.VMEM)] * (len(early) - 1 + len(x))
             + [pl.BlockSpec((1, width, hidden_units), lambda e, info: (e, 0, 0))] * 2,
             out_specs=[
-                pl.BlockSpec(memory_space=pltpu.VMEM),
                 pl.BlockSpec(memory_space=pltpu.VMEM),
                 pl.BlockSpec(memory_space=pltpu.VMEM),
             ],
@@ -281,16 +342,14 @@
                 pltpu.VMEM((experts, parts * rows, width), BF16),
                 pltpu.VMEM((2, parts, 2, here, lanes), F32),
                 pltpu.VMEM((8, tokens), F32),
-                pltpu.VMEM((2, parts, experts * rows, 2 * here), BF16),
             ],
         ),
         out_shape=[
             jax.ShapeDtypeStruct((experts, parts * rows, hidden_units), BF16),
             jax.ShapeDtypeStruct((here, width // members), F32),
-            jax.ShapeDtypeStruct((parts, 2 * here, experts * rows), BF16),
         ],
         compiler_params=pltpu.CompilerParams(
-            vmem_limit_bytes=36 * 1024 * 1024, dimension_semantics=("arbitrary",)
+            vmem_limit_bytes=42 * 1024 * 1024, dimension_semantics=("arbitrary",)
         ),
         cost_estimate=pl.CostEstimate(
             flops=2 * experts * parts * rows * width * 2 * hidden_units,
@@ -298,7 +357,7 @@
             transcendentals=0,
         ),
         name="gate_up",
-    )(info, slots, weights, invgain, *x, w_gate, w_up)
+    )(info, slots, weights, invgain, *early, *x, w_gate, w_up)
 
 
 def down_kernel(rows, place_ref, spread_ref, act_ref, wd0_ref, wd1_ref, *rest):
@@ -565,7 +624,7 @@
     return jnp.concatenate([feature, swapped, jnp.stack([member, device >> 3])])
 
 
-def gather_blocks(first, second):
+def gather_blocks(first, second, make_early):
     def along(bits, block):
         return flip(block, lambda core: bits)
 
@@ -585,15 +644,22 @@
     halves = []
     for early, late in ((first, first_low), (second, second_last)):
         early_first = flip(early, first_axis)
+        if halves:
+            early_first, _ = after(early_first, halves[0][1][0])
         late, early_first = after(late, early_first)
         late_first = flip(late, first_axis)
         halves.append(
-            [
-                [block, came, along(CORE, block), along(CORE, came)]
-                for block, came in ((early, early_first), (late, late_first))
-            ]
+            (
+                [early, early_first, along(CORE, early), along(CORE, early_first)],
+                [late, late_first, along(CORE, late)],
+            )
         )
-    return halves
+    made = make_early([part[array] for half in halves for part in half for array in EARLY])
+    x = []
+    for early, late in halves:
+        late_first, made = after(late[1], made)
+        x += early + [late[0], late_first, late[2], along(CORE, late_first)]
+    return x, made
 
 
 def per_device_tokens(
@@ -639,10 +705,13 @@
         hidden = hidden + total_of([keep[1, window], came[1, window], from_x[window]])
         starts.append((hidden * gain).astype(BF16)[None])
 
-    x = [block for half in gather_blocks(*starts) for part in half for block in part]
     invgain = (1.0 / norm_gain).reshape(groups * members, LANES)
-    act, own_hidden, spread = gate_up(
-        block_table(device, groups, member), slots, weights, invgain, x, w_gate, w_up, rows, members
+    table = block_table(device, groups, member)
+    x, (*early, spread) = gather_blocks(
+        *starts, lambda blocks: early_dispatch(table, slots, invgain, blocks, experts, rows)
+    )
+    act, own_hidden = gate_up(
+        table, slots, weights, invgain, early, x, w_gate, w_up, rows, members
     )
 
     cols = width // members

time: 225 us -> 230 us (1.022)
  waiting for transfers between devices: 123 us -> 110 us
  local copies, waits for them, and re-layouts: 4.84 us -> 16.9 us
  Pallas kernels: 56.5 us -> 60.4 us
    ppermute x35, waiting for transfers between devices: 122 us -> 109 us  [flip(): return lax.ppermute(array, ('expert', 'tensor'), pairs)]
    unnamed x18 -> x38, local copies, waits for them, and re-layouts: 3.68 us -> 13.8 us
    pallas_call x0 -> x1, Pallas kernels: none -> 5.21 us  [early_dispatch(): pl.pallas_call(kernel, in_specs=[pl.BlockSpec(memory_space=pltpu.SMEM)] +...]
  transfers between devices with their start and end apart: 36 -> 36, of which waited for: 21 -> 21; matrix products, arithmetic and copies ran while one was open for 2% -> 3% of each run, Pallas kernels for 6% -> 8%
where the time goes in v11:
time: 230 us; the launch traced here: 229 us
  waiting for transfers between devices  110 us (48%)
  Pallas kernels  60.4 us (26%)
  starting transfers between devices  36.7 us (16%)
  local copies, waits for them, and re-layouts  16.9 us (7%)
  other arithmetic  4.52 us (2%)
    ppermute x35, waiting for transfers between devices, flip(): return lax.ppermute(array, ('expert', 'tensor'), pairs)  109 us
    ppermute x35, starting transfers between devices, flip(): return lax.ppermute(array, ('expert', 'tensor'), pairs)  32.9 us
    pallas_call x1, Pallas kernels, gate_up(): pl.pallas_call(kernel, grid_spec=pltpu.PrefetchScalarGridSpec(num_scalar_...  29.5 us
    pallas_call x3, Pallas kernels, down(): pl.pallas_call(functools.partial(down_kernel, rows), grid_spec=pltpu.Pref...  22.8 us
    unnamed x38, local copies, waits for them, and re-layouts  13.8 us
    pallas_call x1, Pallas kernels, early_dispatch(): pl.pallas_call(kernel, in_specs=[pl.BlockSpec(memory_space=pltpu.SMEM)] +...  5.21 us
  transfers between devices with their start and end apart: 36, of which 21 were waited for; matrix products, arithmetic and copies ran while one was open for 3% of the time, Pallas kernels for 8%

profile of v11, /device:TPU:0, one launch (start us, length us, event | category | flops | bytes accessed | tf_op | source)
XLA Modules:
  0.0 229.4 jit_solution(8781323514985541509)
XLA Ops:
  0.0 4.0 %collective-permute-start = (bf16[1,128,1024]{2,1,0:T(8,128)(2,1)}, bf16[1,128,1024]{2,1,0:T(8,128)(2,1)S(1)}, u32[]{:S(2)}, u32[]{:S(2)}) collective-permute-start(bf16[1,128,1024]{2,1,0:T(8,128)(2,1)} %bitcast.67), channel_id=1, source_target_pairs={{0,16},{1,17},{2,18},{3,19},{4,20},{5,21},{6,22},{7,23},{8,24},{9,... | collective-permute-start | bytes 786440 | tf_op jit(solution)/shard_map/ppermute | solution.py:433
  4.0 1.2 copy-done.10
  5.3 0.7 copy-done.11
  6.0 0.7 copy-done.12
  6.6 0.8 pack.1
  7.5 3.8 %all-to-all-start = ((bf16[8,160,128]{2,1,0:T(8,128)(2,1)}), bf16[8,160,128]{2,1,0:T(8,128)(2,1)S(1)}, u32[]{:S(2)}, u32[]{:S(2)}) async-start(bf16[8,160,128]{2,1,0:T(8,128)(2,1)} %pack.1), calls=%async_computation | async-start | bytes 655360 | tf_op jit(solution)/shard_map/all_to_all | solution.py:676
  11.3 9.3 %collective-permute-done = bf16[1,128,1024]{2,1,0:T(8,128)(2,1)S(1)} collective-permute-done((bf16[1,128,1024]{2,1,0:T(8,128)(2,1)}, bf16[1,128,1024]{2,1,0:T(8,128)(2,1)S(1)}, u32[]{:S(2)}, u32[]{:S(2)}) %collective-permute-start) | collective-permute-done | bytes 262176 | tf_op jit(solution)/shard_map/ppermute | solution.py:433
  20.8 1.9 collective-permute-start.1
  23.3 11.2 %collective-permute-done.2.refs_2_ = bf16[2,128,1024]{2,1,0:T(8,128)(2,1)S(1)} collective-permute-done((bf16[2,128,1024]{2,1,0:T(8,128)(2,1)S(1)}, bf16[2,128,1024]{2,1,0:T(8,128)(2,1)S(1)}, u32[]{:S(2)}, u32[]{:S(2)}) %collective-permute-start.2) | collective-permute-done | bytes 524320 | tf_op jit(solution)/shard_map/ppermute | solution.py:433
  35.1 1.0 collective-permute-start.3
  36.4 0.6 reshape.164
  37.0 0.8 convolution_convert_fusion
  37.9 0.6 convert_element_type.294
  38.5 0.8 bitcast_select_fusion.slot_ref.refs_1_
  39.2 5.1 %collective-permute-done.3.refs_3_ = bf16[2,128,1024]{2,1,0:T(8,128)(2,1)S(1)} collective-permute-done((bf16[2,128,1024]{2,1,0:T(8,128)(2,1)S(1)}, bf16[2,128,1024]{2,1,0:T(8,128)(2,1)S(1)}, u32[]{:S(2)}, u32[]{:S(2)}) %collective-permute-start.3) | collective-permute-done | bytes 524320 | tf_op jit(solution)/shard_map/ppermute | solution.py:433
  44.3 0.8 copy-done.14
  45.2 1.0 copy-done.15
  46.2 2.1 project.1
  48.4 1.9 collective-permute-done.4
  50.3 1.6 collective-permute-start.5
  51.9 0.7 fusion.11
  52.7 6.1 %collective-permute-done.5 = bf16[8,128,128]{2,1,0:T(8,128)(2,1)S(1)} collective-permute-done((bf16[8,128,128]{2,1,0:T(8,128)(2,1)S(1)}, bf16[8,128,128]{2,1,0:T(8,128)(2,1)S(1)}, u32[]{:S(2)}, u32[]{:S(2)}) %collective-permute-start.5) | collective-permute-done | bytes 262176 | tf_op jit(solution)/shard_map/ppermute | solution.py:433
  58.9 2.2 collective-permute-start.6
  61.2 1.4 collective-permute-start.7
  62.6 4.9 %collective-permute-done.6 = bf16[1,4,128,128]{3,2,1,0:T(8,128)(2,1)S(1)} collective-permute-done((bf16[1,4,128,128]{3,2,1,0:T(8,128)(2,1)S(1)}, bf16[1,4,128,128]{3,2,1,0:T(8,128)(2,1)S(1)}, u32[]{:S(2)}, u32[]{:S(2)}) %collective-permute-start.6) | collective-permute-done | bytes 131104 | tf_op jit(solution)/shard_map/ppermute | solution.py:433
  67.5 0.7 collective-permute-start.8
  68.2 3.1 %collective-permute-start.9 = (bf16[2,4,128,128]{3,2,1,0:T(8,128)(2,1)S(1)}, bf16[2,4,128,128]{3,2,1,0:T(8,128)(2,1)S(1)}, u32[]{:S(2)}, u32[]{:S(2)}) collective-permute-start(bf16[2,4,128,128]{3,2,1,0:T(8,128)(2,1)S(1)} %pad_maximum_fusion.3), channel_id=1, source_target_pairs={{0,16},{1,17},{2,18},{3,19},{4,20},{5,21},{6,22},{7,23},{8,24},{9,... | collective-permute-start | bytes 786440 | tf_op jit(solution)/shard_map/ppermute | solution.py:433
  71.3 8.7 %collective-permute-done.8 = bf16[2,4,128,128]{3,2,1,0:T(8,128)(2,1)S(1)} collective-permute-done((bf16[2,4,128,128]{3,2,1,0:T(8,128)(2,1)S(1)}, bf16[2,4,128,128]{3,2,1,0:T(8,128)(2,1)S(1)}, u32[]{:S(2)}, u32[]{:S(2)}) %collective-permute-start.8) | collective-permute-done | bytes 262176 | tf_op jit(solution)/shard_map/ppermute | solution.py:433
  80.0 2.9 %collective-permute-done.9 = bf16[2,4,128,128]{3,2,1,0:T(8,128)(2,1)S(1)} collective-permute-done((bf16[2,4,128,128]{3,2,1,0:T(8,128)(2,1)S(1)}, bf16[2,4,128,128]{3,2,1,0:T(8,128)(2,1)S(1)}, u32[]{:S(2)}, u32[]{:S(2)}) %collective-permute-start.9) | collective-permute-done | bytes 262176 | tf_op jit(solution)/shard_map/ppermute | solution.py:433
  83.0 1.6 collective-permute-start.13
  85.3 1.4 collective-permute-start.10
  86.7 10.9 %collective-permute-done.13.refs_8_ = bf16[4,4,128,128]{3,2,1,0:T(8,128)(2,1)} collective-permute-done((bf16[4,4,128,128]{3,2,1,0:T(8,128)(2,1)S(1)}, bf16[4,4,128,128]{3,2,1,0:T(8,128)(2,1)}, u32[]{:S(2)}, u32[]{:S(2)}) %collective-permute-start.13) | collective-permute-done | bytes 524320 | tf_op jit(solution)/shard_map/ppermute | solution.py:433
  98.2 5.1 %collective-permute-done.11.refs_16_ = bf16[4,4,128,128]{3,2,1,0:T(8,128)(2,1)} collective-permute-done((bf16[4,4,128,128]{3,2,1,0:T(8,128)(2,1)S(1)}, bf16[4,4,128,128]{3,2,1,0:T(8,128)(2,1)}, u32[]{:S(2)}, u32[]{:S(2)}) %collective-permute-start.11) | collective-permute-done | bytes 524320 | tf_op jit(solution)/shard_map/ppermute | solution.py:433
  103.4 1.5 collective-permute-start.15
  106.0 5.2 %early_dispatch.1 = (bf16[8,192,2048]{2,1,0:T(8,128)(2,1)S(1)}, f32[2,4,2,128,128]{4,3,2,1,0:T(8,128)S(1)}, bf16[2,4,384,256]{3,2,1,0:T(8,128)(2,1)S(1)}, bf16[4,256,384]{2,1,0:T(8,128)(2,1)S(1)}) custom-call(s32[66]{0:T(128)S(1)} %pad_add_fusion.info_ref.refs_0_, s32[8,1024]{1,0:T(8,128)S(1)} %bitcast_select_fusion.slot_ref.refs_1_, ...), custom_call_target="tpu_custom_call" | custom-call | flops 805306368 | bytes 8388608 | tf_op jit(solution)/shard_map/early_dispatch/pallas_call | solution.py:212
  111.3 2.7 %copy-done = bf16[8,192,2048]{2,1,0:T(8,128)(2,1)} copy-done((bf16[8,192,2048]{2,1,0:T(8,128)(2,1)}, bf16[8,192,2048]{2,1,0:T(8,128)(2,1)S(1)}, u32[]{:S(2)}) %copy-start) | copy-done | bytes 6291480
  114.0 1.2 copy-done.7
  115.2 1.0 copy-done.8
  116.2 2.0 collective-permute-done.14.refs_20_
  119.5 1.1 collective-permute-done.23.refs_22_
  120.5 0.7 collective-permute-done.21.refs_14_
  121.3 1.0 copy-done.2
  122.3 1.0 copy-done.4
  123.4 1.0 copy-done.6
  124.4 1.2 copy-done.9
  125.6 29.5 %gate_up.1 = (bf16[8,192,384]{2,1,0:T(8,128)(2,1)S(1)}, f32[128,1024]{1,0:T(8,128)S(1)}) custom-call(s32[66]{0:T(128)S(1)} %pad_add_fusion.info_ref.refs_0_, s32[8,1024]{1,0:T(8,128)S(1)} %bitcast_select_fusion.slot_ref.refs_1_, f32[8,1024]{1,0:T(8,128)S(1)} %bitcast.63, f32[32,128]{1,0:T(8,128)S(1)} %divide_bitcast_fusion.invgain_ref.refs_3_, ...), custom_call_target="tpu_custom_call" | custom-call | flops 9663676416 | bytes 58720256 | tf_op jit(solution)/shard_map/gate_up/pallas_call | solution.py:328
  155.1 9.9 %down_mix.4 = (bf16[16,128,512]{2,1,0:T(8,128)(2,1)S(1)}, bf16[16,128,512]{2,1,0:T(8,128)(2,1)S(1)}) custom-call(s32[34]{0:T(128)S(1)} %pad_add_fusion.3.place_ref, bf16[4,256,384]{2,1,0:T(8,128)(2,1)S(1)} %get-tuple-element.78.spread_ref, bf16[8,192,384]{2,1,0:T(8,128)(2,1)S(1)} %get-tuple-element.79.act_ref, bf16[8,384,4096]{2,1,0:T(8,128)(2,1)} %wd1_ref.5, ...), custom_call_target="tpu_custom_call" | custom-call | flops 4831838208 | bytes 16777216 | tf_op jit(solution)/shard_map/down_mix/pallas_call | solution.py:402
  165.8 6.4 %down_mix.3 = bf16[16,128,512]{2,1,0:T(8,128)(2,1)S(1)} custom-call(s32[18]{0:T(128)S(1)} %pad_add_fusion.2.place_ref, bf16[4,256,384]{2,1,0:T(8,128)(2,1)S(1)} %get-tuple-element.78.spread_ref, bf16[8,192,384]{2,1,0:T(8,128)(2,1)S(1)} %get-tuple-element.79.act_ref, bf16[8,384,4096]{2,1,0:T(8,128)(2,1)} %wd1_ref.5, bf16[8,384,4096]{2,1,0:T(8,128)(2,1)} %wd1_ref.5), custom_call_target="tpu_custom_call" | custom-call | flops 2415919104 | bytes 8388608 | tf_op jit(solution)/shard_map/down_mix/pallas_call | solution.py:402
  172.5 1.6 collective-permute-start.25
  174.2 6.4 %down_mix.5 = bf16[16,128,512]{2,1,0:T(8,128)(2,1)S(1)} custom-call(s32[18]{0:T(128)S(1)} %pad_add_fusion.4.place_ref, bf16[4,256,384]{2,1,0:T(8,128)(2,1)S(1)} %get-tuple-element.78.spread_ref, bf16[8,192,384]{2,1,0:T(8,128)(2,1)S(1)} %get-tuple-element.79.act_ref, bf16[8,384,4096]{2,1,0:T(8,128)(2,1)} %wd1_ref.5, bf16[8,384,4096]{2,1,0:T(8,128)(2,1)} %wd1_ref.5), custom_call_target="tpu_custom_call" | custom-call | flops 2415919104 | bytes 8388608 | tf_op jit(solution)/shard_map/down_mix/pallas_call | solution.py:402
  181.0 0.6 collective-permute-start.30
  181.5 5.9 %collective-permute-done.25 = bf16[8,128,512]{2,1,0:T(8,128)(2,1)S(1)} collective-permute-done((bf16[8,128,512]{2,1,0:T(8,128)(2,1)S(1)}, bf16[8,128,512]{2,1,0:T(8,128)(2,1)S(1)}, u32[]{:S(2)}, u32[]{:S(2)}) %collective-permute-start.25) | collective-permute-done | bytes 1048608 | tf_op jit(solution)/shard_map/ppermute | solution.py:433
  188.0 5.1 %collective-permute-done.30 = bf16[4,128,512]{2,1,0:T(8,128)(2,1)S(1)} collective-permute-done((bf16[4,128,512]{2,1,0:T(8,128)(2,1)S(1)}, bf16[4,128,512]{2,1,0:T(8,128)(2,1)S(1)}, u32[]{:S(2)}, u32[]{:S(2)}) %collective-permute-start.30) | collective-permute-done | bytes 524320 | tf_op jit(solution)/shard_map/ppermute | solution.py:433
  193.2 1.5 collective-permute-start.32
  194.7 1.5 collective-permute-start.31
  196.2 4.6 %collective-permute-done.26 = bf16[4,128,512]{2,1,0:T(8,128)(2,1)S(1)} collective-permute-done((bf16[4,128,512]{2,1,0:T(8,128)(2,1)S(1)}, bf16[4,128,512]{2,1,0:T(8,128)(2,1)S(1)}, u32[]{:S(2)}, u32[]{:S(2)}) %collective-permute-start.26) | collective-permute-done | bytes 524320 | tf_op jit(solution)/shard_map/ppermute | solution.py:433
  200.9 1.1 collective-permute-start.27
  202.0 5.7 %collective-permute-done.32 = bf16[4,128,512]{2,1,0:T(8,128)(2,1)S(1)} collective-permute-done((bf16[4,128,512]{2,1,0:T(8,128)(2,1)S(1)}, bf16[4,128,512]{2,1,0:T(8,128)(2,1)S(1)}, u32[]{:S(2)}, u32[]{:S(2)}) %collective-permute-start.32) | collective-permute-done | bytes 524320 | tf_op jit(solution)/shard_map/ppermute | solution.py:433
  208.1 5.8 %collective-permute-done.27 = bf16[2,128,512]{2,1,0:T(8,128)(2,1)S(1)} collective-permute-done((bf16[2,128,512]{2,1,0:T(8,128)(2,1)S(1)}, bf16[2,128,512]{2,1,0:T(8,128)(2,1)S(1)}, u32[]{:S(2)}, u32[]{:S(2)}) %collective-permute-start.27) | collective-permute-done | bytes 262176 | tf_op jit(solution)/shard_map/ppermute | solution.py:433
  214.0 1.5 collective-permute-start.28
  215.4 3.9 %collective-permute-done.33 = bf16[2,128,512]{2,1,0:T(8,128)(2,1)S(1)} collective-permute-done((bf16[2,128,512]{2,1,0:T(8,128)(2,1)S(1)}, bf16[2,128,512]{2,1,0:T(8,128)(2,1)S(1)}, u32[]{:S(2)}, u32[]{:S(2)}) %collective-permute-start.33) | collective-permute-done | bytes 262176 | tf_op jit(solution)/shard_map/ppermute | solution.py:433
  219.5 0.6 collective-permute-start.34
  220.2 8.3 %collective-permute-done.34 = bf16[1,128,512]{2,1,0:T(8,128)(2,1)S(1)} collective-permute-done((bf16[1,128,512]{2,1,0:T(8,128)(2,1)S(1)}, bf16[1,128,512]{2,1,0:T(8,128)(2,1)S(1)}, u32[]{:S(2)}, u32[]{:S(2)}) %collective-permute-start.34) | collective-permute-done | bytes 131104 | tf_op jit(solution)/shard_map/ppermute | solution.py:433
  228.6 0.8 fusion
  (108 shorter events, 9.1 us)
Async XLA Ops:
  0.0 20.6 %collective-permute-start = (bf16[1,128,1024]{2,1,0:T(8,128)(2,1)}, bf16[1,128,1024]{2,1,0:T(8,128)(2,1)S(1)}, u32[]{:S(2)}, u32[]{:S(2)}) collective-permute-start(bf16[1,128,1024]{2,1,0:T(8,128)(2,1)} %bitcast.67), channel_id=1, source_target_pairs={{0,16},{1,17},{2,18},{3,19},{4,20},{5,21},{6,22},{7,23},{8,24},{9,... | collective-permute-start | bytes 786440 | tf_op jit(solution)/shard_map/ppermute | solution.py:433
  4.0 1.2 copy-start.10
  5.3 0.7 copy-start.11
  6.0 0.7 copy-start.12
  6.6 13.9 %copy-start.16 = (bf16[128,1024]{1,0:T(8,128)(2,1)S(1)}, bf16[128,1024]{1,0:T(8,128)(2,1)}, u32[]{:S(2)}) copy-start(bf16[128,1024]{1,0:T(8,128)(2,1)} %param.9) | copy-start | bytes 786436
  6.6 38.5 %copy-start.13 = (bf16[1024,512]{1,0:T(8,128)(2,1)S(1)}, bf16[1024,512]{1,0:T(8,128)(2,1)}, u32[]{:S(2)}) copy-start(bf16[1024,512]{1,0:T(8,128)(2,1)} %refs_4_.1) | copy-start | bytes 3145732
  7.5 15.8 %all-to-all-start = ((bf16[8,160,128]{2,1,0:T(8,128)(2,1)}), bf16[8,160,128]{2,1,0:T(8,128)(2,1)S(1)}, u32[]{:S(2)}, u32[]{:S(2)}) async-start(bf16[8,160,128]{2,1,0:T(8,128)(2,1)} %pack.1), calls=%async_computation | async-start | bytes 655360 | tf_op jit(solution)/shard_map/all_to_all | solution.py:676
  20.6 13.9 %collective-permute-start.2 = (bf16[2,128,1024]{2,1,0:T(8,128)(2,1)S(1)}, bf16[2,128,1024]{2,1,0:T(8,128)(2,1)S(1)}, u32[]{:S(2)}, u32[]{:S(2)}) collective-permute-start(bf16[2,128,1024]{2,1,0:T(8,128)(2,1)S(1)} %pad_maximum_fusion.refs_0_), channel_id=1, source_target_pairs={{0,8},{1,5},{2,10},{3,7},{4,12},{5,1},{6,14},{7,3},{8,0},{9,13},{1... | collective-permute-start | bytes 1572872 | tf_op jit(solution)/shard_map/ppermute | solution.py:433
  20.8 13.7 %collective-permute-start.1 = (bf16[2,128,1024]{2,1,0:T(8,128)(2,1)S(1)}, bf16[2,128,1024]{2,1,0:T(8,128)(2,1)S(1)}, u32[]{:S(2)}, u32[]{:S(2)}) collective-permute-start(bf16[2,128,1024]{2,1,0:T(8,128)(2,1)S(1)} %pad_maximum_fusion.refs_0_), channel_id=1, source_target_pairs={{0,4},{1,9},{2,6},{3,11},{4,0},{5,13},{6,2},{7,15},{8,12},{9,1},{1... | collective-permute-start | bytes 1572872 | tf_op jit(solution)/shard_map/ppermute | solution.py:433
  35.1 9.2 %collective-permute-start.3 = (bf16[2,128,1024]{2,1,0:T(8,128)(2,1)S(1)}, bf16[2,128,1024]{2,1,0:T(8,128)(2,1)S(1)}, u32[]{:S(2)}, u32[]{:S(2)}) collective-permute-start(bf16[2,128,1024]{2,1,0:T(8,128)(2,1)S(1)} %collective-permute-done.1.refs_1_), channel_id=1, source_target_pairs={{0,8},{1,5},{2,10},{3,7},{4,12},{5,1},{6,14},{7,3},{8,0},{9,13},{1... | collective-permute-start | bytes 1572872 | tf_op jit(solution)/shard_map/ppermute | solution.py:433
  44.3 0.8 copy-start.14
  45.1 1.0 copy-start.15
  48.3 2.0 collective-permute-start.4
  50.3 8.4 %collective-permute-start.5 = (bf16[8,128,128]{2,1,0:T(8,128)(2,1)S(1)}, bf16[8,128,128]{2,1,0:T(8,128)(2,1)S(1)}, u32[]{:S(2)}, u32[]{:S(2)}) collective-permute-start(bf16[8,128,128]{2,1,0:T(8,128)(2,1)S(1)} %fusion.2), channel_id=1, source_target_pairs={{0,2},{1,3},{2,0},{3,1},{4,6},{5,7},{6,4},{7,5},{8,10},{9,11},{10,... | collective-permute-start | bytes 786440 | tf_op jit(solution)/shard_map/ppermute | solution.py:433
  58.8 46.7 %copy-start.17 = (f32[4096]{0:T(1024)S(1)}, f32[4096]{0:T(1024)}, u32[]{:S(2)}) copy-start(f32[4096]{0:T(1024)} %param.12) | copy-start | bytes 49156
  58.9 8.5 %collective-permute-start.6 = (bf16[1,4,128,128]{3,2,1,0:T(8,128)(2,1)S(1)}, bf16[1,4,128,128]{3,2,1,0:T(8,128)(2,1)S(1)}, u32[]{:S(2)}, u32[]{:S(2)}) collective-permute-start(bf16[1,4,128,128]{3,2,1,0:T(8,128)(2,1)S(1)} %get-tuple-element.94), channel_id=1, source_target_pairs={{0,16},{1,17},{2,18},{3,19},{4,20},{5,21},{6,22},{7,23},{8,24},{9,... | collective-permute-start | bytes 393224 | tf_op jit(solution)/shard_map/ppermute | solution.py:433
  61.2 6.3 %collective-permute-start.7 = (bf16[1,4,128,128]{3,2,1,0:T(8,128)(2,1)S(1)}, bf16[1,4,128,128]{3,2,1,0:T(8,128)(2,1)S(1)}, u32[]{:S(2)}, u32[]{:S(2)}) collective-permute-start(bf16[1,4,128,128]{3,2,1,0:T(8,128)(2,1)S(1)} %get-tuple-element.93), channel_id=1, source_target_pairs={{0,4},{1,3},{2,6},{3,1},{4,0},{5,7},{6,2},{7,5},{8,12},{9,11},{10,... | collective-permute-start | bytes 393224 | tf_op jit(solution)/shard_map/ppermute | solution.py:433
  67.5 12.5 %collective-permute-start.8 = (bf16[2,4,128,128]{3,2,1,0:T(8,128)(2,1)S(1)}, bf16[2,4,128,128]{3,2,1,0:T(8,128)(2,1)S(1)}, u32[]{:S(2)}, u32[]{:S(2)}) collective-permute-start(bf16[2,4,128,128]{3,2,1,0:T(8,128)(2,1)S(1)} %pad_maximum_fusion.2), channel_id=1, source_target_pairs={{0,8},{1,9},{2,10},{3,11},{4,12},{5,13},{6,14},{7,15},{8,0},{9,1},... | collective-permute-start | bytes 786440 | tf_op jit(solution)/shard_map/ppermute | solution.py:433
  68.2 14.8 %collective-permute-start.9 = (bf16[2,4,128,128]{3,2,1,0:T(8,128)(2,1)S(1)}, bf16[2,4,128,128]{3,2,1,0:T(8,128)(2,1)S(1)}, u32[]{:S(2)}, u32[]{:S(2)}) collective-permute-start(bf16[2,4,128,128]{3,2,1,0:T(8,128)(2,1)S(1)} %pad_maximum_fusion.3), channel_id=1, source_target_pairs={{0,16},{1,17},{2,18},{3,19},{4,20},{5,21},{6,22},{7,23},{8,24},{9,... | collective-permute-start | bytes 786440 | tf_op jit(solution)/shard_map/ppermute | solution.py:433
  83.0 14.7 %collective-permute-start.13 = (bf16[4,4,128,128]{3,2,1,0:T(8,128)(2,1)S(1)}, bf16[4,4,128,128]{3,2,1,0:T(8,128)(2,1)}, u32[]{:S(2)}, u32[]{:S(2)}) collective-permute-start(bf16[4,4,128,128]{3,2,1,0:T(8,128)(2,1)S(1)} %constant_dynamic-update-slice_fusion.rest_0_.refs_7_), channel_id=1, source_target_pairs={{0,2},{1,5},{2,0},{3,7},{4,6},{5,1},{6,4},{7,3},{8,10},{9,13},{10,... | collective-permute-start | bytes 1572872 | tf_op jit(solution)/shard_map/ppermute | solution.py:433
  84.5 13.1 %collective-permute-start.12 = (bf16[4,4,128,128]{3,2,1,0:T(8,128)(2,1)S(1)}, bf16[4,4,128,128]{3,2,1,0:T(8,128)(2,1)S(1)}, u32[]{:S(2)}, u32[]{:S(2)}) collective-permute-start(bf16[4,4,128,128]{3,2,1,0:T(8,128)(2,1)S(1)} %constant_dynamic-update-slice_fusion.rest_0_.refs_7_), channel_id=1, source_target_pairs={{0,8},{1,9},{2,10},{3,11},{4,12},{5,13},{6,14},{7,15},{8,0},{9,1},... | collective-permute-start | bytes 1572872 | tf_op jit(solution)/shard_map/ppermute | solution.py:433
  84.8 18.5 %collective-permute-start.11 = (bf16[4,4,128,128]{3,2,1,0:T(8,128)(2,1)S(1)}, bf16[4,4,128,128]{3,2,1,0:T(8,128)(2,1)}, u32[]{:S(2)}, u32[]{:S(2)}) collective-permute-start(bf16[4,4,128,128]{3,2,1,0:T(8,128)(2,1)S(1)} %pad_maximum_fusion.1.rest_4_.refs_15_), channel_id=1, source_target_pairs={{0,2},{1,5},{2,0},{3,7},{4,6},{5,1},{6,4},{7,3},{8,10},{9,13},{10,... | collective-permute-start | bytes 1572872 | tf_op jit(solution)/shard_map/ppermute | solution.py:433
  85.3 18.0 %collective-permute-start.10 = (bf16[4,4,128,128]{3,2,1,0:T(8,128)(2,1)S(1)}, bf16[4,4,128,128]{3,2,1,0:T(8,128)(2,1)S(1)}, u32[]{:S(2)}, u32[]{:S(2)}) collective-permute-start(bf16[4,4,128,128]{3,2,1,0:T(8,128)(2,1)S(1)} %pad_maximum_fusion.1.rest_4_.refs_15_), channel_id=1, source_target_pairs={{0,4},{1,3},{2,6},{3,1},{4,0},{5,7},{6,2},{7,5},{8,12},{9,11},{10,... | collective-permute-start | bytes 1572872 | tf_op jit(solution)/shard_map/ppermute | solution.py:433
  86.7 18.1 %collective-permute-start.16 = (bf16[4,4,128,128]{3,2,1,0:T(8,128)(2,1)S(1)}, bf16[4,4,128,128]{3,2,1,0:T(8,128)(2,1)S(1)}, u32[]{:S(2)}, u32[]{:S(2)}) collective-permute-start(bf16[4,4,128,128]{3,2,1,0:T(8,128)(2,1)S(1)} %constant_dynamic-update-slice_fusion.rest_0_.refs_7_), channel_id=1, source_target_pairs={{0,1},{1,0},{2,3},{3,2},{4,5},{5,4},{6,7},{7,6},{8,9},{9,8},{10,11... | collective-permute-start | bytes 1572872 | tf_op jit(solution)/shard_map/ppermute | solution.py:433
  97.7 7.8 %collective-permute-start.18 = (bf16[4,4,128,128]{3,2,1,0:T(8,128)(2,1)S(1)}, bf16[4,4,128,128]{3,2,1,0:T(8,128)(2,1)S(1)}, u32[]{:S(2)}, u32[]{:S(2)}) collective-permute-start(bf16[4,4,128,128]{3,2,1,0:T(8,128)(2,1)S(1)} %pad_maximum_fusion.1.rest_4_.refs_15_), channel_id=1, source_target_pairs={{0,1},{1,0},{2,3},{3,2},{4,5},{5,4},{6,7},{7,6},{8,9},{9,8},{10,11... | collective-permute-start | bytes 1572872 | tf_op jit(solution)/shard_map/ppermute | solution.py:433
  97.7 7.8 %collective-permute-start.17 = (bf16[4,4,128,128]{3,2,1,0:T(8,128)(2,1)S(1)}, bf16[4,4,128,128]{3,2,1,0:T(8,128)(2,1)S(1)}, u32[]{:S(2)}, u32[]{:S(2)}) collective-permute-start(bf16[4,4,128,128]{3,2,1,0:T(8,128)(2,1)S(1)} %collective-permute-done.12.rest_2_.refs_11_), channel_id=1, source_target_pairs={{0,1},{1,0},{2,3},{3,2},{4,5},{5,4},{6,7},{7,6},{8,9},{9,8},{10,11... | collective-permute-start | bytes 1572872 | tf_op jit(solution)/shard_map/ppermute | solution.py:433
  103.3 2.7 %collective-permute-start.19 = (bf16[4,4,128,128]{3,2,1,0:T(8,128)(2,1)S(1)}, bf16[4,4,128,128]{3,2,1,0:T(8,128)(2,1)S(1)}, u32[]{:S(2)}, u32[]{:S(2)}) collective-permute-start(bf16[4,4,128,128]{3,2,1,0:T(8,128)(2,1)S(1)} %collective-permute-done.10.rest_6_.refs_19_), channel_id=1, source_target_pairs={{0,1},{1,0},{2,3},{3,2},{4,5},{5,4},{6,7},{7,6},{8,9},{9,8},{10,11... | collective-permute-start | bytes 1572872 | tf_op jit(solution)/shard_map/ppermute | solution.py:433
  103.4 12.9 %collective-permute-start.15 = (bf16[4,4,128,128]{3,2,1,0:T(8,128)(2,1)S(1)}, bf16[4,4,128,128]{3,2,1,0:T(8,128)(2,1)}, u32[]{:S(2)}, u32[]{:S(2)}) collective-permute-start(bf16[4,4,128,128]{3,2,1,0:T(8,128)(2,1)S(1)} %collective-permute-done.12.rest_2_.refs_11_), channel_id=1, source_target_pairs={{0,2},{1,5},{2,0},{3,7},{4,6},{5,1},{6,4},{7,3},{8,10},{9,13},{10,... | collective-permute-start | bytes 1572872 | tf_op jit(solution)/shard_map/ppermute | solution.py:433
  104.9 13.4 %collective-permute-start.14 = (bf16[4,4,128,128]{3,2,1,0:T(8,128)(2,1)S(1)}, bf16[4,4,128,128]{3,2,1,0:T(8,128)(2,1)}, u32[]{:S(2)}, u32[]{:S(2)}) collective-permute-start(bf16[4,4,128,128]{3,2,1,0:T(8,128)(2,1)S(1)} %collective-permute-done.10.rest_6_.refs_19_), channel_id=1, source_target_pairs={{0,2},{1,5},{2,0},{3,7},{4,6},{5,1},{6,4},{7,3},{8,10},{9,13},{10,... | collective-permute-start | bytes 1572872 | tf_op jit(solution)/shard_map/ppermute | solution.py:433
  105.4 5.8 %copy-start.1 = (bf16[4,4,128,128]{3,2,1,0:T(8,128)(2,1)}, bf16[4,4,128,128]{3,2,1,0:T(8,128)(2,1)S(1)}, u32[]{:S(2)}) copy-start(bf16[4,4,128,128]{3,2,1,0:T(8,128)(2,1)S(1)} %collective-permute-done.18.rest_5_.refs_17_) | copy-start | bytes 1572868
  105.4 14.0 %collective-permute-start.20 = (bf16[4,4,128,128]{3,2,1,0:T(8,128)(2,1)}, bf16[4,4,128,128]{3,2,1,0:T(8,128)(2,1)}, u32[]{:S(2)}, u32[]{:S(2)}) collective-permute-start(bf16[4,4,128,128]{3,2,1,0:T(8,128)(2,1)} %collective-permute-done.13.refs_8_), channel_id=1, source_target_pairs={{0,1},{1,0},{2,3},{3,2},{4,5},{5,4},{6,7},{7,6},{8,9},{9,8},{10,11... | collective-permute-start | bytes 1572872 | tf_op jit(solution)/shard_map/ppermute | solution.py:433
  105.5 5.7 %copy-start.3 = (bf16[4,4,128,128]{3,2,1,0:T(8,128)(2,1)}, bf16[4,4,128,128]{3,2,1,0:T(8,128)(2,1)S(1)}, u32[]{:S(2)}) copy-start(bf16[4,4,128,128]{3,2,1,0:T(8,128)(2,1)S(1)} %collective-permute-done.17.rest_3_.refs_13_) | copy-start | bytes 1572868
  105.5 13.9 %collective-permute-start.22 = (bf16[4,4,128,128]{3,2,1,0:T(8,128)(2,1)}, bf16[4,4,128,128]{3,2,1,0:T(8,128)(2,1)}, u32[]{:S(2)}, u32[]{:S(2)}) collective-permute-start(bf16[4,4,128,128]{3,2,1,0:T(8,128)(2,1)} %collective-permute-done.11.refs_16_), channel_id=1, source_target_pairs={{0,1},{1,0},{2,3},{3,2},{4,5},{5,4},{6,7},{7,6},{8,9},{9,8},{10,11... | collective-permute-start | bytes 1572872 | tf_op jit(solution)/shard_map/ppermute | solution.py:433
  106.0 5.2 %copy-start.5 = (bf16[4,4,128,128]{3,2,1,0:T(8,128)(2,1)}, bf16[4,4,128,128]{3,2,1,0:T(8,128)(2,1)S(1)}, u32[]{:S(2)}) copy-start(bf16[4,4,128,128]{3,2,1,0:T(8,128)(2,1)S(1)} %collective-permute-done.19.rest_7_.refs_21_) | copy-start | bytes 1572868
  111.3 2.7 %copy-start = (bf16[8,192,2048]{2,1,0:T(8,128)(2,1)}, bf16[8,192,2048]{2,1,0:T(8,128)(2,1)S(1)}, u32[]{:S(2)}) copy-start(bf16[8,192,2048]{2,1,0:T(8,128)(2,1)S(1)} %get-tuple-element.70.refs_4_) | copy-start | bytes 18874372
  114.0 1.2 copy-start.7
  115.2 1.0 copy-start.8
  118.3 2.3 collective-permute-start.23
  118.3 3.0 %collective-permute-start.21 = (bf16[4,4,128,128]{3,2,1,0:T(8,128)(2,1)}, bf16[4,4,128,128]{3,2,1,0:T(8,128)(2,1)}, u32[]{:S(2)}, u32[]{:S(2)}) collective-permute-start(bf16[4,4,128,128]{3,2,1,0:T(8,128)(2,1)} %collective-permute-done.15.refs_12_), channel_id=1, source_target_pairs={{0,1},{1,0},{2,3},{3,2},{4,5},{5,4},{6,7},{7,6},{8,9},{9,8},{10,11... | collective-permute-start | bytes 1572872 | tf_op jit(solution)/shard_map/ppermute | solution.py:433
  121.3 1.0 copy-start.2
  122.3 1.0 copy-start.4
  123.4 1.0 copy-start.6
  124.4 1.2 copy-start.9
  165.0 7.2 %collective-permute-start.24 = (bf16[16,128,512]{2,1,0:T(8,128)(2,1)S(1)}, bf16[16,128,512]{2,1,0:T(8,128)(2,1)S(1)}, u32[]{:S(2)}, u32[]{:S(2)}) collective-permute-start(bf16[16,128,512]{2,1,0:T(8,128)(2,1)S(1)} %get-tuple-element.80), channel_id=1, source_target_pairs={{0,1},{1,0},{2,3},{3,2},{4,5},{5,4},{6,7},{7,6},{8,9},{9,8},{10,11... | collective-permute-start | bytes 6291464 | tf_op jit(solution)/shard_map/ppermute | solution.py:433
  165.2 15.4 %collective-permute-start.29 = (bf16[16,128,512]{2,1,0:T(8,128)(2,1)S(1)}, bf16[16,128,512]{2,1,0:T(8,128)(2,1)S(1)}, u32[]{:S(2)}, u32[]{:S(2)}) collective-permute-start(bf16[16,128,512]{2,1,0:T(8,128)(2,1)S(1)} %get-tuple-element.82), channel_id=1, source_target_pairs={{0,1},{1,0},{2,3},{3,2},{4,5},{5,4},{6,7},{7,6},{8,9},{9,8},{10,11... | collective-permute-start | bytes 6291464 | tf_op jit(solution)/shard_map/ppermute | solution.py:433
  172.5 14.9 %collective-permute-start.25 = (bf16[8,128,512]{2,1,0:T(8,128)(2,1)S(1)}, bf16[8,128,512]{2,1,0:T(8,128)(2,1)S(1)}, u32[]{:S(2)}, u32[]{:S(2)}) collective-permute-start(bf16[8,128,512]{2,1,0:T(8,128)(2,1)S(1)} %add_convert_fusion), channel_id=1, source_target_pairs={{0,2},{1,5},{2,0},{3,7},{4,6},{5,1},{6,4},{7,3},{8,10},{9,13},{10,... | collective-permute-start | bytes 3145736 | tf_op jit(solution)/shard_map/ppermute | solution.py:433
  181.0 12.1 %collective-permute-start.30 = (bf16[4,128,512]{2,1,0:T(8,128)(2,1)S(1)}, bf16[4,128,512]{2,1,0:T(8,128)(2,1)S(1)}, u32[]{:S(2)}, u32[]{:S(2)}) collective-permute-start(bf16[4,128,512]{2,1,0:T(8,128)(2,1)S(1)} %get-tuple-element.84), channel_id=1, source_target_pairs={{0,2},{1,5},{2,0},{3,7},{4,6},{5,1},{6,4},{7,3},{8,10},{9,13},{10,... | collective-permute-start | bytes 1572872 | tf_op jit(solution)/shard_map/ppermute | solution.py:433
  187.6 13.1 %collective-permute-start.26 = (bf16[4,128,512]{2,1,0:T(8,128)(2,1)S(1)}, bf16[4,128,512]{2,1,0:T(8,128)(2,1)S(1)}, u32[]{:S(2)}, u32[]{:S(2)}) collective-permute-start(bf16[4,128,512]{2,1,0:T(8,128)(2,1)S(1)} %add_convert_fusion.4), channel_id=1, source_target_pairs={{0,8},{1,9},{2,10},{3,11},{4,12},{5,13},{6,14},{7,15},{8,0},{9,1},... | collective-permute-start | bytes 1572872 | tf_op jit(solution)/shard_map/ppermute | solution.py:433
  193.2 14.4 %collective-permute-start.32 = (bf16[4,128,512]{2,1,0:T(8,128)(2,1)S(1)}, bf16[4,128,512]{2,1,0:T(8,128)(2,1)S(1)}, u32[]{:S(2)}, u32[]{:S(2)}) collective-permute-start(bf16[4,128,512]{2,1,0:T(8,128)(2,1)S(1)} %add_convert_fusion.1), channel_id=1, source_target_pairs={{0,4},{1,3},{2,6},{3,1},{4,0},{5,7},{6,2},{7,5},{8,12},{9,11},{10,... | collective-permute-start | bytes 1572872 | tf_op jit(solution)/shard_map/ppermute | solution.py:433
  194.7 12.9 %collective-permute-start.31 = (bf16[4,128,512]{2,1,0:T(8,128)(2,1)S(1)}, bf16[4,128,512]{2,1,0:T(8,128)(2,1)S(1)}, u32[]{:S(2)}, u32[]{:S(2)}) collective-permute-start(bf16[4,128,512]{2,1,0:T(8,128)(2,1)S(1)} %get-tuple-element.86), channel_id=1, source_target_pairs={{0,2},{1,5},{2,0},{3,7},{4,6},{5,1},{6,4},{7,3},{8,10},{9,13},{10,... | collective-permute-start | bytes 1572872 | tf_op jit(solution)/shard_map/ppermute | solution.py:433
  200.9 13.0 %collective-permute-start.27 = (bf16[2,128,512]{2,1,0:T(8,128)(2,1)S(1)}, bf16[2,128,512]{2,1,0:T(8,128)(2,1)S(1)}, u32[]{:S(2)}, u32[]{:S(2)}) collective-permute-start(bf16[2,128,512]{2,1,0:T(8,128)(2,1)S(1)} %add_convert_fusion.6), channel_id=1, source_target_pairs={{0,16},{1,17},{2,18},{3,19},{4,20},{5,21},{6,22},{7,23},{8,24},{9,... | collective-permute-start | bytes 786440 | tf_op jit(solution)/shard_map/ppermute | solution.py:433
  207.8 11.6 %collective-permute-start.33 = (bf16[2,128,512]{2,1,0:T(8,128)(2,1)S(1)}, bf16[2,128,512]{2,1,0:T(8,128)(2,1)S(1)}, u32[]{:S(2)}, u32[]{:S(2)}) collective-permute-start(bf16[2,128,512]{2,1,0:T(8,128)(2,1)S(1)} %add_convert_fusion.5), channel_id=1, source_target_pairs={{0,8},{1,9},{2,10},{3,11},{4,12},{5,13},{6,14},{7,15},{8,0},{9,1},... | collective-permute-start | bytes 786440 | tf_op jit(solution)/shard_map/ppermute | solution.py:433
  214.0 6.1 %collective-permute-start.28 = (bf16[1,128,512]{2,1,0:T(8,128)(2,1)S(1)}, bf16[1,128,512]{2,1,0:T(8,128)(2,1)S(1)}, u32[]{:S(2)}, u32[]{:S(2)}) collective-permute-start(bf16[1,128,512]{2,1,0:T(8,128)(2,1)S(1)} %add_convert_fusion.9), channel_id=1, source_target_pairs={{0,4},{1,3},{2,6},{3,1},{4,0},{5,7},{6,2},{7,5},{8,12},{9,11},{10,... | collective-permute-start | bytes 393224 | tf_op jit(solution)/shard_map/ppermute | solution.py:433
  219.5 9.0 %collective-permute-start.34 = (bf16[1,128,512]{2,1,0:T(8,128)(2,1)S(1)}, bf16[1,128,512]{2,1,0:T(8,128)(2,1)S(1)}, u32[]{:S(2)}, u32[]{:S(2)}) collective-permute-start(bf16[1,128,512]{2,1,0:T(8,128)(2,1)S(1)} %add_convert_fusion.8), channel_id=1, source_target_pairs={{0,16},{1,17},{2,18},{3,19},{4,20},{5,21},{6,22},{7,23},{8,24},{9,... | collective-permute-start | bytes 393224 | tf_op jit(solution)/shard_map/ppermute | solution.py:433

commit v12 on v10

--- a/solution.py
+++ b/solution.py
@@ -13,6 +13,7 @@
 F32 = jnp.float32
 PAIR = 2
 LANES = 128
+STREAMS = 4
 
 
 def slot_places(ids, experts, capacity):
@@ -125,7 +126,7 @@
 
 
 def gate_up_kernel(
-    experts, rows, width, info_ref, slot_ref, weight_ref, invgain_ref, x_refs, wg_ref, wu_ref,
+    experts, rows, width, info_ref, slot_ref, weight_ref, invgain_ref, x_refs, wg_refs, wu_refs,
     act_ref, hidden_ref, spread_ref, xs_ref, sq_ref, scale_ref, hits_ref
 ):
     expert = pl.program_id(0)
@@ -228,12 +229,13 @@
         )
         scale_ref[...] = jnp.broadcast_to(lax.rsqrt(total / width + 1e-06), scale_ref.shape)
 
+    both = [
+        jnp.concatenate([wg_ref[0], wu_ref[0]], axis=1) for wg_ref, wu_ref in zip(wg_refs, wu_refs)
+    ]
     summed = jnp.dot(
-        xs_ref[expert],
-        jnp.concatenate([wg_ref[0], wu_ref[0]], axis=1),
-        preferred_element_type=F32,
-    )
-    hidden_units = wg_ref.shape[2]
+        xs_ref[expert], jnp.concatenate(both, axis=0), preferred_element_type=F32
+    )
+    hidden_units = wg_refs[0].shape[2]
     for part in range(parts):
         window = slice(part * span, (part + 1) * span)
         hits = hits_of(slot_ref[pl.ds(expert, 1), window], rows)
@@ -256,7 +258,13 @@
     def kernel(info_ref, slot_ref, weight_ref, invgain_ref, *rest):
         gate_up_kernel(
             experts, rows, width, info_ref, slot_ref, weight_ref, invgain_ref,
-            rest[: len(x)], *rest[len(x) :]
+            rest[: len(x)], rest[len(x) : len(x) + STREAMS],
+            rest[len(x) + STREAMS : len(x) + 2 * STREAMS], *rest[len(x) + 2 * STREAMS :]
+        )
+
+    def stream(number):
+        return pl.BlockSpec(
+            (1, width // STREAMS, hidden_units), lambda e, info: (e, number, 0)
         )
 
     def whole(shape):
@@ -271,7 +279,7 @@
             grid=(experts,),
             in_specs=[whole(slots.shape), whole(weights.shape), whole(invgain.shape)]
             + [pl.BlockSpec(memory_space=pltpu.VMEM)] * len(x)
-            + [pl.BlockSpec((1, width, hidden_units), lambda e, info: (e, 0, 0))] * 2,
+            + [stream(number) for number in range(STREAMS)] * 2,
             out_specs=[
                 pl.BlockSpec(memory_space=pltpu.VMEM),
                 pl.BlockSpec(memory_space=pltpu.VMEM),
@@ -298,22 +306,22 @@
             transcendentals=0,
         ),
         name="gate_up",
-    )(info, slots, weights, invgain, *x, w_gate, w_up)
-
-
-def down_kernel(rows, place_ref, spread_ref, act_ref, wd0_ref, wd1_ref, *rest):
+    )(info, slots, weights, invgain, *x, *[w_gate] * STREAMS, *[w_up] * STREAMS)
+
+
+def down_kernel(rows, place_ref, spread_ref, act_ref, wd_refs, *rest):
     out_refs, ys_ref = rest[:-1], rest[-1]
     out_cols = out_refs[0].shape[2]
     step = pl.program_id(0)
     experts, all_rows, _ = act_ref.shape
-    per_step = wd0_ref.shape[0]
+    per_step = len(wd_refs) // 2
     parts = all_rows // rows
     groups = parts * PAIR
     for number in range(per_step):
         expert = step * per_step + number
-        for side, wd_ref in enumerate((wd0_ref, wd1_ref)):
+        for side in range(2):
             result = jnp.dot(
-                act_ref[expert], wd_ref[number], preferred_element_type=F32
+                act_ref[expert], wd_refs[2 * number + side][0], preferred_element_type=F32
             ).astype(BF16)
             for part in range(parts):
                 ys_ref[side, part, expert] = result[part * rows : (part + 1) * rows, :]
@@ -340,17 +348,27 @@
     parts, span, _ = spread.shape
     here = parts * span // groups
     out = jax.ShapeDtypeStruct((2 * groups, here, cols // chunks), BF16)
+
+    def kernel(place_ref, spread_ref, act_ref, *rest):
+        down_kernel(
+            rows, place_ref, spread_ref, act_ref, rest[: 2 * per_step], *rest[2 * per_step :]
+        )
+
+    def stream(number, side):
+        return pl.BlockSpec(
+            (1, hidden_units, cols), lambda e, p: (e * per_step + number, 0, p[side])
+        )
+
     return pl.pallas_call(
-        functools.partial(down_kernel, rows),
+        kernel,
         grid_spec=pltpu.PrefetchScalarGridSpec(
             num_scalar_prefetch=1,
             grid=(experts // per_step,),
             in_specs=[
                 pl.BlockSpec(memory_space=pltpu.VMEM),
                 pl.BlockSpec(memory_space=pltpu.VMEM),
-                pl.BlockSpec((per_step, hidden_units, cols), lambda e, p: (e, 0, p[0])),
-                pl.BlockSpec((per_step, hidden_units, cols), lambda e, p: (e, 0, p[1])),
-            ],
+            ]
+            + [stream(number, side) for number in range(per_step) for side in range(2)],
             out_specs=[pl.BlockSpec(out.shape, lambda e, p: (0, 0, 0))] * chunks,
             scratch_shapes=[pltpu.VMEM((2, parts, experts, rows, cols), BF16)],
         ),
@@ -364,7 +382,7 @@
             transcendentals=0,
         ),
         name="down_mix",
-    )(place, spread, act, w_down, w_down)
+    )(place, spread, act, *[w_down] * (2 * per_step))
 
 
 def flip(array, bits_of):

time: 225 us -> 225 us (level)
  no operation moved by 1% of the time
where the time goes in v12:
time: 225 us
  waiting for transfers between devices  123 us (55%)
  Pallas kernels  56.9 us (25%)
  starting transfers between devices  36 us (16%)
  local copies, waits for them, and re-layouts  4.84 us (2%)
  other arithmetic  3.82 us (2%)
    ppermute x35, waiting for transfers between devices, flip(): return lax.ppermute(array, ('expert', 'tensor'), pairs)  122 us
    ppermute x35, starting transfers between devices, flip(): return lax.ppermute(array, ('expert', 'tensor'), pairs)  32.2 us
    pallas_call x1, Pallas kernels, gate_up(): pl.pallas_call(kernel, grid_spec=pltpu.PrefetchScalarGridSpec(num_scalar_...  30.6 us
    pallas_call x3, Pallas kernels, down(): pl.pallas_call(kernel, grid_spec=pltpu.PrefetchScalarGridSpec(num_scalar_...  22.9 us
  transfers between devices with their start and end apart: 36, of which 21 were waited for; matrix products, arithmetic and copies ran while one was open for 2% of the time, Pallas kernels for 6%

profile of v12, /device:TPU:0, one launch (start us, length us, event | category | flops | bytes accessed | tf_op | source)
XLA Modules:
  0.0 225.0 jit_solution(5668479307884222276)
XLA Ops:
  0.0 4.0 %collective-permute-start = (bf16[1,128,1024]{2,1,0:T(8,128)(2,1)}, bf16[1,128,1024]{2,1,0:T(8,128)(2,1)S(1)}, u32[]{:S(2)}, u32[]{:S(2)}) collective-permute-start(bf16[1,128,1024]{2,1,0:T(8,128)(2,1)} %bitcast.67), channel_id=1, source_target_pairs={{0,16},{1,17},{2,18},{3,19},{4,20},{5,21},{6,22},{7,23},{8,24},{9,... | collective-permute-start | bytes 786440 | tf_op jit(solution)/shard_map/ppermute | solution.py:392
  4.0 1.2 copy-done
  5.3 0.7 copy-done.1
  6.0 0.7 copy-done.2
  6.6 0.8 pack.1
  7.4 3.8 %all-to-all-start = ((bf16[8,160,128]{2,1,0:T(8,128)(2,1)}), bf16[8,160,128]{2,1,0:T(8,128)(2,1)S(1)}, u32[]{:S(2)}, u32[]{:S(2)}) async-start(bf16[8,160,128]{2,1,0:T(8,128)(2,1)} %pack.1), calls=%async_computation | async-start | bytes 655360 | tf_op jit(solution)/shard_map/all_to_all | solution.py:628
  11.3 9.3 %collective-permute-done = bf16[1,128,1024]{2,1,0:T(8,128)(2,1)S(1)} collective-permute-done((bf16[1,128,1024]{2,1,0:T(8,128)(2,1)}, bf16[1,128,1024]{2,1,0:T(8,128)(2,1)S(1)}, u32[]{:S(2)}, u32[]{:S(2)}) %collective-permute-start) | collective-permute-done | bytes 262176 | tf_op jit(solution)/shard_map/ppermute | solution.py:392
  20.8 1.9 collective-permute-start.1
  22.7 0.6 all-to-all-done
  23.3 11.2 %collective-permute-done.2.refs_2_ = bf16[2,128,1024]{2,1,0:T(8,128)(2,1)S(1)} collective-permute-done((bf16[2,128,1024]{2,1,0:T(8,128)(2,1)S(1)}, bf16[2,128,1024]{2,1,0:T(8,128)(2,1)S(1)}, u32[]{:S(2)}, u32[]{:S(2)}) %collective-permute-start.2) | collective-permute-done | bytes 524320 | tf_op jit(solution)/shard_map/ppermute | solution.py:392
  34.5 0.6 gather_fusion
  35.1 1.0 collective-permute-start.3
  36.6 7.8 %collective-permute-done.3.refs_3_ = bf16[2,128,1024]{2,1,0:T(8,128)(2,1)} collective-permute-done((bf16[2,128,1024]{2,1,0:T(8,128)(2,1)S(1)}, bf16[2,128,1024]{2,1,0:T(8,128)(2,1)}, u32[]{:S(2)}, u32[]{:S(2)}) %collective-permute-start.3) | collective-permute-done | bytes 524320 | tf_op jit(solution)/shard_map/ppermute | solution.py:392
  44.4 1.0 copy-done.5
  45.5 2.6 %project.1 = (bf16[2,8,128,128]{3,2,1,0:T(8,128)(2,1)S(1)}, bf16[2,8,128,128]{3,2,1,0:T(8,128)(2,1)S(1)}) custom-call(s32[10]{0:T(128)S(1)} %pad_add_fusion.1.info_ref, bf16[2,128,1024]{2,1,0:T(8,128)(2,1)S(1)} %pad_maximum_fusion.refs_0_, bf16[2,128,1024]{2,1,0:T(8,128)(2,1)S(1)} %copy-done.5, bf16[2,128,1024]{2,1,0:T(8,128)(2,1)S(1)} %collective-permute-done.2.refs_2_, ...), custom_call_target="tpu_custom_call" | custom-call | flops 1073741824 | bytes 5242880 | tf_op jit(solution)/shard_map/project/pallas_call | solution.py:113
  48.2 1.9 collective-permute-done.4
  50.2 1.6 collective-permute-start.5
  51.8 6.8 %collective-permute-done.5 = bf16[8,128,128]{2,1,0:T(8,128)(2,1)S(1)} collective-permute-done((bf16[8,128,128]{2,1,0:T(8,128)(2,1)S(1)}, bf16[8,128,128]{2,1,0:T(8,128)(2,1)S(1)}, u32[]{:S(2)}, u32[]{:S(2)}) %collective-permute-start.5) | collective-permute-done | bytes 262176 | tf_op jit(solution)/shard_map/ppermute | solution.py:392
  58.8 2.2 collective-permute-start.7
  61.0 1.4 collective-permute-start.6
  62.4 4.9 %collective-permute-done.7 = bf16[1,4,128,128]{3,2,1,0:T(8,128)(2,1)S(1)} collective-permute-done((bf16[1,4,128,128]{3,2,1,0:T(8,128)(2,1)S(1)}, bf16[1,4,128,128]{3,2,1,0:T(8,128)(2,1)S(1)}, u32[]{:S(2)}, u32[]{:S(2)}) %collective-permute-start.7) | collective-permute-done | bytes 131104 | tf_op jit(solution)/shard_map/ppermute | solution.py:392
  67.3 0.7 collective-permute-start.8
  68.0 3.1 %collective-permute-start.9 = (bf16[2,4,128,128]{3,2,1,0:T(8,128)(2,1)S(1)}, bf16[2,4,128,128]{3,2,1,0:T(8,128)(2,1)S(1)}, u32[]{:S(2)}, u32[]{:S(2)}) collective-permute-start(bf16[2,4,128,128]{3,2,1,0:T(8,128)(2,1)S(1)} %pad_maximum_fusion.2), channel_id=1, source_target_pairs={{0,16},{1,17},{2,18},{3,19},{4,20},{5,21},{6,22},{7,23},{8,24},{9,... | collective-permute-start | bytes 786440 | tf_op jit(solution)/shard_map/ppermute | solution.py:392
  71.1 8.7 %collective-permute-done.8 = bf16[2,4,128,128]{3,2,1,0:T(8,128)(2,1)S(1)} collective-permute-done((bf16[2,4,128,128]{3,2,1,0:T(8,128)(2,1)S(1)}, bf16[2,4,128,128]{3,2,1,0:T(8,128)(2,1)S(1)}, u32[]{:S(2)}, u32[]{:S(2)}) %collective-permute-start.8) | collective-permute-done | bytes 262176 | tf_op jit(solution)/shard_map/ppermute | solution.py:392
  79.9 2.9 %collective-permute-done.9 = bf16[2,4,128,128]{3,2,1,0:T(8,128)(2,1)S(1)} collective-permute-done((bf16[2,4,128,128]{3,2,1,0:T(8,128)(2,1)S(1)}, bf16[2,4,128,128]{3,2,1,0:T(8,128)(2,1)S(1)}, u32[]{:S(2)}, u32[]{:S(2)}) %collective-permute-start.9) | collective-permute-done | bytes 262176 | tf_op jit(solution)/shard_map/ppermute | solution.py:392
  82.8 1.6 collective-permute-start.11
  84.4 0.2 collective-permute-start.10
  84.6 0.5 collective-permute-start.18
  85.2 1.4 collective-permute-start.17
  86.7 10.7 %collective-permute-done.11.rest_1_ = bf16[4,4,128,128]{3,2,1,0:T(8,128)(2,1)S(1)} collective-permute-done((bf16[4,4,128,128]{3,2,1,0:T(8,128)(2,1)S(1)}, bf16[4,4,128,128]{3,2,1,0:T(8,128)(2,1)S(1)}, u32[]{:S(2)}, u32[]{:S(2)}) %collective-permute-start.11) | collective-permute-done | bytes 524320 | tf_op jit(solution)/shard_map/ppermute | solution.py:392
  97.4 0.5 collective-permute-start.13
  97.9 5.1 %collective-permute-done.18.rest_9_ = bf16[4,4,128,128]{3,2,1,0:T(8,128)(2,1)S(1)} collective-permute-done((bf16[4,4,128,128]{3,2,1,0:T(8,128)(2,1)S(1)}, bf16[4,4,128,128]{3,2,1,0:T(8,128)(2,1)S(1)}, u32[]{:S(2)}, u32[]{:S(2)}) %collective-permute-start.18) | collective-permute-done | bytes 524320 | tf_op jit(solution)/shard_map/ppermute | solution.py:392
  103.0 1.5 collective-permute-start.14
  104.5 0.5 collective-permute-start.21
  105.6 0.5 collective-permute-start.22
  106.2 6.1 %collective-permute-done.14.rest_5_ = bf16[4,4,128,128]{3,2,1,0:T(8,128)(2,1)} collective-permute-done((bf16[4,4,128,128]{3,2,1,0:T(8,128)(2,1)S(1)}, bf16[4,4,128,128]{3,2,1,0:T(8,128)(2,1)}, u32[]{:S(2)}, u32[]{:S(2)}) %collective-permute-start.14) | collective-permute-done | bytes 524320 | tf_op jit(solution)/shard_map/ppermute | solution.py:392
  112.3 5.6 %collective-permute-done.21.rest_13_ = bf16[4,4,128,128]{3,2,1,0:T(8,128)(2,1)} collective-permute-done((bf16[4,4,128,128]{3,2,1,0:T(8,128)(2,1)S(1)}, bf16[4,4,128,128]{3,2,1,0:T(8,128)(2,1)}, u32[]{:S(2)}, u32[]{:S(2)}) %collective-permute-start.21) | collective-permute-done | bytes 524320 | tf_op jit(solution)/shard_map/ppermute | solution.py:392
  118.1 2.0 collective-permute-done.23.rest_15_
  120.0 30.6 %gate_up.1 = (bf16[8,192,384]{2,1,0:T(8,128)(2,1)S(1)}, f32[128,1024]{1,0:T(8,128)S(1)}, bf16[4,256,384]{2,1,0:T(8,128)(2,1)S(1)}) custom-call(s32[66]{0:T(128)S(1)} %pad_add_fusion.info_ref, s32[8,1024]{1,0:T(8,128)S(1)} %bitcast_select_fusion.slot_ref, f32[8,1024]{1,0:T(8,128)S(1)} %bitcast.63, f32[32,128]{1,0:T(8,128)S(1)} %divide_bitcast_fusion.invgain_ref, ...), custom_call_target="tpu_custom_call" | custom-call | flops 9663676416 | bytes 58720256 | tf_op jit(solution)/shard_map/gate_up/pallas_call | solution.py:275
  150.7 9.9 %down_mix.4 = (bf16[16,128,512]{2,1,0:T(8,128)(2,1)S(1)}, bf16[16,128,512]{2,1,0:T(8,128)(2,1)S(1)}) custom-call(s32[34]{0:T(128)S(1)} %pad_add_fusion.3.place_ref, bf16[4,256,384]{2,1,0:T(8,128)(2,1)S(1)} %get-tuple-element.50.spread_ref, bf16[8,192,384]{2,1,0:T(8,128)(2,1)S(1)} %get-tuple-element.51.act_ref, bf16[8,384,4096]{2,1,0:T(8,128)(2,1)} %rest_3_.5, ...), custom_call_target="tpu_custom_call" | custom-call | flops 4831838208 | bytes 16777216 | tf_op jit(solution)/shard_map/down_mix/pallas_call | solution.py:362
  160.6 0.2 collective-permute-start.24
  160.9 0.3 collective-permute-start.29
  161.4 6.5 %down_mix.3 = bf16[16,128,512]{2,1,0:T(8,128)(2,1)S(1)} custom-call(s32[18]{0:T(128)S(1)} %pad_add_fusion.2.place_ref, bf16[4,256,384]{2,1,0:T(8,128)(2,1)S(1)} %get-tuple-element.50.spread_ref, bf16[8,192,384]{2,1,0:T(8,128)(2,1)S(1)} %get-tuple-element.51.act_ref, bf16[8,384,4096]{2,1,0:T(8,128)(2,1)} %rest_3_.5, bf16[8,384,4096]{2,1,0:T(8,128)(2,1)} %rest_3_.5, ...), custom_call_target="tpu_custom_call" | custom-call | flops 2415919104 | bytes 8388608 | tf_op jit(solution)/shard_map/down_mix/pallas_call | solution.py:362
  167.8 0.3 add_convert_fusion
  168.2 1.6 collective-permute-start.25
  169.8 6.5 %down_mix.5 = bf16[16,128,512]{2,1,0:T(8,128)(2,1)S(1)} custom-call(s32[18]{0:T(128)S(1)} %pad_add_fusion.4.place_ref, bf16[4,256,384]{2,1,0:T(8,128)(2,1)S(1)} %get-tuple-element.50.spread_ref, bf16[8,192,384]{2,1,0:T(8,128)(2,1)S(1)} %get-tuple-element.51.act_ref, bf16[8,384,4096]{2,1,0:T(8,128)(2,1)} %rest_3_.5, bf16[8,384,4096]{2,1,0:T(8,128)(2,1)} %rest_3_.5, ...), custom_call_target="tpu_custom_call" | custom-call | flops 2415919104 | bytes 8388608 | tf_op jit(solution)/shard_map/down_mix/pallas_call | solution.py:362
  176.3 0.3 add_convert_fusion.2
  176.6 0.6 collective-permute-start.30
  177.2 5.8 %collective-permute-done.25 = bf16[8,128,512]{2,1,0:T(8,128)(2,1)S(1)} collective-permute-done((bf16[8,128,512]{2,1,0:T(8,128)(2,1)S(1)}, bf16[8,128,512]{2,1,0:T(8,128)(2,1)S(1)}, u32[]{:S(2)}, u32[]{:S(2)}) %collective-permute-start.25) | collective-permute-done | bytes 1048608 | tf_op jit(solution)/shard_map/ppermute | solution.py:392
  183.3 0.3 collective-permute-start.26
  183.6 5.1 %collective-permute-done.30 = bf16[4,128,512]{2,1,0:T(8,128)(2,1)S(1)} collective-permute-done((bf16[4,128,512]{2,1,0:T(8,128)(2,1)S(1)}, bf16[4,128,512]{2,1,0:T(8,128)(2,1)S(1)}, u32[]{:S(2)}, u32[]{:S(2)}) %collective-permute-start.30) | collective-permute-done | bytes 524320 | tf_op jit(solution)/shard_map/ppermute | solution.py:392
  188.7 0.2 add_convert_fusion.1
  188.9 1.5 collective-permute-start.32
  190.3 1.5 collective-permute-start.31
  191.9 4.6 %collective-permute-done.26 = bf16[4,128,512]{2,1,0:T(8,128)(2,1)S(1)} collective-permute-done((bf16[4,128,512]{2,1,0:T(8,128)(2,1)S(1)}, bf16[4,128,512]{2,1,0:T(8,128)(2,1)S(1)}, u32[]{:S(2)}, u32[]{:S(2)}) %collective-permute-start.26) | collective-permute-done | bytes 524320 | tf_op jit(solution)/shard_map/ppermute | solution.py:392
  196.6 1.0 collective-permute-start.27
  197.6 5.7 %collective-permute-done.32 = bf16[4,128,512]{2,1,0:T(8,128)(2,1)S(1)} collective-permute-done((bf16[4,128,512]{2,1,0:T(8,128)(2,1)S(1)}, bf16[4,128,512]{2,1,0:T(8,128)(2,1)S(1)}, u32[]{:S(2)}, u32[]{:S(2)}) %collective-permute-start.32) | collective-permute-done | bytes 524320 | tf_op jit(solution)/shard_map/ppermute | solution.py:392
  203.4 0.3 collective-permute-start.33
  203.7 5.9 %collective-permute-done.27 = bf16[2,128,512]{2,1,0:T(8,128)(2,1)S(1)} collective-permute-done((bf16[2,128,512]{2,1,0:T(8,128)(2,1)S(1)}, bf16[2,128,512]{2,1,0:T(8,128)(2,1)S(1)}, u32[]{:S(2)}, u32[]{:S(2)}) %collective-permute-start.27) | collective-permute-done | bytes 262176 | tf_op jit(solution)/shard_map/ppermute | solution.py:392
  209.7 1.4 collective-permute-start.28
  211.1 4.0 %collective-permute-done.33 = bf16[2,128,512]{2,1,0:T(8,128)(2,1)S(1)} collective-permute-done((bf16[2,128,512]{2,1,0:T(8,128)(2,1)S(1)}, bf16[2,128,512]{2,1,0:T(8,128)(2,1)S(1)}, u32[]{:S(2)}, u32[]{:S(2)}) %collective-permute-start.33) | collective-permute-done | bytes 262176 | tf_op jit(solution)/shard_map/ppermute | solution.py:392
  215.2 0.5 collective-permute-start.34
  215.8 8.3 %collective-permute-done.34 = bf16[1,128,512]{2,1,0:T(8,128)(2,1)S(1)} collective-permute-done((bf16[1,128,512]{2,1,0:T(8,128)(2,1)S(1)}, bf16[1,128,512]{2,1,0:T(8,128)(2,1)S(1)}, u32[]{:S(2)}, u32[]{:S(2)}) %collective-permute-start.34) | collective-permute-done | bytes 131104 | tf_op jit(solution)/shard_map/ppermute | solution.py:392
  224.2 0.8 fusion
  (87 shorter events, 3.3 us)
Async XLA Ops:
  0.0 20.6 %collective-permute-start = (bf16[1,128,1024]{2,1,0:T(8,128)(2,1)}, bf16[1,128,1024]{2,1,0:T(8,128)(2,1)S(1)}, u32[]{:S(2)}, u32[]{:S(2)}) collective-permute-start(bf16[1,128,1024]{2,1,0:T(8,128)(2,1)} %bitcast.67), channel_id=1, source_target_pairs={{0,16},{1,17},{2,18},{3,19},{4,20},{5,21},{6,22},{7,23},{8,24},{9,... | collective-permute-start | bytes 786440 | tf_op jit(solution)/shard_map/ppermute | solution.py:392
  4.0 1.2 copy-start
  5.3 0.7 copy-start.1
  6.0 0.7 copy-start.2
  6.6 13.9 %copy-start.6 = (bf16[128,1024]{1,0:T(8,128)(2,1)S(1)}, bf16[128,1024]{1,0:T(8,128)(2,1)}, u32[]{:S(2)}) copy-start(bf16[128,1024]{1,0:T(8,128)(2,1)} %param.9) | copy-start | bytes 786436
  6.6 37.8 %copy-start.3 = (bf16[1024,512]{1,0:T(8,128)(2,1)S(1)}, bf16[1024,512]{1,0:T(8,128)(2,1)}, u32[]{:S(2)}) copy-start(bf16[1024,512]{1,0:T(8,128)(2,1)} %refs_4_.1) | copy-start | bytes 3145732
  7.4 15.8 %all-to-all-start = ((bf16[8,160,128]{2,1,0:T(8,128)(2,1)}), bf16[8,160,128]{2,1,0:T(8,128)(2,1)S(1)}, u32[]{:S(2)}, u32[]{:S(2)}) async-start(bf16[8,160,128]{2,1,0:T(8,128)(2,1)} %pack.1), calls=%async_computation | async-start | bytes 655360 | tf_op jit(solution)/shard_map/all_to_all | solution.py:628
  20.6 13.9 %collective-permute-start.2 = (bf16[2,128,1024]{2,1,0:T(8,128)(2,1)S(1)}, bf16[2,128,1024]{2,1,0:T(8,128)(2,1)S(1)}, u32[]{:S(2)}, u32[]{:S(2)}) collective-permute-start(bf16[2,128,1024]{2,1,0:T(8,128)(2,1)S(1)} %pad_maximum_fusion.refs_0_), channel_id=1, source_target_pairs={{0,8},{1,5},{2,10},{3,7},{4,12},{5,1},{6,14},{7,3},{8,0},{9,13},{1... | collective-permute-start | bytes 1572872 | tf_op jit(solution)/shard_map/ppermute | solution.py:392
  20.8 13.7 %collective-permute-start.1 = (bf16[2,128,1024]{2,1,0:T(8,128)(2,1)S(1)}, bf16[2,128,1024]{2,1,0:T(8,128)(2,1)S(1)}, u32[]{:S(2)}, u32[]{:S(2)}) collective-permute-start(bf16[2,128,1024]{2,1,0:T(8,128)(2,1)S(1)} %pad_maximum_fusion.refs_0_), channel_id=1, source_target_pairs={{0,4},{1,9},{2,6},{3,11},{4,0},{5,13},{6,2},{7,15},{8,12},{9,1},{1... | collective-permute-start | bytes 1572872 | tf_op jit(solution)/shard_map/ppermute | solution.py:392
  34.5 2.1 copy-start.4
  35.1 9.4 %collective-permute-start.3 = (bf16[2,128,1024]{2,1,0:T(8,128)(2,1)S(1)}, bf16[2,128,1024]{2,1,0:T(8,128)(2,1)}, u32[]{:S(2)}, u32[]{:S(2)}) collective-permute-start(bf16[2,128,1024]{2,1,0:T(8,128)(2,1)S(1)} %collective-permute-done.1.refs_1_), channel_id=1, source_target_pairs={{0,8},{1,5},{2,10},{3,7},{4,12},{5,1},{6,14},{7,3},{8,0},{9,13},{1... | collective-permute-start | bytes 1572872 | tf_op jit(solution)/shard_map/ppermute | solution.py:392
  44.4 1.0 copy-start.5
  45.5 6.3 %copy-start.7 = (f32[4096]{0:T(1024)S(1)}, f32[4096]{0:T(1024)}, u32[]{:S(2)}) copy-start(f32[4096]{0:T(1024)} %param.12) | copy-start | bytes 49156
  48.1 2.0 collective-permute-start.4
  50.2 8.4 %collective-permute-start.5 = (bf16[8,128,128]{2,1,0:T(8,128)(2,1)S(1)}, bf16[8,128,128]{2,1,0:T(8,128)(2,1)S(1)}, u32[]{:S(2)}, u32[]{:S(2)}) collective-permute-start(bf16[8,128,128]{2,1,0:T(8,128)(2,1)S(1)} %fusion.2), channel_id=1, source_target_pairs={{0,2},{1,3},{2,0},{3,1},{4,6},{5,7},{6,4},{7,5},{8,10},{9,11},{10,... | collective-permute-start | bytes 786440 | tf_op jit(solution)/shard_map/ppermute | solution.py:392
  58.8 8.5 %collective-permute-start.7 = (bf16[1,4,128,128]{3,2,1,0:T(8,128)(2,1)S(1)}, bf16[1,4,128,128]{3,2,1,0:T(8,128)(2,1)S(1)}, u32[]{:S(2)}, u32[]{:S(2)}) collective-permute-start(bf16[1,4,128,128]{3,2,1,0:T(8,128)(2,1)S(1)} %get-tuple-element.65), channel_id=1, source_target_pairs={{0,16},{1,17},{2,18},{3,19},{4,20},{5,21},{6,22},{7,23},{8,24},{9,... | collective-permute-start | bytes 393224 | tf_op jit(solution)/shard_map/ppermute | solution.py:392
  61.0 6.3 %collective-permute-start.6 = (bf16[1,4,128,128]{3,2,1,0:T(8,128)(2,1)S(1)}, bf16[1,4,128,128]{3,2,1,0:T(8,128)(2,1)S(1)}, u32[]{:S(2)}, u32[]{:S(2)}) collective-permute-start(bf16[1,4,128,128]{3,2,1,0:T(8,128)(2,1)S(1)} %get-tuple-element.66), channel_id=1, source_target_pairs={{0,4},{1,3},{2,6},{3,1},{4,0},{5,7},{6,2},{7,5},{8,12},{9,11},{10,... | collective-permute-start | bytes 393224 | tf_op jit(solution)/shard_map/ppermute | solution.py:392
  67.3 12.5 %collective-permute-start.8 = (bf16[2,4,128,128]{3,2,1,0:T(8,128)(2,1)S(1)}, bf16[2,4,128,128]{3,2,1,0:T(8,128)(2,1)S(1)}, u32[]{:S(2)}, u32[]{:S(2)}) collective-permute-start(bf16[2,4,128,128]{3,2,1,0:T(8,128)(2,1)S(1)} %pad_maximum_fusion.3), channel_id=1, source_target_pairs={{0,8},{1,9},{2,10},{3,11},{4,12},{5,13},{6,14},{7,15},{8,0},{9,1},... | collective-permute-start | bytes 786440 | tf_op jit(solution)/shard_map/ppermute | solution.py:392
  68.0 14.8 %collective-permute-start.9 = (bf16[2,4,128,128]{3,2,1,0:T(8,128)(2,1)S(1)}, bf16[2,4,128,128]{3,2,1,0:T(8,128)(2,1)S(1)}, u32[]{:S(2)}, u32[]{:S(2)}) collective-permute-start(bf16[2,4,128,128]{3,2,1,0:T(8,128)(2,1)S(1)} %pad_maximum_fusion.2), channel_id=1, source_target_pairs={{0,16},{1,17},{2,18},{3,19},{4,20},{5,21},{6,22},{7,23},{8,24},{9,... | collective-permute-start | bytes 786440 | tf_op jit(solution)/shard_map/ppermute | solution.py:392
  82.8 14.6 %collective-permute-start.11 = (bf16[4,4,128,128]{3,2,1,0:T(8,128)(2,1)S(1)}, bf16[4,4,128,128]{3,2,1,0:T(8,128)(2,1)S(1)}, u32[]{:S(2)}, u32[]{:S(2)}) collective-permute-start(bf16[4,4,128,128]{3,2,1,0:T(8,128)(2,1)S(1)} %constant_dynamic-update-slice_fusion.rest_0_), channel_id=1, source_target_pairs={{0,2},{1,5},{2,0},{3,7},{4,6},{5,1},{6,4},{7,3},{8,10},{9,13},{10,... | collective-permute-start | bytes 1572872 | tf_op jit(solution)/shard_map/ppermute | solution.py:392
  84.4 13.0 %collective-permute-start.10 = (bf16[4,4,128,128]{3,2,1,0:T(8,128)(2,1)S(1)}, bf16[4,4,128,128]{3,2,1,0:T(8,128)(2,1)S(1)}, u32[]{:S(2)}, u32[]{:S(2)}) collective-permute-start(bf16[4,4,128,128]{3,2,1,0:T(8,128)(2,1)S(1)} %constant_dynamic-update-slice_fusion.rest_0_), channel_id=1, source_target_pairs={{0,8},{1,9},{2,10},{3,11},{4,12},{5,13},{6,14},{7,15},{8,0},{9,1},... | collective-permute-start | bytes 1572872 | tf_op jit(solution)/shard_map/ppermute | solution.py:392
  84.6 18.4 %collective-permute-start.18 = (bf16[4,4,128,128]{3,2,1,0:T(8,128)(2,1)S(1)}, bf16[4,4,128,128]{3,2,1,0:T(8,128)(2,1)S(1)}, u32[]{:S(2)}, u32[]{:S(2)}) collective-permute-start(bf16[4,4,128,128]{3,2,1,0:T(8,128)(2,1)S(1)} %pad_maximum_fusion.1.rest_8_), channel_id=1, source_target_pairs={{0,2},{1,5},{2,0},{3,7},{4,6},{5,1},{6,4},{7,3},{8,10},{9,13},{10,... | collective-permute-start | bytes 1572872 | tf_op jit(solution)/shard_map/ppermute | solution.py:392
  85.2 19.4 %collective-permute-start.17 = (bf16[4,4,128,128]{3,2,1,0:T(8,128)(2,1)S(1)}, bf16[4,4,128,128]{3,2,1,0:T(8,128)(2,1)S(1)}, u32[]{:S(2)}, u32[]{:S(2)}) collective-permute-start(bf16[4,4,128,128]{3,2,1,0:T(8,128)(2,1)S(1)} %pad_maximum_fusion.1.rest_8_), channel_id=1, source_target_pairs={{0,4},{1,3},{2,6},{3,1},{4,0},{5,7},{6,2},{7,5},{8,12},{9,11},{10,... | collective-permute-start | bytes 1572872 | tf_op jit(solution)/shard_map/ppermute | solution.py:392
  86.7 18.8 %collective-permute-start.12 = (bf16[4,4,128,128]{3,2,1,0:T(8,128)(2,1)S(1)}, bf16[4,4,128,128]{3,2,1,0:T(8,128)(2,1)}, u32[]{:S(2)}, u32[]{:S(2)}) collective-permute-start(bf16[4,4,128,128]{3,2,1,0:T(8,128)(2,1)S(1)} %constant_dynamic-update-slice_fusion.rest_0_), channel_id=1, source_target_pairs={{0,1},{1,0},{2,3},{3,2},{4,5},{5,4},{6,7},{7,6},{8,9},{9,8},{10,11... | collective-permute-start | bytes 1572872 | tf_op jit(solution)/shard_map/ppermute | solution.py:392
  97.4 8.2 %collective-permute-start.19 = (bf16[4,4,128,128]{3,2,1,0:T(8,128)(2,1)S(1)}, bf16[4,4,128,128]{3,2,1,0:T(8,128)(2,1)}, u32[]{:S(2)}, u32[]{:S(2)}) collective-permute-start(bf16[4,4,128,128]{3,2,1,0:T(8,128)(2,1)S(1)} %pad_maximum_fusion.1.rest_8_), channel_id=1, source_target_pairs={{0,1},{1,0},{2,3},{3,2},{4,5},{5,4},{6,7},{7,6},{8,9},{9,8},{10,11... | collective-permute-start | bytes 1572872 | tf_op jit(solution)/shard_map/ppermute | solution.py:392
  97.4 8.7 %collective-permute-start.13 = (bf16[4,4,128,128]{3,2,1,0:T(8,128)(2,1)S(1)}, bf16[4,4,128,128]{3,2,1,0:T(8,128)(2,1)}, u32[]{:S(2)}, u32[]{:S(2)}) collective-permute-start(bf16[4,4,128,128]{3,2,1,0:T(8,128)(2,1)S(1)} %collective-permute-done.11.rest_1_), channel_id=1, source_target_pairs={{0,1},{1,0},{2,3},{3,2},{4,5},{5,4},{6,7},{7,6},{8,9},{9,8},{10,11... | collective-permute-start | bytes 1572872 | tf_op jit(solution)/shard_map/ppermute | solution.py:392
  103.0 9.3 %collective-permute-start.14 = (bf16[4,4,128,128]{3,2,1,0:T(8,128)(2,1)S(1)}, bf16[4,4,128,128]{3,2,1,0:T(8,128)(2,1)}, u32[]{:S(2)}, u32[]{:S(2)}) collective-permute-start(bf16[4,4,128,128]{3,2,1,0:T(8,128)(2,1)S(1)} %collective-permute-done.10.rest_4_), channel_id=1, source_target_pairs={{0,2},{1,5},{2,0},{3,7},{4,6},{5,1},{6,4},{7,3},{8,10},{9,13},{10,... | collective-permute-start | bytes 1572872 | tf_op jit(solution)/shard_map/ppermute | solution.py:392
  104.5 13.4 %collective-permute-start.21 = (bf16[4,4,128,128]{3,2,1,0:T(8,128)(2,1)S(1)}, bf16[4,4,128,128]{3,2,1,0:T(8,128)(2,1)}, u32[]{:S(2)}, u32[]{:S(2)}) collective-permute-start(bf16[4,4,128,128]{3,2,1,0:T(8,128)(2,1)S(1)} %collective-permute-done.17.rest_12_), channel_id=1, source_target_pairs={{0,2},{1,5},{2,0},{3,7},{4,6},{5,1},{6,4},{7,3},{8,10},{9,13},{10,... | collective-permute-start | bytes 1572872 | tf_op jit(solution)/shard_map/ppermute | solution.py:392
  105.6 12.5 %collective-permute-start.15 = (bf16[4,4,128,128]{3,2,1,0:T(8,128)(2,1)S(1)}, bf16[4,4,128,128]{3,2,1,0:T(8,128)(2,1)S(1)}, u32[]{:S(2)}, u32[]{:S(2)}) collective-permute-start(bf16[4,4,128,128]{3,2,1,0:T(8,128)(2,1)S(1)} %collective-permute-done.10.rest_4_), channel_id=1, source_target_pairs={{0,1},{1,0},{2,3},{3,2},{4,5},{5,4},{6,7},{7,6},{8,9},{9,8},{10,11... | collective-permute-start | bytes 1572872 | tf_op jit(solution)/shard_map/ppermute | solution.py:392
  105.6 12.4 %collective-permute-start.22 = (bf16[4,4,128,128]{3,2,1,0:T(8,128)(2,1)S(1)}, bf16[4,4,128,128]{3,2,1,0:T(8,128)(2,1)S(1)}, u32[]{:S(2)}, u32[]{:S(2)}) collective-permute-start(bf16[4,4,128,128]{3,2,1,0:T(8,128)(2,1)S(1)} %collective-permute-done.17.rest_12_), channel_id=1, source_target_pairs={{0,1},{1,0},{2,3},{3,2},{4,5},{5,4},{6,7},{7,6},{8,9},{9,8},{10,11... | collective-permute-start | bytes 1572872 | tf_op jit(solution)/shard_map/ppermute | solution.py:392
  106.1 11.9 %collective-permute-start.20 = (bf16[4,4,128,128]{3,2,1,0:T(8,128)(2,1)S(1)}, bf16[4,4,128,128]{3,2,1,0:T(8,128)(2,1)S(1)}, u32[]{:S(2)}, u32[]{:S(2)}) collective-permute-start(bf16[4,4,128,128]{3,2,1,0:T(8,128)(2,1)S(1)} %collective-permute-done.18.rest_9_), channel_id=1, source_target_pairs={{0,1},{1,0},{2,3},{3,2},{4,5},{5,4},{6,7},{7,6},{8,9},{9,8},{10,11... | collective-permute-start | bytes 1572872 | tf_op jit(solution)/shard_map/ppermute | solution.py:392
  112.3 5.7 %collective-permute-start.16 = (bf16[4,4,128,128]{3,2,1,0:T(8,128)(2,1)}, bf16[4,4,128,128]{3,2,1,0:T(8,128)(2,1)S(1)}, u32[]{:S(2)}, u32[]{:S(2)}) collective-permute-start(bf16[4,4,128,128]{3,2,1,0:T(8,128)(2,1)} %collective-permute-done.14.rest_5_), channel_id=1, source_target_pairs={{0,1},{1,0},{2,3},{3,2},{4,5},{5,4},{6,7},{7,6},{8,9},{9,8},{10,11... | collective-permute-start | bytes 1572872 | tf_op jit(solution)/shard_map/ppermute | solution.py:392
  117.9 2.1 collective-permute-start.23
  160.6 7.2 %collective-permute-start.24 = (bf16[16,128,512]{2,1,0:T(8,128)(2,1)S(1)}, bf16[16,128,512]{2,1,0:T(8,128)(2,1)S(1)}, u32[]{:S(2)}, u32[]{:S(2)}) collective-permute-start(bf16[16,128,512]{2,1,0:T(8,128)(2,1)S(1)} %get-tuple-element.52), channel_id=1, source_target_pairs={{0,1},{1,0},{2,3},{3,2},{4,5},{5,4},{6,7},{7,6},{8,9},{9,8},{10,11... | collective-permute-start | bytes 6291464 | tf_op jit(solution)/shard_map/ppermute | solution.py:392
  160.9 15.4 %collective-permute-start.29 = (bf16[16,128,512]{2,1,0:T(8,128)(2,1)S(1)}, bf16[16,128,512]{2,1,0:T(8,128)(2,1)S(1)}, u32[]{:S(2)}, u32[]{:S(2)}) collective-permute-start(bf16[16,128,512]{2,1,0:T(8,128)(2,1)S(1)} %get-tuple-element.54), channel_id=1, source_target_pairs={{0,1},{1,0},{2,3},{3,2},{4,5},{5,4},{6,7},{7,6},{8,9},{9,8},{10,11... | collective-permute-start | bytes 6291464 | tf_op jit(solution)/shard_map/ppermute | solution.py:392
  168.2 14.9 %collective-permute-start.25 = (bf16[8,128,512]{2,1,0:T(8,128)(2,1)S(1)}, bf16[8,128,512]{2,1,0:T(8,128)(2,1)S(1)}, u32[]{:S(2)}, u32[]{:S(2)}) collective-permute-start(bf16[8,128,512]{2,1,0:T(8,128)(2,1)S(1)} %add_convert_fusion), channel_id=1, source_target_pairs={{0,2},{1,5},{2,0},{3,7},{4,6},{5,1},{6,4},{7,3},{8,10},{9,13},{10,... | collective-permute-start | bytes 3145736 | tf_op jit(solution)/shard_map/ppermute | solution.py:392
  176.6 12.0 %collective-permute-start.30 = (bf16[4,128,512]{2,1,0:T(8,128)(2,1)S(1)}, bf16[4,128,512]{2,1,0:T(8,128)(2,1)S(1)}, u32[]{:S(2)}, u32[]{:S(2)}) collective-permute-start(bf16[4,128,512]{2,1,0:T(8,128)(2,1)S(1)} %get-tuple-element.56), channel_id=1, source_target_pairs={{0,2},{1,5},{2,0},{3,7},{4,6},{5,1},{6,4},{7,3},{8,10},{9,13},{10,... | collective-permute-start | bytes 1572872 | tf_op jit(solution)/shard_map/ppermute | solution.py:392
  183.3 13.2 %collective-permute-start.26 = (bf16[4,128,512]{2,1,0:T(8,128)(2,1)S(1)}, bf16[4,128,512]{2,1,0:T(8,128)(2,1)S(1)}, u32[]{:S(2)}, u32[]{:S(2)}) collective-permute-start(bf16[4,128,512]{2,1,0:T(8,128)(2,1)S(1)} %add_convert_fusion.4), channel_id=1, source_target_pairs={{0,8},{1,9},{2,10},{3,11},{4,12},{5,13},{6,14},{7,15},{8,0},{9,1},... | collective-permute-start | bytes 1572872 | tf_op jit(solution)/shard_map/ppermute | solution.py:392
  188.9 14.4 %collective-permute-start.32 = (bf16[4,128,512]{2,1,0:T(8,128)(2,1)S(1)}, bf16[4,128,512]{2,1,0:T(8,128)(2,1)S(1)}, u32[]{:S(2)}, u32[]{:S(2)}) collective-permute-start(bf16[4,128,512]{2,1,0:T(8,128)(2,1)S(1)} %add_convert_fusion.1), channel_id=1, source_target_pairs={{0,4},{1,3},{2,6},{3,1},{4,0},{5,7},{6,2},{7,5},{8,12},{9,11},{10,... | collective-permute-start | bytes 1572872 | tf_op jit(solution)/shard_map/ppermute | solution.py:392
  190.3 12.9 %collective-permute-start.31 = (bf16[4,128,512]{2,1,0:T(8,128)(2,1)S(1)}, bf16[4,128,512]{2,1,0:T(8,128)(2,1)S(1)}, u32[]{:S(2)}, u32[]{:S(2)}) collective-permute-start(bf16[4,128,512]{2,1,0:T(8,128)(2,1)S(1)} %get-tuple-element.58), channel_id=1, source_target_pairs={{0,2},{1,5},{2,0},{3,7},{4,6},{5,1},{6,4},{7,3},{8,10},{9,13},{10,... | collective-permute-start | bytes 1572872 | tf_op jit(solution)/shard_map/ppermute | solution.py:392
  196.6 13.0 %collective-permute-start.27 = (bf16[2,128,512]{2,1,0:T(8,128)(2,1)S(1)}, bf16[2,128,512]{2,1,0:T(8,128)(2,1)S(1)}, u32[]{:S(2)}, u32[]{:S(2)}) collective-permute-start(bf16[2,128,512]{2,1,0:T(8,128)(2,1)S(1)} %add_convert_fusion.6), channel_id=1, source_target_pairs={{0,16},{1,17},{2,18},{3,19},{4,20},{5,21},{6,22},{7,23},{8,24},{9,... | collective-permute-start | bytes 786440 | tf_op jit(solution)/shard_map/ppermute | solution.py:392
  203.4 11.7 %collective-permute-start.33 = (bf16[2,128,512]{2,1,0:T(8,128)(2,1)S(1)}, bf16[2,128,512]{2,1,0:T(8,128)(2,1)S(1)}, u32[]{:S(2)}, u32[]{:S(2)}) collective-permute-start(bf16[2,128,512]{2,1,0:T(8,128)(2,1)S(1)} %add_convert_fusion.5), channel_id=1, source_target_pairs={{0,8},{1,9},{2,10},{3,11},{4,12},{5,13},{6,14},{7,15},{8,0},{9,1},... | collective-permute-start | bytes 786440 | tf_op jit(solution)/shard_map/ppermute | solution.py:392
  209.7 6.0 %collective-permute-start.28 = (bf16[1,128,512]{2,1,0:T(8,128)(2,1)S(1)}, bf16[1,128,512]{2,1,0:T(8,128)(2,1)S(1)}, u32[]{:S(2)}, u32[]{:S(2)}) collective-permute-start(bf16[1,128,512]{2,1,0:T(8,128)(2,1)S(1)} %add_convert_fusion.9), channel_id=1, source_target_pairs={{0,4},{1,3},{2,6},{3,1},{4,0},{5,7},{6,2},{7,5},{8,12},{9,11},{10,... | collective-permute-start | bytes 393224 | tf_op jit(solution)/shard_map/ppermute | solution.py:392
  215.2 8.9 %collective-permute-start.34 = (bf16[1,128,512]{2,1,0:T(8,128)(2,1)S(1)}, bf16[1,128,512]{2,1,0:T(8,128)(2,1)S(1)}, u32[]{:S(2)}, u32[]{:S(2)}) collective-permute-start(bf16[1,128,512]{2,1,0:T(8,128)(2,1)S(1)} %add_convert_fusion.8), channel_id=1, source_target_pairs={{0,16},{1,17},{2,18},{3,19},{4,20},{5,21},{6,22},{7,23},{8,24},{9,... | collective-permute-start | bytes 393224 | tf_op jit(solution)/shard_map/ppermute | solution.py:392

commit v13 on v10

--- a/solution.py
+++ b/solution.py
@@ -482,10 +482,12 @@
     )
 
 
-def gather_heads(heads, beside):
+def gather_heads(heads, make_beside):
     first, second, third = HEAD_STAGES
     heads = heads[None]
-    heads = jnp.concatenate([heads, flip(heads, first)], axis=0)
+    came = flip(heads, first)
+    beside = make_beside(came)
+    heads = jnp.concatenate([heads, came], axis=0)
     came = flip(heads, second)
     early = flip(heads, third)
     late, (early, beside) = after(came, (early, beside))
@@ -607,18 +609,16 @@
     rows = -(-PAIR * CAP // 16) * 16
     x_side, core, y_side = member >> 1, member & 1, group & 1
 
-    moved = lax.all_to_all(
-        pack(member, residual, route_ids, route_weights, groups),
-        "expert",
-        split_axis=0,
-        concat_axis=0,
-        tiled=True,
-    )
+    def exchange_residual(earlier):
+        own, _ = after(member, earlier)
+        packed = pack(own, residual, route_ids, route_weights, groups)
+        return lax.all_to_all(packed, "expert", split_axis=0, concat_axis=0, tiled=True)
+
     gain = lax.dynamic_index_in_dim(
         norm_gain.reshape(groups * members, LANES), device, 0, keepdims=False
     )
 
-    pieces, moved = gather_heads(attn_heads, moved)
+    pieces, moved = gather_heads(attn_heads, exchange_residual)
     numbers = jnp.arange(groups, dtype=jnp.int32)
     arrival = (head_bits(numbers, core) ^ group) ^ y_side
     info = jnp.concatenate(

time: 225 us -> 233 us (1.036)
  waiting for transfers between devices: 123 us -> 131 us
    ppermute x35, waiting for transfers between devices: 122 us -> 131 us  [flip(): return lax.ppermute(array, ('expert', 'tensor'), pairs)]
  transfers between devices with their start and end apart: 36 -> 36, of which waited for: 21 -> 20; matrix products, arithmetic and copies ran while one was open for 2% -> 1% of each run, Pallas kernels for 6% -> 6%
where the time goes in v13:
time: 233 us
  waiting for transfers between devices  131 us (56%)
  Pallas kernels  56.5 us (24%)
  starting transfers between devices  36.7 us (16%)
  local copies, waits for them, and re-layouts  4.84 us (2%)
  other arithmetic  3.82 us (2%)
    ppermute x35, waiting for transfers between devices, flip(): return lax.ppermute(array, ('expert', 'tensor'), pairs)  131 us
    ppermute x35, starting transfers between devices, flip(): return lax.ppermute(array, ('expert', 'tensor'), pairs)  31 us
    pallas_call x1, Pallas kernels, gate_up(): pl.pallas_call(kernel, grid_spec=pltpu.PrefetchScalarGridSpec(num_scalar_...  30.1 us
    pallas_call x3, Pallas kernels, down(): pl.pallas_call(functools.partial(down_kernel, rows), grid_spec=pltpu.Pref...  22.9 us
    all_to_all x1, starting transfers between devices, exchange_residual(): lax.all_to_all(packed, 'expert', split_axis=0, concat_axis=0, tiled=True)  5.77 us
  transfers between devices with their start and end apart: 36, of which 20 were waited for; matrix products, arithmetic and copies ran while one was open for 1% of the time, Pallas kernels for 6%

profile of v13, /device:TPU:0, one launch (start us, length us, event | category | flops | bytes accessed | tf_op | source)
XLA Modules:
  0.0 233.0 jit_solution(17172917873246954414)
XLA Ops:
  0.0 4.0 %collective-permute-start = (bf16[1,128,1024]{2,1,0:T(8,128)(2,1)}, bf16[1,128,1024]{2,1,0:T(8,128)(2,1)S(1)}, u32[]{:S(2)}, u32[]{:S(2)}) collective-permute-start(bf16[1,128,1024]{2,1,0:T(8,128)(2,1)} %bitcast.68), channel_id=1, source_target_pairs={{0,16},{1,17},{2,18},{3,19},{4,20},{5,21},{6,22},{7,23},{8,24},{9,... | collective-permute-start | bytes 786440 | tf_op jit(solution)/shard_map/ppermute | solution.py:374
  4.0 12.1 %collective-permute-done = bf16[1,128,1024]{2,1,0:T(8,128)(2,1)S(1)} collective-permute-done((bf16[1,128,1024]{2,1,0:T(8,128)(2,1)}, bf16[1,128,1024]{2,1,0:T(8,128)(2,1)S(1)}, u32[]{:S(2)}, u32[]{:S(2)}) %collective-permute-start) | collective-permute-done | bytes 262176 | tf_op jit(solution)/shard_map/ppermute | solution.py:374
  16.2 1.2 copy-done
  17.4 0.7 copy-done.1
  18.1 0.7 copy-done.2
  18.8 0.8 pack.1
  19.6 5.8 %all-to-all-start = ((bf16[8,160,128]{2,1,0:T(8,128)(2,1)}), bf16[8,160,128]{2,1,0:T(8,128)(2,1)S(1)}, u32[]{:S(2)}, u32[]{:S(2)}) async-start(bf16[8,160,128]{2,1,0:T(8,128)(2,1)} %pack.1), calls=%async_computation | async-start | bytes 655360 | tf_op jit(solution)/shard_map/all_to_all | solution.py:615
  25.4 2.1 collective-permute-start.2
  27.5 1.5 collective-permute-start.1
  29.1 15.7 %collective-permute-done.2.refs_2_ = bf16[2,128,1024]{2,1,0:T(8,128)(2,1)S(1)} collective-permute-done((bf16[2,128,1024]{2,1,0:T(8,128)(2,1)S(1)}, bf16[2,128,1024]{2,1,0:T(8,128)(2,1)S(1)}, u32[]{:S(2)}, u32[]{:S(2)}) %collective-permute-start.2) | collective-permute-done | bytes 524320 | tf_op jit(solution)/shard_map/ppermute | solution.py:374
  44.8 0.6 gather_fusion
  45.4 0.1 fusion.1
  45.6 0.2 compare_reduce_fusion
  45.8 0.2 convolution_convert_fusion
  46.0 8.7 %collective-permute-done.3.refs_3_ = bf16[2,128,1024]{2,1,0:T(8,128)(2,1)} collective-permute-done((bf16[2,128,1024]{2,1,0:T(8,128)(2,1)S(1)}, bf16[2,128,1024]{2,1,0:T(8,128)(2,1)}, u32[]{:S(2)}, u32[]{:S(2)}) %collective-permute-start.3) | collective-permute-done | bytes 524320 | tf_op jit(solution)/shard_map/ppermute | solution.py:374
  54.7 1.0 copy-done.5
  55.8 2.6 %project.1 = (bf16[2,8,128,128]{3,2,1,0:T(8,128)(2,1)S(1)}, bf16[2,8,128,128]{3,2,1,0:T(8,128)(2,1)S(1)}) custom-call(s32[10]{0:T(128)S(1)} %pad_add_fusion.1.info_ref, bf16[2,128,1024]{2,1,0:T(8,128)(2,1)S(1)} %pad_maximum_fusion.refs_0_, bf16[2,128,1024]{2,1,0:T(8,128)(2,1)S(1)} %copy-done.5, bf16[2,128,1024]{2,1,0:T(8,128)(2,1)S(1)} %collective-permute-done.2.refs_2_, ...), custom_call_target="tpu_custom_call" | custom-call | flops 1073741824 | bytes 5242880 | tf_op jit(solution)/shard_map/project/pallas_call | solution.py:112
  58.5 1.9 collective-permute-done.4
  60.5 1.6 collective-permute-start.5
  62.0 6.8 %collective-permute-done.5 = bf16[8,128,128]{2,1,0:T(8,128)(2,1)S(1)} collective-permute-done((bf16[8,128,128]{2,1,0:T(8,128)(2,1)S(1)}, bf16[8,128,128]{2,1,0:T(8,128)(2,1)S(1)}, u32[]{:S(2)}, u32[]{:S(2)}) %collective-permute-start.5) | collective-permute-done | bytes 262176 | tf_op jit(solution)/shard_map/ppermute | solution.py:374
  68.9 0.2 fusion.8
  69.0 2.1 collective-permute-start.7
  71.1 1.5 collective-permute-start.6
  72.6 4.4 %collective-permute-done.7 = bf16[1,4,128,128]{3,2,1,0:T(8,128)(2,1)S(1)} collective-permute-done((bf16[1,4,128,128]{3,2,1,0:T(8,128)(2,1)S(1)}, bf16[1,4,128,128]{3,2,1,0:T(8,128)(2,1)S(1)}, u32[]{:S(2)}, u32[]{:S(2)}) %collective-permute-start.7) | collective-permute-done | bytes 131104 | tf_op jit(solution)/shard_map/ppermute | solution.py:374
  77.1 2.9 %collective-permute-start.9 = (bf16[2,4,128,128]{3,2,1,0:T(8,128)(2,1)S(1)}, bf16[2,4,128,128]{3,2,1,0:T(8,128)(2,1)S(1)}, u32[]{:S(2)}, u32[]{:S(2)}) collective-permute-start(bf16[2,4,128,128]{3,2,1,0:T(8,128)(2,1)S(1)} %pad_maximum_fusion.2), channel_id=1, source_target_pairs={{0,16},{1,17},{2,18},{3,19},{4,20},{5,21},{6,22},{7,23},{8,24},{9,... | collective-permute-start | bytes 786440 | tf_op jit(solution)/shard_map/ppermute | solution.py:374
  80.0 9.2 %collective-permute-done.8 = bf16[2,4,128,128]{3,2,1,0:T(8,128)(2,1)S(1)} collective-permute-done((bf16[2,4,128,128]{3,2,1,0:T(8,128)(2,1)S(1)}, bf16[2,4,128,128]{3,2,1,0:T(8,128)(2,1)S(1)}, u32[]{:S(2)}, u32[]{:S(2)}) %collective-permute-start.8) | collective-permute-done | bytes 262176 | tf_op jit(solution)/shard_map/ppermute | solution.py:374
  89.3 2.5 %collective-permute-done.9 = bf16[2,4,128,128]{3,2,1,0:T(8,128)(2,1)S(1)} collective-permute-done((bf16[2,4,128,128]{3,2,1,0:T(8,128)(2,1)S(1)}, bf16[2,4,128,128]{3,2,1,0:T(8,128)(2,1)S(1)}, u32[]{:S(2)}, u32[]{:S(2)}) %collective-permute-start.9) | collective-permute-done | bytes 262176 | tf_op jit(solution)/shard_map/ppermute | solution.py:374
  91.9 1.6 collective-permute-start.11
  93.4 0.5 collective-permute-start.18
  93.9 1.7 collective-permute-start.17
  95.8 10.5 %collective-permute-done.11.rest_1_ = bf16[4,4,128,128]{3,2,1,0:T(8,128)(2,1)S(1)} collective-permute-done((bf16[4,4,128,128]{3,2,1,0:T(8,128)(2,1)S(1)}, bf16[4,4,128,128]{3,2,1,0:T(8,128)(2,1)S(1)}, u32[]{:S(2)}, u32[]{:S(2)}) %collective-permute-start.11) | collective-permute-done | bytes 524320 | tf_op jit(solution)/shard_map/ppermute | solution.py:374
  106.3 0.5 collective-permute-start.13
  106.8 5.1 %collective-permute-done.18.rest_9_ = bf16[4,4,128,128]{3,2,1,0:T(8,128)(2,1)S(1)} collective-permute-done((bf16[4,4,128,128]{3,2,1,0:T(8,128)(2,1)S(1)}, bf16[4,4,128,128]{3,2,1,0:T(8,128)(2,1)S(1)}, u32[]{:S(2)}, u32[]{:S(2)}) %collective-permute-start.18) | collective-permute-done | bytes 524320 | tf_op jit(solution)/shard_map/ppermute | solution.py:374
  111.9 1.5 collective-permute-start.14
  113.4 0.5 collective-permute-start.21
  114.5 0.5 collective-permute-start.22
  115.1 6.2 %collective-permute-done.14.rest_5_ = bf16[4,4,128,128]{3,2,1,0:T(8,128)(2,1)} collective-permute-done((bf16[4,4,128,128]{3,2,1,0:T(8,128)(2,1)S(1)}, bf16[4,4,128,128]{3,2,1,0:T(8,128)(2,1)}, u32[]{:S(2)}, u32[]{:S(2)}) %collective-permute-start.14) | collective-permute-done | bytes 524320 | tf_op jit(solution)/shard_map/ppermute | solution.py:374
  121.2 5.6 %collective-permute-done.21.rest_13_ = bf16[4,4,128,128]{3,2,1,0:T(8,128)(2,1)} collective-permute-done((bf16[4,4,128,128]{3,2,1,0:T(8,128)(2,1)S(1)}, bf16[4,4,128,128]{3,2,1,0:T(8,128)(2,1)}, u32[]{:S(2)}, u32[]{:S(2)}) %collective-permute-start.21) | collective-permute-done | bytes 524320 | tf_op jit(solution)/shard_map/ppermute | solution.py:374
  127.1 1.9 collective-permute-done.23.rest_15_
  129.0 30.1 %gate_up.1 = (bf16[8,192,384]{2,1,0:T(8,128)(2,1)S(1)}, f32[128,1024]{1,0:T(8,128)S(1)}, bf16[4,256,384]{2,1,0:T(8,128)(2,1)S(1)}) custom-call(s32[66]{0:T(128)S(1)} %pad_add_fusion.info_ref, s32[8,1024]{1,0:T(8,128)S(1)} %bitcast_select_fusion.slot_ref, f32[8,1024]{1,0:T(8,128)S(1)} %bitcast.64, f32[32,128]{1,0:T(8,128)S(1)} %divide_bitcast_fusion.invgain_ref, ...), custom_call_target="tpu_custom_call" | custom-call | flops 9663676416 | bytes 58720256 | tf_op jit(solution)/shard_map/gate_up/pallas_call | solution.py:267
  159.1 10.0 %down_mix.4 = (bf16[16,128,512]{2,1,0:T(8,128)(2,1)S(1)}, bf16[16,128,512]{2,1,0:T(8,128)(2,1)S(1)}) custom-call(s32[34]{0:T(128)S(1)} %pad_add_fusion.3.place_ref, bf16[4,256,384]{2,1,0:T(8,128)(2,1)S(1)} %get-tuple-element.52.spread_ref, bf16[8,192,384]{2,1,0:T(8,128)(2,1)S(1)} %get-tuple-element.53.act_ref, bf16[8,384,4096]{2,1,0:T(8,128)(2,1)} %wd1_ref.5, ...), custom_call_target="tpu_custom_call" | custom-call | flops 4831838208 | bytes 16777216 | tf_op jit(solution)/shard_map/down_mix/pallas_call | solution.py:343
  169.1 0.2 collective-permute-start.24
  169.3 0.3 collective-permute-start.29
  169.8 6.5 %down_mix.3 = bf16[16,128,512]{2,1,0:T(8,128)(2,1)S(1)} custom-call(s32[18]{0:T(128)S(1)} %pad_add_fusion.2.place_ref, bf16[4,256,384]{2,1,0:T(8,128)(2,1)S(1)} %get-tuple-element.52.spread_ref, bf16[8,192,384]{2,1,0:T(8,128)(2,1)S(1)} %get-tuple-element.53.act_ref, bf16[8,384,4096]{2,1,0:T(8,128)(2,1)} %wd1_ref.5, bf16[8,384,4096]{2,1,0:T(8,128)(2,1)} %wd1_ref.5), custom_call_target="tpu_custom_call" | custom-call | flops 2415919104 | bytes 8388608 | tf_op jit(solution)/shard_map/down_mix/pallas_call | solution.py:343
  176.3 0.3 add_convert_fusion
  176.6 1.6 collective-permute-start.25
  178.3 6.5 %down_mix.5 = bf16[16,128,512]{2,1,0:T(8,128)(2,1)S(1)} custom-call(s32[18]{0:T(128)S(1)} %pad_add_fusion.4.place_ref, bf16[4,256,384]{2,1,0:T(8,128)(2,1)S(1)} %get-tuple-element.52.spread_ref, bf16[8,192,384]{2,1,0:T(8,128)(2,1)S(1)} %get-tuple-element.53.act_ref, bf16[8,384,4096]{2,1,0:T(8,128)(2,1)} %wd1_ref.5, bf16[8,384,4096]{2,1,0:T(8,128)(2,1)} %wd1_ref.5), custom_call_target="tpu_custom_call" | custom-call | flops 2415919104 | bytes 8388608 | tf_op jit(solution)/shard_map/down_mix/pallas_call | solution.py:343
  184.8 0.3 add_convert_fusion.2
  185.1 0.6 collective-permute-start.30
  185.7 5.8 %collective-permute-done.25 = bf16[8,128,512]{2,1,0:T(8,128)(2,1)S(1)} collective-permute-done((bf16[8,128,512]{2,1,0:T(8,128)(2,1)S(1)}, bf16[8,128,512]{2,1,0:T(8,128)(2,1)S(1)}, u32[]{:S(2)}, u32[]{:S(2)}) %collective-permute-start.25) | collective-permute-done | bytes 1048608 | tf_op jit(solution)/shard_map/ppermute | solution.py:374
  191.5 0.2 add_convert_fusion.4
  191.8 5.3 %collective-permute-done.30 = bf16[4,128,512]{2,1,0:T(8,128)(2,1)S(1)} collective-permute-done((bf16[4,128,512]{2,1,0:T(8,128)(2,1)S(1)}, bf16[4,128,512]{2,1,0:T(8,128)(2,1)S(1)}, u32[]{:S(2)}, u32[]{:S(2)}) %collective-permute-start.30) | collective-permute-done | bytes 524320 | tf_op jit(solution)/shard_map/ppermute | solution.py:374
  197.1 0.2 add_convert_fusion.1
  197.3 1.7 collective-permute-start.32
  199.0 1.5 collective-permute-start.31
  200.5 4.4 %collective-permute-done.26 = bf16[4,128,512]{2,1,0:T(8,128)(2,1)S(1)} collective-permute-done((bf16[4,128,512]{2,1,0:T(8,128)(2,1)S(1)}, bf16[4,128,512]{2,1,0:T(8,128)(2,1)S(1)}, u32[]{:S(2)}, u32[]{:S(2)}) %collective-permute-start.26) | collective-permute-done | bytes 524320 | tf_op jit(solution)/shard_map/ppermute | solution.py:374
  204.9 0.1 add_convert_fusion.6
  205.1 0.5 collective-permute-start.27
  205.6 6.2 %collective-permute-done.32 = bf16[4,128,512]{2,1,0:T(8,128)(2,1)S(1)} collective-permute-done((bf16[4,128,512]{2,1,0:T(8,128)(2,1)S(1)}, bf16[4,128,512]{2,1,0:T(8,128)(2,1)S(1)}, u32[]{:S(2)}, u32[]{:S(2)}) %collective-permute-start.32) | collective-permute-done | bytes 524320 | tf_op jit(solution)/shard_map/ppermute | solution.py:374
  212.0 6.4 %collective-permute-done.27 = bf16[2,128,512]{2,1,0:T(8,128)(2,1)S(1)} collective-permute-done((bf16[2,128,512]{2,1,0:T(8,128)(2,1)S(1)}, bf16[2,128,512]{2,1,0:T(8,128)(2,1)S(1)}, u32[]{:S(2)}, u32[]{:S(2)}) %collective-permute-start.27) | collective-permute-done | bytes 262176 | tf_op jit(solution)/shard_map/ppermute | solution.py:374
  218.4 1.6 collective-permute-start.28
  220.0 3.8 %collective-permute-done.33 = bf16[2,128,512]{2,1,0:T(8,128)(2,1)S(1)} collective-permute-done((bf16[2,128,512]{2,1,0:T(8,128)(2,1)S(1)}, bf16[2,128,512]{2,1,0:T(8,128)(2,1)S(1)}, u32[]{:S(2)}, u32[]{:S(2)}) %collective-permute-start.33) | collective-permute-done | bytes 262176 | tf_op jit(solution)/shard_map/ppermute | solution.py:374
  224.1 8.0 %collective-permute-done.34 = bf16[1,128,512]{2,1,0:T(8,128)(2,1)S(1)} collective-permute-done((bf16[1,128,512]{2,1,0:T(8,128)(2,1)S(1)}, bf16[1,128,512]{2,1,0:T(8,128)(2,1)S(1)}, u32[]{:S(2)}, u32[]{:S(2)}) %collective-permute-start.34) | collective-permute-done | bytes 131104 | tf_op jit(solution)/shard_map/ppermute | solution.py:374
  232.2 0.8 fusion
  (87 shorter events, 2.7 us)
Async XLA Ops:
  0.0 16.2 %collective-permute-start = (bf16[1,128,1024]{2,1,0:T(8,128)(2,1)}, bf16[1,128,1024]{2,1,0:T(8,128)(2,1)S(1)}, u32[]{:S(2)}, u32[]{:S(2)}) collective-permute-start(bf16[1,128,1024]{2,1,0:T(8,128)(2,1)} %bitcast.68), channel_id=1, source_target_pairs={{0,16},{1,17},{2,18},{3,19},{4,20},{5,21},{6,22},{7,23},{8,24},{9,... | collective-permute-start | bytes 786440 | tf_op jit(solution)/shard_map/ppermute | solution.py:374
  16.2 1.2 copy-start
  17.4 0.7 copy-start.1
  18.1 0.7 copy-start.2
  18.8 6.6 %copy-start.6 = (bf16[128,1024]{1,0:T(8,128)(2,1)S(1)}, bf16[128,1024]{1,0:T(8,128)(2,1)}, u32[]{:S(2)}) copy-start(bf16[128,1024]{1,0:T(8,128)(2,1)} %param.9) | copy-start | bytes 786436
  18.8 35.9 %copy-start.3 = (bf16[1024,512]{1,0:T(8,128)(2,1)S(1)}, bf16[1024,512]{1,0:T(8,128)(2,1)}, u32[]{:S(2)}) copy-start(bf16[1024,512]{1,0:T(8,128)(2,1)} %refs_4_.1) | copy-start | bytes 3145732
  19.6 25.2 %all-to-all-start = ((bf16[8,160,128]{2,1,0:T(8,128)(2,1)}), bf16[8,160,128]{2,1,0:T(8,128)(2,1)S(1)}, u32[]{:S(2)}, u32[]{:S(2)}) async-start(bf16[8,160,128]{2,1,0:T(8,128)(2,1)} %pack.1), calls=%async_computation | async-start | bytes 655360 | tf_op jit(solution)/shard_map/all_to_all | solution.py:615
  25.4 19.3 %collective-permute-start.2 = (bf16[2,128,1024]{2,1,0:T(8,128)(2,1)S(1)}, bf16[2,128,1024]{2,1,0:T(8,128)(2,1)S(1)}, u32[]{:S(2)}, u32[]{:S(2)}) collective-permute-start(bf16[2,128,1024]{2,1,0:T(8,128)(2,1)S(1)} %pad_maximum_fusion.refs_0_), channel_id=1, source_target_pairs={{0,8},{1,5},{2,10},{3,7},{4,12},{5,1},{6,14},{7,3},{8,0},{9,13},{1... | collective-permute-start | bytes 1572872 | tf_op jit(solution)/shard_map/ppermute | solution.py:374
  27.5 17.2 %collective-permute-start.1 = (bf16[2,128,1024]{2,1,0:T(8,128)(2,1)S(1)}, bf16[2,128,1024]{2,1,0:T(8,128)(2,1)S(1)}, u32[]{:S(2)}, u32[]{:S(2)}) collective-permute-start(bf16[2,128,1024]{2,1,0:T(8,128)(2,1)S(1)} %pad_maximum_fusion.refs_0_), channel_id=1, source_target_pairs={{0,4},{1,9},{2,6},{3,11},{4,0},{5,13},{6,2},{7,15},{8,12},{9,1},{1... | collective-permute-start | bytes 1572872 | tf_op jit(solution)/shard_map/ppermute | solution.py:374
  44.7 1.3 copy-start.4
  45.4 9.4 %collective-permute-start.3 = (bf16[2,128,1024]{2,1,0:T(8,128)(2,1)S(1)}, bf16[2,128,1024]{2,1,0:T(8,128)(2,1)}, u32[]{:S(2)}, u32[]{:S(2)}) collective-permute-start(bf16[2,128,1024]{2,1,0:T(8,128)(2,1)S(1)} %collective-permute-done.1.refs_1_), channel_id=1, source_target_pairs={{0,8},{1,5},{2,10},{3,7},{4,12},{5,1},{6,14},{7,3},{8,0},{9,13},{1... | collective-permute-start | bytes 1572872 | tf_op jit(solution)/shard_map/ppermute | solution.py:374
  54.7 1.0 copy-start.5
  55.8 6.3 %copy-start.7 = (f32[4096]{0:T(1024)S(1)}, f32[4096]{0:T(1024)}, u32[]{:S(2)}) copy-start(f32[4096]{0:T(1024)} %param.12) | copy-start | bytes 49156
  58.4 2.0 collective-permute-start.4
  60.5 8.4 %collective-permute-start.5 = (bf16[8,128,128]{2,1,0:T(8,128)(2,1)S(1)}, bf16[8,128,128]{2,1,0:T(8,128)(2,1)S(1)}, u32[]{:S(2)}, u32[]{:S(2)}) collective-permute-start(bf16[8,128,128]{2,1,0:T(8,128)(2,1)S(1)} %fusion.2), channel_id=1, source_target_pairs={{0,2},{1,3},{2,0},{3,1},{4,6},{5,7},{6,4},{7,5},{8,10},{9,11},{10,... | collective-permute-start | bytes 786440 | tf_op jit(solution)/shard_map/ppermute | solution.py:374
  69.0 7.9 %collective-permute-start.7 = (bf16[1,4,128,128]{3,2,1,0:T(8,128)(2,1)S(1)}, bf16[1,4,128,128]{3,2,1,0:T(8,128)(2,1)S(1)}, u32[]{:S(2)}, u32[]{:S(2)}) collective-permute-start(bf16[1,4,128,128]{3,2,1,0:T(8,128)(2,1)S(1)} %get-tuple-element.67), channel_id=1, source_target_pairs={{0,16},{1,17},{2,18},{3,19},{4,20},{5,21},{6,22},{7,23},{8,24},{9,... | collective-permute-start | bytes 393224 | tf_op jit(solution)/shard_map/ppermute | solution.py:374
  71.1 5.9 %collective-permute-start.6 = (bf16[1,4,128,128]{3,2,1,0:T(8,128)(2,1)S(1)}, bf16[1,4,128,128]{3,2,1,0:T(8,128)(2,1)S(1)}, u32[]{:S(2)}, u32[]{:S(2)}) collective-permute-start(bf16[1,4,128,128]{3,2,1,0:T(8,128)(2,1)S(1)} %get-tuple-element.68), channel_id=1, source_target_pairs={{0,4},{1,3},{2,6},{3,1},{4,0},{5,7},{6,2},{7,5},{8,12},{9,11},{10,... | collective-permute-start | bytes 393224 | tf_op jit(solution)/shard_map/ppermute | solution.py:374
  77.0 12.2 %collective-permute-start.8 = (bf16[2,4,128,128]{3,2,1,0:T(8,128)(2,1)S(1)}, bf16[2,4,128,128]{3,2,1,0:T(8,128)(2,1)S(1)}, u32[]{:S(2)}, u32[]{:S(2)}) collective-permute-start(bf16[2,4,128,128]{3,2,1,0:T(8,128)(2,1)S(1)} %pad_maximum_fusion.3), channel_id=1, source_target_pairs={{0,8},{1,9},{2,10},{3,11},{4,12},{5,13},{6,14},{7,15},{8,0},{9,1},... | collective-permute-start | bytes 786440 | tf_op jit(solution)/shard_map/ppermute | solution.py:374
  77.1 14.7 %collective-permute-start.9 = (bf16[2,4,128,128]{3,2,1,0:T(8,128)(2,1)S(1)}, bf16[2,4,128,128]{3,2,1,0:T(8,128)(2,1)S(1)}, u32[]{:S(2)}, u32[]{:S(2)}) collective-permute-start(bf16[2,4,128,128]{3,2,1,0:T(8,128)(2,1)S(1)} %pad_maximum_fusion.2), channel_id=1, source_target_pairs={{0,16},{1,17},{2,18},{3,19},{4,20},{5,21},{6,22},{7,23},{8,24},{9,... | collective-permute-start | bytes 786440 | tf_op jit(solution)/shard_map/ppermute | solution.py:374
  91.9 14.5 %collective-permute-start.11 = (bf16[4,4,128,128]{3,2,1,0:T(8,128)(2,1)S(1)}, bf16[4,4,128,128]{3,2,1,0:T(8,128)(2,1)S(1)}, u32[]{:S(2)}, u32[]{:S(2)}) collective-permute-start(bf16[4,4,128,128]{3,2,1,0:T(8,128)(2,1)S(1)} %constant_dynamic-update-slice_fusion.rest_0_), channel_id=1, source_target_pairs={{0,2},{1,5},{2,0},{3,7},{4,6},{5,1},{6,4},{7,3},{8,10},{9,13},{10,... | collective-permute-start | bytes 1572872 | tf_op jit(solution)/shard_map/ppermute | solution.py:374
  93.4 12.9 %collective-permute-start.10 = (bf16[4,4,128,128]{3,2,1,0:T(8,128)(2,1)S(1)}, bf16[4,4,128,128]{3,2,1,0:T(8,128)(2,1)S(1)}, u32[]{:S(2)}, u32[]{:S(2)}) collective-permute-start(bf16[4,4,128,128]{3,2,1,0:T(8,128)(2,1)S(1)} %constant_dynamic-update-slice_fusion.rest_0_), channel_id=1, source_target_pairs={{0,8},{1,9},{2,10},{3,11},{4,12},{5,13},{6,14},{7,15},{8,0},{9,1},... | collective-permute-start | bytes 1572872 | tf_op jit(solution)/shard_map/ppermute | solution.py:374
  93.4 18.5 %collective-permute-start.18 = (bf16[4,4,128,128]{3,2,1,0:T(8,128)(2,1)S(1)}, bf16[4,4,128,128]{3,2,1,0:T(8,128)(2,1)S(1)}, u32[]{:S(2)}, u32[]{:S(2)}) collective-permute-start(bf16[4,4,128,128]{3,2,1,0:T(8,128)(2,1)S(1)} %pad_maximum_fusion.1.rest_8_), channel_id=1, source_target_pairs={{0,2},{1,5},{2,0},{3,7},{4,6},{5,1},{6,4},{7,3},{8,10},{9,13},{10,... | collective-permute-start | bytes 1572872 | tf_op jit(solution)/shard_map/ppermute | solution.py:374
  93.9 19.5 %collective-permute-start.17 = (bf16[4,4,128,128]{3,2,1,0:T(8,128)(2,1)S(1)}, bf16[4,4,128,128]{3,2,1,0:T(8,128)(2,1)S(1)}, u32[]{:S(2)}, u32[]{:S(2)}) collective-permute-start(bf16[4,4,128,128]{3,2,1,0:T(8,128)(2,1)S(1)} %pad_maximum_fusion.1.rest_8_), channel_id=1, source_target_pairs={{0,4},{1,3},{2,6},{3,1},{4,0},{5,7},{6,2},{7,5},{8,12},{9,11},{10,... | collective-permute-start | bytes 1572872 | tf_op jit(solution)/shard_map/ppermute | solution.py:374
  95.8 18.6 %collective-permute-start.12 = (bf16[4,4,128,128]{3,2,1,0:T(8,128)(2,1)S(1)}, bf16[4,4,128,128]{3,2,1,0:T(8,128)(2,1)}, u32[]{:S(2)}, u32[]{:S(2)}) collective-permute-start(bf16[4,4,128,128]{3,2,1,0:T(8,128)(2,1)S(1)} %constant_dynamic-update-slice_fusion.rest_0_), channel_id=1, source_target_pairs={{0,1},{1,0},{2,3},{3,2},{4,5},{5,4},{6,7},{7,6},{8,9},{9,8},{10,11... | collective-permute-start | bytes 1572872 | tf_op jit(solution)/shard_map/ppermute | solution.py:374
  106.3 8.2 %collective-permute-start.19 = (bf16[4,4,128,128]{3,2,1,0:T(8,128)(2,1)S(1)}, bf16[4,4,128,128]{3,2,1,0:T(8,128)(2,1)}, u32[]{:S(2)}, u32[]{:S(2)}) collective-permute-start(bf16[4,4,128,128]{3,2,1,0:T(8,128)(2,1)S(1)} %pad_maximum_fusion.1.rest_8_), channel_id=1, source_target_pairs={{0,1},{1,0},{2,3},{3,2},{4,5},{5,4},{6,7},{7,6},{8,9},{9,8},{10,11... | collective-permute-start | bytes 1572872 | tf_op jit(solution)/shard_map/ppermute | solution.py:374
  106.3 8.7 %collective-permute-start.13 = (bf16[4,4,128,128]{3,2,1,0:T(8,128)(2,1)S(1)}, bf16[4,4,128,128]{3,2,1,0:T(8,128)(2,1)}, u32[]{:S(2)}, u32[]{:S(2)}) collective-permute-start(bf16[4,4,128,128]{3,2,1,0:T(8,128)(2,1)S(1)} %collective-permute-done.11.rest_1_), channel_id=1, source_target_pairs={{0,1},{1,0},{2,3},{3,2},{4,5},{5,4},{6,7},{7,6},{8,9},{9,8},{10,11... | collective-permute-start | bytes 1572872 | tf_op jit(solution)/shard_map/ppermute | solution.py:374
  111.9 9.3 %collective-permute-start.14 = (bf16[4,4,128,128]{3,2,1,0:T(8,128)(2,1)S(1)}, bf16[4,4,128,128]{3,2,1,0:T(8,128)(2,1)}, u32[]{:S(2)}, u32[]{:S(2)}) collective-permute-start(bf16[4,4,128,128]{3,2,1,0:T(8,128)(2,1)S(1)} %collective-permute-done.10.rest_4_), channel_id=1, source_target_pairs={{0,2},{1,5},{2,0},{3,7},{4,6},{5,1},{6,4},{7,3},{8,10},{9,13},{10,... | collective-permute-start | bytes 1572872 | tf_op jit(solution)/shard_map/ppermute | solution.py:374
  113.4 13.4 %collective-permute-start.21 = (bf16[4,4,128,128]{3,2,1,0:T(8,128)(2,1)S(1)}, bf16[4,4,128,128]{3,2,1,0:T(8,128)(2,1)}, u32[]{:S(2)}, u32[]{:S(2)}) collective-permute-start(bf16[4,4,128,128]{3,2,1,0:T(8,128)(2,1)S(1)} %collective-permute-done.17.rest_12_), channel_id=1, source_target_pairs={{0,2},{1,5},{2,0},{3,7},{4,6},{5,1},{6,4},{7,3},{8,10},{9,13},{10,... | collective-permute-start | bytes 1572872 | tf_op jit(solution)/shard_map/ppermute | solution.py:374
  114.4 12.6 %collective-permute-start.15 = (bf16[4,4,128,128]{3,2,1,0:T(8,128)(2,1)S(1)}, bf16[4,4,128,128]{3,2,1,0:T(8,128)(2,1)S(1)}, u32[]{:S(2)}, u32[]{:S(2)}) collective-permute-start(bf16[4,4,128,128]{3,2,1,0:T(8,128)(2,1)S(1)} %collective-permute-done.10.rest_4_), channel_id=1, source_target_pairs={{0,1},{1,0},{2,3},{3,2},{4,5},{5,4},{6,7},{7,6},{8,9},{9,8},{10,11... | collective-permute-start | bytes 1572872 | tf_op jit(solution)/shard_map/ppermute | solution.py:374
  114.5 12.6 %collective-permute-start.22 = (bf16[4,4,128,128]{3,2,1,0:T(8,128)(2,1)S(1)}, bf16[4,4,128,128]{3,2,1,0:T(8,128)(2,1)S(1)}, u32[]{:S(2)}, u32[]{:S(2)}) collective-permute-start(bf16[4,4,128,128]{3,2,1,0:T(8,128)(2,1)S(1)} %collective-permute-done.17.rest_12_), channel_id=1, source_target_pairs={{0,1},{1,0},{2,3},{3,2},{4,5},{5,4},{6,7},{7,6},{8,9},{9,8},{10,11... | collective-permute-start | bytes 1572872 | tf_op jit(solution)/shard_map/ppermute | solution.py:374
  115.0 12.1 %collective-permute-start.20 = (bf16[4,4,128,128]{3,2,1,0:T(8,128)(2,1)S(1)}, bf16[4,4,128,128]{3,2,1,0:T(8,128)(2,1)S(1)}, u32[]{:S(2)}, u32[]{:S(2)}) collective-permute-start(bf16[4,4,128,128]{3,2,1,0:T(8,128)(2,1)S(1)} %collective-permute-done.18.rest_9_), channel_id=1, source_target_pairs={{0,1},{1,0},{2,3},{3,2},{4,5},{5,4},{6,7},{7,6},{8,9},{9,8},{10,11... | collective-permute-start | bytes 1572872 | tf_op jit(solution)/shard_map/ppermute | solution.py:374
  121.2 5.8 %collective-permute-start.16 = (bf16[4,4,128,128]{3,2,1,0:T(8,128)(2,1)}, bf16[4,4,128,128]{3,2,1,0:T(8,128)(2,1)S(1)}, u32[]{:S(2)}, u32[]{:S(2)}) collective-permute-start(bf16[4,4,128,128]{3,2,1,0:T(8,128)(2,1)} %collective-permute-done.14.rest_5_), channel_id=1, source_target_pairs={{0,1},{1,0},{2,3},{3,2},{4,5},{5,4},{6,7},{7,6},{8,9},{9,8},{10,11... | collective-permute-start | bytes 1572872 | tf_op jit(solution)/shard_map/ppermute | solution.py:374
  126.8 2.1 collective-permute-start.23
  169.1 7.2 %collective-permute-start.24 = (bf16[16,128,512]{2,1,0:T(8,128)(2,1)S(1)}, bf16[16,128,512]{2,1,0:T(8,128)(2,1)S(1)}, u32[]{:S(2)}, u32[]{:S(2)}) collective-permute-start(bf16[16,128,512]{2,1,0:T(8,128)(2,1)S(1)} %get-tuple-element.54), channel_id=1, source_target_pairs={{0,1},{1,0},{2,3},{3,2},{4,5},{5,4},{6,7},{7,6},{8,9},{9,8},{10,11... | collective-permute-start | bytes 6291464 | tf_op jit(solution)/shard_map/ppermute | solution.py:374
  169.3 15.5 %collective-permute-start.29 = (bf16[16,128,512]{2,1,0:T(8,128)(2,1)S(1)}, bf16[16,128,512]{2,1,0:T(8,128)(2,1)S(1)}, u32[]{:S(2)}, u32[]{:S(2)}) collective-permute-start(bf16[16,128,512]{2,1,0:T(8,128)(2,1)S(1)} %get-tuple-element.56), channel_id=1, source_target_pairs={{0,1},{1,0},{2,3},{3,2},{4,5},{5,4},{6,7},{7,6},{8,9},{9,8},{10,11... | collective-permute-start | bytes 6291464 | tf_op jit(solution)/shard_map/ppermute | solution.py:374
  176.6 14.9 %collective-permute-start.25 = (bf16[8,128,512]{2,1,0:T(8,128)(2,1)S(1)}, bf16[8,128,512]{2,1,0:T(8,128)(2,1)S(1)}, u32[]{:S(2)}, u32[]{:S(2)}) collective-permute-start(bf16[8,128,512]{2,1,0:T(8,128)(2,1)S(1)} %add_convert_fusion), channel_id=1, source_target_pairs={{0,2},{1,5},{2,0},{3,7},{4,6},{5,1},{6,4},{7,3},{8,10},{9,13},{10,... | collective-permute-start | bytes 3145736 | tf_op jit(solution)/shard_map/ppermute | solution.py:374
  185.1 12.0 %collective-permute-start.30 = (bf16[4,128,512]{2,1,0:T(8,128)(2,1)S(1)}, bf16[4,128,512]{2,1,0:T(8,128)(2,1)S(1)}, u32[]{:S(2)}, u32[]{:S(2)}) collective-permute-start(bf16[4,128,512]{2,1,0:T(8,128)(2,1)S(1)} %get-tuple-element.58), channel_id=1, source_target_pairs={{0,2},{1,5},{2,0},{3,7},{4,6},{5,1},{6,4},{7,3},{8,10},{9,13},{10,... | collective-permute-start | bytes 1572872 | tf_op jit(solution)/shard_map/ppermute | solution.py:374
  191.7 13.2 %collective-permute-start.26 = (bf16[4,128,512]{2,1,0:T(8,128)(2,1)S(1)}, bf16[4,128,512]{2,1,0:T(8,128)(2,1)S(1)}, u32[]{:S(2)}, u32[]{:S(2)}) collective-permute-start(bf16[4,128,512]{2,1,0:T(8,128)(2,1)S(1)} %add_convert_fusion.4), channel_id=1, source_target_pairs={{0,8},{1,9},{2,10},{3,11},{4,12},{5,13},{6,14},{7,15},{8,0},{9,1},... | collective-permute-start | bytes 1572872 | tf_op jit(solution)/shard_map/ppermute | solution.py:374
  197.3 14.4 %collective-permute-start.32 = (bf16[4,128,512]{2,1,0:T(8,128)(2,1)S(1)}, bf16[4,128,512]{2,1,0:T(8,128)(2,1)S(1)}, u32[]{:S(2)}, u32[]{:S(2)}) collective-permute-start(bf16[4,128,512]{2,1,0:T(8,128)(2,1)S(1)} %add_convert_fusion.1), channel_id=1, source_target_pairs={{0,4},{1,3},{2,6},{3,1},{4,0},{5,7},{6,2},{7,5},{8,12},{9,11},{10,... | collective-permute-start | bytes 1572872 | tf_op jit(solution)/shard_map/ppermute | solution.py:374
  199.0 12.7 %collective-permute-start.31 = (bf16[4,128,512]{2,1,0:T(8,128)(2,1)S(1)}, bf16[4,128,512]{2,1,0:T(8,128)(2,1)S(1)}, u32[]{:S(2)}, u32[]{:S(2)}) collective-permute-start(bf16[4,128,512]{2,1,0:T(8,128)(2,1)S(1)} %get-tuple-element.60), channel_id=1, source_target_pairs={{0,2},{1,5},{2,0},{3,7},{4,6},{5,1},{6,4},{7,3},{8,10},{9,13},{10,... | collective-permute-start | bytes 1572872 | tf_op jit(solution)/shard_map/ppermute | solution.py:374
  205.1 13.3 %collective-permute-start.27 = (bf16[2,128,512]{2,1,0:T(8,128)(2,1)S(1)}, bf16[2,128,512]{2,1,0:T(8,128)(2,1)S(1)}, u32[]{:S(2)}, u32[]{:S(2)}) collective-permute-start(bf16[2,128,512]{2,1,0:T(8,128)(2,1)S(1)} %add_convert_fusion.6), channel_id=1, source_target_pairs={{0,16},{1,17},{2,18},{3,19},{4,20},{5,21},{6,22},{7,23},{8,24},{9,... | collective-permute-start | bytes 786440 | tf_op jit(solution)/shard_map/ppermute | solution.py:374
  211.9 12.0 %collective-permute-start.33 = (bf16[2,128,512]{2,1,0:T(8,128)(2,1)S(1)}, bf16[2,128,512]{2,1,0:T(8,128)(2,1)S(1)}, u32[]{:S(2)}, u32[]{:S(2)}) collective-permute-start(bf16[2,128,512]{2,1,0:T(8,128)(2,1)S(1)} %add_convert_fusion.5), channel_id=1, source_target_pairs={{0,8},{1,9},{2,10},{3,11},{4,12},{5,13},{6,14},{7,15},{8,0},{9,1},... | collective-permute-start | bytes 786440 | tf_op jit(solution)/shard_map/ppermute | solution.py:374
  218.4 5.6 %collective-permute-start.28 = (bf16[1,128,512]{2,1,0:T(8,128)(2,1)S(1)}, bf16[1,128,512]{2,1,0:T(8,128)(2,1)S(1)}, u32[]{:S(2)}, u32[]{:S(2)}) collective-permute-start(bf16[1,128,512]{2,1,0:T(8,128)(2,1)S(1)} %add_convert_fusion.9), channel_id=1, source_target_pairs={{0,4},{1,3},{2,6},{3,1},{4,0},{5,7},{6,2},{7,5},{8,12},{9,11},{10,... | collective-permute-start | bytes 393224 | tf_op jit(solution)/shard_map/ppermute | solution.py:374
  223.9 8.2 %collective-permute-start.34 = (bf16[1,128,512]{2,1,0:T(8,128)(2,1)S(1)}, bf16[1,128,512]{2,1,0:T(8,128)(2,1)S(1)}, u32[]{:S(2)}, u32[]{:S(2)}) collective-permute-start(bf16[1,128,512]{2,1,0:T(8,128)(2,1)S(1)} %add_convert_fusion.8), channel_id=1, source_target_pairs={{0,16},{1,17},{2,18},{3,19},{4,20},{5,21},{6,22},{7,23},{8,24},{9,... | collective-permute-start | bytes 393224 | tf_op jit(solution)/shard_map/ppermute | solution.py:374
